TPU v7x, 32 devices: a whole 2x2x4 slice. The times are simulated.
32 devices in a mesh: dp: 4 (over x, core), fsdp: 8 (over z, y).
Axes of the slice: x: 2, y: 2, z: 4, core: 2. Of those that a mesh axis runs over, the one named last changes fastest.
Arguments:
- queries: bfloat16 [8, 256, 4096], P('fsdp', 'dp'), may hold values from -0.21875 to 0.21875
- candidates: bfloat16 [8, 4, 80, 4096], P('fsdp', 'dp'), may hold values from -0.21875 to 0.21875
- positives: int32 [8, 256], P('fsdp', 'dp'), may hold values from 0 to 255, as said below
- hard_blocks: int32 [8, 256], P('fsdp', 'dp'), may hold values from 0 to 3, as said below
- query_hidden: bfloat16 [8, 256, 4096], P('fsdp', 'dp'), may hold values from -6 to 6
- candidate_hidden: bfloat16 [8, 4, 80, 4096], P('fsdp', 'dp'), may hold values from -6 to 6
- adapter_down: bfloat16 [16, 4096], P(None, 'fsdp'), may hold values from -0.09375 to 0.09375
- adapter_up: bfloat16 [16, 4096], P(None, 'fsdp'), may hold values from -0.0234375 to 0.0234375
Outputs:
- question_derivative_vectors: bfloat16 [8, 256, 4096], P('fsdp', 'dp')
- candidate_grad_rows: bfloat16 [8, 4, 80, 4096], P('fsdp', 'dp')
- down_gradient: float32 [16, 4096], P(None, 'fsdp')
- up_gradient: float32 [16, 4096], P(None, 'fsdp')
Inputs may be any that keep to these rules, and one draw needn't show every extreme that they name: Within each group the positives are a permutation of the 256 passages. `hard_blocks`: within each group every block is named by some query.
All inputs are finite; a program needn't handle non-finite values.
Results may differ from a plain program's by a relative error of at most 0.012.
Values may be sent and summed in bfloat16 or wider, within the bound.
No kernel may reach another device: no remote copies, remote signals or barrier semaphores. Data moves between devices by JAX's collectives and lax.ppermute only.
A program may use at most 64 MiB of HBM per device.

v0:
```python
import jax
import jax.numpy as jnp
from jax import lax
from jax.sharding import PartitionSpec as P

sharpness_factor = 50.0
adapter_scale = 2.0


def merged(shard, axis, combine):
    everything = jax.tree.map(lambda part: lax.all_gather(part, axis), shard)
    first = jax.tree.map(lambda part: part[0], everything)

    def lap(k, so_far):
        return combine(so_far, jax.tree.map(lambda part: part[k], everything))

    return lax.fori_loop(1, lax.axis_size(axis), lap, first)


def pairing_matrix(left, right):
    return lax.dot_general(
        left, right, (((1,), (1,)), ((), ())), preferred_element_type=jnp.float32
    )


def flipped_pairing_matrix(left, right):
    return lax.dot_general(
        left, right, (((0,), (0,)), ((), ())), preferred_element_type=jnp.float32
    )


def combine_stats(earlier, later):
    larger = jnp.maximum(earlier[0], later[0])
    return (
        larger,
        earlier[1] * jnp.exp(earlier[0] - larger) + later[1] * jnp.exp(later[0] - larger),
    )


def on_device(
    queries,
    candidates,
    positives,
    hard_blocks,
    query_hidden,
    candidate_hidden,
    adapter_down,
    adapter_up,
):
    row_count = queries.shape[1]
    block_size = candidates.shape[2]
    model_width = queries.shape[2]
    position = lax.axis_index("dp")
    shard_question_vectors = queries[0]
    shard_document_vectors = candidates[0, 0]
    all_question_vectors, all_positives, all_hard = (
        lax.all_gather(queries, "dp", axis=1, tiled=True),
        lax.all_gather(positives, "dp", axis=1, tiled=True),
        lax.all_gather(hard_blocks, "dp", axis=1, tiled=True),
    )
    all_question_vectors = all_question_vectors[0]
    all_positives = all_positives[0]
    all_hard = all_hard[0]
    affinity_matrix = (
        pairing_matrix(all_question_vectors, shard_document_vectors) * sharpness_factor
    )
    columns = jnp.arange(block_size, dtype=jnp.int32)
    allowed = (columns[None, :] < row_count) | (all_hard[:, None] == position)
    masked = jnp.where(allowed, affinity_matrix, -jnp.inf)
    local_max = jnp.max(masked, axis=1)
    local_sum = jnp.sum(jnp.exp(masked - local_max[:, None]), axis=1)
    row_max, row_sum = merged((local_max, local_sum), "dp", combine_stats)
    log_total = row_max + jnp.log(row_sum)
    target = (all_positives[:, None] == position * row_count + columns[None, :]) & (
        columns[None, :] < row_count
    )
    normalized_exponent_shares = (
        jnp.exp(jnp.where(allowed, affinity_matrix - log_total[:, None], -jnp.inf))
        - target.astype(jnp.float32)
    ).astype(jnp.bfloat16)
    candidate_grad_rows = (
        flipped_pairing_matrix(normalized_exponent_shares, all_question_vectors) * sharpness_factor
    ).astype(jnp.bfloat16)
    own_logtotal = lax.dynamic_slice_in_dim(log_total, position * row_count, row_count)
    own_positives = positives[0]
    own_hard = hard_blocks[0]
    shard_piece = lax.all_gather(candidates, "dp", axis=1, tiled=True)
    piece_count = shard_piece.shape[1]
    merged_line_entries = shard_piece[0].reshape(piece_count * block_size, model_width)
    interim_outcome = pairing_matrix(shard_question_vectors, merged_line_entries) * sharpness_factor
    spots = jnp.arange(piece_count * block_size, dtype=jnp.int32)
    owners = spots // block_size
    slots = spots % block_size
    keep_mask = (slots[None, :] < row_count) | (own_hard[:, None] == owners[None, :])
    hit_mask = (own_positives[:, None] == (owners * row_count + slots)[None, :]) & (
        slots[None, :] < row_count
    )
    coefficients = (
        jnp.exp(jnp.where(keep_mask, interim_outcome - own_logtotal[:, None], -jnp.inf))
        - hit_mask.astype(jnp.float32)
    ).astype(jnp.bfloat16)
    aggregate_amount = jnp.dot(
        coefficients, merged_line_entries, preferred_element_type=jnp.float32
    )
    question_derivative_vectors = (aggregate_amount * sharpness_factor).astype(jnp.bfloat16)
    down_full, up_full = (
        lax.all_gather(adapter_down, "fsdp", axis=1, tiled=True),
        lax.all_gather(adapter_up, "fsdp", axis=1, tiled=True),
    )
    hidden_rows = [query_hidden[0], candidate_hidden[0, 0]]
    gradient_rows = [question_derivative_vectors, candidate_grad_rows]
    up_terms = jnp.zeros(down_full.shape, jnp.float32)
    down_terms = jnp.zeros(down_full.shape, jnp.float32)
    for hidden, gradient in zip(hidden_rows, gradient_rows):
        low = pairing_matrix(hidden, down_full).astype(jnp.bfloat16)
        back = pairing_matrix(gradient, up_full).astype(jnp.bfloat16)
        up_terms = up_terms + flipped_pairing_matrix(low, gradient)
        down_terms = down_terms + flipped_pairing_matrix(back, hidden)
    stacked = jnp.stack([down_terms, up_terms], axis=0)
    shard_terms = lax.psum_scatter(
        stacked.astype(jnp.bfloat16), "fsdp", scatter_dimension=2, tiled=True
    ).astype(jnp.float32)
    reduced = lax.psum(shard_terms, "dp")
    reduced = reduced * adapter_scale
    return (
        question_derivative_vectors[None],
        candidate_grad_rows[None, None],
        reduced[0],
        reduced[1],
    )


def solution(mesh):
    placed = (
        P("fsdp", "dp", None),
        P("fsdp", "dp", None, None),
        P("fsdp", "dp"),
        P("fsdp", "dp"),
        P("fsdp", "dp", None),
        P("fsdp", "dp", None, None),
        P(None, "fsdp"),
        P(None, "fsdp"),
    )
    return jax.shard_map(
        on_device,
        mesh=mesh,
        in_specs=placed,
        out_specs=(
            P("fsdp", "dp", None),
            P("fsdp", "dp", None, None),
            P(None, "fsdp"),
            P(None, "fsdp"),
        ),
        check_vma=False,
    )
```

profile of v0, /device:TPU:0, one launch (start us, length us, event | category | flops | bytes accessed | tf_op | source)
XLA Modules:
  0.0 188.9 jit_solution(5170827497129366919)
XLA Ops:
  7.2 0.0 copy-start
  7.2 0.0 all-gather.9.cloned.1.call-start
  7.2 0.7 all-gather.9.cloned.1.call-update
  7.9 0.0 all-gather.7.cloned.1.call-start
  8.0 0.7 all-gather.7.cloned.1.call-update
  8.7 0.0 reduce-scatter.2.cloned.1.call-start
  8.7 1.2 dynamic-slice
  10.6 0.8 bitcast_dynamic-update-slice_fusion
  11.4 0.7 bitcast_dynamic-update-slice_fusion.1
  12.1 6.9 %all-reduce.2 = (s32[256]{0:T(256)S(1)}, s32[256]{0:T(256)}) all-reduce(s32[256]{0:T(256)S(1)} %bitcast_dynamic-update-slice_fusion.1, s32[256]{0:T(256)S(1)} %bitcast_dynamic-update-slice_fusion), channel_id=1, replica_groups=mesh['dp'=4,'fsdp'=8] {'dp'}, use_global_device_ids=true, to_apply=%add | all-reduce | flops 512 | bytes 4096
  19.0 33.1 %all_gather.38 = bf16[16,4096]{1,0:T(8,128)(2,1)} all-gather(bf16[16,512]{1,0:T(8,128)(2,1)} %param.17), channel_id=1, replica_groups=mesh['dp'=4,'fsdp'=8] {'fsdp'}, dimensions={1}, use_global_device_ids=true | all-gather | bytes 147456 | tf_op jit(solution)/shard_map/all_gather | solution.py:108
  52.2 30.7 %all_gather.39 = bf16[16,4096]{1,0:T(8,128)(2,1)S(1)} all-gather(bf16[16,512]{1,0:T(8,128)(2,1)} %param.16), channel_id=1, replica_groups=mesh['dp'=4,'fsdp'=8] {'fsdp'}, dimensions={1}, use_global_device_ids=true | all-gather | bytes 147456 | tf_op jit(solution)/shard_map/all_gather | solution.py:107
  82.9 0.6 fusion.55
  83.5 0.5 iota_add_fusion
  84.0 0.0 all-gather.9.cloned.1.call-done
  84.0 0.0 copy-start.1
  84.1 2.6 %fusion.36 = (f32[256]{0:T(256)S(1)}, f32[256,80]{0,1:T(8,128)S(1)}) fusion(pred[256]{0:T(512)(128)(4,1)S(1)} %broadcast_compare_fusion, pred[80]{0:T(512)(128)(4,1)S(1)} %iota_compare_fusion, bf16[1,1,80,4096]{3,2,1,0:T(8,128)(2,1)} %param.11, bf16[1,256,4096]{2,1,0:T(8,128)(2,1)} %all-gather.9.cloned.1.call-done), kind=kOutput, calls=%fused_computation.47 | convolution fusion | flops 167853824 | bytes 2835792 | tf_op jit(solution)/shard_map/dot_general | solution.py:21
  86.7 0.0 copy-start.6
  86.7 0.6 copy-done.6
  87.3 0.1 exponential_reduce_fusion
  87.4 5.1 %all-gather.3 = f32[4,1,256]{2,1,0:T(1,128)S(1)} all-gather(f32[1,1,256]{2,1,0:T(1,128)S(1)} %bitcast.84), channel_id=3, replica_groups=mesh['dp'=4,'fsdp'=8] {'dp'}, dimensions={0}, use_global_device_ids=true | all-gather | bytes 5120 | tf_op jit(solution)/shard_map/all_gather | solution.py:11
  92.5 5.1 %all-gather.2 = f32[4,1,256]{2,1,0:T(1,128)S(1)} all-gather(f32[1,1,256]{2,1,0:T(1,128)S(1)} %bitcast.83), channel_id=2, replica_groups=mesh['dp'=4,'fsdp'=8] {'dp'}, dimensions={0}, use_global_device_ids=true | all-gather | bytes 5120 | tf_op jit(solution)/shard_map/all_gather | solution.py:11
  97.6 0.1 while.17
  97.7 0.6 dynamic_slice.23
  98.3 0.0 copy-done.1
  98.3 1.5 fusion
  99.8 0.0 copy-start.2
  99.8 0.0 all-gather.7.cloned.1.call-done
  99.8 0.0 copy-start.4
  99.8 0.0 copy-start.5
  99.9 5.2 %fusion.1 = bf16[64,4096]{1,0:T(8,128)(2,1)S(1)} fusion(bf16[320,4096]{1,0:T(8,128)(2,1)} %bitcast.73, bf16[1,64,4096]{2,1,0:T(8,128)(2,1)} %param.10, s32[320]{0:T(512)S(1)} %get-tuple-element.160, f32[64]{0:T(128)} %dynamic_slice.23, s32[320]{0:T(512)S(1)} %get-tuple-element.159, s32[64]{0:T(128)} %bitcast.86, s32[64]{0:T(128)} %bitcast.85, ...), kind=kOutput, calls=%fused_computation.6 | convolution fusion | flops 336273408 | bytes 3673664 | tf_op jit(solution)/shard_map/dot_general | solution.py:102
  105.0 0.0 copy-done.4
  105.1 0.0 copy-done.5
  105.1 0.0 copy-start.3
  105.1 0.6 fusion.17
  105.7 0.6 fusion.18
  106.3 0.0 copy-done
  106.3 0.7 fusion.5
  107.1 0.0 copy-done.2
  107.1 0.0 copy-done.3
  107.1 0.7 fusion.4
  107.8 0.7 pad_maximum_fusion
  108.5 0.0 reduce-scatter.2.cloned.1.call-update
  108.5 62.1 %reduce-scatter.2.cloned.1.call-done = bf16[2,16,512]{2,1,0:T(8,128)(2,1)} async-done(((bf16[2,16,4096]{2,1,0:T(8,128)(2,1)}), bf16[2,16,512]{2,1,0:T(8,128)(2,1)}) %reduce-scatter.2.cloned.1.call-update) | async-done | bytes 32784 | tf_op jit(solution)/shard_map/reduce_scatter | solution.py:120
  170.6 11.2 %all-reduce.4 = f32[2,16,512]{2,1,0:T(8,128)S(1)} all-reduce(bf16[2,16,512]{2,1,0:T(8,128)(2,1)} %reduce-scatter.2.cloned.1.call-done), channel_id=1, replica_groups=mesh['dp'=4,'fsdp'=8] {'dp'}, use_global_device_ids=true, to_apply=%region_5.6 | all-reduce | flops 16384 | bytes 98304 | tf_op jit(solution)/shard_map/psum | solution.py:123
  181.8 0.6 slice_bitcast_fusion
  (17 shorter events, 0.1 us)
Async XLA Ops:
  7.2 99.2 %copy-start = (bf16[1,1,80,4096]{3,2,1,0:T(8,128)(2,1)S(1)}, bf16[1,1,80,4096]{3,2,1,0:T(8,128)(2,1)}, u32[]{:S(2)}) copy-start(bf16[1,1,80,4096]{3,2,1,0:T(8,128)(2,1)} %param.15) | copy-start | bytes 1966084
  7.2 76.9 %all-gather.9.cloned.1.call-start = ((), (), s32[]{:S(2)}) async-start(), calls=%async_computation.2 | async-start | bytes 2621440 | tf_op jit(solution)/shard_map/all_gather | solution.py:57
  7.9 91.9 %all-gather.7.cloned.1.call-start = ((), (), s32[]{:S(2)}) async-start(), calls=%async_computation.1 | async-start | bytes 3276800 | tf_op jit(solution)/shard_map/all_gather | solution.py:87
  8.7 161.9 %reduce-scatter.2.cloned.1.call-start = ((), (), s32[]{:S(2)}) async-start(), calls=%async_computation.3 | async-start | bytes 294912 | tf_op jit(solution)/shard_map/reduce_scatter | solution.py:120
  84.0 14.3 %copy-start.1 = (bf16[1,256,4096]{2,1,0:T(8,128)(2,1)S(1)}, bf16[1,256,4096]{2,1,0:T(8,128)(2,1)}, u32[]{:S(2)}) copy-start(bf16[1,256,4096]{2,1,0:T(8,128)(2,1)} %all-gather.9.cloned.1.call-done) | copy-start | bytes 6291460
  86.7 0.6 copy-start.6
  99.8 7.3 %copy-start.2 = (bf16[80,4096]{1,0:T(8,128)(2,1)}, bf16[80,4096]{1,0:T(8,128)(2,1)S(1)}, u32[]{:S(2)}) copy-start(bf16[80,4096]{1,0:T(8,128)(2,1)S(1)} %fusion) | copy-start | bytes 1966084
  99.8 5.2 %copy-start.4 = (bf16[1,64,4096]{2,1,0:T(8,128)(2,1)S(1)}, bf16[1,64,4096]{2,1,0:T(8,128)(2,1)}, u32[]{:S(2)}) copy-start(bf16[1,64,4096]{2,1,0:T(8,128)(2,1)} %param.14) | copy-start | bytes 1572868
  99.8 5.2 %copy-start.5 = (bf16[16,4096]{1,0:T(8,128)(2,1)S(1)}, bf16[16,4096]{1,0:T(8,128)(2,1)}, u32[]{:S(2)}) copy-start(bf16[16,4096]{1,0:T(8,128)(2,1)} %all_gather.38) | copy-start | bytes 393220
  105.1 2.0 %copy-start.3 = (bf16[64,4096]{1,0:T(8,128)(2,1)}, bf16[64,4096]{1,0:T(8,128)(2,1)S(1)}, u32[]{:S(2)}) copy-start(bf16[64,4096]{1,0:T(8,128)(2,1)S(1)} %fusion.1) | copy-start | bytes 1572868
Sparse Core Ops, SparseCore 0:
  9.6 25.2 all-gather.8
  36.4 25.5 all-gather.6
  108.6 61.8 reduce-scatter.1
where the time goes:
time: 189 us
  blocking collectives  92.1 us (49%)
  waiting for transfers between devices  63.5 us (34%)
  between operations  14.6 us (8%)
  matrix products  12 us (6%)
  local copies, waits for them, and re-layouts  4.65 us (2%)
  other arithmetic  2.02 us (1%)
    reduce_scatter x1, waiting for transfers between devices, on_device(): lax.psum_scatter(stacked.astype(jnp.bfloat16), 'fsdp', scatter_dimension=...  62.1 us
    all_gather x1, blocking collectives, on_device(): lax.all_gather(adapter_up, 'fsdp', axis=1, tiled=True)  33.1 us
    all_gather x1, blocking collectives, on_device(): lax.all_gather(adapter_down, 'fsdp', axis=1, tiled=True)  30.7 us
    psum x1, blocking collectives, on_device(): reduced = lax.psum(shard_terms, 'dp')  11.2 us
    all_gather x2, blocking collectives, merged(): everything = jax.tree.map(lambda part: lax.all_gather(part, axis), shard)  10.1 us
    unnamed x1, blocking collectives  6.91 us
    dot_general x1, matrix products, on_device(): jnp.dot(coefficients, merged_line_entries, preferred_element_type=jnp.flo...  5.19 us
    dot_general x5, matrix products, flipped_pairing_matrix(): lax.dot_general(left, right, (((0,), (0,)), ((), ())), preferred_element_...  4.13 us
  transfers between devices with their start and end apart: 3, of which 1 were waited for; matrix products, arithmetic and copies ran while one was open for 5% of the time, Pallas kernels for 0%

commit v1 on v0

v1 whole, which is shorter than its diff:
```python
import functools

import jax
import jax.numpy as jnp
from jax import lax
from jax.experimental import pallas as pl
from jax.experimental.pallas import tpu as pltpu
from jax.sharding import PartitionSpec as P

sharpness_factor = 50.0
adapter_scale = 2.0
STEP = 512
MAX, SUM, POSITIVE, HARD, BODY = 0, 1, 2, 3, 8

f32 = jnp.float32
bf16 = jnp.bfloat16


def dot(left, right, left_dim, right_dim):
    return lax.dot_general(
        left, right, (((left_dim,), (right_dim,)), ((), ())), preferred_element_type=f32
    )


def dot_wide(left, right, left_dim, right_dim):
    high = left.astype(bf16)
    low = (left - high.astype(f32)).astype(bf16)
    return dot(high, right, left_dim, right_dim) + dot(low, right, left_dim, right_dim)


def layout(position, block, shape):
    row = lax.broadcasted_iota(jnp.int32, shape, 0)
    own = row < block
    return jnp.where(own, position, position ^ 1), jnp.where(own, row, row - block)


def allowed(owner, slot, hard, rows):
    return (slot < rows) | (hard.astype(jnp.int32) == owner)


def hits(owner, slot, positive, rows):
    return (slot < rows) & (positive.astype(jnp.int32) == owner * rows + slot)


def merge(stats):
    top = functools.reduce(jnp.maximum, [m for m, _ in stats])
    return top + jnp.log(sum(s * jnp.exp(m - top) for m, s in stats))


def columns(ref, at, width):
    return ref[:, pl.ds(pl.multiple_of(at * width, width), width)]


def scores_kernel(place, c_own, c_sib, q_own, q_sib, positives, hard, scores, stats):
    block, rows = c_own.shape[0], q_own.shape[0]

    def step(i, total):
        c = jnp.concatenate([columns(c_own, i, STEP), columns(c_sib, i, STEP)], 0)
        q = jnp.concatenate([columns(q_own, i, STEP), columns(q_sib, i, STEP)], 0)
        return total + dot(c, q, 1, 1)

    total = lax.fori_loop(
        0, c_own.shape[1] // STEP, step, jnp.zeros((2 * block, 2 * rows), f32), unroll=True
    )
    total = total * sharpness_factor
    scores[...] = total
    mine = total[:, :rows]
    owner, slot = layout(place[0], block, mine.shape)
    mine = jnp.where(allowed(owner, slot, hard[...], rows), mine, -jnp.inf)
    top = jnp.max(mine, axis=0, keepdims=True)
    stats[...] = jnp.zeros_like(stats)
    stats[MAX : MAX + 1] = top
    stats[SUM : SUM + 1] = jnp.sum(jnp.exp(mine - top), axis=0, keepdims=True)
    stats[POSITIVE : POSITIVE + 1] = positives[...].astype(f32)
    stats[HARD : HARD + 1] = hard[...].astype(f32)


def adapter_slice(place, mine, got, at):
    here = place[1] ^ at
    a, b = mine[here], got[here]
    even = (place[0] & 1) == 0
    return jnp.where(even, a, b), jnp.where(even, b, a)


def low_kernel(place, maps, other, hq, hc, c_own, c_sib, stats, message, low_c, c_up):
    shards, rank, width = maps.shape
    rows, block = hq.shape[0], hc.shape[0]

    def step(i, so_far):
        down, up = adapter_slice(place, maps, other, i)
        c = jnp.concatenate([columns(c_own, i, width), columns(c_sib, i, width)], 0)
        return (
            so_far[0] + dot(down, columns(hq, i, width), 1, 1),
            so_far[1] + dot(down, columns(hc, i, width), 1, 1),
            so_far[2] + dot(up, c, 1, 1),
        )

    sums = lax.fori_loop(
        0, shards, step, tuple(jnp.zeros((rank, n), f32) for n in (rows, block, 2 * block))
    )
    message[:BODY] = stats[...]
    message[BODY:] = sums[0].astype(bf16).astype(f32)
    low_c[...] = sums[1].astype(bf16)
    c_up[...] = sums[2]


def partner_kernel(place, c_own, c_sib, q, message, c_up, answer, w_own, w_sib, low_w):
    block, rows = c_own.shape[0], q.shape[0]

    def step(i, total):
        c = jnp.concatenate([columns(c_own, i, STEP), columns(c_sib, i, STEP)], 0)
        return total + dot(c, columns(q, i, STEP), 1, 1)

    total = lax.fori_loop(
        0, c_own.shape[1] // STEP, step, jnp.zeros((2 * block, rows), f32), unroll=True
    )
    owner, slot = layout(place[0], block, total.shape)
    keep = allowed(owner, slot, message[HARD : HARD + 1], rows)
    total = jnp.where(keep, total * sharpness_factor, -jnp.inf)
    top = jnp.max(total, axis=0, keepdims=True)
    share = jnp.sum(jnp.exp(total - top), axis=0, keepdims=True)
    answer[...] = jnp.zeros_like(answer)
    answer[MAX : MAX + 1] = top
    answer[SUM : SUM + 1] = share
    log_total = merge([(message[MAX : MAX + 1], message[SUM : SUM + 1]), (top, share)])
    hit = hits(owner, slot, message[POSITIVE : POSITIVE + 1], rows)
    weights = (jnp.exp(total - log_total) - hit.astype(f32)).astype(bf16)
    answer[BODY:] = dot_wide(c_up[...], weights, 1, 0) * sharpness_factor
    w_own[...] = weights[:block]
    w_sib[...] = weights[block:]
    low_w[...] = dot(message[BODY:].astype(bf16), weights, 1, 1) * sharpness_factor


def share_kernel(w_own, w_sib, c_own, c_sib, share):
    weights = jnp.concatenate([w_own[...], w_sib[...]], 0)
    for i in range(c_own.shape[1] // STEP):
        c = jnp.concatenate([columns(c_own, i, STEP), columns(c_sib, i, STEP)], 0)
        share[:, i * STEP : (i + 1) * STEP] = (dot(weights, c, 0, 0) * sharpness_factor).astype(bf16)


def final_kernel(w_own, w_sib, c_own, c_sib, *rest):
    shares, out = rest[:-1], rest[-1]
    weights = jnp.concatenate([w_own[...], w_sib[...]], 0)
    for i in range(c_own.shape[1] // STEP):
        c = jnp.concatenate([columns(c_own, i, STEP), columns(c_sib, i, STEP)], 0)
        total = dot(weights, c, 0, 0) * sharpness_factor
        for share in shares:
            total = total + share[:, i * STEP : (i + 1) * STEP].astype(f32)
        out[:, i * STEP : (i + 1) * STEP] = total.astype(bf16)


def sums_kernel(partners, place, *refs):
    (c_own, c_sib, q_own, q_sib, hq, hc, maps, other, scores, own, sib, low_c, c_up), refs = refs[:13], refs[13:]
    answers, refs = refs[:partners], refs[partners:]
    sib_answers, refs = refs[:partners], refs[partners:]
    far_q, refs = refs[:partners], refs[partners:]
    far_q_sib, refs = refs[:partners], refs[partners:]
    far_w, refs = refs[:partners], refs[partners:]
    far_w_sib, refs = refs[:partners], refs[partners:]
    far_low, refs = refs[:partners], refs[partners:]
    grad, w_own, w_sib, keep, send, up_terms = refs
    block, rows = c_own.shape[0], q_own.shape[0]
    shards, rank, width = maps.shape

    def stats_of(ref):
        return ref[MAX : MAX + 1], ref[SUM : SUM + 1]

    def both(at):
        return jnp.concatenate([own[at : at + 1], sib[at : at + 1]], 1)

    log_total = jnp.concatenate(
        [
            merge([stats_of(own)] + [stats_of(a) for a in answers]),
            merge([stats_of(sib)] + [stats_of(a) for a in sib_answers]),
        ],
        1,
    )
    owner, slot = layout(place[0], block, scores.shape)
    kept = allowed(owner, slot, both(HARD), rows)
    hit = hits(owner, slot, both(POSITIVE), rows)
    weights = jnp.exp(jnp.where(kept, scores[...] - log_total, -jnp.inf)) - hit.astype(f32)
    weights = weights.astype(bf16)
    mine = weights[:, :rows]
    w_own[...] = mine[:block]
    w_sib[...] = mine[block:]
    low_w = dot(own[BODY:].astype(bf16), mine, 1, 1) * sharpness_factor
    for ref in far_low:
        low_w = low_w + ref[...]
    back_q = dot_wide(c_up[...], mine, 1, 0) * sharpness_factor
    for ref in answers:
        back_q = back_q + ref[BODY:]
    back_q = back_q.astype(bf16)
    all_weights = jnp.concatenate(
        [weights[:block]] + [w[...] for w in far_w] + [w[...] for w in far_w_sib], 1
    )
    all_queries = [q_own, q_sib] + list(far_q) + list(far_q_sib)

    def first(i, back_c):
        _, up = adapter_slice(place, maps, other, i)
        c = jnp.concatenate([columns(c_own, i, width), columns(c_sib, i, width)], 0)
        q = jnp.concatenate([columns(q, i, width) for q in all_queries], 0)
        rows_here = (dot(all_weights, q, 1, 0) * sharpness_factor).astype(bf16)
        grad[:, pl.ds(pl.multiple_of(i * width, width), width)] = rows_here
        up_terms[i] = dot_wide(low_w, c, 1, 0) + dot(low_c[...], rows_here, 1, 0)
        return back_c + dot(up, rows_here, 1, 1)

    back_c = lax.fori_loop(0, shards, first, jnp.zeros((rank, block), f32)).astype(bf16)
    even = (place[0] & 1) == 0

    def second(i, carry):
        down = dot(back_q, columns(hq, i, width), 1, 0) + dot(back_c, columns(hc, i, width), 1, 0)
        up = up_terms[i]
        apart = place[1] ^ i
        slot = (apart & 1) * (shards // 2) + (apart >> 1)
        keep[slot] = jnp.where(even, down, up).astype(bf16)
        send[slot] = jnp.where(even, up, down).astype(bf16)
        return carry

    lax.fori_loop(0, shards, second, 0)


def call(kernel, outs, scratch=(), flops=10_000_000, moved=2_000_000):
    smem = pl.BlockSpec(memory_space=pltpu.SMEM)
    vmem = pl.BlockSpec(memory_space=pltpu.VMEM)

    def run(*args):
        return pl.pallas_call(
            kernel,
            out_shape=outs,
            in_specs=[smem if a.dtype == jnp.int32 and a.ndim == 1 else vmem for a in args],
            out_specs=jax.tree.map(lambda _: vmem, outs),
            scratch_shapes=list(scratch),
            compiler_params=pltpu.CompilerParams(vmem_limit_bytes=40 * 2**20),
            cost_estimate=pl.CostEstimate(flops=flops, bytes_accessed=moved, transcendentals=0),
        )(*args)

    return run


def shaped(shape, dtype=f32):
    return jax.ShapeDtypeStruct(shape, dtype)


def swap(array, axis, apart):
    size = lax.axis_size(axis)
    return lax.ppermute(array, axis, [(i, i ^ apart) for i in range(size)])


def bits_of(size):
    return [1 << b for b in range(size.bit_length() - 1)]


def on_device(
    queries, candidates, positives, hard_blocks, query_hidden, candidate_hidden, adapter_down, adapter_up
):
    q_own, c_own = queries[0], candidates[0, 0]
    hq, hc = query_hidden[0], candidate_hidden[0, 0]
    rows, width = q_own.shape
    block = c_own.shape[0]
    rank, shard_width = adapter_down.shape
    devices, shards = lax.axis_size("dp"), lax.axis_size("fsdp")
    position, shard = lax.axis_index("dp"), lax.axis_index("fsdp")
    place = jnp.stack([position, shard]).astype(jnp.int32)
    partners = list(range(2, devices, 2))
    even = (position & 1) == 0

    far_q = [swap(q_own, "dp", k) for k in partners]
    c_sib, q_sib = swap(c_own, "dp", 1), swap(q_own, "dp", 1)

    maps = jnp.where(even, adapter_down, adapter_up)[None]
    for bit in bits_of(shards):
        maps = jnp.concatenate([maps, swap(maps, "fsdp", bit)], 0)
    other_maps = swap(maps, "dp", 1)

    scores, stats = call(
        scores_kernel, (shaped((2 * block, 2 * rows)), shaped((BODY, rows)))
    )(place, c_own, c_sib, q_own, q_sib, positives, hard_blocks)
    message, low_c, c_up = call(
        low_kernel,
        (shaped((BODY + rank, rows)), shaped((rank, block), bf16), shaped((rank, 2 * block))),
    )(place, maps, other_maps, hq, hc, c_own, c_sib, stats)
    sib_message = swap(message, "dp", 1)
    far_messages = [swap(message, "dp", k) for k in partners]

    answers, sib_answers, far_w, far_w_sib, far_low, shares = [], [], [], [], [], []
    for k, q, far_message in zip(partners, far_q, far_messages):
        answer, w_own, w_sib, low_w = call(
            partner_kernel,
            (
                shaped((BODY + rank, rows)),
                shaped((block, rows), bf16),
                shaped((block, rows), bf16),
                shaped((rank, 2 * block)),
            ),
        )(place, c_own, c_sib, q, far_message, c_up)
        answers.append(swap(answer, "dp", k))
        sib_answers.append(swap(answer, "dp", k ^ 1))
        far_w.append(w_own)
        far_w_sib.append(swap(w_sib, "dp", 1))
        far_low.append(low_w)
        share = call(share_kernel, shaped((rows, width), bf16))(w_own, w_sib, c_own, c_sib)
        shares.append(swap(share, "dp", k))
    far_q_sib = [swap(q, "dp", 1) for q in far_q]

    grad, w_own, w_sib, keep, send = call(
        functools.partial(sums_kernel, len(partners)),
        (
            shaped((block, width), bf16),
            shaped((block, rows), bf16),
            shaped((block, rows), bf16),
            shaped((shards, rank, shard_width), bf16),
            shaped((shards, rank, shard_width), bf16),
        ),
        [pltpu.VMEM((shards, rank, shard_width), f32)],
    )(
        place, c_own, c_sib, q_own, q_sib, hq, hc, maps, other_maps, scores, message, sib_message,
        low_c, c_up, *answers, *sib_answers, *far_q, *far_q_sib, *far_w, *far_w_sib, *far_low,
    )
    question = call(final_kernel, shaped((rows, width), bf16))(w_own, w_sib, c_own, c_sib, *shares)

    terms = keep.astype(f32) + swap(send, "dp", 1).astype(f32)
    for bit in bits_of(shards)[:1] + bits_of(shards)[:0:-1]:
        half = terms.shape[0] // 2
        terms = terms[:half] + swap(terms[half:].astype(bf16), "fsdp", bit).astype(f32)
    terms = terms[0]
    for bit in bits_of(devices)[1:]:
        terms = terms + swap(terms, "dp", bit)
    terms = terms * adapter_scale
    others = swap(terms, "dp", 1)
    return (
        question[None],
        grad[None, None],
        jnp.where(even, terms, others),
        jnp.where(even, others, terms),
    )


def solution(mesh):
    placed = (
        P("fsdp", "dp", None),
        P("fsdp", "dp", None, None),
        P("fsdp", "dp"),
        P("fsdp", "dp"),
        P("fsdp", "dp", None),
        P("fsdp", "dp", None, None),
        P(None, "fsdp"),
        P(None, "fsdp"),
    )
    return jax.shard_map(
        on_device,
        mesh=mesh,
        in_specs=placed,
        out_specs=(
            P("fsdp", "dp", None),
            P("fsdp", "dp", None, None),
            P(None, "fsdp"),
            P(None, "fsdp"),
        ),
        check_vma=False,
    )
```

time: 189 us -> 73.8 us (0.39)
  blocking collectives: 92.1 us -> 0 us
  waiting for transfers between devices: 63.5 us -> 37.5 us
  starting transfers between devices: 0.11 us -> 20.6 us
  between operations: 14.6 us -> 0.78 us
  matrix products: 12 us -> 0 us
  Pallas kernels: 0 us -> 11.3 us
  local copies, waits for them, and re-layouts: 4.65 us -> 1.82 us
    all_gather x4 -> x0, blocking collectives: 74 us -> none  [the longest x1 33.1 us: on_device(): lax.all_gather(adapter_up, 'fsdp', axis=1, tiled=True)]
    reduce_scatter x1 -> x0, waiting for transfers between devices: 62.1 us -> none  [on_device(): lax.psum_scatter(stacked.astype(jnp.bfloat16), 'fsdp', scatter_dimension=...]
    ppermute x0 -> x20, waiting for transfers between devices: none -> 37.5 us  [swap(): return lax.ppermute(array, axis, [(i, i ^ apart) for i in range(size)])]
    ppermute x0 -> x20, starting transfers between devices: none -> 20.6 us  [swap(): return lax.ppermute(array, axis, [(i, i ^ apart) for i in range(size)])]
    dot_general x7 -> x0, matrix products: 12 us -> none  [the longest x1 5.19 us: on_device(): jnp.dot(coefficients, merged_line_entries, preferred_element_type=jnp.flo...]
    pallas_call x0 -> x6, Pallas kernels: none -> 11.3 us  [run(): pl.pallas_call(kernel, out_shape=outs, in_specs=[smem if a.dtype == jnp.i...]
    psum x1 -> x0, blocking collectives: 11.2 us -> none  [on_device(): reduced = lax.psum(shard_terms, 'dp')]
    unnamed x1 -> x0, blocking collectives: 6.91 us -> none
  transfers between devices with their start and end apart: 3 -> 20, of which waited for: 1 -> 11; matrix products, arithmetic and copies ran while one was open for 5% -> 1% of each run, Pallas kernels for 0% -> 8%
where the time goes in v1:
time: 73.8 us; the launch traced here: 73.5 us
  waiting for transfers between devices  37.5 us (51%)
  starting transfers between devices  20.6 us (28%)
  Pallas kernels  11.3 us (15%)
  local copies, waits for them, and re-layouts  1.82 us (2%)
  other arithmetic  1.53 us (2%)
  between operations  0.78 us (1%)
    ppermute x20, waiting for transfers between devices, swap(): return lax.ppermute(array, axis, [(i, i ^ apart) for i in range(size)])  37.5 us
    ppermute x20, starting transfers between devices, swap(): return lax.ppermute(array, axis, [(i, i ^ apart) for i in range(size)])  20.6 us
    pallas_call x6, Pallas kernels, run(): pl.pallas_call(kernel, out_shape=outs, in_specs=[smem if a.dtype == jnp.i...  11.3 us
    unnamed x14, local copies, waits for them, and re-layouts  1.79 us
  transfers between devices with their start and end apart: 20, of which 11 were waited for; matrix products, arithmetic and copies ran while one was open for 1% of the time, Pallas kernels for 8%

profile of v1, /device:TPU:0, one launch (start us, length us, event | category | flops | bytes accessed | tf_op | source)
XLA Modules:
  0.0 73.5 jit_solution(567372694045090394)
XLA Ops:
  0.6 0.0 copy-start.3
  0.6 3.0 %collective-permute-start.7 = (bf16[64,4096]{1,0:T(8,128)(2,1)}, bf16[64,4096]{1,0:T(8,128)(2,1)S(1)}, u32[]{:S(2)}, u32[]{:S(2)}) collective-permute-start(bf16[64,4096]{1,0:T(8,128)(2,1)} %bitcast.21), channel_id=1, source_target_pairs={{0,16},{8,24},{16,0},{24,8},{1,17},{9,25},{17,1},{25,9},{2,18},{10... | collective-permute-start | bytes 1572872 | tf_op jit(solution)/shard_map/ppermute | solution.py:246
  3.6 0.0 collective-permute-start
  3.6 0.7 select_bitcast_fusion
  4.4 1.5 %collective-permute-start.2 = (bf16[1,16,512]{2,1,0:T(8,128)(2,1)S(1)}, bf16[1,16,512]{2,1,0:T(8,128)(2,1)S(1)}, u32[]{:S(2)}, u32[]{:S(2)}) collective-permute-start(bf16[1,16,512]{2,1,0:T(8,128)(2,1)S(1)} %select_bitcast_fusion), channel_id=1, source_target_pairs={{0,1},{1,0},{2,3},{3,2},{4,5},{5,4},{6,7},{7,6},{8,9},{9,8},{10,11... | collective-permute-start | bytes 49160 | tf_op jit(solution)/shard_map/ppermute | solution.py:246
  5.9 0.2 collective-permute-start.1
  6.1 9.7 %collective-permute-done.7.q.refs_15_ = bf16[64,4096]{1,0:T(8,128)(2,1)S(1)} collective-permute-done((bf16[64,4096]{1,0:T(8,128)(2,1)}, bf16[64,4096]{1,0:T(8,128)(2,1)S(1)}, u32[]{:S(2)}, u32[]{:S(2)}) %collective-permute-start.7) | collective-permute-done | bytes 524320 | tf_op jit(solution)/shard_map/ppermute | solution.py:246
  15.8 0.0 collective-permute-start.11
  15.8 0.0 collective-permute-done.2
  15.8 1.9 %collective-permute-start.3 = (bf16[2,16,512]{2,1,0:T(8,128)(2,1)S(1)}, bf16[2,16,512]{2,1,0:T(8,128)(2,1)S(1)}, u32[]{:S(2)}, u32[]{:S(2)}) collective-permute-start(bf16[2,16,512]{2,1,0:T(8,128)(2,1)S(1)} %pad_maximum_fusion.2), channel_id=1, source_target_pairs={{0,2},{1,3},{2,0},{3,1},{4,6},{5,7},{6,4},{7,5},{8,10},{9,11},{10,... | collective-permute-start | bytes 98312 | tf_op jit(solution)/shard_map/ppermute | solution.py:246
  17.7 2.1 %collective-permute-done.3 = bf16[2,16,512]{2,1,0:T(8,128)(2,1)S(1)} collective-permute-done((bf16[2,16,512]{2,1,0:T(8,128)(2,1)S(1)}, bf16[2,16,512]{2,1,0:T(8,128)(2,1)S(1)}, u32[]{:S(2)}, u32[]{:S(2)}) %collective-permute-start.3) | collective-permute-done | bytes 32800 | tf_op jit(solution)/shard_map/ppermute | solution.py:246
  19.8 2.9 %collective-permute-start.4 = (bf16[4,16,512]{2,1,0:T(8,128)(2,1)S(1)}, bf16[4,16,512]{2,1,0:T(8,128)(2,1)S(1)}, u32[]{:S(2)}, u32[]{:S(2)}) collective-permute-start(bf16[4,16,512]{2,1,0:T(8,128)(2,1)S(1)} %pad_maximum_fusion.1), channel_id=1, source_target_pairs={{0,4},{1,5},{2,6},{3,7},{4,0},{5,1},{6,2},{7,3},{8,12},{9,13},{10,... | collective-permute-start | bytes 196616 | tf_op jit(solution)/shard_map/ppermute | solution.py:246
  22.7 2.7 %collective-permute-done.4 = bf16[4,16,512]{2,1,0:T(8,128)(2,1)S(1)} collective-permute-done((bf16[4,16,512]{2,1,0:T(8,128)(2,1)S(1)}, bf16[4,16,512]{2,1,0:T(8,128)(2,1)S(1)}, u32[]{:S(2)}, u32[]{:S(2)}) %collective-permute-start.4) | collective-permute-done | bytes 65568 | tf_op jit(solution)/shard_map/ppermute | solution.py:246
  25.4 0.1 collective-permute-start.5
  25.5 0.0 copy-start.5
  25.5 0.0 copy-start.6
  25.5 0.1 pad_add_fusion.place
  25.6 0.0 collective-permute-done.1.q_sib.refs_3_
  25.6 0.0 collective-permute-done.c_sib.refs_1_
  25.6 0.0 copy-done.3
  25.6 0.5 copy-done.5
  26.1 0.0 copy-done.6
  26.1 0.0 copy-start
  26.1 1.1 %copy-done = bf16[1,1,80,4096]{3,2,1,0:T(8,128)(2,1)S(1)} copy-done((bf16[1,1,80,4096]{3,2,1,0:T(8,128)(2,1)S(1)}, bf16[1,1,80,4096]{3,2,1,0:T(8,128)(2,1)}, u32[]{:S(2)}) %copy-start) | copy-done | bytes 655384
  27.2 0.0 copy-start.2
  27.2 0.0 copy-start.4
  27.2 1.1 %shard_map.111 = (f32[160,128]{1,0:T(8,128)S(1)}, f32[8,64]{1,0:T(8,128)S(1)}) custom-call(s32[2]{0:T(128)S(1)} %pad_add_fusion.place, bf16[80,4096]{1,0:T(8,128)(2,1)S(1)} %bitcast.13, bf16[80,4096]{1,0:T(8,128)(2,1)S(1)} %collective-permute-done.c_sib.refs_1_, bf16[64,4096]{1,0:T(8,128)(2,1)S(1)} %bitcast.23, ...), custom_call_target="tpu_custom_call" | custom-call | flops 10000000 | bytes 2000000 | tf_op jit(solution)/shard_map/pallas_call | solution.py:227
  28.3 0.0 collective-permute-done.5.other.refs_7_
  28.3 0.0 copy-done.2
  28.4 0.1 copy-done.4
  28.5 2.1 %shard_map.112 = (f32[24,64]{1,0:T(8,128)S(1)}, bf16[16,80]{1,0:T(8,128)(2,1)S(1)}, f32[16,160]{1,0:T(8,128)S(1)}) custom-call(s32[2]{0:T(128)S(1)} %pad_add_fusion.place, bf16[8,16,512]{2,1,0:T(8,128)(2,1)S(1)} %pad_maximum_fusion.maps.refs_6_, bf16[8,16,512]{2,1,0:T(8,128)(2,1)S(1)} %collective-permute-done.5.other.refs_7_, bf16[64,4096]{1,0:T(8,128)(2,1)S(1)} %bitcast.25, ...), custom_call_target="tpu_custom_call" | custom-call | flops 10000000 | bytes 2000000 | tf_op jit(solution)/shard_map/pallas_call | solution.py:227
  30.6 1.6 %collective-permute-start.8 = (f32[24,64]{1,0:T(8,128)S(1)}, f32[24,64]{1,0:T(8,128)S(1)}, u32[]{:S(2)}, u32[]{:S(2)}) collective-permute-start(f32[24,64]{1,0:T(8,128)S(1)} %get-tuple-element.20.refs_9_), channel_id=1, source_target_pairs={{0,16},{8,24},{16,0},{24,8},{1,17},{9,25},{17,1},{25,9},{2,18},{10... | collective-permute-start | bytes 18440 | tf_op jit(solution)/shard_map/ppermute | solution.py:246
  32.1 2.2 %collective-permute-done.8.message = f32[24,64]{1,0:T(8,128)S(1)} collective-permute-done((f32[24,64]{1,0:T(8,128)S(1)}, f32[24,64]{1,0:T(8,128)S(1)}, u32[]{:S(2)}, u32[]{:S(2)}) %collective-permute-start.8) | collective-permute-done | bytes 6176 | tf_op jit(solution)/shard_map/ppermute | solution.py:246
  34.3 1.3 %shard_map.113 = (f32[24,64]{1,0:T(8,128)S(1)}, bf16[80,64]{1,0:T(8,128)(2,1)S(1)}, bf16[80,64]{1,0:T(8,128)(2,1)S(1)}, f32[16,160]{1,0:T(8,128)S(1)}) custom-call(s32[2]{0:T(128)S(1)} %pad_add_fusion.place, bf16[80,4096]{1,0:T(8,128)(2,1)S(1)} %bitcast.15, bf16[80,4096]{1,0:T(8,128)(2,1)S(1)} %collective-permute-done.c_sib.refs_1_, ...), custom_call_target="tpu_custom_call" | custom-call | flops 10000000 | bytes 2000000 | tf_op jit(solution)/shard_map/pallas_call | solution.py:227
  35.6 0.0 collective-permute-start.12
  35.7 0.5 collective-permute-start.6
  36.2 1.1 %collective-permute-start.10 = (f32[24,64]{1,0:T(8,128)S(1)}, f32[24,64]{1,0:T(8,128)S(1)}, u32[]{:S(2)}, u32[]{:S(2)}) collective-permute-start(f32[24,64]{1,0:T(8,128)S(1)} %get-tuple-element.23), channel_id=1, source_target_pairs={{0,24},{8,16},{16,8},{24,0},{1,25},{9,17},{17,9},{25,1},{2,26},{10... | collective-permute-start | bytes 18440 | tf_op jit(solution)/shard_map/ppermute | solution.py:246
  37.3 0.5 collective-permute-start.9
  37.9 0.0 collective-permute-done.6.refs_10_
  37.9 1.5 %collective-permute-done.10.refs_14_ = f32[24,64]{1,0:T(8,128)S(1)} collective-permute-done((f32[24,64]{1,0:T(8,128)S(1)}, f32[24,64]{1,0:T(8,128)S(1)}, u32[]{:S(2)}, u32[]{:S(2)}) %collective-permute-start.10) | collective-permute-done | bytes 6176 | tf_op jit(solution)/shard_map/ppermute | solution.py:246
  39.3 1.7 %collective-permute-done.9.refs_13_ = f32[24,64]{1,0:T(8,128)S(1)} collective-permute-done((f32[24,64]{1,0:T(8,128)S(1)}, f32[24,64]{1,0:T(8,128)S(1)}, u32[]{:S(2)}, u32[]{:S(2)}) %collective-permute-start.9) | collective-permute-done | bytes 6176 | tf_op jit(solution)/shard_map/ppermute | solution.py:246
  41.0 0.0 collective-permute-done.12.refs_18_
  41.0 0.0 collective-permute-done.11.refs_16_
  41.0 5.3 %shard_map.114 = (bf16[80,4096]{1,0:T(8,128)(2,1)}, bf16[80,64]{1,0:T(8,128)(2,1)S(1)}, bf16[80,64]{1,0:T(8,128)(2,1)S(1)}, bf16[8,16,512]{2,1,0:T(8,128)(2,1)S(1)}, bf16[8,16,512]{2,1,0:T(8,128)(2,1)S(1)}) custom-call(s32[2]{0:T(128)S(1)} %pad_add_fusion.place, bf16[80,4096]{1,0:T(8,128)(2,1)S(1)} %bitcast.16, ...), custom_call_target="tpu_custom_call" | custom-call | flops 10000000 | bytes 2000000 | tf_op jit(solution)/shard_map/pallas_call | solution.py:227
  46.3 0.0 copy-start.1
  46.3 0.0 collective-permute-start.14
  46.3 1.3 %collective-permute-done.14 = bf16[8,16,512]{2,1,0:T(8,128)(2,1)S(1)} collective-permute-done((bf16[8,16,512]{2,1,0:T(8,128)(2,1)S(1)}, bf16[8,16,512]{2,1,0:T(8,128)(2,1)S(1)}, u32[]{:S(2)}, u32[]{:S(2)}) %collective-permute-start.14) | collective-permute-done | bytes 131104 | tf_op jit(solution)/shard_map/ppermute | solution.py:246
  47.7 1.6 %collective-permute-start.15 = (bf16[4,16,512]{2,1,0:T(8,128)(2,1)S(1)}, bf16[4,16,512]{2,1,0:T(8,128)(2,1)S(1)}, u32[]{:S(2)}, u32[]{:S(2)}) collective-permute-start(bf16[4,16,512]{2,1,0:T(8,128)(2,1)S(1)} %slice.41), channel_id=1, source_target_pairs={{0,1},{1,0},{2,3},{3,2},{4,5},{5,4},{6,7},{7,6},{8,9},{9,8},{10,11... | collective-permute-start | bytes 196616 | tf_op jit(solution)/shard_map/ppermute | solution.py:246
  49.3 2.7 %collective-permute-done.15 = bf16[4,16,512]{2,1,0:T(8,128)(2,1)S(1)} collective-permute-done((bf16[4,16,512]{2,1,0:T(8,128)(2,1)S(1)}, bf16[4,16,512]{2,1,0:T(8,128)(2,1)S(1)}, u32[]{:S(2)}, u32[]{:S(2)}) %collective-permute-start.15) | collective-permute-done | bytes 65568 | tf_op jit(solution)/shard_map/ppermute | solution.py:246
  52.1 2.6 %collective-permute-start.16 = (bf16[2,16,512]{2,1,0:T(8,128)(2,1)S(1)}, bf16[2,16,512]{2,1,0:T(8,128)(2,1)S(1)}, u32[]{:S(2)}, u32[]{:S(2)}) collective-permute-start(bf16[2,16,512]{2,1,0:T(8,128)(2,1)S(1)} %slice.42), channel_id=1, source_target_pairs={{0,4},{1,5},{2,6},{3,7},{4,0},{5,1},{6,2},{7,3},{8,12},{9,13},{10,... | collective-permute-start | bytes 98312 | tf_op jit(solution)/shard_map/ppermute | solution.py:246
  54.7 2.3 %collective-permute-done.16 = bf16[2,16,512]{2,1,0:T(8,128)(2,1)S(1)} collective-permute-done((bf16[2,16,512]{2,1,0:T(8,128)(2,1)S(1)}, bf16[2,16,512]{2,1,0:T(8,128)(2,1)S(1)}, u32[]{:S(2)}, u32[]{:S(2)}) %collective-permute-start.16) | collective-permute-done | bytes 32800 | tf_op jit(solution)/shard_map/ppermute | solution.py:246
  57.0 1.8 %collective-permute-start.17 = (bf16[1,16,512]{2,1,0:T(8,128)(2,1)S(1)}, bf16[1,16,512]{2,1,0:T(8,128)(2,1)S(1)}, u32[]{:S(2)}, u32[]{:S(2)}) collective-permute-start(bf16[1,16,512]{2,1,0:T(8,128)(2,1)S(1)} %slice.43), channel_id=1, source_target_pairs={{0,2},{1,3},{2,0},{3,1},{4,6},{5,7},{6,4},{7,5},{8,10},{9,11},{10,... | collective-permute-start | bytes 49160 | tf_op jit(solution)/shard_map/ppermute | solution.py:246
  58.8 0.0 copy-done.1
  58.8 0.4 shard_map.115
  59.1 0.6 collective-permute-start.13
  59.8 1.0 %collective-permute-done.17 = bf16[1,16,512]{2,1,0:T(8,128)(2,1)S(1)} collective-permute-done((bf16[1,16,512]{2,1,0:T(8,128)(2,1)S(1)}, bf16[1,16,512]{2,1,0:T(8,128)(2,1)S(1)}, u32[]{:S(2)}, u32[]{:S(2)}) %collective-permute-start.17) | collective-permute-done | bytes 16416 | tf_op jit(solution)/shard_map/ppermute | solution.py:246
  60.8 0.5 collective-permute-start.18
  61.3 10.3 %collective-permute-done.18 = f32[16,512]{1,0:T(8,128)S(1)} collective-permute-done((f32[16,512]{1,0:T(8,128)S(1)}, f32[16,512]{1,0:T(8,128)S(1)}, u32[]{:S(2)}, u32[]{:S(2)}) %collective-permute-start.18) | collective-permute-done | bytes 32800 | tf_op jit(solution)/shard_map/ppermute | solution.py:246
  71.6 0.1 collective-permute-start.19
  71.7 0.0 collective-permute-done.13.rest_0_
  71.7 1.2 %shard_map.116 = bf16[64,4096]{1,0:T(8,128)(2,1)} custom-call(bf16[80,64]{1,0:T(8,128)(2,1)S(1)} %get-tuple-element.27.w_own, bf16[80,64]{1,0:T(8,128)(2,1)S(1)} %get-tuple-element.28.w_sib, bf16[80,4096]{1,0:T(8,128)(2,1)S(1)} %bitcast.18, bf16[80,4096]{1,0:T(8,128)(2,1)S(1)} %collective-permute-done.c_sib.refs_1_, ...), custom_call_target="tpu_custom_call" | custom-call | flops 10000000 | bytes 2000000 | tf_op jit(solution)/shard_map/pallas_call | solution.py:227
  72.9 0.0 collective-permute-done.19
  72.9 0.6 broadcast_select_fusion
  (11 shorter events, 0.1 us)
Async XLA Ops:
  0.6 25.0 %copy-start.3 = (bf16[1,64,4096]{2,1,0:T(8,128)(2,1)S(1)}, bf16[1,64,4096]{2,1,0:T(8,128)(2,1)}, u32[]{:S(2)}) copy-start(bf16[1,64,4096]{2,1,0:T(8,128)(2,1)} %param.8) | copy-start | bytes 1572868
  0.6 15.1 %collective-permute-start.7 = (bf16[64,4096]{1,0:T(8,128)(2,1)}, bf16[64,4096]{1,0:T(8,128)(2,1)S(1)}, u32[]{:S(2)}, u32[]{:S(2)}) collective-permute-start(bf16[64,4096]{1,0:T(8,128)(2,1)} %bitcast.21), channel_id=1, source_target_pairs={{0,16},{8,24},{16,0},{24,8},{1,17},{9,25},{17,1},{25,9},{2,18},{10... | collective-permute-start | bytes 1572872 | tf_op jit(solution)/shard_map/ppermute | solution.py:246
  3.6 21.9 %collective-permute-start = (bf16[80,4096]{1,0:T(8,128)(2,1)}, bf16[80,4096]{1,0:T(8,128)(2,1)S(1)}, u32[]{:S(2)}, u32[]{:S(2)}) collective-permute-start(bf16[80,4096]{1,0:T(8,128)(2,1)} %bitcast.12), channel_id=1, source_target_pairs={{0,8},{8,0},{16,24},{24,16},{1,9},{9,1},{17,25},{25,17},{2,10},{10... | collective-permute-start | bytes 1966088 | tf_op jit(solution)/shard_map/ppermute | solution.py:246
  4.4 11.4 %collective-permute-start.2 = (bf16[1,16,512]{2,1,0:T(8,128)(2,1)S(1)}, bf16[1,16,512]{2,1,0:T(8,128)(2,1)S(1)}, u32[]{:S(2)}, u32[]{:S(2)}) collective-permute-start(bf16[1,16,512]{2,1,0:T(8,128)(2,1)S(1)} %select_bitcast_fusion), channel_id=1, source_target_pairs={{0,1},{1,0},{2,3},{3,2},{4,5},{5,4},{6,7},{7,6},{8,9},{9,8},{10,11... | collective-permute-start | bytes 49160 | tf_op jit(solution)/shard_map/ppermute | solution.py:246
  5.9 19.7 %collective-permute-start.1 = (bf16[64,4096]{1,0:T(8,128)(2,1)}, bf16[64,4096]{1,0:T(8,128)(2,1)S(1)}, u32[]{:S(2)}, u32[]{:S(2)}) collective-permute-start(bf16[64,4096]{1,0:T(8,128)(2,1)} %bitcast.22), channel_id=1, source_target_pairs={{0,8},{8,0},{16,24},{24,16},{1,9},{9,1},{17,25},{25,17},{2,10},{10... | collective-permute-start | bytes 1572872 | tf_op jit(solution)/shard_map/ppermute | solution.py:246
  15.8 25.2 %collective-permute-start.11 = (bf16[64,4096]{1,0:T(8,128)(2,1)S(1)}, bf16[64,4096]{1,0:T(8,128)(2,1)S(1)}, u32[]{:S(2)}, u32[]{:S(2)}) collective-permute-start(bf16[64,4096]{1,0:T(8,128)(2,1)S(1)} %collective-permute-done.7.q.refs_15_), channel_id=1, source_target_pairs={{0,8},{8,0},{16,24},{24,16},{1,9},{9,1},{17,25},{25,17},{2,10},{10... | collective-permute-start | bytes 1572872 | tf_op jit(solution)/shard_map/ppermute | solution.py:246
  15.8 4.0 %collective-permute-start.3 = (bf16[2,16,512]{2,1,0:T(8,128)(2,1)S(1)}, bf16[2,16,512]{2,1,0:T(8,128)(2,1)S(1)}, u32[]{:S(2)}, u32[]{:S(2)}) collective-permute-start(bf16[2,16,512]{2,1,0:T(8,128)(2,1)S(1)} %pad_maximum_fusion.2), channel_id=1, source_target_pairs={{0,2},{1,3},{2,0},{3,1},{4,6},{5,7},{6,4},{7,5},{8,10},{9,11},{10,... | collective-permute-start | bytes 98312 | tf_op jit(solution)/shard_map/ppermute | solution.py:246
  19.8 5.6 %collective-permute-start.4 = (bf16[4,16,512]{2,1,0:T(8,128)(2,1)S(1)}, bf16[4,16,512]{2,1,0:T(8,128)(2,1)S(1)}, u32[]{:S(2)}, u32[]{:S(2)}) collective-permute-start(bf16[4,16,512]{2,1,0:T(8,128)(2,1)S(1)} %pad_maximum_fusion.1), channel_id=1, source_target_pairs={{0,4},{1,5},{2,6},{3,7},{4,0},{5,1},{6,2},{7,3},{8,12},{9,13},{10,... | collective-permute-start | bytes 196616 | tf_op jit(solution)/shard_map/ppermute | solution.py:246
  25.4 2.9 %collective-permute-start.5 = (bf16[8,16,512]{2,1,0:T(8,128)(2,1)S(1)}, bf16[8,16,512]{2,1,0:T(8,128)(2,1)S(1)}, u32[]{:S(2)}, u32[]{:S(2)}) collective-permute-start(bf16[8,16,512]{2,1,0:T(8,128)(2,1)S(1)} %pad_maximum_fusion.maps.refs_6_), channel_id=1, source_target_pairs={{0,8},{8,0},{16,24},{24,16},{1,9},{9,1},{17,25},{25,17},{2,10},{10... | collective-permute-start | bytes 393224 | tf_op jit(solution)/shard_map/ppermute | solution.py:246
  25.5 0.7 copy-start.5
  25.5 0.7 copy-start.6
  26.1 1.1 %copy-start = (bf16[1,1,80,4096]{3,2,1,0:T(8,128)(2,1)S(1)}, bf16[1,1,80,4096]{3,2,1,0:T(8,128)(2,1)}, u32[]{:S(2)}) copy-start(bf16[1,1,80,4096]{3,2,1,0:T(8,128)(2,1)} %param.9) | copy-start | bytes 1966084
  27.2 1.1 %copy-start.2 = (bf16[1,1,80,4096]{3,2,1,0:T(8,128)(2,1)S(1)}, bf16[1,1,80,4096]{3,2,1,0:T(8,128)(2,1)}, u32[]{:S(2)}) copy-start(bf16[1,1,80,4096]{3,2,1,0:T(8,128)(2,1)} %param.13) | copy-start | bytes 1966084
  27.2 1.2 %copy-start.4 = (bf16[1,64,4096]{2,1,0:T(8,128)(2,1)S(1)}, bf16[1,64,4096]{2,1,0:T(8,128)(2,1)}, u32[]{:S(2)}) copy-start(bf16[1,64,4096]{2,1,0:T(8,128)(2,1)} %param.12) | copy-start | bytes 1572868
  30.6 3.8 %collective-permute-start.8 = (f32[24,64]{1,0:T(8,128)S(1)}, f32[24,64]{1,0:T(8,128)S(1)}, u32[]{:S(2)}, u32[]{:S(2)}) collective-permute-start(f32[24,64]{1,0:T(8,128)S(1)} %get-tuple-element.20.refs_9_), channel_id=1, source_target_pairs={{0,16},{8,24},{16,0},{24,8},{1,17},{9,25},{17,1},{25,9},{2,18},{10... | collective-permute-start | bytes 18440 | tf_op jit(solution)/shard_map/ppermute | solution.py:246
  35.6 5.4 %collective-permute-start.12 = (bf16[80,64]{1,0:T(8,128)(2,1)S(1)}, bf16[80,64]{1,0:T(8,128)(2,1)S(1)}, u32[]{:S(2)}, u32[]{:S(2)}) collective-permute-start(bf16[80,64]{1,0:T(8,128)(2,1)S(1)} %get-tuple-element.25.w_sib), channel_id=1, source_target_pairs={{0,8},{8,0},{16,24},{24,16},{1,9},{9,1},{17,25},{25,17},{2,10},{10... | collective-permute-start | bytes 30728 | tf_op jit(solution)/shard_map/ppermute | solution.py:246
  35.7 2.2 %collective-permute-start.6 = (f32[24,64]{1,0:T(8,128)S(1)}, f32[24,64]{1,0:T(8,128)S(1)}, u32[]{:S(2)}, u32[]{:S(2)}) collective-permute-start(f32[24,64]{1,0:T(8,128)S(1)} %get-tuple-element.20.refs_9_), channel_id=1, source_target_pairs={{0,8},{8,0},{16,24},{24,16},{1,9},{9,1},{17,25},{25,17},{2,10},{10... | collective-permute-start | bytes 18440 | tf_op jit(solution)/shard_map/ppermute | solution.py:246
  36.2 3.1 %collective-permute-start.10 = (f32[24,64]{1,0:T(8,128)S(1)}, f32[24,64]{1,0:T(8,128)S(1)}, u32[]{:S(2)}, u32[]{:S(2)}) collective-permute-start(f32[24,64]{1,0:T(8,128)S(1)} %get-tuple-element.23), channel_id=1, source_target_pairs={{0,24},{8,16},{16,8},{24,0},{1,25},{9,17},{17,9},{25,1},{2,26},{10... | collective-permute-start | bytes 18440 | tf_op jit(solution)/shard_map/ppermute | solution.py:246
  37.3 3.7 %collective-permute-start.9 = (f32[24,64]{1,0:T(8,128)S(1)}, f32[24,64]{1,0:T(8,128)S(1)}, u32[]{:S(2)}, u32[]{:S(2)}) collective-permute-start(f32[24,64]{1,0:T(8,128)S(1)} %get-tuple-element.23), channel_id=1, source_target_pairs={{0,16},{8,24},{16,0},{24,8},{1,17},{9,25},{17,1},{25,9},{2,18},{10... | collective-permute-start | bytes 18440 | tf_op jit(solution)/shard_map/ppermute | solution.py:246
  46.3 12.5 %copy-start.1 = (bf16[1,1,80,4096]{3,2,1,0:T(8,128)(2,1)S(1)}, bf16[1,1,80,4096]{3,2,1,0:T(8,128)(2,1)}, u32[]{:S(2)}) copy-start(bf16[1,1,80,4096]{3,2,1,0:T(8,128)(2,1)} %param.9) | copy-start | bytes 1966084
  46.3 1.3 %collective-permute-start.14 = (bf16[8,16,512]{2,1,0:T(8,128)(2,1)S(1)}, bf16[8,16,512]{2,1,0:T(8,128)(2,1)S(1)}, u32[]{:S(2)}, u32[]{:S(2)}) collective-permute-start(bf16[8,16,512]{2,1,0:T(8,128)(2,1)S(1)} %get-tuple-element.31), channel_id=1, source_target_pairs={{0,8},{8,0},{16,24},{24,16},{1,9},{9,1},{17,25},{25,17},{2,10},{10... | collective-permute-start | bytes 393224 | tf_op jit(solution)/shard_map/ppermute | solution.py:246
  47.7 4.3 %collective-permute-start.15 = (bf16[4,16,512]{2,1,0:T(8,128)(2,1)S(1)}, bf16[4,16,512]{2,1,0:T(8,128)(2,1)S(1)}, u32[]{:S(2)}, u32[]{:S(2)}) collective-permute-start(bf16[4,16,512]{2,1,0:T(8,128)(2,1)S(1)} %slice.41), channel_id=1, source_target_pairs={{0,1},{1,0},{2,3},{3,2},{4,5},{5,4},{6,7},{7,6},{8,9},{9,8},{10,11... | collective-permute-start | bytes 196616 | tf_op jit(solution)/shard_map/ppermute | solution.py:246
  52.1 4.9 %collective-permute-start.16 = (bf16[2,16,512]{2,1,0:T(8,128)(2,1)S(1)}, bf16[2,16,512]{2,1,0:T(8,128)(2,1)S(1)}, u32[]{:S(2)}, u32[]{:S(2)}) collective-permute-start(bf16[2,16,512]{2,1,0:T(8,128)(2,1)S(1)} %slice.42), channel_id=1, source_target_pairs={{0,4},{1,5},{2,6},{3,7},{4,0},{5,1},{6,2},{7,3},{8,12},{9,13},{10,... | collective-permute-start | bytes 98312 | tf_op jit(solution)/shard_map/ppermute | solution.py:246
  57.0 3.8 %collective-permute-start.17 = (bf16[1,16,512]{2,1,0:T(8,128)(2,1)S(1)}, bf16[1,16,512]{2,1,0:T(8,128)(2,1)S(1)}, u32[]{:S(2)}, u32[]{:S(2)}) collective-permute-start(bf16[1,16,512]{2,1,0:T(8,128)(2,1)S(1)} %slice.43), channel_id=1, source_target_pairs={{0,2},{1,3},{2,0},{3,1},{4,6},{5,7},{6,4},{7,5},{8,10},{9,11},{10,... | collective-permute-start | bytes 49160 | tf_op jit(solution)/shard_map/ppermute | solution.py:246
  59.1 12.5 %collective-permute-start.13 = (bf16[64,4096]{1,0:T(8,128)(2,1)S(1)}, bf16[64,4096]{1,0:T(8,128)(2,1)S(1)}, u32[]{:S(2)}, u32[]{:S(2)}) collective-permute-start(bf16[64,4096]{1,0:T(8,128)(2,1)S(1)} %shard_map.115), channel_id=1, source_target_pairs={{0,16},{8,24},{16,0},{24,8},{1,17},{9,25},{17,1},{25,9},{2,18},{10... | collective-permute-start | bytes 1572872 | tf_op jit(solution)/shard_map/ppermute | solution.py:246
  60.8 10.8 %collective-permute-start.18 = (f32[16,512]{1,0:T(8,128)S(1)}, f32[16,512]{1,0:T(8,128)S(1)}, u32[]{:S(2)}, u32[]{:S(2)}) collective-permute-start(f32[16,512]{1,0:T(8,128)S(1)} %fusion), channel_id=1, source_target_pairs={{0,16},{8,24},{16,0},{24,8},{1,17},{9,25},{17,1},{25,9},{2,18},{10... | collective-permute-start | bytes 98312 | tf_op jit(solution)/shard_map/ppermute | solution.py:246
  71.6 1.3 %collective-permute-start.19 = (f32[16,512]{1,0:T(8,128)S(1)}, f32[16,512]{1,0:T(8,128)S(1)}, u32[]{:S(2)}, u32[]{:S(2)}) collective-permute-start(f32[16,512]{1,0:T(8,128)S(1)} %add_multiply_fusion), channel_id=1, source_target_pairs={{0,8},{8,0},{16,24},{24,16},{1,9},{9,1},{17,25},{25,17},{2,10},{10... | collective-permute-start | bytes 98312 | tf_op jit(solution)/shard_map/ppermute | solution.py:246

commit v2 on v1

v2 whole, which is shorter than its diff:
```python
import functools

import jax
import jax.numpy as jnp
from jax import lax
from jax.experimental import pallas as pl
from jax.experimental.pallas import tpu as pltpu
from jax.sharding import PartitionSpec as P

sharpness_factor = 50.0
adapter_scale = 2.0
STEP = 512
MAX, SUM, POSITIVE, HARD, BODY = 0, 1, 2, 3, 8

f32 = jnp.float32
bf16 = jnp.bfloat16


def bits_of(size):
    return [1 << b for b in range(size.bit_length() - 1)]


def reversed_bits(size):
    bits = bits_of(size)
    return [sum(low for low, high in zip(bits, bits[::-1]) if i & high) for i in range(size)]


def dot(left, right, left_dim, right_dim):
    return lax.dot_general(
        left, right, (((left_dim,), (right_dim,)), ((), ())), preferred_element_type=f32
    )


def dot_wide(left, right, left_dim, right_dim):
    high = left.astype(bf16)
    low = (left - high.astype(f32)).astype(bf16)
    return dot(high, right, left_dim, right_dim) + dot(low, right, left_dim, right_dim)


def layout(position, block, shape):
    row = lax.broadcasted_iota(jnp.int32, shape, 0)
    own = row < block
    return jnp.where(own, position, position ^ 1), jnp.where(own, row, row - block)


def allowed(owner, slot, hard, rows):
    return (slot < rows) | (hard.astype(jnp.int32) == owner)


def hits(owner, slot, positive, rows):
    return (slot < rows) & (positive.astype(jnp.int32) == owner * rows + slot)


def merge(stats):
    top = functools.reduce(jnp.maximum, [m for m, _ in stats])
    return top + jnp.log(sum(s * jnp.exp(m - top) for m, s in stats))


def columns(ref, at, width):
    return ref[:, pl.ds(pl.multiple_of(at * width, width), width)]


def scores_kernel(place, c_own, c_sib, q_own, q_sib, positives, hard, scores, stats):
    block, rows = c_own.shape[0], q_own.shape[0]
    c = jnp.concatenate([c_own[...], c_sib[...]], 0)
    q = jnp.concatenate([q_own[...], q_sib[...]], 0)
    total = dot(c, q, 1, 1) * sharpness_factor
    scores[...] = total
    mine = total[:, :rows]
    owner, slot = layout(place[0], block, mine.shape)
    mine = jnp.where(allowed(owner, slot, hard[...], rows), mine, -jnp.inf)
    top = jnp.max(mine, axis=0, keepdims=True)
    stats[...] = jnp.zeros_like(stats)
    stats[MAX : MAX + 1] = top
    stats[SUM : SUM + 1] = jnp.sum(jnp.exp(mine - top), axis=0, keepdims=True)
    stats[POSITIVE : POSITIVE + 1] = positives[...].astype(f32)
    stats[HARD : HARD + 1] = hard[...].astype(f32)


def adapter_kernel(place, maps, other, hq, hq_sib, hc, hc_sib, c_own, c_sib, q_own, q_sib, message, low_c, c_up):
    shards, rank, width = maps.shape
    places = reversed_bits(shards)
    core = place[0] & 1

    def product(gathered, parts):
        total = 0.0
        for at in range(shards):
            rows = jnp.concatenate([columns(r, at ^ place[1], width) for r in parts], 0)
            total = total + dot(gathered[places[at]], rows, 1, 1)
        return total

    @pl.when(core == 0)
    def _():
        message[...] = product(maps, [hq, hq_sib]).astype(bf16).astype(f32)
        low_c[...] = product(maps, [hc, hc_sib]).astype(bf16)
        c_up[...] = product(other, [c_own, c_sib])

    @pl.when(core == 1)
    def _():
        message[...] = product(maps, [q_own, q_sib])
        low_c[...] = jnp.zeros_like(low_c)
        c_up[...] = product(maps, [c_own, c_sib])


def partner_kernel(place, c_own, c_sib, q, stats, c_up, answer, weights, q_again):
    block, rows = c_own.shape[0], q.shape[0]
    c = jnp.concatenate([c_own[...], c_sib[...]], 0)
    q_again[...] = q[...]
    total = dot(c, q[...], 1, 1)
    owner, slot = layout(place[0], block, total.shape)
    keep = allowed(owner, slot, stats[HARD : HARD + 1], rows)
    total = jnp.where(keep, total * sharpness_factor, -jnp.inf)
    top = jnp.max(total, axis=0, keepdims=True)
    share = jnp.sum(jnp.exp(total - top), axis=0, keepdims=True)
    answer[...] = jnp.zeros_like(answer)
    answer[MAX : MAX + 1] = top
    answer[SUM : SUM + 1] = share
    log_total = merge([(stats[MAX : MAX + 1], stats[SUM : SUM + 1]), (top, share)])
    hit = hits(owner, slot, stats[POSITIVE : POSITIVE + 1], rows)
    here = (jnp.exp(total - log_total) - hit.astype(f32)).astype(bf16)
    answer[BODY:] = dot_wide(c_up[...], here, 1, 0) * sharpness_factor
    weights[...] = here


def share_kernel(weights, c_own, c_sib, share):
    for i in range(c_own.shape[1] // STEP):
        at = slice(i * STEP, (i + 1) * STEP)
        c = jnp.concatenate([c_own[:, at], c_sib[:, at]], 0)
        share[:, at] = (dot(weights[...], c, 0, 0) * sharpness_factor).astype(bf16)


def question_kernel(weights, c_own, c_sib, *rest):
    shares, out = rest[:-1], rest[-1]
    for i in range(c_own.shape[1] // STEP):
        at = slice(i * STEP, (i + 1) * STEP)
        c = jnp.concatenate([c_own[:, at], c_sib[:, at]], 0)
        total = dot(weights[...], c, 0, 0) * sharpness_factor
        for share in shares:
            total = total + share[:, at].astype(f32)
        out[:, at] = total.astype(bf16)


def candidate_kernel(weights, *rest):
    queries, out = rest[:-1], rest[-1]
    for i in range(out.shape[1] // STEP):
        at = slice(i * STEP, (i + 1) * STEP)
        q = jnp.concatenate([r[:, at] for r in queries], 0)
        out[:, at] = (dot(weights[...], q, 1, 0) * sharpness_factor).astype(bf16)


def taken(refs, *counts):
    out, at = [], 0
    for count in counts:
        out.append(list(refs[at : at + count]))
        at += count
    return out


def sums_kernel(partners, place, *refs):
    n = partners
    (c, q, far_q, far_q_sib, hq, hc, stats, answers, sib_answers, far_w, far_w_sib, message, far_messages,
     (scores, low_c, c_up), (share,), (w_grad, w_own, keep, send)) = taken(
        refs, 2, 2, n, n, 2, 2, 2, n, n, n, n, 1, n, 3, n and 1, 4)
    block, rows = c[0].shape[0], q[0].shape[0]
    half, rank, width = keep.shape

    def stats_of(ref):
        return ref[MAX : MAX + 1], ref[SUM : SUM + 1]

    def both(at):
        return jnp.concatenate([ref[at : at + 1] for ref in stats], 1)

    log_total = jnp.concatenate(
        [merge([stats_of(r) for r in group]) for group in ([stats[0]] + answers, [stats[1]] + sib_answers)], 1
    )
    owner, slot = layout(place[0], block, scores.shape)
    kept = allowed(owner, slot, both(HARD), rows)
    hit = hits(owner, slot, both(POSITIVE), rows)
    near = jnp.exp(jnp.where(kept, scores[...] - log_total, -jnp.inf)) - hit.astype(f32)
    near = near.astype(bf16)
    w_own[...] = near[:, :rows]
    pieces = [near]
    for mine, other in zip(far_w, far_w_sib):
        pieces += [mine[...], jnp.concatenate([other[block:], other[:block]], 0)]
    weights = jnp.concatenate(pieces, 1)
    w_grad[...] = weights[:block]
    messages = jnp.concatenate([message[0][...]] + [r[...] for r in far_messages], 1)
    queries = list(q)
    for pair in zip(far_q, far_q_sib):
        queries += pair

    def store(at, total):
        if at & 1:
            send[at >> 1] = total.astype(bf16)
        else:
            keep[at >> 1] = total

    def split(terms):
        high = terms.astype(bf16)
        return jnp.concatenate([high, (terms - high.astype(f32)).astype(bf16)], 0)

    core = place[0] & 1

    @pl.when(core == 0)
    def _():
        by_candidate = split(dot(messages.astype(bf16), weights, 1, 1) * sharpness_factor)
        by_query = split(dot(low_c[...], weights, 1, 0) * sharpness_factor)
        for at in range(2 * half):
            from_c = jnp.concatenate([columns(r, at ^ place[1], width) for r in c], 0)
            from_q = jnp.concatenate([columns(r, at ^ place[1], width) for r in queries], 0)
            total = dot(by_candidate, from_c, 1, 0) + dot(by_query, from_q, 1, 0)
            store(at, total[:rank] + total[rank:])

    @pl.when(core == 1)
    def _():
        back_q = dot_wide(c_up[...], near, 1, 0) * sharpness_factor
        for mine, other in zip(answers, sib_answers):
            back_q = back_q + jnp.concatenate([mine[BODY:], other[BODY:]], 1)
        back_q = back_q.astype(bf16)
        back_c = (dot_wide(messages, weights, 1, 1) * sharpness_factor).astype(bf16)
        for at in range(2 * half):
            from_q = jnp.concatenate([columns(r, at ^ place[1], width) for r in hq], 0)
            from_c = jnp.concatenate([columns(r, at ^ place[1], width) for r in hc], 0)
            store(at, dot(back_q, from_q, 1, 0) + dot(back_c, from_c, 1, 0))


def call(kernel, outs):
    smem = pl.BlockSpec(memory_space=pltpu.SMEM)
    vmem = pl.BlockSpec(memory_space=pltpu.VMEM)

    def run(*args):
        return pl.pallas_call(
            kernel,
            out_shape=outs,
            in_specs=[smem if a.dtype == jnp.int32 and a.ndim == 1 else vmem for a in args],
            out_specs=jax.tree.map(lambda _: vmem, outs),
            compiler_params=pltpu.CompilerParams(vmem_limit_bytes=40 * 2**20),
            cost_estimate=pl.CostEstimate(flops=1000, bytes_accessed=1000, transcendentals=0),
        )(*args)

    return run


def shaped(shape, dtype=f32):
    return jax.ShapeDtypeStruct(shape, dtype)


def swap(array, axis, apart):
    size = lax.axis_size(axis)
    return lax.ppermute(array, axis, [(i, i ^ apart) for i in range(size)])


def on_device(
    queries, candidates, positives, hard_blocks, query_hidden, candidate_hidden, adapter_down, adapter_up
):
    q_own, c_own = queries[0], candidates[0, 0]
    hq, hc = query_hidden[0], candidate_hidden[0, 0]
    rows, width = q_own.shape
    block = c_own.shape[0]
    rank, shard_width = adapter_down.shape
    devices, shards = lax.axis_size("dp"), lax.axis_size("fsdp")
    position, shard = lax.axis_index("dp"), lax.axis_index("fsdp")
    place = jnp.stack([position, shard]).astype(jnp.int32)
    partners = list(range(2, devices, 2))
    even = (position & 1) == 0

    far_q = [swap(q_own, "dp", k) for k in partners]
    c_sib, q_sib, hq_sib, hc_sib = (swap(a, "dp", 1) for a in (c_own, q_own, hq, hc))

    maps = jnp.where(even, adapter_down, adapter_up)[None]
    for bit in bits_of(shards)[::-1]:
        maps = jnp.concatenate([maps, swap(maps, "fsdp", bit)], 0)
    other_maps = swap(maps, "dp", 1)

    scores, stats = call(scores_kernel, (shaped((2 * block, 2 * rows)), shaped((BODY, rows))))(
        place, c_own, c_sib, q_own, q_sib, positives, hard_blocks
    )
    sib_stats = swap(stats, "dp", 1)
    far_stats = [swap(stats, "dp", k) for k in partners]
    message, low_c, c_up = call(
        adapter_kernel, (shaped((rank, 2 * rows)), shaped((rank, 2 * block), bf16), shaped((rank, 2 * block)))
    )(place, maps, other_maps, hq, hq_sib, hc, hc_sib, c_own, c_sib, q_own, q_sib)
    far_messages = [swap(message, "dp", k) for k in partners]

    answers, sib_answers, far_w, far_w_sib, far_q_sib, shares, own_shares = [], [], [], [], [], [], []
    for k, q, far in zip(partners, far_q, far_stats):
        answer, weights, q_again = call(
            partner_kernel,
            (shaped((BODY + rank, rows)), shaped((2 * block, rows), bf16), shaped((rows, width), bf16)),
        )(place, c_own, c_sib, q, far, c_up)
        answers.append(swap(answer, "dp", k))
        sib_answers.append(swap(answer, "dp", k ^ 1))
        far_w.append(weights)
        far_w_sib.append(swap(weights, "dp", 1))
        far_q_sib.append(swap(q_again, "dp", 1))
        own_shares.append(call(share_kernel, shaped((rows, width), bf16))(weights, c_own, c_sib))
        shares.append(swap(own_shares[-1], "dp", k))

    w_grad, w_own, keep, send = call(
        functools.partial(sums_kernel, len(partners)),
        (
            shaped((block, rows * devices), bf16),
            shaped((2 * block, rows), bf16),
            shaped((shards // 2, rank, shard_width)),
            shaped((shards // 2, rank, shard_width), bf16),
        ),
    )(
        place, c_own, c_sib, q_own, q_sib, *far_q, *far_q_sib, hq, hq_sib, hc, hc_sib, stats, sib_stats,
        *answers, *sib_answers, *far_w, *far_w_sib, message, *far_messages, scores, low_c, c_up,
        *own_shares[:1],
    )
    queries = [q_own, q_sib]
    for pair in zip(far_q, far_q_sib):
        queries += pair
    grad = call(candidate_kernel, shaped((block, width), bf16))(w_grad, *queries)
    question = call(question_kernel, shaped((rows, width), bf16))(w_own, c_own, c_sib, *shares)

    bits = bits_of(shards)[:1] + bits_of(shards)[:0:-1]
    terms = keep + swap(send, "fsdp", bits[0]).astype(f32)
    for bit in bits[1:]:
        half = terms.shape[0] // 2
        terms = terms[:half] + swap(terms[half:].astype(bf16), "fsdp", bit).astype(f32)
    terms = terms[0]
    for bit in bits_of(devices)[1:]:
        terms = terms + swap(terms, "dp", bit)
    terms = terms * adapter_scale
    others = swap(terms, "dp", 1)
    return (
        question[None],
        grad[None, None],
        jnp.where(even, others, terms),
        jnp.where(even, terms, others),
    )


def solution(mesh):
    placed = (
        P("fsdp", "dp", None),
        P("fsdp", "dp", None, None),
        P("fsdp", "dp"),
        P("fsdp", "dp"),
        P("fsdp", "dp", None),
        P("fsdp", "dp", None, None),
        P(None, "fsdp"),
        P(None, "fsdp"),
    )
    return jax.shard_map(
        on_device,
        mesh=mesh,
        in_specs=placed,
        out_specs=(
            P("fsdp", "dp", None),
            P("fsdp", "dp", None, None),
            P(None, "fsdp"),
            P(None, "fsdp"),
        ),
        check_vma=False,
    )
```

time: 73.8 us -> 62.6 us (0.85)
  waiting for transfers between devices: 37.5 us -> 27.1 us
  Pallas kernels: 11.3 us -> 8.68 us
  starting transfers between devices: 20.6 us -> 22.5 us
    ppermute x20 -> x22, waiting for transfers between devices: 37.5 us -> 27.1 us  [swap(): return lax.ppermute(array, axis, [(i, i ^ apart) for i in range(size)])]
    pallas_call x6 -> x7, Pallas kernels: 11.3 us -> 8.68 us  [run(): pl.pallas_call(kernel, out_shape=outs, in_specs=[smem if a.dtype == jnp.i...]
    ppermute x20 -> x22, starting transfers between devices: 20.6 us -> 22.5 us  [swap(): return lax.ppermute(array, axis, [(i, i ^ apart) for i in range(size)])]
  transfers between devices with their start and end apart: 20 -> 22, of which waited for: 11 -> 9; matrix products, arithmetic and copies ran while one was open for 1% -> 0% of each run, Pallas kernels for 8% -> 10%
where the time goes in v2:
time: 62.6 us; the launch traced here: 62.3 us
  waiting for transfers between devices  27.1 us (43%)
  starting transfers between devices  22.5 us (36%)
  Pallas kernels  8.68 us (14%)
  local copies, waits for them, and re-layouts  1.69 us (3%)
  other arithmetic  1.56 us (2%)
  between operations  0.8 us (1%)
    ppermute x22, waiting for transfers between devices, swap(): return lax.ppermute(array, axis, [(i, i ^ apart) for i in range(size)])  27.1 us
    ppermute x22, starting transfers between devices, swap(): return lax.ppermute(array, axis, [(i, i ^ apart) for i in range(size)])  22.5 us
    pallas_call x7, Pallas kernels, run(): pl.pallas_call(kernel, out_shape=outs, in_specs=[smem if a.dtype == jnp.i...  8.68 us
    unnamed x14, local copies, waits for them, and re-layouts  1.68 us
  transfers between devices with their start and end apart: 22, of which 9 were waited for; matrix products, arithmetic and copies ran while one was open for 0% of the time, Pallas kernels for 10%

profile of v2, /device:TPU:0, one launch (start us, length us, event | category | flops | bytes accessed | tf_op | source)
XLA Modules:
  0.0 62.3 jit_solution(9630276565766269253)
XLA Ops:
  0.6 0.0 copy-start.2
  0.7 0.8 %select_bitcast_fusion = bf16[1,16,512]{2,1,0:T(8,128)(2,1)S(1)} fusion(bf16[16,512]{1,0:T(8,128)(2,1)} %param.14, bf16[16,512]{1,0:T(8,128)(2,1)} %param.15, pred[]{:T(512)S(6)} %eq.3), kind=kLoop, calls=%fused_computation.10 | loop fusion | flops 8192 | bytes 49153 | tf_op jit(solution)/shard_map/broadcast_in_dim | solution.py:270
  1.4 4.0 %collective-permute-start.4 = (bf16[1,16,512]{2,1,0:T(8,128)(2,1)S(1)}, bf16[1,16,512]{2,1,0:T(8,128)(2,1)S(1)}, u32[]{:S(2)}, u32[]{:S(2)}) collective-permute-start(bf16[1,16,512]{2,1,0:T(8,128)(2,1)S(1)} %select_bitcast_fusion), channel_id=1, source_target_pairs={{0,4},{1,5},{2,6},{3,7},{4,0},{5,1},{6,2},{7,3},{8,12},{9,13},{10,... | collective-permute-start | bytes 49160 | tf_op jit(solution)/shard_map/ppermute | solution.py:250
  5.5 1.7 %collective-permute-done.4 = bf16[1,16,512]{2,1,0:T(8,128)(2,1)S(1)} collective-permute-done((bf16[1,16,512]{2,1,0:T(8,128)(2,1)S(1)}, bf16[1,16,512]{2,1,0:T(8,128)(2,1)S(1)}, u32[]{:S(2)}, u32[]{:S(2)}) %collective-permute-start.4) | collective-permute-done | bytes 16416 | tf_op jit(solution)/shard_map/ppermute | solution.py:250
  7.2 1.9 %collective-permute-start.5 = (bf16[2,16,512]{2,1,0:T(8,128)(2,1)S(1)}, bf16[2,16,512]{2,1,0:T(8,128)(2,1)S(1)}, u32[]{:S(2)}, u32[]{:S(2)}) collective-permute-start(bf16[2,16,512]{2,1,0:T(8,128)(2,1)S(1)} %pad_maximum_fusion.2), channel_id=1, source_target_pairs={{0,2},{1,3},{2,0},{3,1},{4,6},{5,7},{6,4},{7,5},{8,10},{9,11},{10,... | collective-permute-start | bytes 98312 | tf_op jit(solution)/shard_map/ppermute | solution.py:250
  9.1 0.0 collective-permute-start
  9.1 0.5 collective-permute-start.1
  9.6 0.0 collective-permute-start.9
  9.6 1.5 %collective-permute-done.5 = bf16[2,16,512]{2,1,0:T(8,128)(2,1)S(1)} collective-permute-done((bf16[2,16,512]{2,1,0:T(8,128)(2,1)S(1)}, bf16[2,16,512]{2,1,0:T(8,128)(2,1)S(1)}, u32[]{:S(2)}, u32[]{:S(2)}) %collective-permute-start.5) | collective-permute-done | bytes 32800 | tf_op jit(solution)/shard_map/ppermute | solution.py:250
  11.1 2.0 %collective-permute-start.6 = (bf16[4,16,512]{2,1,0:T(8,128)(2,1)S(1)}, bf16[4,16,512]{2,1,0:T(8,128)(2,1)S(1)}, u32[]{:S(2)}, u32[]{:S(2)}) collective-permute-start(bf16[4,16,512]{2,1,0:T(8,128)(2,1)S(1)} %pad_maximum_fusion.1), channel_id=1, source_target_pairs={{0,1},{1,0},{2,3},{3,2},{4,5},{5,4},{6,7},{7,6},{8,9},{9,8},{10,11... | collective-permute-start | bytes 196616 | tf_op jit(solution)/shard_map/ppermute | solution.py:250
  13.1 0.0 collective-permute-start.8
  13.1 2.4 %collective-permute-done.6 = bf16[4,16,512]{2,1,0:T(8,128)(2,1)S(1)} collective-permute-done((bf16[4,16,512]{2,1,0:T(8,128)(2,1)S(1)}, bf16[4,16,512]{2,1,0:T(8,128)(2,1)S(1)}, u32[]{:S(2)}, u32[]{:S(2)}) %collective-permute-start.6) | collective-permute-done | bytes 65568 | tf_op jit(solution)/shard_map/ppermute | solution.py:250
  15.5 1.9 %collective-permute-start.2 = (bf16[64,4096]{1,0:T(8,128)(2,1)}, bf16[64,4096]{1,0:T(8,128)(2,1)S(1)}, u32[]{:S(2)}, u32[]{:S(2)}) collective-permute-start(bf16[64,4096]{1,0:T(8,128)(2,1)} %bitcast.20), channel_id=1, source_target_pairs={{0,16},{8,24},{16,0},{24,8},{1,17},{9,25},{17,1},{25,9},{2,18},{10... | collective-permute-start | bytes 1572872 | tf_op jit(solution)/shard_map/ppermute | solution.py:250
  17.4 0.0 collective-permute-done.1.q_sib.refs_3_.rest_1_
  17.4 0.1 collective-permute-start.7
  17.4 0.0 copy-start.5
  17.5 0.0 copy-start.6
  17.5 0.1 pad_add_fusion.place
  17.5 0.0 collective-permute-done.c_sib.refs_1_
  17.6 0.0 copy-done.2
  17.6 0.6 copy-done.5
  18.1 0.0 copy-done.6
  18.1 1.1 %copy-done = bf16[1,1,80,4096]{3,2,1,0:T(8,128)(2,1)S(1)} copy-done((bf16[1,1,80,4096]{3,2,1,0:T(8,128)(2,1)S(1)}, bf16[1,1,80,4096]{3,2,1,0:T(8,128)(2,1)}, u32[]{:S(2)}) %copy-start) | copy-done | bytes 655384
  19.2 1.1 %shard_map.111 = (f32[160,128]{1,0:T(8,128)S(1)}, f32[8,64]{1,0:T(8,128)S(1)}) custom-call(s32[2]{0:T(128)S(1)} %pad_add_fusion.place, bf16[80,4096]{1,0:T(8,128)(2,1)S(1)} %bitcast.13, bf16[80,4096]{1,0:T(8,128)(2,1)S(1)} %collective-permute-done.c_sib.refs_1_, bf16[64,4096]{1,0:T(8,128)(2,1)S(1)} %bitcast.21, ...), custom_call_target="tpu_custom_call" | custom-call | flops 1000 | bytes 1000 | tf_op jit(solution)/shard_map/pallas_call | solution.py:232
  20.3 0.2 collective-permute-start.3
  20.5 0.0 collective-permute-done.7.other
  20.5 0.0 collective-permute-done.8.hq_sib.refs_7_
  20.5 0.0 collective-permute-done.9.hc_sib.refs_9_
  20.5 0.0 copy-done.3
  20.5 0.0 copy-done.4
  20.6 2.0 %shard_map.112 = (f32[16,128]{1,0:T(8,128)S(1)}, bf16[16,160]{1,0:T(8,128)(2,1)S(1)}, f32[16,160]{1,0:T(8,128)S(1)}) custom-call(s32[2]{0:T(128)S(1)} %pad_add_fusion.place, bf16[8,16,512]{2,1,0:T(8,128)(2,1)S(1)} %pad_maximum_fusion.maps, bf16[8,16,512]{2,1,0:T(8,128)(2,1)} %collective-permute-done.7.other, bf16[64,4096]{1,0:T(8,128)(2,1)S(1)} %bitcast.29, ...), custom_call_target="tpu_custom_call" | custom-call | flops 1000 | bytes 1000 | tf_op jit(solution)/shard_map/pallas_call | solution.py:232
  22.5 5.2 %collective-permute-done.2.q.refs_4_.rest_2_ = bf16[64,4096]{1,0:T(8,128)(2,1)S(1)} collective-permute-done((bf16[64,4096]{1,0:T(8,128)(2,1)}, bf16[64,4096]{1,0:T(8,128)(2,1)S(1)}, u32[]{:S(2)}, u32[]{:S(2)}) %collective-permute-start.2) | collective-permute-done | bytes 524320 | tf_op jit(solution)/shard_map/ppermute | solution.py:250
  27.7 0.0 collective-permute-done.3.stats
  27.7 1.3 %shard_map.113 = (f32[24,64]{1,0:T(8,128)S(1)}, bf16[160,64]{1,0:T(8,128)(2,1)S(1)}, bf16[64,4096]{1,0:T(8,128)(2,1)S(1)}) custom-call(s32[2]{0:T(128)S(1)} %pad_add_fusion.place, bf16[80,4096]{1,0:T(8,128)(2,1)S(1)} %bitcast.15, bf16[80,4096]{1,0:T(8,128)(2,1)S(1)} %collective-permute-done.c_sib.refs_1_, ...), custom_call_target="tpu_custom_call" | custom-call | flops 1000 | bytes 1000 | tf_op jit(solution)/shard_map/pallas_call | solution.py:232
  29.0 0.0 collective-permute-start.10
  29.0 0.5 collective-permute-start.14
  29.5 0.0 collective-permute-start.11
  29.6 1.5 %collective-permute-start.15 = (f32[16,128]{1,0:T(8,128)S(1)}, f32[16,128]{1,0:T(8,128)S(1)}, u32[]{:S(2)}, u32[]{:S(2)}) collective-permute-start(f32[16,128]{1,0:T(8,128)S(1)} %get-tuple-element.21.refs_16_), channel_id=1, source_target_pairs={{0,16},{8,24},{16,0},{24,8},{1,17},{9,25},{17,1},{25,9},{2,18},{10... | collective-permute-start | bytes 24584 | tf_op jit(solution)/shard_map/ppermute | solution.py:250
  31.1 0.5 collective-permute-start.12
  31.6 0.0 collective-permute-done.11.refs_11_
  31.6 1.0 %collective-permute-start.13 = (f32[24,64]{1,0:T(8,128)S(1)}, f32[24,64]{1,0:T(8,128)S(1)}, u32[]{:S(2)}, u32[]{:S(2)}) collective-permute-start(f32[24,64]{1,0:T(8,128)S(1)} %get-tuple-element.19), channel_id=1, source_target_pairs={{0,24},{8,16},{16,8},{24,0},{1,25},{9,17},{17,9},{25,1},{2,26},{10... | collective-permute-start | bytes 18440 | tf_op jit(solution)/shard_map/ppermute | solution.py:250
  32.6 0.0 copy-done.1
  32.6 0.4 shard_map.114.refs_21_
  33.0 1.8 %collective-permute-done.12.refs_12_ = f32[24,64]{1,0:T(8,128)S(1)} collective-permute-done((f32[24,64]{1,0:T(8,128)S(1)}, f32[24,64]{1,0:T(8,128)S(1)}, u32[]{:S(2)}, u32[]{:S(2)}) %collective-permute-start.12) | collective-permute-done | bytes 6176 | tf_op jit(solution)/shard_map/ppermute | solution.py:250
  34.8 0.0 collective-permute-done.13.refs_13_
  34.8 0.0 collective-permute-done.15.refs_17_
  34.9 0.0 collective-permute-done.14.refs_15_
  34.9 0.0 collective-permute-done.10.refs_5_.rest_3_
  34.9 1.4 %shard_map.115 = (bf16[80,256]{1,0:T(8,128)(2,1)S(1)}, bf16[160,64]{1,0:T(8,128)(2,1)S(1)}, f32[4,16,512]{2,1,0:T(8,128)S(1)}, bf16[4,16,512]{2,1,0:T(8,128)(2,1)S(1)}) custom-call(s32[2]{0:T(128)S(1)} %pad_add_fusion.place, bf16[80,4096]{1,0:T(8,128)(2,1)S(1)} %bitcast.17, bf16[80,4096]{1,0:T(8,128)(2,1)S(1)} %collective-permute-done.c_sib.refs_1_, ...), custom_call_target="tpu_custom_call" | custom-call | flops 1000 | bytes 1000 | tf_op jit(solution)/shard_map/pallas_call | solution.py:232
  36.3 1.3 %collective-permute-start.17 = (bf16[4,16,512]{2,1,0:T(8,128)(2,1)S(1)}, bf16[4,16,512]{2,1,0:T(8,128)(2,1)S(1)}, u32[]{:S(2)}, u32[]{:S(2)}) collective-permute-start(bf16[4,16,512]{2,1,0:T(8,128)(2,1)S(1)} %get-tuple-element.27), channel_id=1, source_target_pairs={{0,1},{1,0},{2,3},{3,2},{4,5},{5,4},{6,7},{7,6},{8,9},{9,8},{10,11... | collective-permute-start | bytes 196616 | tf_op jit(solution)/shard_map/ppermute | solution.py:250
  37.6 3.0 %collective-permute-done.17 = bf16[4,16,512]{2,1,0:T(8,128)(2,1)S(1)} collective-permute-done((bf16[4,16,512]{2,1,0:T(8,128)(2,1)S(1)}, bf16[4,16,512]{2,1,0:T(8,128)(2,1)S(1)}, u32[]{:S(2)}, u32[]{:S(2)}) %collective-permute-start.17) | collective-permute-done | bytes 65568 | tf_op jit(solution)/shard_map/ppermute | solution.py:250
  40.7 2.6 %collective-permute-start.18 = (bf16[2,16,512]{2,1,0:T(8,128)(2,1)S(1)}, bf16[2,16,512]{2,1,0:T(8,128)(2,1)S(1)}, u32[]{:S(2)}, u32[]{:S(2)}) collective-permute-start(bf16[2,16,512]{2,1,0:T(8,128)(2,1)S(1)} %slice.28), channel_id=1, source_target_pairs={{0,4},{1,5},{2,6},{3,7},{4,0},{5,1},{6,2},{7,3},{8,12},{9,13},{10,... | collective-permute-start | bytes 98312 | tf_op jit(solution)/shard_map/ppermute | solution.py:250
  43.3 2.3 %collective-permute-done.18 = bf16[2,16,512]{2,1,0:T(8,128)(2,1)S(1)} collective-permute-done((bf16[2,16,512]{2,1,0:T(8,128)(2,1)S(1)}, bf16[2,16,512]{2,1,0:T(8,128)(2,1)S(1)}, u32[]{:S(2)}, u32[]{:S(2)}) %collective-permute-start.18) | collective-permute-done | bytes 32800 | tf_op jit(solution)/shard_map/ppermute | solution.py:250
  45.6 1.6 %collective-permute-start.19 = (bf16[1,16,512]{2,1,0:T(8,128)(2,1)S(1)}, bf16[1,16,512]{2,1,0:T(8,128)(2,1)S(1)}, u32[]{:S(2)}, u32[]{:S(2)}) collective-permute-start(bf16[1,16,512]{2,1,0:T(8,128)(2,1)S(1)} %slice.29), channel_id=1, source_target_pairs={{0,2},{1,3},{2,0},{3,1},{4,6},{5,7},{6,4},{7,5},{8,10},{9,11},{10,... | collective-permute-start | bytes 49160 | tf_op jit(solution)/shard_map/ppermute | solution.py:250
  47.2 1.4 %collective-permute-start.16 = (bf16[64,4096]{1,0:T(8,128)(2,1)S(1)}, bf16[64,4096]{1,0:T(8,128)(2,1)S(1)}, u32[]{:S(2)}, u32[]{:S(2)}) collective-permute-start(bf16[64,4096]{1,0:T(8,128)(2,1)S(1)} %shard_map.114.refs_21_), channel_id=1, source_target_pairs={{0,16},{8,24},{16,0},{24,8},{1,17},{9,25},{17,1},{25,9},{2,18},{10... | collective-permute-start | bytes 1572872 | tf_op jit(solution)/shard_map/ppermute | solution.py:250
  48.6 0.8 %collective-permute-done.19 = bf16[1,16,512]{2,1,0:T(8,128)(2,1)S(1)} collective-permute-done((bf16[1,16,512]{2,1,0:T(8,128)(2,1)S(1)}, bf16[1,16,512]{2,1,0:T(8,128)(2,1)S(1)}, u32[]{:S(2)}, u32[]{:S(2)}) %collective-permute-start.19) | collective-permute-done | bytes 16416 | tf_op jit(solution)/shard_map/ppermute | solution.py:250
  49.4 1.4 %collective-permute-start.20 = (f32[16,512]{1,0:T(8,128)S(1)}, f32[16,512]{1,0:T(8,128)S(1)}, u32[]{:S(2)}, u32[]{:S(2)}) collective-permute-start(f32[16,512]{1,0:T(8,128)S(1)} %fusion), channel_id=1, source_target_pairs={{0,16},{8,24},{16,0},{24,8},{1,17},{9,25},{17,1},{25,9},{2,18},{10... | collective-permute-start | bytes 98312 | tf_op jit(solution)/shard_map/ppermute | solution.py:250
  50.8 8.3 %collective-permute-done.20 = f32[16,512]{1,0:T(8,128)S(1)} collective-permute-done((f32[16,512]{1,0:T(8,128)S(1)}, f32[16,512]{1,0:T(8,128)S(1)}, u32[]{:S(2)}, u32[]{:S(2)}) %collective-permute-start.20) | collective-permute-done | bytes 32800 | tf_op jit(solution)/shard_map/ppermute | solution.py:250
  59.1 0.1 collective-permute-start.21
  59.1 1.3 %shard_map.117 = bf16[80,4096]{1,0:T(8,128)(2,1)} custom-call(bf16[80,256]{1,0:T(8,128)(2,1)S(1)} %get-tuple-element.25.weights, bf16[64,4096]{1,0:T(8,128)(2,1)S(1)} %bitcast.24, bf16[64,4096]{1,0:T(8,128)(2,1)S(1)} %collective-permute-done.1.q_sib.refs_3_.rest_1_, bf16[64,4096]{1,0:T(8,128)(2,1)S(1)} %collective-permute-done.2.q.refs_4_.rest_2_, ...), custom_call_target="tpu_custom_call" | custom-call | flops 1000 | bytes 1000 | tf_op jit(solution)/shard_map/pallas_call | solution.py:232
  60.5 0.0 collective-permute-done.16.rest_0_
  60.5 1.2 %shard_map.116 = bf16[64,4096]{1,0:T(8,128)(2,1)} custom-call(bf16[160,64]{1,0:T(8,128)(2,1)S(1)} %get-tuple-element.24.weights, bf16[80,4096]{1,0:T(8,128)(2,1)S(1)} %bitcast.18, bf16[80,4096]{1,0:T(8,128)(2,1)S(1)} %collective-permute-done.c_sib.refs_1_, bf16[64,4096]{1,0:T(8,128)(2,1)S(1)} %collective-permute-done.16.rest_0_), custom_call_target="tpu_custom_call" | custom-call | flops 1000 | bytes 1000 | tf_op jit(solution)/shard_map/pallas_call | solution.py:232
  61.7 0.0 collective-permute-done.21
  61.7 0.6 %broadcast_select_fusion = (f32[16,512]{1,0:T(8,128)}, f32[16,512]{1,0:T(8,128)}) fusion(f32[16,512]{1,0:T(8,128)S(1)} %add_multiply_fusion, f32[16,512]{1,0:T(8,128)S(1)} %collective-permute-done.21, pred[]{:T(512)S(6)} %eq.3), kind=kLoop, calls=%fused_computation.11 | loop fusion | flops 16384 | bytes 131073 | tf_op jit(solution)/shard_map/jit(_where)/select_n | solution.py:332
  (13 shorter events, 0.1 us)
Async XLA Ops:
  0.6 16.9 %copy-start.2 = (bf16[1,64,4096]{2,1,0:T(8,128)(2,1)S(1)}, bf16[1,64,4096]{2,1,0:T(8,128)(2,1)}, u32[]{:S(2)}) copy-start(bf16[1,64,4096]{2,1,0:T(8,128)(2,1)} %param.8) | copy-start | bytes 1572868
  1.4 5.8 %collective-permute-start.4 = (bf16[1,16,512]{2,1,0:T(8,128)(2,1)S(1)}, bf16[1,16,512]{2,1,0:T(8,128)(2,1)S(1)}, u32[]{:S(2)}, u32[]{:S(2)}) collective-permute-start(bf16[1,16,512]{2,1,0:T(8,128)(2,1)S(1)} %select_bitcast_fusion), channel_id=1, source_target_pairs={{0,4},{1,5},{2,6},{3,7},{4,0},{5,1},{6,2},{7,3},{8,12},{9,13},{10,... | collective-permute-start | bytes 49160 | tf_op jit(solution)/shard_map/ppermute | solution.py:250
  7.2 3.9 %collective-permute-start.5 = (bf16[2,16,512]{2,1,0:T(8,128)(2,1)S(1)}, bf16[2,16,512]{2,1,0:T(8,128)(2,1)S(1)}, u32[]{:S(2)}, u32[]{:S(2)}) collective-permute-start(bf16[2,16,512]{2,1,0:T(8,128)(2,1)S(1)} %pad_maximum_fusion.2), channel_id=1, source_target_pairs={{0,2},{1,3},{2,0},{3,1},{4,6},{5,7},{6,4},{7,5},{8,10},{9,11},{10,... | collective-permute-start | bytes 98312 | tf_op jit(solution)/shard_map/ppermute | solution.py:250
  9.1 8.4 %collective-permute-start = (bf16[80,4096]{1,0:T(8,128)(2,1)}, bf16[80,4096]{1,0:T(8,128)(2,1)S(1)}, u32[]{:S(2)}, u32[]{:S(2)}) collective-permute-start(bf16[80,4096]{1,0:T(8,128)(2,1)} %bitcast.12), channel_id=1, source_target_pairs={{0,8},{8,0},{16,24},{24,16},{1,9},{9,1},{17,25},{25,17},{2,10},{10... | collective-permute-start | bytes 1966088 | tf_op jit(solution)/shard_map/ppermute | solution.py:250
  9.1 8.2 %collective-permute-start.1 = (bf16[64,4096]{1,0:T(8,128)(2,1)}, bf16[64,4096]{1,0:T(8,128)(2,1)S(1)}, u32[]{:S(2)}, u32[]{:S(2)}) collective-permute-start(bf16[64,4096]{1,0:T(8,128)(2,1)} %bitcast.19), channel_id=1, source_target_pairs={{0,8},{8,0},{16,24},{24,16},{1,9},{9,1},{17,25},{25,17},{2,10},{10... | collective-permute-start | bytes 1572872 | tf_op jit(solution)/shard_map/ppermute | solution.py:250
  9.6 10.9 %collective-permute-start.9 = (bf16[80,4096]{1,0:T(8,128)(2,1)}, bf16[80,4096]{1,0:T(8,128)(2,1)S(1)}, u32[]{:S(2)}, u32[]{:S(2)}) collective-permute-start(bf16[80,4096]{1,0:T(8,128)(2,1)} %bitcast.25), channel_id=1, source_target_pairs={{0,8},{8,0},{16,24},{24,16},{1,9},{9,1},{17,25},{25,17},{2,10},{10... | collective-permute-start | bytes 1966088 | tf_op jit(solution)/shard_map/ppermute | solution.py:250
  11.1 4.3 %collective-permute-start.6 = (bf16[4,16,512]{2,1,0:T(8,128)(2,1)S(1)}, bf16[4,16,512]{2,1,0:T(8,128)(2,1)S(1)}, u32[]{:S(2)}, u32[]{:S(2)}) collective-permute-start(bf16[4,16,512]{2,1,0:T(8,128)(2,1)S(1)} %pad_maximum_fusion.1), channel_id=1, source_target_pairs={{0,1},{1,0},{2,3},{3,2},{4,5},{5,4},{6,7},{7,6},{8,9},{9,8},{10,11... | collective-permute-start | bytes 196616 | tf_op jit(solution)/shard_map/ppermute | solution.py:250
  13.1 7.4 %collective-permute-start.8 = (bf16[64,4096]{1,0:T(8,128)(2,1)}, bf16[64,4096]{1,0:T(8,128)(2,1)S(1)}, u32[]{:S(2)}, u32[]{:S(2)}) collective-permute-start(bf16[64,4096]{1,0:T(8,128)(2,1)} %bitcast.28), channel_id=1, source_target_pairs={{0,8},{8,0},{16,24},{24,16},{1,9},{9,1},{17,25},{25,17},{2,10},{10... | collective-permute-start | bytes 1572872 | tf_op jit(solution)/shard_map/ppermute | solution.py:250
  15.5 12.2 %collective-permute-start.2 = (bf16[64,4096]{1,0:T(8,128)(2,1)}, bf16[64,4096]{1,0:T(8,128)(2,1)S(1)}, u32[]{:S(2)}, u32[]{:S(2)}) collective-permute-start(bf16[64,4096]{1,0:T(8,128)(2,1)} %bitcast.20), channel_id=1, source_target_pairs={{0,16},{8,24},{16,0},{24,8},{1,17},{9,25},{17,1},{25,9},{2,18},{10... | collective-permute-start | bytes 1572872 | tf_op jit(solution)/shard_map/ppermute | solution.py:250
  17.4 3.2 %collective-permute-start.7 = (bf16[8,16,512]{2,1,0:T(8,128)(2,1)S(1)}, bf16[8,16,512]{2,1,0:T(8,128)(2,1)}, u32[]{:S(2)}, u32[]{:S(2)}) collective-permute-start(bf16[8,16,512]{2,1,0:T(8,128)(2,1)S(1)} %pad_maximum_fusion.maps), channel_id=1, source_target_pairs={{0,8},{8,0},{16,24},{24,16},{1,9},{9,1},{17,25},{25,17},{2,10},{10... | collective-permute-start | bytes 393224 | tf_op jit(solution)/shard_map/ppermute | solution.py:250
  17.4 0.7 %copy-start.5 = (s32[1,64]{1,0:T(1,128)S(1)}, s32[1,64]{1,0:T(1,128)}, u32[]{:S(2)}) copy-start(s32[1,64]{1,0:T(1,128)} %positives.1) | copy-start | bytes 772
  17.5 0.7 %copy-start.6 = (s32[1,64]{1,0:T(1,128)S(1)}, s32[1,64]{1,0:T(1,128)}, u32[]{:S(2)}) copy-start(s32[1,64]{1,0:T(1,128)} %hard.1) | copy-start | bytes 772
  18.1 1.1 %copy-start = (bf16[1,1,80,4096]{3,2,1,0:T(8,128)(2,1)S(1)}, bf16[1,1,80,4096]{3,2,1,0:T(8,128)(2,1)}, u32[]{:S(2)}) copy-start(bf16[1,1,80,4096]{3,2,1,0:T(8,128)(2,1)} %param.9) | copy-start | bytes 1966084
  19.2 1.3 %copy-start.3 = (bf16[1,1,80,4096]{3,2,1,0:T(8,128)(2,1)S(1)}, bf16[1,1,80,4096]{3,2,1,0:T(8,128)(2,1)}, u32[]{:S(2)}) copy-start(bf16[1,1,80,4096]{3,2,1,0:T(8,128)(2,1)} %param.13) | copy-start | bytes 1966084
  19.2 1.3 %copy-start.4 = (bf16[1,64,4096]{2,1,0:T(8,128)(2,1)S(1)}, bf16[1,64,4096]{2,1,0:T(8,128)(2,1)}, u32[]{:S(2)}) copy-start(bf16[1,64,4096]{2,1,0:T(8,128)(2,1)} %param.12) | copy-start | bytes 1572868
  20.3 7.4 %collective-permute-start.3 = (f32[8,64]{1,0:T(8,128)S(1)}, f32[8,64]{1,0:T(8,128)S(1)}, u32[]{:S(2)}, u32[]{:S(2)}) collective-permute-start(f32[8,64]{1,0:T(8,128)S(1)} %get-tuple-element.16.refs_10_), channel_id=1, source_target_pairs={{0,16},{8,24},{16,0},{24,8},{1,17},{9,25},{17,1},{25,9},{2,18},{10... | collective-permute-start | bytes 6152 | tf_op jit(solution)/shard_map/ppermute | solution.py:250
  27.7 4.9 %copy-start.1 = (bf16[1,1,80,4096]{3,2,1,0:T(8,128)(2,1)S(1)}, bf16[1,1,80,4096]{3,2,1,0:T(8,128)(2,1)}, u32[]{:S(2)}) copy-start(bf16[1,1,80,4096]{3,2,1,0:T(8,128)(2,1)} %param.9) | copy-start | bytes 1966084
  29.0 5.9 %collective-permute-start.10 = (bf16[64,4096]{1,0:T(8,128)(2,1)S(1)}, bf16[64,4096]{1,0:T(8,128)(2,1)S(1)}, u32[]{:S(2)}, u32[]{:S(2)}) collective-permute-start(bf16[64,4096]{1,0:T(8,128)(2,1)S(1)} %get-tuple-element.18), channel_id=1, source_target_pairs={{0,8},{8,0},{16,24},{24,16},{1,9},{9,1},{17,25},{25,17},{2,10},{10... | collective-permute-start | bytes 1572872 | tf_op jit(solution)/shard_map/ppermute | solution.py:250
  29.0 5.8 %collective-permute-start.14 = (bf16[160,64]{1,0:T(8,128)(2,1)S(1)}, bf16[160,64]{1,0:T(8,128)(2,1)S(1)}, u32[]{:S(2)}, u32[]{:S(2)}) collective-permute-start(bf16[160,64]{1,0:T(8,128)(2,1)S(1)} %get-tuple-element.20.weights.refs_14_), channel_id=1, source_target_pairs={{0,8},{8,0},{16,24},{24,16},{1,9},{9,1},{17,25},{25,17},{2,10},{10... | collective-permute-start | bytes 61448 | tf_op jit(solution)/shard_map/ppermute | solution.py:250
  29.5 2.1 %collective-permute-start.11 = (f32[8,64]{1,0:T(8,128)S(1)}, f32[8,64]{1,0:T(8,128)S(1)}, u32[]{:S(2)}, u32[]{:S(2)}) collective-permute-start(f32[8,64]{1,0:T(8,128)S(1)} %get-tuple-element.16.refs_10_), channel_id=1, source_target_pairs={{0,8},{8,0},{16,24},{24,16},{1,9},{9,1},{17,25},{25,17},{2,10},{10... | collective-permute-start | bytes 6152 | tf_op jit(solution)/shard_map/ppermute | solution.py:250
  29.6 5.3 %collective-permute-start.15 = (f32[16,128]{1,0:T(8,128)S(1)}, f32[16,128]{1,0:T(8,128)S(1)}, u32[]{:S(2)}, u32[]{:S(2)}) collective-permute-start(f32[16,128]{1,0:T(8,128)S(1)} %get-tuple-element.21.refs_16_), channel_id=1, source_target_pairs={{0,16},{8,24},{16,0},{24,8},{1,17},{9,25},{17,1},{25,9},{2,18},{10... | collective-permute-start | bytes 24584 | tf_op jit(solution)/shard_map/ppermute | solution.py:250
  31.1 3.8 %collective-permute-start.12 = (f32[24,64]{1,0:T(8,128)S(1)}, f32[24,64]{1,0:T(8,128)S(1)}, u32[]{:S(2)}, u32[]{:S(2)}) collective-permute-start(f32[24,64]{1,0:T(8,128)S(1)} %get-tuple-element.19), channel_id=1, source_target_pairs={{0,16},{8,24},{16,0},{24,8},{1,17},{9,25},{17,1},{25,9},{2,18},{10... | collective-permute-start | bytes 18440 | tf_op jit(solution)/shard_map/ppermute | solution.py:250
  31.6 3.3 %collective-permute-start.13 = (f32[24,64]{1,0:T(8,128)S(1)}, f32[24,64]{1,0:T(8,128)S(1)}, u32[]{:S(2)}, u32[]{:S(2)}) collective-permute-start(f32[24,64]{1,0:T(8,128)S(1)} %get-tuple-element.19), channel_id=1, source_target_pairs={{0,24},{8,16},{16,8},{24,0},{1,25},{9,17},{17,9},{25,1},{2,26},{10... | collective-permute-start | bytes 18440 | tf_op jit(solution)/shard_map/ppermute | solution.py:250
  36.3 4.3 %collective-permute-start.17 = (bf16[4,16,512]{2,1,0:T(8,128)(2,1)S(1)}, bf16[4,16,512]{2,1,0:T(8,128)(2,1)S(1)}, u32[]{:S(2)}, u32[]{:S(2)}) collective-permute-start(bf16[4,16,512]{2,1,0:T(8,128)(2,1)S(1)} %get-tuple-element.27), channel_id=1, source_target_pairs={{0,1},{1,0},{2,3},{3,2},{4,5},{5,4},{6,7},{7,6},{8,9},{9,8},{10,11... | collective-permute-start | bytes 196616 | tf_op jit(solution)/shard_map/ppermute | solution.py:250
  40.7 4.9 %collective-permute-start.18 = (bf16[2,16,512]{2,1,0:T(8,128)(2,1)S(1)}, bf16[2,16,512]{2,1,0:T(8,128)(2,1)S(1)}, u32[]{:S(2)}, u32[]{:S(2)}) collective-permute-start(bf16[2,16,512]{2,1,0:T(8,128)(2,1)S(1)} %slice.28), channel_id=1, source_target_pairs={{0,4},{1,5},{2,6},{3,7},{4,0},{5,1},{6,2},{7,3},{8,12},{9,13},{10,... | collective-permute-start | bytes 98312 | tf_op jit(solution)/shard_map/ppermute | solution.py:250
  45.6 3.8 %collective-permute-start.19 = (bf16[1,16,512]{2,1,0:T(8,128)(2,1)S(1)}, bf16[1,16,512]{2,1,0:T(8,128)(2,1)S(1)}, u32[]{:S(2)}, u32[]{:S(2)}) collective-permute-start(bf16[1,16,512]{2,1,0:T(8,128)(2,1)S(1)} %slice.29), channel_id=1, source_target_pairs={{0,2},{1,3},{2,0},{3,1},{4,6},{5,7},{6,4},{7,5},{8,10},{9,11},{10,... | collective-permute-start | bytes 49160 | tf_op jit(solution)/shard_map/ppermute | solution.py:250
  47.2 13.3 %collective-permute-start.16 = (bf16[64,4096]{1,0:T(8,128)(2,1)S(1)}, bf16[64,4096]{1,0:T(8,128)(2,1)S(1)}, u32[]{:S(2)}, u32[]{:S(2)}) collective-permute-start(bf16[64,4096]{1,0:T(8,128)(2,1)S(1)} %shard_map.114.refs_21_), channel_id=1, source_target_pairs={{0,16},{8,24},{16,0},{24,8},{1,17},{9,25},{17,1},{25,9},{2,18},{10... | collective-permute-start | bytes 1572872 | tf_op jit(solution)/shard_map/ppermute | solution.py:250
  49.4 9.7 %collective-permute-start.20 = (f32[16,512]{1,0:T(8,128)S(1)}, f32[16,512]{1,0:T(8,128)S(1)}, u32[]{:S(2)}, u32[]{:S(2)}) collective-permute-start(f32[16,512]{1,0:T(8,128)S(1)} %fusion), channel_id=1, source_target_pairs={{0,16},{8,24},{16,0},{24,8},{1,17},{9,25},{17,1},{25,9},{2,18},{10... | collective-permute-start | bytes 98312 | tf_op jit(solution)/shard_map/ppermute | solution.py:250
  59.1 2.6 %collective-permute-start.21 = (f32[16,512]{1,0:T(8,128)S(1)}, f32[16,512]{1,0:T(8,128)S(1)}, u32[]{:S(2)}, u32[]{:S(2)}) collective-permute-start(f32[16,512]{1,0:T(8,128)S(1)} %add_multiply_fusion), channel_id=1, source_target_pairs={{0,8},{8,0},{16,24},{24,16},{1,9},{9,1},{17,25},{25,17},{2,10},{10... | collective-permute-start | bytes 98312 | tf_op jit(solution)/shard_map/ppermute | solution.py:250

commit v3 on v2

--- a/solution.py
+++ b/solution.py
@@ -77,36 +77,39 @@
     stats[HARD : HARD + 1] = hard[...].astype(f32)
 
 
-def adapter_kernel(place, maps, other, hq, hq_sib, hc, hc_sib, c_own, c_sib, q_own, q_sib, message, low_c, c_up):
-    shards, rank, width = maps.shape
+def adapter_kernel(place, maps, hq, hq_sib, hc, hc_sib, c_own, c_sib, q_own, q_sib, message, low_c, c_up):
+    shards, _, rank, width = maps.shape
     places = reversed_bits(shards)
     core = place[0] & 1
 
-    def product(gathered, parts):
+    def product(which, parts):
         total = 0.0
         for at in range(shards):
             rows = jnp.concatenate([columns(r, at ^ place[1], width) for r in parts], 0)
-            total = total + dot(gathered[places[at]], rows, 1, 1)
+            total = total + dot(maps[places[at], which], rows, 1, 1)
         return total
+
+    c_up[...] = product(1, [c_own, c_sib])
 
     @pl.when(core == 0)
     def _():
-        message[...] = product(maps, [hq, hq_sib]).astype(bf16).astype(f32)
-        low_c[...] = product(maps, [hc, hc_sib]).astype(bf16)
-        c_up[...] = product(other, [c_own, c_sib])
+        message[...] = product(0, [hq, hq_sib]).astype(bf16).astype(f32)
+        low_c[...] = product(0, [hc, hc_sib]).astype(bf16)
 
     @pl.when(core == 1)
     def _():
-        message[...] = product(maps, [q_own, q_sib])
+        message[...] = product(1, [q_own, q_sib])
         low_c[...] = jnp.zeros_like(low_c)
-        c_up[...] = product(maps, [c_own, c_sib])
-
-
-def partner_kernel(place, c_own, c_sib, q, stats, c_up, answer, weights, q_again):
-    block, rows = c_own.shape[0], q.shape[0]
+
+
+def partner_kernel(place, c_own, c_sib, *refs):
+    *parts, stats, c_up, answer, weights, q_again = refs
+    block = c_own.shape[0]
+    q = jnp.concatenate([part[...] for part in parts], 1)
+    rows = q.shape[0]
     c = jnp.concatenate([c_own[...], c_sib[...]], 0)
-    q_again[...] = q[...]
-    total = dot(c, q[...], 1, 1)
+    q_again[...] = q
+    total = dot(c, q, 1, 1)
     owner, slot = layout(place[0], block, total.shape)
     keep = allowed(owner, slot, stats[HARD : HARD + 1], rows)
     total = jnp.where(keep, total * sharpness_factor, -jnp.inf)
@@ -122,22 +125,29 @@
     weights[...] = here
 
 
-def share_kernel(weights, c_own, c_sib, share):
-    for i in range(c_own.shape[1] // STEP):
-        at = slice(i * STEP, (i + 1) * STEP)
-        c = jnp.concatenate([c_own[:, at], c_sib[:, at]], 0)
-        share[:, at] = (dot(weights[...], c, 0, 0) * sharpness_factor).astype(bf16)
-
-
-def question_kernel(weights, c_own, c_sib, *rest):
+def share_kernel(weights, c_own, c_sib, *shares):
+    start = 0
+    for share in shares:
+        for i in range(0, share.shape[1], STEP):
+            at = slice(start + i, start + i + STEP)
+            c = jnp.concatenate([c_own[:, at], c_sib[:, at]], 0)
+            share[:, i : i + STEP] = (dot(weights[...], c, 0, 0) * sharpness_factor).astype(bf16)
+        start += share.shape[1]
+
+
+def question_kernel(pieces, weights, c_own, c_sib, *rest):
     shares, out = rest[:-1], rest[-1]
-    for i in range(c_own.shape[1] // STEP):
-        at = slice(i * STEP, (i + 1) * STEP)
-        c = jnp.concatenate([c_own[:, at], c_sib[:, at]], 0)
-        total = dot(weights[...], c, 0, 0) * sharpness_factor
-        for share in shares:
-            total = total + share[:, at].astype(f32)
-        out[:, at] = total.astype(bf16)
+    start = 0
+    for at_piece in range(pieces):
+        here = shares[at_piece::pieces]
+        for i in range(0, here[0].shape[1], STEP):
+            at = slice(start + i, start + i + STEP)
+            c = jnp.concatenate([c_own[:, at], c_sib[:, at]], 0)
+            total = dot(weights[...], c, 0, 0) * sharpness_factor
+            for share in here:
+                total = total + share[:, i : i + STEP].astype(f32)
+            out[:, at] = total.astype(bf16)
+        start += here[0].shape[1]
 
 
 def candidate_kernel(weights, *rest):
@@ -159,8 +169,8 @@
 def sums_kernel(partners, place, *refs):
     n = partners
     (c, q, far_q, far_q_sib, hq, hc, stats, answers, sib_answers, far_w, far_w_sib, message, far_messages,
-     (scores, low_c, c_up), (share,), (w_grad, w_own, keep, send)) = taken(
-        refs, 2, 2, n, n, 2, 2, 2, n, n, n, n, 1, n, 3, n and 1, 4)
+     (scores, low_c, c_up), (w_grad, w_own, keep, send)) = taken(
+        refs, 2, 2, n, n, 2, 2, 2, n, n, n, n, 1, n, 3, 4)
     block, rows = c[0].shape[0], q[0].shape[0]
     half, rank, width = keep.shape
 
@@ -241,6 +251,12 @@
     return run
 
 
+def cut(width, weights):
+    steps, total = width // STEP, sum(weights)
+    edges = [steps * sum(weights[:i]) // total * STEP for i in range(len(weights) + 1)]
+    return [slice(a, b) for a, b in zip(edges, edges[1:])]
+
+
 def shaped(shape, dtype=f32):
     return jax.ShapeDtypeStruct(shape, dtype)
 
@@ -264,38 +280,52 @@
     partners = list(range(2, devices, 2))
     even = (position & 1) == 0
 
-    far_q = [swap(q_own, "dp", k) for k in partners]
-    c_sib, q_sib, hq_sib, hc_sib = (swap(a, "dp", 1) for a in (c_own, q_own, hq, hc))
-
-    maps = jnp.where(even, adapter_down, adapter_up)[None]
-    for bit in bits_of(shards)[::-1]:
-        maps = jnp.concatenate([maps, swap(maps, "fsdp", bit)], 0)
-    other_maps = swap(maps, "dp", 1)
+    def after(array, *others):
+        return lax.optimization_barrier((array, *others))[0]
+
+    far_q = [[swap(q_own[:, at], "dp", k) for at in cut(width, (4, 2, 2))] for k in partners]
+    c_sib, q_sib = swap(c_own, "dp", 1), swap(q_own, "dp", 1)
+    hq_sib, hc_sib = (swap(after(a, c_sib, q_sib), "dp", 1) for a in (hq, hc))
 
     scores, stats = call(scores_kernel, (shaped((2 * block, 2 * rows)), shaped((BODY, rows))))(
         place, c_own, c_sib, q_own, q_sib, positives, hard_blocks
     )
+    far_stats = [swap(stats, "dp", k) for k in partners]
     sib_stats = swap(stats, "dp", 1)
-    far_stats = [swap(stats, "dp", k) for k in partners]
+
+    bits = bits_of(shards)[::-1]
+    maps = jnp.stack([adapter_down, adapter_up])[None]
+    for at, bit in enumerate(bits):
+        if at == len(bits) - 2:
+            maps = after(maps, c_sib, q_sib)
+        if at == len(bits) - 1:
+            maps = after(maps, scores, *[q[0] for q in far_q])
+        maps = jnp.concatenate([maps, swap(maps, "fsdp", bit)], 0)
+    maps = after(maps, *[q[1] for q in far_q])
     message, low_c, c_up = call(
         adapter_kernel, (shaped((rank, 2 * rows)), shaped((rank, 2 * block), bf16), shaped((rank, 2 * block)))
-    )(place, maps, other_maps, hq, hq_sib, hc, hc_sib, c_own, c_sib, q_own, q_sib)
+    )(place, maps, hq, hq_sib, hc, hc_sib, c_own, c_sib, q_own, q_sib)
     far_messages = [swap(message, "dp", k) for k in partners]
-
-    answers, sib_answers, far_w, far_w_sib, far_q_sib, shares, own_shares = [], [], [], [], [], [], []
+    c_up = after(c_up, sib_stats, *far_messages)
+
+    cuts = [at.stop - at.start for at in cut(width, (2, 3) + (2,) * (len(bits) - 2) + (1,))]
+    answers, sib_answers, far_w, far_w_sib, far_q_near, far_q_sib, sent, shares = [], [], [], [], [], [], [], []
     for k, q, far in zip(partners, far_q, far_stats):
         answer, weights, q_again = call(
             partner_kernel,
             (shaped((BODY + rank, rows)), shaped((2 * block, rows), bf16), shaped((rows, width), bf16)),
-        )(place, c_own, c_sib, q, far, c_up)
+        )(place, c_own, c_sib, *q, far, c_up)
         answers.append(swap(answer, "dp", k))
         sib_answers.append(swap(answer, "dp", k ^ 1))
         far_w.append(weights)
         far_w_sib.append(swap(weights, "dp", 1))
+        far_q_near.append(q_again)
         far_q_sib.append(swap(q_again, "dp", 1))
-        own_shares.append(call(share_kernel, shaped((rows, width), bf16))(weights, c_own, c_sib))
-        shares.append(swap(own_shares[-1], "dp", k))
-
+        parts = call(share_kernel, [shaped((rows, n), bf16) for n in cuts])(weights, c_own, c_sib)
+        sent.append(parts)
+        shares.append([swap(part, "dp", k) for part in parts])
+
+    scores = after(scores, *[part for parts in sent for part in parts])
     w_grad, w_own, keep, send = call(
         functools.partial(sums_kernel, len(partners)),
         (
@@ -305,24 +335,26 @@
             shaped((shards // 2, rank, shard_width), bf16),
         ),
     )(
-        place, c_own, c_sib, q_own, q_sib, *far_q, *far_q_sib, hq, hq_sib, hc, hc_sib, stats, sib_stats,
+        place, c_own, c_sib, q_own, q_sib, *far_q_near, *far_q_sib, hq, hq_sib, hc, hc_sib, stats, sib_stats,
         *answers, *sib_answers, *far_w, *far_w_sib, message, *far_messages, scores, low_c, c_up,
-        *own_shares[:1],
     )
     queries = [q_own, q_sib]
-    for pair in zip(far_q, far_q_sib):
+    for pair in zip(far_q_near, far_q_sib):
         queries += pair
     grad = call(candidate_kernel, shaped((block, width), bf16))(w_grad, *queries)
-    question = call(question_kernel, shaped((rows, width), bf16))(w_own, c_own, c_sib, *shares)
+    all_shares = [part for parts in shares for part in parts]
+    question = call(functools.partial(question_kernel, len(cuts)), shaped((rows, width), bf16))(w_own, c_own, c_sib, *all_shares)
 
     bits = bits_of(shards)[:1] + bits_of(shards)[:0:-1]
     terms = keep + swap(send, "fsdp", bits[0]).astype(f32)
-    for bit in bits[1:]:
+    for at, bit in enumerate(bits[1:]):
+        terms = after(terms, *[parts[at] for parts in shares])
         half = terms.shape[0] // 2
         terms = terms[:half] + swap(terms[half:].astype(bf16), "fsdp", bit).astype(f32)
-    terms = terms[0]
+    terms = after(terms[0], *[parts[-2] for parts in shares])
     for bit in bits_of(devices)[1:]:
         terms = terms + swap(terms, "dp", bit)
+    terms = after(terms, *[parts[-1] for parts in shares])
     terms = terms * adapter_scale
     others = swap(terms, "dp", 1)
     return (

time: 62.6 us -> 68.5 us (1.094)
  local copies, waits for them, and re-layouts: 1.69 us -> 6.01 us
  starting transfers between devices: 22.5 us -> 25 us
  waiting for transfers between devices: 27.1 us -> 25 us
  other arithmetic: 1.56 us -> 2.91 us
    unnamed x14 -> x38, local copies, waits for them, and re-layouts: 1.68 us -> 5.02 us
    ppermute x22 -> x26, starting transfers between devices: 22.5 us -> 25 us  [swap(): return lax.ppermute(array, axis, [(i, i ^ apart) for i in range(size)])]
    ppermute x22 -> x26, waiting for transfers between devices: 27.1 us -> 25 us  [swap(): return lax.ppermute(array, axis, [(i, i ^ apart) for i in range(size)])]
    slice x0 -> x2, local copies, waits for them, and re-layouts: none -> 0.98 us  [on_device(): q_own[:, at]]
    select_n x1, other arithmetic: 0.63 us -> 1.39 us  [on_device(): jnp.where(even, terms, others)]
  transfers between devices with their start and end apart: 22 -> 26, of which waited for: 9 -> 15; matrix products, arithmetic and copies ran while one was open for 0% -> 3% of each run, Pallas kernels for 10% -> 8%
where the time goes in v3:
time: 68.5 us; the launch traced here: 68 us
  starting transfers between devices  25 us (36%)
  waiting for transfers between devices  25 us (36%)
  Pallas kernels  8.36 us (12%)
  local copies, waits for them, and re-layouts  6.01 us (9%)
  other arithmetic  2.91 us (4%)
  between operations  0.84 us (1%)
    ppermute x26, waiting for transfers between devices, swap(): return lax.ppermute(array, axis, [(i, i ^ apart) for i in range(size)])  25 us
    ppermute x26, starting transfers between devices, swap(): return lax.ppermute(array, axis, [(i, i ^ apart) for i in range(size)])  25 us
    pallas_call x7, Pallas kernels, run(): pl.pallas_call(kernel, out_shape=outs, in_specs=[smem if a.dtype == jnp.i...  8.36 us
    unnamed x38, local copies, waits for them, and re-layouts  5.02 us
    select_n x1, other arithmetic, on_device(): jnp.where(even, terms, others)  1.39 us
  transfers between devices with their start and end apart: 26, of which 15 were waited for; matrix products, arithmetic and copies ran while one was open for 3% of the time, Pallas kernels for 8%

profile of v3, /device:TPU:0, one launch (start us, length us, event | category | flops | bytes accessed | tf_op | source)
XLA Modules:
  0.0 68.0 jit_solution(14013693851864884597)
XLA Ops:
  0.6 0.5 collective-permute-start
  1.2 0.1 collective-permute-start.1
  1.2 0.7 %maximum_bitcast_fusion = bf16[1,2,16,512]{3,2,1,0:T(8,128)(2,1)S(1)} fusion(bf16[1,16,512]{2,1,0:T(8,128)(2,1)} %bitcast.36, bf16[1,16,512]{2,1,0:T(8,128)(2,1)} %bitcast.37), kind=kLoop, calls=%fused_computation.7 | loop fusion | flops 16384 | bytes 65536 | tf_op jit(solution)/shard_map/broadcast_in_dim | solution.py:297
  2.0 4.0 %collective-permute-start.6 = (bf16[1,2,16,512]{3,2,1,0:T(8,128)(2,1)S(1)}, bf16[1,2,16,512]{3,2,1,0:T(8,128)(2,1)S(1)}, u32[]{:S(2)}, u32[]{:S(2)}) collective-permute-start(bf16[1,2,16,512]{3,2,1,0:T(8,128)(2,1)S(1)} %maximum_bitcast_fusion), channel_id=1, source_target_pairs={{0,4},{1,5},{2,6},{3,7},{4,0},{5,1},{6,2},{7,3},{8,12},{9,13},{10,... | collective-permute-start | bytes 98312 | tf_op jit(solution)/shard_map/ppermute | solution.py:266
  6.0 1.0 %slice.30 = bf16[64,2048]{1,0:T(8,128)(2,1)S(1)} slice(bf16[64,4096]{1,0:T(8,128)(2,1)} %bitcast.22), slice={[0:64], [0:2048]} | slice | bytes 524288 | tf_op jit(solution)/shard_map/slice | solution.py:286
  7.0 1.6 %collective-permute-start.2 = (bf16[64,2048]{1,0:T(8,128)(2,1)S(1)}, bf16[64,2048]{1,0:T(8,128)(2,1)S(1)}, u32[]{:S(2)}, u32[]{:S(2)}) collective-permute-start(bf16[64,2048]{1,0:T(8,128)(2,1)S(1)} %slice.30), channel_id=1, source_target_pairs={{0,16},{8,24},{16,0},{24,8},{1,17},{9,25},{17,1},{25,9},{2,18},{10... | collective-permute-start | bytes 786440 | tf_op jit(solution)/shard_map/ppermute | solution.py:266
  8.5 0.0 collective-permute-done.1.q_sib.refs_3_.rest_1_
  8.5 0.0 collective-permute-start.10
  8.6 1.6 %collective-permute-start.7 = (bf16[2,2,16,512]{3,2,1,0:T(8,128)(2,1)S(1)}, bf16[2,2,16,512]{3,2,1,0:T(8,128)(2,1)S(1)}, u32[]{:S(2)}, u32[]{:S(2)}) collective-permute-start(bf16[2,2,16,512]{3,2,1,0:T(8,128)(2,1)S(1)} %pad_maximum_fusion.2), channel_id=1, source_target_pairs={{0,2},{1,3},{2,0},{3,1},{4,6},{5,7},{6,4},{7,5},{8,10},{9,11},{10,... | collective-permute-start | bytes 196616 | tf_op jit(solution)/shard_map/ppermute | solution.py:266
  10.2 0.2 collective-permute-start.9
  10.4 0.1 pad_add_fusion.place
  10.5 0.6 copy-done.15
  11.1 0.0 copy-done.16
  11.1 1.0 %copy-done.1 = bf16[1,64,4096]{2,1,0:T(8,128)(2,1)S(1)} copy-done((bf16[1,64,4096]{2,1,0:T(8,128)(2,1)S(1)}, bf16[1,64,4096]{2,1,0:T(8,128)(2,1)}, u32[]{:S(2)}) %copy-start.1) | copy-done | bytes 524312
  12.1 1.1 %shard_map.111 = (f32[160,128]{1,0:T(8,128)S(1)}, f32[8,64]{1,0:T(8,128)S(1)}) custom-call(s32[2]{0:T(128)S(1)} %pad_add_fusion.place, bf16[80,4096]{1,0:T(8,128)(2,1)S(1)} %bitcast.15, bf16[80,4096]{1,0:T(8,128)(2,1)S(1)} %collective-permute-done.c_sib.refs_1_, bf16[64,4096]{1,0:T(8,128)(2,1)S(1)} %bitcast.23, ...), custom_call_target="tpu_custom_call" | custom-call | flops 1000 | bytes 1000 | tf_op jit(solution)/shard_map/pallas_call | solution.py:242
  13.2 0.0 copy-start.3
  13.3 1.8 %collective-permute-done.2.refs_0_ = bf16[64,2048]{1,0:T(8,128)(2,1)S(1)} collective-permute-done((bf16[64,2048]{1,0:T(8,128)(2,1)S(1)}, bf16[64,2048]{1,0:T(8,128)(2,1)S(1)}, u32[]{:S(2)}, u32[]{:S(2)}) %collective-permute-start.2) | collective-permute-done | bytes 262176 | tf_op jit(solution)/shard_map/ppermute | solution.py:266
  15.0 1.5 %collective-permute-start.8 = (bf16[4,2,16,512]{3,2,1,0:T(8,128)(2,1)S(1)}, bf16[4,2,16,512]{3,2,1,0:T(8,128)(2,1)S(1)}, u32[]{:S(2)}, u32[]{:S(2)}) collective-permute-start(bf16[4,2,16,512]{3,2,1,0:T(8,128)(2,1)S(1)} %pad_maximum_fusion.1), channel_id=1, source_target_pairs={{0,1},{1,0},{2,3},{3,2},{4,5},{5,4},{6,7},{7,6},{8,9},{9,8},{10,11... | collective-permute-start | bytes 393224 | tf_op jit(solution)/shard_map/ppermute | solution.py:266
  16.6 1.6 %collective-permute-start.3 = (bf16[64,1024]{1,0:T(8,128)(2,1)S(1)}, bf16[64,1024]{1,0:T(8,128)(2,1)S(1)}, u32[]{:S(2)}, u32[]{:S(2)}) collective-permute-start(bf16[64,1024]{1,0:T(8,128)(2,1)S(1)} %get-tuple-element.59), channel_id=1, source_target_pairs={{0,16},{8,24},{16,0},{24,8},{1,17},{9,25},{17,1},{25,9},{2,18},{10... | collective-permute-start | bytes 393224 | tf_op jit(solution)/shard_map/ppermute | solution.py:266
  18.1 0.5 collective-permute-start.4
  18.7 1.3 %collective-permute-done.8 = bf16[4,2,16,512]{3,2,1,0:T(8,128)(2,1)S(1)} collective-permute-done((bf16[4,2,16,512]{3,2,1,0:T(8,128)(2,1)S(1)}, bf16[4,2,16,512]{3,2,1,0:T(8,128)(2,1)S(1)}, u32[]{:S(2)}, u32[]{:S(2)}) %collective-permute-start.8) | collective-permute-done | bytes 131104 | tf_op jit(solution)/shard_map/ppermute | solution.py:266
  20.0 2.1 %collective-permute-done.3.refs_1_ = bf16[64,1024]{1,0:T(8,128)(2,1)S(1)} collective-permute-done((bf16[64,1024]{1,0:T(8,128)(2,1)S(1)}, bf16[64,1024]{1,0:T(8,128)(2,1)S(1)}, u32[]{:S(2)}, u32[]{:S(2)}) %collective-permute-start.3) | collective-permute-done | bytes 131104 | tf_op jit(solution)/shard_map/ppermute | solution.py:266
  22.1 1.7 %shard_map.112 = (f32[16,128]{1,0:T(8,128)S(1)}, bf16[16,160]{1,0:T(8,128)(2,1)S(1)}, f32[16,160]{1,0:T(8,128)S(1)}) custom-call(s32[2]{0:T(128)S(1)} %pad_add_fusion.place, bf16[8,2,16,512]{3,2,1,0:T(8,128)(2,1)S(1)} %pad_maximum_fusion.maps, bf16[64,4096]{1,0:T(8,128)(2,1)S(1)} %bitcast.32, bf16[64,4096]{1,0:T(8,128)(2,1)S(1)} %collective-permute-done.9.hq_sib.refs_7_, ...), custom_call_target="tpu_custom_call" | custom-call | flops 1000 | bytes 1000 | tf_op jit(solution)/shard_map/pallas_call | solution.py:242
  23.8 1.5 %collective-permute-start.12 = (f32[16,128]{1,0:T(8,128)S(1)}, f32[16,128]{1,0:T(8,128)S(1)}, u32[]{:S(2)}, u32[]{:S(2)}) collective-permute-start(f32[16,128]{1,0:T(8,128)S(1)} %get-tuple-element.39.refs_16_), channel_id=1, source_target_pairs={{0,16},{8,24},{16,0},{24,8},{1,17},{9,25},{17,1},{25,9},{2,18},{10... | collective-permute-start | bytes 24584 | tf_op jit(solution)/shard_map/ppermute | solution.py:266
  25.4 0.5 collective-permute-start.5
  25.9 0.6 collective-permute-done.11.refs_11_
  26.5 1.0 %collective-permute-done.12.refs_17_ = f32[16,128]{1,0:T(8,128)S(1)} collective-permute-done((f32[16,128]{1,0:T(8,128)S(1)}, f32[16,128]{1,0:T(8,128)S(1)}, u32[]{:S(2)}, u32[]{:S(2)}) %collective-permute-start.12) | collective-permute-done | bytes 8224 | tf_op jit(solution)/shard_map/ppermute | solution.py:266
  27.5 1.4 %collective-permute-done.5.refs_3_ = f32[8,64]{1,0:T(8,128)S(1)} collective-permute-done((f32[8,64]{1,0:T(8,128)S(1)}, f32[8,64]{1,0:T(8,128)S(1)}, u32[]{:S(2)}, u32[]{:S(2)}) %collective-permute-start.5) | collective-permute-done | bytes 2080 | tf_op jit(solution)/shard_map/ppermute | solution.py:266
  29.0 1.2 %shard_map.113 = (f32[24,64]{1,0:T(8,128)S(1)}, bf16[160,64]{1,0:T(8,128)(2,1)S(1)}, bf16[64,4096]{1,0:T(8,128)(2,1)S(1)}) custom-call(s32[2]{0:T(128)S(1)} %pad_add_fusion.place, bf16[80,4096]{1,0:T(8,128)(2,1)S(1)} %bitcast.17, bf16[80,4096]{1,0:T(8,128)(2,1)S(1)} %collective-permute-done.c_sib.refs_1_, ...), custom_call_target="tpu_custom_call" | custom-call | flops 1000 | bytes 1000 | tf_op jit(solution)/shard_map/pallas_call | solution.py:242
  30.2 0.5 collective-permute-start.16
  30.7 0.2 collective-permute-start.15
  30.9 1.5 %collective-permute-start.14 = (f32[24,64]{1,0:T(8,128)S(1)}, f32[24,64]{1,0:T(8,128)S(1)}, u32[]{:S(2)}, u32[]{:S(2)}) collective-permute-start(f32[24,64]{1,0:T(8,128)S(1)} %get-tuple-element.42), channel_id=1, source_target_pairs={{0,16},{8,24},{16,0},{24,8},{1,17},{9,25},{17,1},{25,9},{2,18},{10... | collective-permute-start | bytes 18440 | tf_op jit(solution)/shard_map/ppermute | solution.py:266
  32.4 0.4 shard_map.114
  32.8 1.1 %collective-permute-done.15.refs_13_ = f32[24,64]{1,0:T(8,128)S(1)} collective-permute-done((f32[24,64]{1,0:T(8,128)S(1)}, f32[24,64]{1,0:T(8,128)S(1)}, u32[]{:S(2)}, u32[]{:S(2)}) %collective-permute-start.15) | collective-permute-done | bytes 6176 | tf_op jit(solution)/shard_map/ppermute | solution.py:266
  33.9 0.7 %collective-permute-done.14.refs_12_ = f32[24,64]{1,0:T(8,128)S(1)} collective-permute-done((f32[24,64]{1,0:T(8,128)S(1)}, f32[24,64]{1,0:T(8,128)S(1)}, u32[]{:S(2)}, u32[]{:S(2)}) %collective-permute-start.14) | collective-permute-done | bytes 6176 | tf_op jit(solution)/shard_map/ppermute | solution.py:266
  34.6 1.4 %shard_map.115 = (bf16[80,256]{1,0:T(8,128)(2,1)S(1)}, bf16[160,64]{1,0:T(8,128)(2,1)S(1)}, f32[4,16,512]{2,1,0:T(8,128)S(1)}, bf16[4,16,512]{2,1,0:T(8,128)(2,1)S(1)}) custom-call(s32[2]{0:T(128)S(1)} %pad_add_fusion.place, bf16[80,4096]{1,0:T(8,128)(2,1)S(1)} %bitcast.19, bf16[80,4096]{1,0:T(8,128)(2,1)S(1)} %collective-permute-done.c_sib.refs_1_, ...), custom_call_target="tpu_custom_call" | custom-call | flops 1000 | bytes 1000 | tf_op jit(solution)/shard_map/pallas_call | solution.py:242
  36.1 0.0 copy-start.11
  36.1 0.0 copy-start.13
  36.1 0.0 copy-start.2
  36.1 0.6 collective-permute-start.21
  36.7 1.5 %collective-permute-start.17 = (bf16[64,1024]{1,0:T(8,128)(2,1)S(1)}, bf16[64,1024]{1,0:T(8,128)(2,1)S(1)}, u32[]{:S(2)}, u32[]{:S(2)}) collective-permute-start(bf16[64,1024]{1,0:T(8,128)(2,1)S(1)} %get-tuple-element.44), channel_id=1, source_target_pairs={{0,16},{8,24},{16,0},{24,8},{1,17},{9,25},{17,1},{25,9},{2,18},{10... | collective-permute-start | bytes 393224 | tf_op jit(solution)/shard_map/ppermute | solution.py:266
  38.2 2.3 %collective-permute-done.21 = bf16[4,16,512]{2,1,0:T(8,128)(2,1)S(1)} collective-permute-done((bf16[4,16,512]{2,1,0:T(8,128)(2,1)S(1)}, bf16[4,16,512]{2,1,0:T(8,128)(2,1)S(1)}, u32[]{:S(2)}, u32[]{:S(2)}) %collective-permute-start.21) | collective-permute-done | bytes 65568 | tf_op jit(solution)/shard_map/ppermute | solution.py:266
  40.5 1.2 %collective-permute-done.17.rest_0_ = bf16[64,1024]{1,0:T(8,128)(2,1)S(1)} collective-permute-done((bf16[64,1024]{1,0:T(8,128)(2,1)S(1)}, bf16[64,1024]{1,0:T(8,128)(2,1)S(1)}, u32[]{:S(2)}, u32[]{:S(2)}) %collective-permute-start.17) | collective-permute-done | bytes 131104 | tf_op jit(solution)/shard_map/ppermute | solution.py:266
  41.6 1.5 %collective-permute-start.22 = (bf16[2,16,512]{2,1,0:T(8,128)(2,1)S(1)}, bf16[2,16,512]{2,1,0:T(8,128)(2,1)S(1)}, u32[]{:S(2)}, u32[]{:S(2)}) collective-permute-start(bf16[2,16,512]{2,1,0:T(8,128)(2,1)S(1)} %slice.39), channel_id=1, source_target_pairs={{0,4},{1,5},{2,6},{3,7},{4,0},{5,1},{6,2},{7,3},{8,12},{9,13},{10,... | collective-permute-start | bytes 98312 | tf_op jit(solution)/shard_map/ppermute | solution.py:266
  43.1 1.5 %collective-permute-start.18 = (bf16[64,1536]{1,0:T(8,128)(2,1)S(1)}, bf16[64,1536]{1,0:T(8,128)(2,1)S(1)}, u32[]{:S(2)}, u32[]{:S(2)}) collective-permute-start(bf16[64,1536]{1,0:T(8,128)(2,1)S(1)} %get-tuple-element.45), channel_id=1, source_target_pairs={{0,16},{8,24},{16,0},{24,8},{1,17},{9,25},{17,1},{25,9},{2,18},{10... | collective-permute-start | bytes 589832 | tf_op jit(solution)/shard_map/ppermute | solution.py:266
  44.6 1.8 %collective-permute-done.22 = bf16[2,16,512]{2,1,0:T(8,128)(2,1)S(1)} collective-permute-done((bf16[2,16,512]{2,1,0:T(8,128)(2,1)S(1)}, bf16[2,16,512]{2,1,0:T(8,128)(2,1)S(1)}, u32[]{:S(2)}, u32[]{:S(2)}) %collective-permute-start.22) | collective-permute-done | bytes 32800 | tf_op jit(solution)/shard_map/ppermute | solution.py:266
  46.5 2.3 %collective-permute-done.18.rest_1_ = bf16[64,1536]{1,0:T(8,128)(2,1)S(1)} collective-permute-done((bf16[64,1536]{1,0:T(8,128)(2,1)S(1)}, bf16[64,1536]{1,0:T(8,128)(2,1)S(1)}, u32[]{:S(2)}, u32[]{:S(2)}) %collective-permute-start.18) | collective-permute-done | bytes 196640 | tf_op jit(solution)/shard_map/ppermute | solution.py:266
  48.8 0.7 copy-done.5
  49.5 0.9 %collective-permute-start.23 = (bf16[1,16,512]{2,1,0:T(8,128)(2,1)S(1)}, bf16[1,16,512]{2,1,0:T(8,128)(2,1)S(1)}, u32[]{:S(2)}, u32[]{:S(2)}) collective-permute-start(bf16[1,16,512]{2,1,0:T(8,128)(2,1)S(1)} %slice.40), channel_id=1, source_target_pairs={{0,2},{1,3},{2,0},{3,1},{4,6},{5,7},{6,4},{7,5},{8,10},{9,11},{10,... | collective-permute-start | bytes 49160 | tf_op jit(solution)/shard_map/ppermute | solution.py:266
  50.4 1.5 %collective-permute-start.20 = (bf16[64,512]{1,0:T(8,128)(2,1)S(1)}, bf16[64,512]{1,0:T(8,128)(2,1)S(1)}, u32[]{:S(2)}, u32[]{:S(2)}) collective-permute-start(bf16[64,512]{1,0:T(8,128)(2,1)S(1)} %get-tuple-element.47), channel_id=1, source_target_pairs={{0,16},{8,24},{16,0},{24,8},{1,17},{9,25},{17,1},{25,9},{2,18},{10... | collective-permute-start | bytes 196616 | tf_op jit(solution)/shard_map/ppermute | solution.py:266
  51.9 0.5 collective-permute-start.19
  52.4 0.8 %collective-permute-done.23 = bf16[1,16,512]{2,1,0:T(8,128)(2,1)S(1)} collective-permute-done((bf16[1,16,512]{2,1,0:T(8,128)(2,1)S(1)}, bf16[1,16,512]{2,1,0:T(8,128)(2,1)S(1)}, u32[]{:S(2)}, u32[]{:S(2)}) %collective-permute-start.23) | collective-permute-done | bytes 16416 | tf_op jit(solution)/shard_map/ppermute | solution.py:266
  53.2 3.7 %collective-permute-done.19.rest_2_ = bf16[64,1024]{1,0:T(8,128)(2,1)S(1)} collective-permute-done((bf16[64,1024]{1,0:T(8,128)(2,1)S(1)}, bf16[64,1024]{1,0:T(8,128)(2,1)S(1)}, u32[]{:S(2)}, u32[]{:S(2)}) %collective-permute-start.19) | collective-permute-done | bytes 131104 | tf_op jit(solution)/shard_map/ppermute | solution.py:266
  56.9 0.6 copy-done.7
  57.5 1.1 %collective-permute-start.24 = (f32[16,512]{1,0:T(8,128)S(1)}, f32[16,512]{1,0:T(8,128)S(1)}, u32[]{:S(2)}, u32[]{:S(2)}) collective-permute-start(f32[16,512]{1,0:T(8,128)S(1)} %add_bitcast_fusion), channel_id=1, source_target_pairs={{0,16},{8,24},{16,0},{24,8},{1,17},{9,25},{17,1},{25,9},{2,18},{10... | collective-permute-start | bytes 98312 | tf_op jit(solution)/shard_map/ppermute | solution.py:266
  58.6 2.9 %collective-permute-done.24 = f32[16,512]{1,0:T(8,128)S(1)} collective-permute-done((f32[16,512]{1,0:T(8,128)S(1)}, f32[16,512]{1,0:T(8,128)S(1)}, u32[]{:S(2)}, u32[]{:S(2)}) %collective-permute-start.24) | collective-permute-done | bytes 32800 | tf_op jit(solution)/shard_map/ppermute | solution.py:266
  61.5 0.6 copy-done.17
  62.1 0.6 copy-done.9
  62.7 0.6 broadcast_multiply_fusion
  63.3 0.8 %copy-done.14 = bf16[80,256]{1,0:T(8,128)(2,1)S(1)} copy-done((bf16[80,256]{1,0:T(8,128)(2,1)S(1)}, bf16[80,256]{1,0:T(8,128)(2,1)}, u32[]{:S(2)}) %copy-start.14) | copy-done | bytes 40984
  64.1 1.3 %shard_map.117 = bf16[80,4096]{1,0:T(8,128)(2,1)} custom-call(bf16[80,256]{1,0:T(8,128)(2,1)S(1)} %copy-done.14, bf16[64,4096]{1,0:T(8,128)(2,1)S(1)} %bitcast.27, bf16[64,4096]{1,0:T(8,128)(2,1)S(1)} %collective-permute-done.1.q_sib.refs_3_.rest_1_, bf16[64,4096]{1,0:T(8,128)(2,1)S(1)} %get-tuple-element.41.refs_4_.rest_2_, ...), custom_call_target="tpu_custom_call" | custom-call | flops 1000 | bytes 1000 | tf_op jit(solution)/shard_map/pallas_call | solution.py:242
  65.4 0.0 copy-start.18
  65.5 1.2 %shard_map.116 = bf16[64,4096]{1,0:T(8,128)(2,1)} custom-call(bf16[160,64]{1,0:T(8,128)(2,1)S(1)} %copy-done.12, bf16[80,4096]{1,0:T(8,128)(2,1)S(1)} %bitcast.20, bf16[80,4096]{1,0:T(8,128)(2,1)S(1)} %collective-permute-done.c_sib.refs_1_, bf16[64,1024]{1,0:T(8,128)(2,1)S(1)} %collective-permute-done.17.rest_0_, bf16[64,1536]{1,0:T(8,128)(2,1)S(1)} %copy-done.6, ...), custom_call_target="tpu_custom_call" | custom-call | flops 1000 | bytes 1000 | tf_op jit(solution)/shard_map/pallas_call | solution.py:242
  66.7 1.4 %broadcast_select_fusion = (f32[16,512]{1,0:T(8,128)}, f32[16,512]{1,0:T(8,128)}) fusion(f32[16,512]{1,0:T(8,128)} %collective-permute-done.25, pred[]{:T(512)S(6)} %eq.3, f32[16,512]{1,0:T(8,128)S(1)} %copy-done.18), kind=kLoop, calls=%fused_computation.10 | loop fusion | flops 24576 | bytes 131073 | tf_op jit(solution)/shard_map/jit(_where)/select_n | solution.py:364
  (48 shorter events, 0.2 us)
Async XLA Ops:
  0.6 9.9 %copy-start = (bf16[1,1,80,4096]{3,2,1,0:T(8,128)(2,1)S(1)}, bf16[1,1,80,4096]{3,2,1,0:T(8,128)(2,1)}, u32[]{:S(2)}) copy-start(bf16[1,1,80,4096]{3,2,1,0:T(8,128)(2,1)} %param.9) | copy-start | bytes 1966084
  0.6 7.9 %collective-permute-start = (bf16[80,4096]{1,0:T(8,128)(2,1)}, bf16[80,4096]{1,0:T(8,128)(2,1)S(1)}, u32[]{:S(2)}, u32[]{:S(2)}) collective-permute-start(bf16[80,4096]{1,0:T(8,128)(2,1)} %bitcast.14), channel_id=1, source_target_pairs={{0,8},{8,0},{16,24},{24,16},{1,9},{9,1},{17,25},{25,17},{2,10},{10... | collective-permute-start | bytes 1966088 | tf_op jit(solution)/shard_map/ppermute | solution.py:266
  1.2 7.4 %collective-permute-start.1 = (bf16[64,4096]{1,0:T(8,128)(2,1)}, bf16[64,4096]{1,0:T(8,128)(2,1)S(1)}, u32[]{:S(2)}, u32[]{:S(2)}) collective-permute-start(bf16[64,4096]{1,0:T(8,128)(2,1)} %bitcast.21), channel_id=1, source_target_pairs={{0,8},{8,0},{16,24},{24,16},{1,9},{9,1},{17,25},{25,17},{2,10},{10... | collective-permute-start | bytes 1572872 | tf_op jit(solution)/shard_map/ppermute | solution.py:266
  2.0 6.6 %collective-permute-start.6 = (bf16[1,2,16,512]{3,2,1,0:T(8,128)(2,1)S(1)}, bf16[1,2,16,512]{3,2,1,0:T(8,128)(2,1)S(1)}, u32[]{:S(2)}, u32[]{:S(2)}) collective-permute-start(bf16[1,2,16,512]{3,2,1,0:T(8,128)(2,1)S(1)} %maximum_bitcast_fusion), channel_id=1, source_target_pairs={{0,4},{1,5},{2,6},{3,7},{4,0},{5,1},{6,2},{7,3},{8,12},{9,13},{10,... | collective-permute-start | bytes 98312 | tf_op jit(solution)/shard_map/ppermute | solution.py:266
  7.0 8.1 %collective-permute-start.2 = (bf16[64,2048]{1,0:T(8,128)(2,1)S(1)}, bf16[64,2048]{1,0:T(8,128)(2,1)S(1)}, u32[]{:S(2)}, u32[]{:S(2)}) collective-permute-start(bf16[64,2048]{1,0:T(8,128)(2,1)S(1)} %slice.30), channel_id=1, source_target_pairs={{0,16},{8,24},{16,0},{24,8},{1,17},{9,25},{17,1},{25,9},{2,18},{10... | collective-permute-start | bytes 786440 | tf_op jit(solution)/shard_map/ppermute | solution.py:266
  8.5 13.6 %collective-permute-start.10 = (bf16[80,4096]{1,0:T(8,128)(2,1)}, bf16[80,4096]{1,0:T(8,128)(2,1)S(1)}, u32[]{:S(2)}, u32[]{:S(2)}) collective-permute-start(bf16[80,4096]{1,0:T(8,128)(2,1)} %bitcast.28), channel_id=1, source_target_pairs={{0,8},{8,0},{16,24},{24,16},{1,9},{9,1},{17,25},{25,17},{2,10},{10... | collective-permute-start | bytes 1966088 | tf_op jit(solution)/shard_map/ppermute | solution.py:266
  8.6 4.7 %collective-permute-start.7 = (bf16[2,2,16,512]{3,2,1,0:T(8,128)(2,1)S(1)}, bf16[2,2,16,512]{3,2,1,0:T(8,128)(2,1)S(1)}, u32[]{:S(2)}, u32[]{:S(2)}) collective-permute-start(bf16[2,2,16,512]{3,2,1,0:T(8,128)(2,1)S(1)} %pad_maximum_fusion.2), channel_id=1, source_target_pairs={{0,2},{1,3},{2,0},{3,1},{4,6},{5,7},{6,4},{7,5},{8,10},{9,11},{10,... | collective-permute-start | bytes 196616 | tf_op jit(solution)/shard_map/ppermute | solution.py:266
  10.2 11.9 %collective-permute-start.9 = (bf16[64,4096]{1,0:T(8,128)(2,1)}, bf16[64,4096]{1,0:T(8,128)(2,1)S(1)}, u32[]{:S(2)}, u32[]{:S(2)}) collective-permute-start(bf16[64,4096]{1,0:T(8,128)(2,1)} %bitcast.31), channel_id=1, source_target_pairs={{0,8},{8,0},{16,24},{24,16},{1,9},{9,1},{17,25},{25,17},{2,10},{10... | collective-permute-start | bytes 1572872 | tf_op jit(solution)/shard_map/ppermute | solution.py:266
  10.4 0.7 copy-start.15
  10.4 0.7 copy-start.16
  11.1 1.0 %copy-start.1 = (bf16[1,64,4096]{2,1,0:T(8,128)(2,1)S(1)}, bf16[1,64,4096]{2,1,0:T(8,128)(2,1)}, u32[]{:S(2)}) copy-start(bf16[1,64,4096]{2,1,0:T(8,128)(2,1)} %param.8) | copy-start | bytes 1572868
  13.2 8.9 %copy-start.3 = (bf16[1,1,80,4096]{3,2,1,0:T(8,128)(2,1)S(1)}, bf16[1,1,80,4096]{3,2,1,0:T(8,128)(2,1)}, u32[]{:S(2)}) copy-start(bf16[1,1,80,4096]{3,2,1,0:T(8,128)(2,1)} %param.13) | copy-start | bytes 1966084
  15.0 7.1 %copy-start.4 = (bf16[1,64,4096]{2,1,0:T(8,128)(2,1)S(1)}, bf16[1,64,4096]{2,1,0:T(8,128)(2,1)}, u32[]{:S(2)}) copy-start(bf16[1,64,4096]{2,1,0:T(8,128)(2,1)} %param.12) | copy-start | bytes 1572868
  15.0 5.0 %collective-permute-start.8 = (bf16[4,2,16,512]{3,2,1,0:T(8,128)(2,1)S(1)}, bf16[4,2,16,512]{3,2,1,0:T(8,128)(2,1)S(1)}, u32[]{:S(2)}, u32[]{:S(2)}) collective-permute-start(bf16[4,2,16,512]{3,2,1,0:T(8,128)(2,1)S(1)} %pad_maximum_fusion.1), channel_id=1, source_target_pairs={{0,1},{1,0},{2,3},{3,2},{4,5},{5,4},{6,7},{7,6},{8,9},{9,8},{10,11... | collective-permute-start | bytes 393224 | tf_op jit(solution)/shard_map/ppermute | solution.py:266
  16.6 5.5 %collective-permute-start.3 = (bf16[64,1024]{1,0:T(8,128)(2,1)S(1)}, bf16[64,1024]{1,0:T(8,128)(2,1)S(1)}, u32[]{:S(2)}, u32[]{:S(2)}) collective-permute-start(bf16[64,1024]{1,0:T(8,128)(2,1)S(1)} %get-tuple-element.59), channel_id=1, source_target_pairs={{0,16},{8,24},{16,0},{24,8},{1,17},{9,25},{17,1},{25,9},{2,18},{10... | collective-permute-start | bytes 393224 | tf_op jit(solution)/shard_map/ppermute | solution.py:266
  18.1 9.4 %collective-permute-start.4 = (bf16[64,1024]{1,0:T(8,128)(2,1)S(1)}, bf16[64,1024]{1,0:T(8,128)(2,1)S(1)}, u32[]{:S(2)}, u32[]{:S(2)}) collective-permute-start(bf16[64,1024]{1,0:T(8,128)(2,1)S(1)} %get-tuple-element.58), channel_id=1, source_target_pairs={{0,16},{8,24},{16,0},{24,8},{1,17},{9,25},{17,1},{25,9},{2,18},{10... | collective-permute-start | bytes 393224 | tf_op jit(solution)/shard_map/ppermute | solution.py:266
  23.8 3.7 %collective-permute-start.12 = (f32[16,128]{1,0:T(8,128)S(1)}, f32[16,128]{1,0:T(8,128)S(1)}, u32[]{:S(2)}, u32[]{:S(2)}) collective-permute-start(f32[16,128]{1,0:T(8,128)S(1)} %get-tuple-element.39.refs_16_), channel_id=1, source_target_pairs={{0,16},{8,24},{16,0},{24,8},{1,17},{9,25},{17,1},{25,9},{2,18},{10... | collective-permute-start | bytes 24584 | tf_op jit(solution)/shard_map/ppermute | solution.py:266
  25.4 1.2 %collective-permute-start.11 = (f32[8,64]{1,0:T(8,128)S(1)}, f32[8,64]{1,0:T(8,128)S(1)}, u32[]{:S(2)}, u32[]{:S(2)}) collective-permute-start(f32[8,64]{1,0:T(8,128)S(1)} %get-tuple-element.31.refs_10_), channel_id=1, source_target_pairs={{0,8},{8,0},{16,24},{24,16},{1,9},{9,1},{17,25},{25,17},{2,10},{10... | collective-permute-start | bytes 6152 | tf_op jit(solution)/shard_map/ppermute | solution.py:266
  25.4 3.6 %collective-permute-start.5 = (f32[8,64]{1,0:T(8,128)S(1)}, f32[8,64]{1,0:T(8,128)S(1)}, u32[]{:S(2)}, u32[]{:S(2)}) collective-permute-start(f32[8,64]{1,0:T(8,128)S(1)} %get-tuple-element.31.refs_10_), channel_id=1, source_target_pairs={{0,16},{8,24},{16,0},{24,8},{1,17},{9,25},{17,1},{25,9},{2,18},{10... | collective-permute-start | bytes 6152 | tf_op jit(solution)/shard_map/ppermute | solution.py:266
  30.2 4.4 %collective-permute-start.13 = (bf16[64,4096]{1,0:T(8,128)(2,1)S(1)}, bf16[64,4096]{1,0:T(8,128)(2,1)S(1)}, u32[]{:S(2)}, u32[]{:S(2)}) collective-permute-start(bf16[64,4096]{1,0:T(8,128)(2,1)S(1)} %get-tuple-element.41.refs_4_.rest_2_), channel_id=1, source_target_pairs={{0,8},{8,0},{16,24},{24,16},{1,9},{9,1},{17,25},{25,17},{2,10},{10... | collective-permute-start | bytes 1572872 | tf_op jit(solution)/shard_map/ppermute | solution.py:266
  30.2 4.4 %collective-permute-start.16 = (bf16[160,64]{1,0:T(8,128)(2,1)S(1)}, bf16[160,64]{1,0:T(8,128)(2,1)S(1)}, u32[]{:S(2)}, u32[]{:S(2)}) collective-permute-start(bf16[160,64]{1,0:T(8,128)(2,1)S(1)} %get-tuple-element.43.weights.refs_14_), channel_id=1, source_target_pairs={{0,8},{8,0},{16,24},{24,16},{1,9},{9,1},{17,25},{25,17},{2,10},{10... | collective-permute-start | bytes 61448 | tf_op jit(solution)/shard_map/ppermute | solution.py:266
  30.7 3.1 %collective-permute-start.15 = (f32[24,64]{1,0:T(8,128)S(1)}, f32[24,64]{1,0:T(8,128)S(1)}, u32[]{:S(2)}, u32[]{:S(2)}) collective-permute-start(f32[24,64]{1,0:T(8,128)S(1)} %get-tuple-element.42), channel_id=1, source_target_pairs={{0,24},{8,16},{16,8},{24,0},{1,25},{9,17},{17,9},{25,1},{2,26},{10... | collective-permute-start | bytes 18440 | tf_op jit(solution)/shard_map/ppermute | solution.py:266
  30.9 3.7 %collective-permute-start.14 = (f32[24,64]{1,0:T(8,128)S(1)}, f32[24,64]{1,0:T(8,128)S(1)}, u32[]{:S(2)}, u32[]{:S(2)}) collective-permute-start(f32[24,64]{1,0:T(8,128)S(1)} %get-tuple-element.42), channel_id=1, source_target_pairs={{0,16},{8,24},{16,0},{24,8},{1,17},{9,25},{17,1},{25,9},{2,18},{10... | collective-permute-start | bytes 18440 | tf_op jit(solution)/shard_map/ppermute | solution.py:266
  36.1 4.4 %copy-start.11 = (bf16[160,64]{1,0:T(8,128)(2,1)}, bf16[160,64]{1,0:T(8,128)(2,1)S(1)}, u32[]{:S(2)}) copy-start(bf16[160,64]{1,0:T(8,128)(2,1)S(1)} %get-tuple-element.50.weights) | copy-start | bytes 61444
  36.1 4.4 %copy-start.13 = (bf16[80,256]{1,0:T(8,128)(2,1)}, bf16[80,256]{1,0:T(8,128)(2,1)S(1)}, u32[]{:S(2)}) copy-start(bf16[80,256]{1,0:T(8,128)(2,1)S(1)} %get-tuple-element.51.weights) | copy-start | bytes 122884
  36.1 27.2 %copy-start.2 = (bf16[1,64,4096]{2,1,0:T(8,128)(2,1)S(1)}, bf16[1,64,4096]{2,1,0:T(8,128)(2,1)}, u32[]{:S(2)}) copy-start(bf16[1,64,4096]{2,1,0:T(8,128)(2,1)} %param.8) | copy-start | bytes 1572868
  36.1 4.3 %collective-permute-start.21 = (bf16[4,16,512]{2,1,0:T(8,128)(2,1)S(1)}, bf16[4,16,512]{2,1,0:T(8,128)(2,1)S(1)}, u32[]{:S(2)}, u32[]{:S(2)}) collective-permute-start(bf16[4,16,512]{2,1,0:T(8,128)(2,1)S(1)} %get-tuple-element.53), channel_id=1, source_target_pairs={{0,1},{1,0},{2,3},{3,2},{4,5},{5,4},{6,7},{7,6},{8,9},{9,8},{10,11... | collective-permute-start | bytes 196616 | tf_op jit(solution)/shard_map/ppermute | solution.py:266
  36.7 5.0 %collective-permute-start.17 = (bf16[64,1024]{1,0:T(8,128)(2,1)S(1)}, bf16[64,1024]{1,0:T(8,128)(2,1)S(1)}, u32[]{:S(2)}, u32[]{:S(2)}) collective-permute-start(bf16[64,1024]{1,0:T(8,128)(2,1)S(1)} %get-tuple-element.44), channel_id=1, source_target_pairs={{0,16},{8,24},{16,0},{24,8},{1,17},{9,25},{17,1},{25,9},{2,18},{10... | collective-permute-start | bytes 393224 | tf_op jit(solution)/shard_map/ppermute | solution.py:266
  41.6 4.8 %collective-permute-start.22 = (bf16[2,16,512]{2,1,0:T(8,128)(2,1)S(1)}, bf16[2,16,512]{2,1,0:T(8,128)(2,1)S(1)}, u32[]{:S(2)}, u32[]{:S(2)}) collective-permute-start(bf16[2,16,512]{2,1,0:T(8,128)(2,1)S(1)} %slice.39), channel_id=1, source_target_pairs={{0,4},{1,5},{2,6},{3,7},{4,0},{5,1},{6,2},{7,3},{8,12},{9,13},{10,... | collective-permute-start | bytes 98312 | tf_op jit(solution)/shard_map/ppermute | solution.py:266
  43.1 5.7 %collective-permute-start.18 = (bf16[64,1536]{1,0:T(8,128)(2,1)S(1)}, bf16[64,1536]{1,0:T(8,128)(2,1)S(1)}, u32[]{:S(2)}, u32[]{:S(2)}) collective-permute-start(bf16[64,1536]{1,0:T(8,128)(2,1)S(1)} %get-tuple-element.45), channel_id=1, source_target_pairs={{0,16},{8,24},{16,0},{24,8},{1,17},{9,25},{17,1},{25,9},{2,18},{10... | collective-permute-start | bytes 589832 | tf_op jit(solution)/shard_map/ppermute | solution.py:266
  48.8 0.7 copy-start.5
  49.5 3.7 %collective-permute-start.23 = (bf16[1,16,512]{2,1,0:T(8,128)(2,1)S(1)}, bf16[1,16,512]{2,1,0:T(8,128)(2,1)S(1)}, u32[]{:S(2)}, u32[]{:S(2)}) collective-permute-start(bf16[1,16,512]{2,1,0:T(8,128)(2,1)S(1)} %slice.40), channel_id=1, source_target_pairs={{0,2},{1,3},{2,0},{3,1},{4,6},{5,7},{6,4},{7,5},{8,10},{9,11},{10,... | collective-permute-start | bytes 49160 | tf_op jit(solution)/shard_map/ppermute | solution.py:266
  50.4 11.0 %collective-permute-start.20 = (bf16[64,512]{1,0:T(8,128)(2,1)S(1)}, bf16[64,512]{1,0:T(8,128)(2,1)S(1)}, u32[]{:S(2)}, u32[]{:S(2)}) collective-permute-start(bf16[64,512]{1,0:T(8,128)(2,1)S(1)} %get-tuple-element.47), channel_id=1, source_target_pairs={{0,16},{8,24},{16,0},{24,8},{1,17},{9,25},{17,1},{25,9},{2,18},{10... | collective-permute-start | bytes 196616 | tf_op jit(solution)/shard_map/ppermute | solution.py:266
  51.9 5.0 %collective-permute-start.19 = (bf16[64,1024]{1,0:T(8,128)(2,1)S(1)}, bf16[64,1024]{1,0:T(8,128)(2,1)S(1)}, u32[]{:S(2)}, u32[]{:S(2)}) collective-permute-start(bf16[64,1024]{1,0:T(8,128)(2,1)S(1)} %get-tuple-element.46), channel_id=1, source_target_pairs={{0,16},{8,24},{16,0},{24,8},{1,17},{9,25},{17,1},{25,9},{2,18},{10... | collective-permute-start | bytes 393224 | tf_op jit(solution)/shard_map/ppermute | solution.py:266
  56.9 0.6 copy-start.7
  57.5 3.9 %collective-permute-start.24 = (f32[16,512]{1,0:T(8,128)S(1)}, f32[16,512]{1,0:T(8,128)S(1)}, u32[]{:S(2)}, u32[]{:S(2)}) collective-permute-start(f32[16,512]{1,0:T(8,128)S(1)} %add_bitcast_fusion), channel_id=1, source_target_pairs={{0,16},{8,24},{16,0},{24,8},{1,17},{9,25},{17,1},{25,9},{2,18},{10... | collective-permute-start | bytes 98312 | tf_op jit(solution)/shard_map/ppermute | solution.py:266
  61.4 0.6 copy-start.17
  62.1 0.6 copy-start.9
  63.3 3.3 %collective-permute-start.25 = (f32[16,512]{1,0:T(8,128)}, f32[16,512]{1,0:T(8,128)}, u32[]{:S(2)}, u32[]{:S(2)}) collective-permute-start(f32[16,512]{1,0:T(8,128)} %broadcast_multiply_fusion), channel_id=1, source_target_pairs={{0,8},{8,0},{16,24},{24,16},{1,9},{9,1},{17,25},{25,17},{2,10},{10... | collective-permute-start | bytes 98312 | tf_op jit(solution)/shard_map/ppermute | solution.py:266
  63.3 0.8 %copy-start.14 = (bf16[80,256]{1,0:T(8,128)(2,1)S(1)}, bf16[80,256]{1,0:T(8,128)(2,1)}, u32[]{:S(2)}) copy-start(bf16[80,256]{1,0:T(8,128)(2,1)} %copy-done.13) | copy-start | bytes 122884
  64.1 1.3 %copy-start.6 = (bf16[64,1536]{1,0:T(8,128)(2,1)S(1)}, bf16[64,1536]{1,0:T(8,128)(2,1)}, u32[]{:S(2)}) copy-start(bf16[64,1536]{1,0:T(8,128)(2,1)} %copy-done.5) | copy-start | bytes 589828
  64.1 1.3 %copy-start.8 = (bf16[64,1024]{1,0:T(8,128)(2,1)S(1)}, bf16[64,1024]{1,0:T(8,128)(2,1)}, u32[]{:S(2)}) copy-start(bf16[64,1024]{1,0:T(8,128)(2,1)} %copy-done.7) | copy-start | bytes 393220
  64.1 1.3 %copy-start.10 = (bf16[64,512]{1,0:T(8,128)(2,1)S(1)}, bf16[64,512]{1,0:T(8,128)(2,1)}, u32[]{:S(2)}) copy-start(bf16[64,512]{1,0:T(8,128)(2,1)} %copy-done.9) | copy-start | bytes 196612
  64.1 1.3 %copy-start.12 = (bf16[160,64]{1,0:T(8,128)(2,1)S(1)}, bf16[160,64]{1,0:T(8,128)(2,1)}, u32[]{:S(2)}) copy-start(bf16[160,64]{1,0:T(8,128)(2,1)} %copy-done.11) | copy-start | bytes 61444
  65.4 1.2 %copy-start.18 = (f32[16,512]{1,0:T(8,128)S(1)}, f32[16,512]{1,0:T(8,128)}, u32[]{:S(2)}) copy-start(f32[16,512]{1,0:T(8,128)} %copy-done.17) | copy-start | bytes 98308

commit v4 on v3

--- a/solution.py
+++ b/solution.py
@@ -10,6 +10,7 @@
 sharpness_factor = 50.0
 adapter_scale = 2.0
 STEP = 512
+PICKS = {1: [(1,)], 2: [(1,), (0, 1), (1, 1)]}
 MAX, SUM, POSITIVE, HARD, BODY = 0, 1, 2, 3, 8
 
 f32 = jnp.float32
@@ -20,9 +21,20 @@
     return [1 << b for b in range(size.bit_length() - 1)]
 
 
-def reversed_bits(size):
-    bits = bits_of(size)
-    return [sum(low for low, high in zip(bits, bits[::-1]) if i & high) for i in range(size)]
+def stages_of(size):
+    stages, bits = [], bits_of(size)
+    while bits:
+        take = 1 if not stages else 2
+        stages.append(sorted({sum(b for b, on in zip(bits[:take], pick) if on) for pick in PICKS[take]}))
+        bits = bits[take:]
+    return stages
+
+
+def places_of(size):
+    order = [0]
+    for stage in stages_of(size)[::-1]:
+        order = [apart ^ i for apart in [0] + stage for i in order]
+    return [order.index(i) for i in range(size)]
 
 
 def dot(left, right, left_dim, right_dim):
@@ -79,7 +91,7 @@
 
 def adapter_kernel(place, maps, hq, hq_sib, hc, hc_sib, c_own, c_sib, q_own, q_sib, message, low_c, c_up):
     shards, _, rank, width = maps.shape
-    places = reversed_bits(shards)
+    places = places_of(shards)
     core = place[0] & 1
 
     def product(which, parts):
@@ -105,7 +117,7 @@
 def partner_kernel(place, c_own, c_sib, *refs):
     *parts, stats, c_up, answer, weights, q_again = refs
     block = c_own.shape[0]
-    q = jnp.concatenate([part[...] for part in parts], 1)
+    q = jnp.concatenate([part[...] for part in parts], 0)
     rows = q.shape[0]
     c = jnp.concatenate([c_own[...], c_sib[...]], 0)
     q_again[...] = q
@@ -199,11 +211,14 @@
     for pair in zip(far_q, far_q_sib):
         queries += pair
 
+    order = places_of(2 * half)
+
     def store(at, total):
-        if at & 1:
-            send[at >> 1] = total.astype(bf16)
+        slot = order[at]
+        if slot >= half:
+            send[slot - half] = total.astype(bf16)
         else:
-            keep[at >> 1] = total
+            keep[slot] = total
 
     def split(terms):
         high = terms.astype(bf16)
@@ -244,7 +259,7 @@
             out_shape=outs,
             in_specs=[smem if a.dtype == jnp.int32 and a.ndim == 1 else vmem for a in args],
             out_specs=jax.tree.map(lambda _: vmem, outs),
-            compiler_params=pltpu.CompilerParams(vmem_limit_bytes=40 * 2**20),
+            compiler_params=pltpu.CompilerParams(vmem_limit_bytes=16 * 2**20),
             cost_estimate=pl.CostEstimate(flops=1000, bytes_accessed=1000, transcendentals=0),
         )(*args)
 
@@ -255,6 +270,10 @@
     steps, total = width // STEP, sum(weights)
     edges = [steps * sum(weights[:i]) // total * STEP for i in range(len(weights) + 1)]
     return [slice(a, b) for a, b in zip(edges, edges[1:])]
+
+
+def halves(size):
+    return slice(0, size // 2), slice(size // 2, size)
 
 
 def shaped(shape, dtype=f32):
@@ -283,32 +302,26 @@
     def after(array, *others):
         return lax.optimization_barrier((array, *others))[0]
 
-    far_q = [[swap(q_own[:, at], "dp", k) for at in cut(width, (4, 2, 2))] for k in partners]
-    c_sib, q_sib = swap(c_own, "dp", 1), swap(q_own, "dp", 1)
-    hq_sib, hc_sib = (swap(after(a, c_sib, q_sib), "dp", 1) for a in (hq, hc))
-
+    far_q = [[swap(q_own[at], "dp", k) for at in halves(rows)] for k in partners]
+    stages = stages_of(shards)
+    maps = jnp.stack([adapter_down, adapter_up])[None]
+    c_sib = swap(c_own, "dp", 1)
+    for stage in stages[::-1]:
+        if stage is stages[0]:
+            maps = after(maps, c_sib, *[q[0] for q in far_q])
+            q_sib, hq_sib, hc_sib = (swap(after(a, maps), "dp", 1) for a in (q_own, hq, hc))
+        maps = jnp.concatenate([maps] + [swap(maps, "fsdp", apart) for apart in stage], 0)
     scores, stats = call(scores_kernel, (shaped((2 * block, 2 * rows)), shaped((BODY, rows))))(
         place, c_own, c_sib, q_own, q_sib, positives, hard_blocks
     )
     far_stats = [swap(stats, "dp", k) for k in partners]
     sib_stats = swap(stats, "dp", 1)
-
-    bits = bits_of(shards)[::-1]
-    maps = jnp.stack([adapter_down, adapter_up])[None]
-    for at, bit in enumerate(bits):
-        if at == len(bits) - 2:
-            maps = after(maps, c_sib, q_sib)
-        if at == len(bits) - 1:
-            maps = after(maps, scores, *[q[0] for q in far_q])
-        maps = jnp.concatenate([maps, swap(maps, "fsdp", bit)], 0)
-    maps = after(maps, *[q[1] for q in far_q])
     message, low_c, c_up = call(
         adapter_kernel, (shaped((rank, 2 * rows)), shaped((rank, 2 * block), bf16), shaped((rank, 2 * block)))
     )(place, maps, hq, hq_sib, hc, hc_sib, c_own, c_sib, q_own, q_sib)
     far_messages = [swap(message, "dp", k) for k in partners]
-    c_up = after(c_up, sib_stats, *far_messages)
-
-    cuts = [at.stop - at.start for at in cut(width, (2, 3) + (2,) * (len(bits) - 2) + (1,))]
+
+    cuts = [width // 4, width // 2, width // 4]
     answers, sib_answers, far_w, far_w_sib, far_q_near, far_q_sib, sent, shares = [], [], [], [], [], [], [], []
     for k, q, far in zip(partners, far_q, far_stats):
         answer, weights, q_again = call(
@@ -321,9 +334,8 @@
         far_w_sib.append(swap(weights, "dp", 1))
         far_q_near.append(q_again)
         far_q_sib.append(swap(q_again, "dp", 1))
-        parts = call(share_kernel, [shaped((rows, n), bf16) for n in cuts])(weights, c_own, c_sib)
-        sent.append(parts)
-        shares.append([swap(part, "dp", k) for part in parts])
+        sent.append(call(share_kernel, [shaped((rows, n), bf16) for n in cuts])(weights, c_own, c_sib))
+        shares.append([swap(part, "dp", k) for part in sent[-1]])
 
     scores = after(scores, *[part for parts in sent for part in parts])
     w_grad, w_own, keep, send = call(
@@ -342,19 +354,19 @@
     for pair in zip(far_q_near, far_q_sib):
         queries += pair
     grad = call(candidate_kernel, shaped((block, width), bf16))(w_grad, *queries)
-    all_shares = [part for parts in shares for part in parts]
-    question = call(functools.partial(question_kernel, len(cuts)), shaped((rows, width), bf16))(w_own, c_own, c_sib, *all_shares)
-
-    bits = bits_of(shards)[:1] + bits_of(shards)[:0:-1]
-    terms = keep + swap(send, "fsdp", bits[0]).astype(f32)
-    for at, bit in enumerate(bits[1:]):
-        terms = after(terms, *[parts[at] for parts in shares])
-        half = terms.shape[0] // 2
-        terms = terms[:half] + swap(terms[half:].astype(bf16), "fsdp", bit).astype(f32)
-    terms = after(terms[0], *[parts[-2] for parts in shares])
+    question = call(functools.partial(question_kernel, len(cuts)), shaped((rows, width), bf16))(
+        w_own, c_own, c_sib, *[part for parts in shares for part in parts]
+    )
+
+    terms = keep + swap(send, "fsdp", 1).astype(f32)
+    for at, stage in enumerate(stages[1:]):
+        terms = after(terms, *[parts[0] for parts in shares]) if at == 0 else terms
+        part = terms.shape[0] // (len(stage) + 1)
+        got = [swap(terms[(i + 1) * part : (i + 2) * part].astype(bf16), "fsdp", apart) for i, apart in enumerate(stage)]
+        terms = sum([g.astype(f32) for g in got], terms[:part])
+    terms = after(terms[0], *[parts[1] for parts in shares])
     for bit in bits_of(devices)[1:]:
         terms = terms + swap(terms, "dp", bit)
-    terms = after(terms, *[parts[-1] for parts in shares])
     terms = terms * adapter_scale
     others = swap(terms, "dp", 1)
     return (

time: 68.5 us -> 60.3 us (0.88)
  waiting for transfers between devices: 25 us -> 18.1 us
  local copies, waits for them, and re-layouts: 6.01 us -> 3.58 us
  Pallas kernels: 8.36 us -> 9.46 us
    ppermute x26, waiting for transfers between devices: 25 us -> 18.1 us  [swap(): return lax.ppermute(array, axis, [(i, i ^ apart) for i in range(size)])]
    unnamed x38 -> x32, local copies, waits for them, and re-layouts: 5.02 us -> 1.81 us
    concatenate x3 -> x2, other arithmetic: 0.05 us -> 1.66 us  [on_device(): jnp.concatenate([maps] + [swap(maps, 'fsdp', apart) for apart in stage], 0)]
    pallas_call x7, Pallas kernels: 8.36 us -> 9.46 us  [run(): pl.pallas_call(kernel, out_shape=outs, in_specs=[smem if a.dtype == jnp.i...]
    slice x4 -> x2, local copies, waits for them, and re-layouts: 1 us -> 1.77 us  [the longest x1 1.76 us: on_device(): q_own[at]]
    select_n x1, other arithmetic: 1.39 us -> 0.63 us  [on_device(): jnp.where(even, terms, others)]
  transfers between devices with their start and end apart: 26 -> 26, of which waited for: 15 -> 13; matrix products, arithmetic and copies ran while one was open for 3% -> 7% of each run, Pallas kernels for 8% -> 11%
where the time goes in v4:
time: 60.3 us; the launch traced here: 60 us
  starting transfers between devices  24.8 us (41%)
  waiting for transfers between devices  18.1 us (30%)
  Pallas kernels  9.46 us (16%)
  local copies, waits for them, and re-layouts  3.58 us (6%)
  other arithmetic  3.16 us (5%)
  between operations  0.93 us (2%)
    ppermute x26, starting transfers between devices, swap(): return lax.ppermute(array, axis, [(i, i ^ apart) for i in range(size)])  24.8 us
    ppermute x26, waiting for transfers between devices, swap(): return lax.ppermute(array, axis, [(i, i ^ apart) for i in range(size)])  18.1 us
    pallas_call x7, Pallas kernels, run(): pl.pallas_call(kernel, out_shape=outs, in_specs=[smem if a.dtype == jnp.i...  9.46 us
    unnamed x32, local copies, waits for them, and re-layouts  1.81 us
    slice x1, local copies, waits for them, and re-layouts, on_device(): q_own[at]  1.76 us
    concatenate x2, other arithmetic, on_device(): jnp.concatenate([maps] + [swap(maps, 'fsdp', apart) for apart in stage], 0)  1.66 us
  transfers between devices with their start and end apart: 26, of which 13 were waited for; matrix products, arithmetic and copies ran while one was open for 7% of the time, Pallas kernels for 11%

profile of v4, /device:TPU:0, one launch (start us, length us, event | category | flops | bytes accessed | tf_op | source)
XLA Modules:
  0.0 60.0 jit_solution(2207180616040377453)
XLA Ops:
  0.7 0.5 collective-permute-start
  1.2 1.8 %slice_bitcast_fusion = (bf16[32,4096]{1,0:T(8,128)(2,1)}, bf16[32,4096]{1,0:T(8,128)(2,1)S(1)}) fusion(bf16[1,64,4096]{2,1,0:T(8,128)(2,1)} %param.8), kind=kLoop, calls=%fused_computation.1 | loop fusion | bytes 1048576 | tf_op jit(solution)/shard_map/slice | solution.py:305
  2.9 2.6 %collective-permute-start.4 = (bf16[32,4096]{1,0:T(8,128)(2,1)S(1)}, bf16[32,4096]{1,0:T(8,128)(2,1)S(1)}, u32[]{:S(2)}, u32[]{:S(2)}) collective-permute-start(bf16[32,4096]{1,0:T(8,128)(2,1)S(1)} %get-tuple-element.49), channel_id=1, source_target_pairs={{0,16},{8,24},{16,0},{24,8},{1,17},{9,25},{17,1},{25,9},{2,18},{10... | collective-permute-start | bytes 786440 | tf_op jit(solution)/shard_map/ppermute | solution.py:285
  5.5 0.7 %maximum_bitcast_fusion = bf16[1,2,16,512]{3,2,1,0:T(8,128)(2,1)S(1)} fusion(bf16[1,16,512]{2,1,0:T(8,128)(2,1)} %bitcast.38, bf16[1,16,512]{2,1,0:T(8,128)(2,1)} %bitcast.39), kind=kLoop, calls=%fused_computation.5 | loop fusion | flops 16384 | bytes 65536 | tf_op jit(solution)/shard_map/broadcast_in_dim | solution.py:307
  6.3 3.6 %collective-permute-start.3 = (bf16[1,2,16,512]{3,2,1,0:T(8,128)(2,1)S(1)}, bf16[1,2,16,512]{3,2,1,0:T(8,128)(2,1)S(1)}, u32[]{:S(2)}, u32[]{:S(2)}) collective-permute-start(bf16[1,2,16,512]{3,2,1,0:T(8,128)(2,1)S(1)} %maximum_bitcast_fusion), channel_id=1, source_target_pairs={{0,6},{1,7},{2,4},{3,5},{4,2},{5,3},{6,0},{7,1},{8,14},{9,15},{10,... | collective-permute-start | bytes 98312 | tf_op jit(solution)/shard_map/ppermute | solution.py:285
  9.9 0.8 %collective-permute-start.1 = (bf16[1,2,16,512]{3,2,1,0:T(8,128)(2,1)S(1)}, bf16[1,2,16,512]{3,2,1,0:T(8,128)(2,1)S(1)}, u32[]{:S(2)}, u32[]{:S(2)}) collective-permute-start(bf16[1,2,16,512]{3,2,1,0:T(8,128)(2,1)S(1)} %maximum_bitcast_fusion), channel_id=1, source_target_pairs={{0,2},{1,3},{2,0},{3,1},{4,6},{5,7},{6,4},{7,5},{8,10},{9,11},{10,... | collective-permute-start | bytes 98312 | tf_op jit(solution)/shard_map/ppermute | solution.py:285
  10.6 1.3 %collective-permute-done.3 = bf16[1,2,16,512]{3,2,1,0:T(8,128)(2,1)S(1)} collective-permute-done((bf16[1,2,16,512]{3,2,1,0:T(8,128)(2,1)S(1)}, bf16[1,2,16,512]{3,2,1,0:T(8,128)(2,1)S(1)}, u32[]{:S(2)}, u32[]{:S(2)}) %collective-permute-start.3) | collective-permute-done | bytes 32800 | tf_op jit(solution)/shard_map/ppermute | solution.py:285
  12.0 2.7 %collective-permute-done.2 = bf16[1,2,16,512]{3,2,1,0:T(8,128)(2,1)S(1)} collective-permute-done((bf16[1,2,16,512]{3,2,1,0:T(8,128)(2,1)S(1)}, bf16[1,2,16,512]{3,2,1,0:T(8,128)(2,1)S(1)}, u32[]{:S(2)}, u32[]{:S(2)}) %collective-permute-start.2) | collective-permute-done | bytes 32800 | tf_op jit(solution)/shard_map/ppermute | solution.py:285
  14.7 0.0 collective-permute-done.1
  14.7 0.7 %pad_maximum_fusion.1 = bf16[4,2,16,512]{3,2,1,0:T(8,128)(2,1)} fusion(bf16[1,2,16,512]{3,2,1,0:T(8,128)(2,1)S(1)} %collective-permute-done.3, bf16[1,2,16,512]{3,2,1,0:T(8,128)(2,1)S(1)} %collective-permute-done.2, bf16[1,2,16,512]{3,2,1,0:T(8,128)(2,1)S(1)} %collective-permute-done.1, bf16[1,2,16,512]{3,2,1,0:T(8,128)(2,1)S(1)} %maximum_bitcast_fusion), kind=kLoop, calls=%fused_computation.3 | loop fusion | flops 196608 | bytes 262144 | tf_op jit(solution)/shard_map/concatenate | solution.py:313
  15.3 0.7 %copy-done.8 = bf16[32,4096]{1,0:T(8,128)(2,1)} copy-done((bf16[32,4096]{1,0:T(8,128)(2,1)}, bf16[32,4096]{1,0:T(8,128)(2,1)S(1)}, u32[]{:S(2)}) %copy-start.8) | copy-done | bytes 262168
  16.1 0.5 collective-permute-start.5
  16.6 0.1 collective-permute-start.9
  16.6 0.5 collective-permute-start.6
  17.2 1.5 %collective-permute-start.8 = (bf16[4,2,16,512]{3,2,1,0:T(8,128)(2,1)}, bf16[4,2,16,512]{3,2,1,0:T(8,128)(2,1)}, u32[]{:S(2)}, u32[]{:S(2)}) collective-permute-start(bf16[4,2,16,512]{3,2,1,0:T(8,128)(2,1)} %pad_maximum_fusion.1), channel_id=1, source_target_pairs={{0,1},{1,0},{2,3},{3,2},{4,5},{5,4},{6,7},{7,6},{8,9},{9,8},{10,11... | collective-permute-start | bytes 393224 | tf_op jit(solution)/shard_map/ppermute | solution.py:285
  18.7 0.1 pad_add_fusion.place
  18.8 0.7 %collective-permute-done.5.q_sib.refs_3_.rest_1_ = bf16[64,4096]{1,0:T(8,128)(2,1)S(1)} collective-permute-done((bf16[64,4096]{1,0:T(8,128)(2,1)S(1)}, bf16[64,4096]{1,0:T(8,128)(2,1)S(1)}, u32[]{:S(2)}, u32[]{:S(2)}) %collective-permute-start.5) | collective-permute-done | bytes 524320 | tf_op jit(solution)/shard_map/ppermute | solution.py:285
  19.5 0.0 copy-start.2
  19.5 1.1 %shard_map.111 = (f32[160,128]{1,0:T(8,128)S(1)}, f32[8,64]{1,0:T(8,128)S(1)}) custom-call(s32[2]{0:T(128)S(1)} %pad_add_fusion.place, bf16[80,4096]{1,0:T(8,128)(2,1)S(1)} %bitcast.19, bf16[80,4096]{1,0:T(8,128)(2,1)S(1)} %collective-permute-done.c_sib.refs_1_, bf16[64,4096]{1,0:T(8,128)(2,1)S(1)} %bitcast.26, ...), custom_call_target="tpu_custom_call" | custom-call | flops 1000 | bytes 1000 | tf_op jit(solution)/shard_map/pallas_call | solution.py:257
  20.6 0.0 copy-start.3
  20.6 1.5 %collective-permute-start.7 = (f32[8,64]{1,0:T(8,128)S(1)}, f32[8,64]{1,0:T(8,128)S(1)}, u32[]{:S(2)}, u32[]{:S(2)}) collective-permute-start(f32[8,64]{1,0:T(8,128)S(1)} %get-tuple-element.28.refs_10_), channel_id=1, source_target_pairs={{0,16},{8,24},{16,0},{24,8},{1,17},{9,25},{17,1},{25,9},{2,18},{10... | collective-permute-start | bytes 6152 | tf_op jit(solution)/shard_map/ppermute | solution.py:285
  22.0 1.0 %collective-permute-done.8 = bf16[4,2,16,512]{3,2,1,0:T(8,128)(2,1)} collective-permute-done((bf16[4,2,16,512]{3,2,1,0:T(8,128)(2,1)}, bf16[4,2,16,512]{3,2,1,0:T(8,128)(2,1)}, u32[]{:S(2)}, u32[]{:S(2)}) %collective-permute-start.8) | collective-permute-done | bytes 131104 | tf_op jit(solution)/shard_map/ppermute | solution.py:285
  23.0 1.0 %pad_maximum_fusion.maps = bf16[8,2,16,512]{3,2,1,0:T(8,128)(2,1)S(1)} fusion(bf16[4,2,16,512]{3,2,1,0:T(8,128)(2,1)} %collective-permute-done.8, bf16[4,2,16,512]{3,2,1,0:T(8,128)(2,1)} %pad_maximum_fusion.1), kind=kLoop, calls=%fused_computation | loop fusion | flops 131072 | bytes 524288 | tf_op jit(solution)/shard_map/concatenate | solution.py:313
  24.0 0.0 copy-start.9
  24.1 0.0 collective-permute-done.9.hq_sib.refs_7_
  24.1 1.7 %shard_map.112 = (f32[16,128]{1,0:T(8,128)S(1)}, bf16[16,160]{1,0:T(8,128)(2,1)S(1)}, f32[16,160]{1,0:T(8,128)S(1)}) custom-call(s32[2]{0:T(128)S(1)} %pad_add_fusion.place, bf16[8,2,16,512]{3,2,1,0:T(8,128)(2,1)S(1)} %pad_maximum_fusion.maps, bf16[64,4096]{1,0:T(8,128)(2,1)S(1)} %bitcast.34, bf16[64,4096]{1,0:T(8,128)(2,1)S(1)} %collective-permute-done.9.hq_sib.refs_7_, ...), custom_call_target="tpu_custom_call" | custom-call | flops 1000 | bytes 1000 | tf_op jit(solution)/shard_map/pallas_call | solution.py:257
  25.8 0.0 collective-permute-done.6.refs_1_
  25.8 0.0 collective-permute-done.7.refs_2_
  25.9 1.7 %shard_map.113 = (f32[24,64]{1,0:T(8,128)S(1)}, bf16[160,64]{1,0:T(8,128)(2,1)S(1)}, bf16[64,4096]{1,0:T(8,128)(2,1)S(1)}) custom-call(s32[2]{0:T(128)S(1)} %pad_add_fusion.place, bf16[80,4096]{1,0:T(8,128)(2,1)S(1)} %bitcast.21, bf16[80,4096]{1,0:T(8,128)(2,1)S(1)} %collective-permute-done.c_sib.refs_1_, bf16[32,4096]{1,0:T(8,128)(2,1)S(1)} %copy-done.9, ...), custom_call_target="tpu_custom_call" | custom-call | flops 1000 | bytes 1000 | tf_op jit(solution)/shard_map/pallas_call | solution.py:257
  27.5 0.0 collective-permute-start.11
  27.5 0.5 collective-permute-start.15
  28.1 0.1 collective-permute-start.12
  28.1 1.5 %collective-permute-start.16 = (f32[16,128]{1,0:T(8,128)S(1)}, f32[16,128]{1,0:T(8,128)S(1)}, u32[]{:S(2)}, u32[]{:S(2)}) collective-permute-start(f32[16,128]{1,0:T(8,128)S(1)} %get-tuple-element.35.refs_16_), channel_id=1, source_target_pairs={{0,16},{8,24},{16,0},{24,8},{1,17},{9,25},{17,1},{25,9},{2,18},{10... | collective-permute-start | bytes 24584 | tf_op jit(solution)/shard_map/ppermute | solution.py:285
  29.6 0.3 collective-permute-start.14
  29.9 0.0 collective-permute-done.12.refs_11_
  29.9 1.5 %collective-permute-start.13 = (f32[24,64]{1,0:T(8,128)S(1)}, f32[24,64]{1,0:T(8,128)S(1)}, u32[]{:S(2)}, u32[]{:S(2)}) collective-permute-start(f32[24,64]{1,0:T(8,128)S(1)} %get-tuple-element.33), channel_id=1, source_target_pairs={{0,16},{8,24},{16,0},{24,8},{1,17},{9,25},{17,1},{25,9},{2,18},{10... | collective-permute-start | bytes 18440 | tf_op jit(solution)/shard_map/ppermute | solution.py:285
  31.4 1.0 %shard_map.114 = (bf16[64,1024]{1,0:T(8,128)(2,1)S(1)}, bf16[64,2048]{1,0:T(8,128)(2,1)S(1)}, bf16[64,1024]{1,0:T(8,128)(2,1)}) custom-call(bf16[160,64]{1,0:T(8,128)(2,1)S(1)} %get-tuple-element.34.weights.refs_14_, bf16[80,4096]{1,0:T(8,128)(2,1)S(1)} %bitcast.22, bf16[80,4096]{1,0:T(8,128)(2,1)S(1)} %collective-permute-done.c_sib.refs_1_), custom_call_target="tpu_custom_call" | custom-call | flops 1000 | bytes 1000 | tf_op jit(solution)/shard_map/pallas_call | solution.py:257
  32.5 0.3 collective-permute-done.14.refs_13_
  32.7 0.9 %collective-permute-done.13.refs_12_ = f32[24,64]{1,0:T(8,128)S(1)} collective-permute-done((f32[24,64]{1,0:T(8,128)S(1)}, f32[24,64]{1,0:T(8,128)S(1)}, u32[]{:S(2)}, u32[]{:S(2)}) %collective-permute-start.13) | collective-permute-done | bytes 6176 | tf_op jit(solution)/shard_map/ppermute | solution.py:285
  33.6 0.0 copy-start.6
  33.7 1.4 %shard_map.115 = (bf16[80,256]{1,0:T(8,128)(2,1)S(1)}, bf16[160,64]{1,0:T(8,128)(2,1)S(1)}, f32[4,16,512]{2,1,0:T(8,128)S(1)}, bf16[4,16,512]{2,1,0:T(8,128)(2,1)S(1)}) custom-call(s32[2]{0:T(128)S(1)} %pad_add_fusion.place, bf16[80,4096]{1,0:T(8,128)(2,1)S(1)} %bitcast.23, bf16[80,4096]{1,0:T(8,128)(2,1)S(1)} %collective-permute-done.c_sib.refs_1_, ...), custom_call_target="tpu_custom_call" | custom-call | flops 1000 | bytes 1000 | tf_op jit(solution)/shard_map/pallas_call | solution.py:257
  35.1 0.0 copy-done.6
  35.2 0.0 copy-start.5
  35.2 1.6 %collective-permute-start.20 = (bf16[4,16,512]{2,1,0:T(8,128)(2,1)S(1)}, bf16[4,16,512]{2,1,0:T(8,128)(2,1)S(1)}, u32[]{:S(2)}, u32[]{:S(2)}) collective-permute-start(bf16[4,16,512]{2,1,0:T(8,128)(2,1)S(1)} %get-tuple-element.45), channel_id=1, source_target_pairs={{0,1},{1,0},{2,3},{3,2},{4,5},{5,4},{6,7},{7,6},{8,9},{9,8},{10,11... | collective-permute-start | bytes 196616 | tf_op jit(solution)/shard_map/ppermute | solution.py:285
  36.8 1.5 %collective-permute-start.17 = (bf16[64,1024]{1,0:T(8,128)(2,1)S(1)}, bf16[64,1024]{1,0:T(8,128)(2,1)S(1)}, u32[]{:S(2)}, u32[]{:S(2)}) collective-permute-start(bf16[64,1024]{1,0:T(8,128)(2,1)S(1)} %get-tuple-element.37), channel_id=1, source_target_pairs={{0,16},{8,24},{16,0},{24,8},{1,17},{9,25},{17,1},{25,9},{2,18},{10... | collective-permute-start | bytes 393224 | tf_op jit(solution)/shard_map/ppermute | solution.py:285
  38.2 0.5 collective-permute-start.18
  38.8 0.7 %collective-permute-done.20 = bf16[4,16,512]{2,1,0:T(8,128)(2,1)S(1)} collective-permute-done((bf16[4,16,512]{2,1,0:T(8,128)(2,1)S(1)}, bf16[4,16,512]{2,1,0:T(8,128)(2,1)S(1)}, u32[]{:S(2)}, u32[]{:S(2)}) %collective-permute-start.20) | collective-permute-done | bytes 65568 | tf_op jit(solution)/shard_map/ppermute | solution.py:285
  39.5 3.6 %collective-permute-done.17.rest_0_ = bf16[64,1024]{1,0:T(8,128)(2,1)S(1)} collective-permute-done((bf16[64,1024]{1,0:T(8,128)(2,1)S(1)}, bf16[64,1024]{1,0:T(8,128)(2,1)S(1)}, u32[]{:S(2)}, u32[]{:S(2)}) %collective-permute-start.17) | collective-permute-done | bytes 131104 | tf_op jit(solution)/shard_map/ppermute | solution.py:285
  43.2 0.1 collective-permute-start.21
  43.3 3.4 %collective-permute-start.23 = (bf16[1,16,512]{2,1,0:T(8,128)(2,1)S(1)}, bf16[1,16,512]{2,1,0:T(8,128)(2,1)S(1)}, u32[]{:S(2)}, u32[]{:S(2)}) collective-permute-start(bf16[1,16,512]{2,1,0:T(8,128)(2,1)S(1)} %get-tuple-element.53), channel_id=1, source_target_pairs={{0,6},{1,7},{2,4},{3,5},{4,2},{5,3},{6,0},{7,1},{8,14},{9,15},{10,... | collective-permute-start | bytes 49160 | tf_op jit(solution)/shard_map/ppermute | solution.py:285
  46.8 0.0 collective-permute-start.22
  46.8 0.2 collective-permute-done.21
  47.0 1.9 %collective-permute-done.23 = bf16[1,16,512]{2,1,0:T(8,128)(2,1)S(1)} collective-permute-done((bf16[1,16,512]{2,1,0:T(8,128)(2,1)S(1)}, bf16[1,16,512]{2,1,0:T(8,128)(2,1)S(1)}, u32[]{:S(2)}, u32[]{:S(2)}) %collective-permute-start.23) | collective-permute-done | bytes 16416 | tf_op jit(solution)/shard_map/ppermute | solution.py:285
  48.9 2.5 %collective-permute-done.22 = bf16[1,16,512]{2,1,0:T(8,128)(2,1)S(1)} collective-permute-done((bf16[1,16,512]{2,1,0:T(8,128)(2,1)S(1)}, bf16[1,16,512]{2,1,0:T(8,128)(2,1)S(1)}, u32[]{:S(2)}, u32[]{:S(2)}) %collective-permute-start.22) | collective-permute-done | bytes 16416 | tf_op jit(solution)/shard_map/ppermute | solution.py:285
  51.4 1.6 %collective-permute-start.24 = (f32[16,512]{1,0:T(8,128)S(1)}, f32[16,512]{1,0:T(8,128)S(1)}, u32[]{:S(2)}, u32[]{:S(2)}) collective-permute-start(f32[16,512]{1,0:T(8,128)S(1)} %add_bitcast_fusion), channel_id=1, source_target_pairs={{0,16},{8,24},{16,0},{24,8},{1,17},{9,25},{17,1},{25,9},{2,18},{10... | collective-permute-start | bytes 98312 | tf_op jit(solution)/shard_map/ppermute | solution.py:285
  53.0 0.5 collective-permute-start.19
  53.5 1.9 %collective-permute-done.24 = f32[16,512]{1,0:T(8,128)S(1)} collective-permute-done((f32[16,512]{1,0:T(8,128)S(1)}, f32[16,512]{1,0:T(8,128)S(1)}, u32[]{:S(2)}, u32[]{:S(2)}) %collective-permute-start.24) | collective-permute-done | bytes 32800 | tf_op jit(solution)/shard_map/ppermute | solution.py:285
  55.4 0.1 collective-permute-start.25
  55.5 0.0 copy-start.7
  55.5 1.0 %copy-done.7 = bf16[64,4096]{1,0:T(8,128)(2,1)S(1)} copy-done((bf16[64,4096]{1,0:T(8,128)(2,1)S(1)}, bf16[64,4096]{1,0:T(8,128)(2,1)}, u32[]{:S(2)}) %copy-start.7) | copy-done | bytes 524312
  56.6 1.3 %shard_map.117 = bf16[80,4096]{1,0:T(8,128)(2,1)} custom-call(bf16[80,256]{1,0:T(8,128)(2,1)S(1)} %copy-done.13, bf16[64,4096]{1,0:T(8,128)(2,1)S(1)} %bitcast.29, bf16[64,4096]{1,0:T(8,128)(2,1)S(1)} %collective-permute-done.5.q_sib.refs_3_.rest_1_, bf16[64,4096]{1,0:T(8,128)(2,1)S(1)} %copy-done.5, bf16[64,4096]{1,0:T(8,128)(2,1)S(1)} %copy-done.7), custom_call_target="tpu_custom_call" | custom-call | flops 1000 | bytes 1000 | tf_op jit(solution)/shard_map/pallas_call | solution.py:257
  57.9 0.3 collective-permute-done.19.rest_2_
  58.2 1.2 %shard_map.116 = bf16[64,4096]{1,0:T(8,128)(2,1)} custom-call(bf16[160,64]{1,0:T(8,128)(2,1)S(1)} %copy-done.11, bf16[80,4096]{1,0:T(8,128)(2,1)S(1)} %bitcast.24, bf16[80,4096]{1,0:T(8,128)(2,1)S(1)} %collective-permute-done.c_sib.refs_1_, bf16[64,1024]{1,0:T(8,128)(2,1)S(1)} %collective-permute-done.17.rest_0_, ...), custom_call_target="tpu_custom_call" | custom-call | flops 1000 | bytes 1000 | tf_op jit(solution)/shard_map/pallas_call | solution.py:257
  59.4 0.6 %broadcast_select_fusion = (f32[16,512]{1,0:T(8,128)}, f32[16,512]{1,0:T(8,128)}) fusion(f32[16,512]{1,0:T(8,128)S(1)} %add_multiply_fusion, f32[16,512]{1,0:T(8,128)S(1)} %collective-permute-done.25, pred[]{:T(512)S(6)} %eq.3), kind=kLoop, calls=%fused_computation.8 | loop fusion | flops 16384 | bytes 131073 | tf_op jit(solution)/shard_map/jit(_where)/select_n | solution.py:376
  (38 shorter events, 0.1 us)
Async XLA Ops:
  0.6 15.4 %copy-start.1 = (bf16[1,64,4096]{2,1,0:T(8,128)(2,1)S(1)}, bf16[1,64,4096]{2,1,0:T(8,128)(2,1)}, u32[]{:S(2)}) copy-start(bf16[1,64,4096]{2,1,0:T(8,128)(2,1)} %param.8) | copy-start | bytes 1572868
  0.6 18.8 %copy-start = (bf16[1,1,80,4096]{3,2,1,0:T(8,128)(2,1)S(1)}, bf16[1,1,80,4096]{3,2,1,0:T(8,128)(2,1)}, u32[]{:S(2)}) copy-start(bf16[1,1,80,4096]{3,2,1,0:T(8,128)(2,1)} %param.9) | copy-start | bytes 1966084
  0.7 15.4 %collective-permute-start = (bf16[80,4096]{1,0:T(8,128)(2,1)}, bf16[80,4096]{1,0:T(8,128)(2,1)S(1)}, u32[]{:S(2)}, u32[]{:S(2)}) collective-permute-start(bf16[80,4096]{1,0:T(8,128)(2,1)} %bitcast.18), channel_id=1, source_target_pairs={{0,8},{8,0},{16,24},{24,16},{1,9},{9,1},{17,25},{25,17},{2,10},{10... | collective-permute-start | bytes 1966088 | tf_op jit(solution)/shard_map/ppermute | solution.py:285
  2.9 12.4 %collective-permute-start.4 = (bf16[32,4096]{1,0:T(8,128)(2,1)S(1)}, bf16[32,4096]{1,0:T(8,128)(2,1)S(1)}, u32[]{:S(2)}, u32[]{:S(2)}) collective-permute-start(bf16[32,4096]{1,0:T(8,128)(2,1)S(1)} %get-tuple-element.49), channel_id=1, source_target_pairs={{0,16},{8,24},{16,0},{24,8},{1,17},{9,25},{17,1},{25,9},{2,18},{10... | collective-permute-start | bytes 786440 | tf_op jit(solution)/shard_map/ppermute | solution.py:285
  6.3 5.7 %collective-permute-start.3 = (bf16[1,2,16,512]{3,2,1,0:T(8,128)(2,1)S(1)}, bf16[1,2,16,512]{3,2,1,0:T(8,128)(2,1)S(1)}, u32[]{:S(2)}, u32[]{:S(2)}) collective-permute-start(bf16[1,2,16,512]{3,2,1,0:T(8,128)(2,1)S(1)} %maximum_bitcast_fusion), channel_id=1, source_target_pairs={{0,6},{1,7},{2,4},{3,5},{4,2},{5,3},{6,0},{7,1},{8,14},{9,15},{10,... | collective-permute-start | bytes 98312 | tf_op jit(solution)/shard_map/ppermute | solution.py:285
  9.9 4.8 %collective-permute-start.2 = (bf16[1,2,16,512]{3,2,1,0:T(8,128)(2,1)S(1)}, bf16[1,2,16,512]{3,2,1,0:T(8,128)(2,1)S(1)}, u32[]{:S(2)}, u32[]{:S(2)}) collective-permute-start(bf16[1,2,16,512]{3,2,1,0:T(8,128)(2,1)S(1)} %maximum_bitcast_fusion), channel_id=1, source_target_pairs={{0,4},{1,5},{2,6},{3,7},{4,0},{5,1},{6,2},{7,3},{8,12},{9,13},{10,... | collective-permute-start | bytes 98312 | tf_op jit(solution)/shard_map/ppermute | solution.py:285
  9.9 4.8 %collective-permute-start.1 = (bf16[1,2,16,512]{3,2,1,0:T(8,128)(2,1)S(1)}, bf16[1,2,16,512]{3,2,1,0:T(8,128)(2,1)S(1)}, u32[]{:S(2)}, u32[]{:S(2)}) collective-permute-start(bf16[1,2,16,512]{3,2,1,0:T(8,128)(2,1)S(1)} %maximum_bitcast_fusion), channel_id=1, source_target_pairs={{0,2},{1,3},{2,0},{3,1},{4,6},{5,7},{6,4},{7,5},{8,10},{9,11},{10,... | collective-permute-start | bytes 98312 | tf_op jit(solution)/shard_map/ppermute | solution.py:285
  15.3 0.7 %copy-start.8 = (bf16[32,4096]{1,0:T(8,128)(2,1)}, bf16[32,4096]{1,0:T(8,128)(2,1)S(1)}, u32[]{:S(2)}) copy-start(bf16[32,4096]{1,0:T(8,128)(2,1)S(1)} %collective-permute-done.4.refs_0_) | copy-start | bytes 786436
  16.0 8.0 %collective-permute-start.10 = (bf16[80,4096]{1,0:T(8,128)(2,1)}, bf16[80,4096]{1,0:T(8,128)(2,1)S(1)}, u32[]{:S(2)}, u32[]{:S(2)}) collective-permute-start(bf16[80,4096]{1,0:T(8,128)(2,1)} %bitcast.30), channel_id=1, source_target_pairs={{0,8},{8,0},{16,24},{24,16},{1,9},{9,1},{17,25},{25,17},{2,10},{10... | collective-permute-start | bytes 1966088 | tf_op jit(solution)/shard_map/ppermute | solution.py:285
  16.1 3.4 %collective-permute-start.5 = (bf16[64,4096]{1,0:T(8,128)(2,1)S(1)}, bf16[64,4096]{1,0:T(8,128)(2,1)S(1)}, u32[]{:S(2)}, u32[]{:S(2)}) collective-permute-start(bf16[64,4096]{1,0:T(8,128)(2,1)S(1)} %bitcast.25), channel_id=1, source_target_pairs={{0,8},{8,0},{16,24},{24,16},{1,9},{9,1},{17,25},{25,17},{2,10},{10... | collective-permute-start | bytes 1572872 | tf_op jit(solution)/shard_map/ppermute | solution.py:285
  16.6 7.5 %collective-permute-start.9 = (bf16[64,4096]{1,0:T(8,128)(2,1)}, bf16[64,4096]{1,0:T(8,128)(2,1)S(1)}, u32[]{:S(2)}, u32[]{:S(2)}) collective-permute-start(bf16[64,4096]{1,0:T(8,128)(2,1)} %bitcast.33), channel_id=1, source_target_pairs={{0,8},{8,0},{16,24},{24,16},{1,9},{9,1},{17,25},{25,17},{2,10},{10... | collective-permute-start | bytes 1572872 | tf_op jit(solution)/shard_map/ppermute | solution.py:285
  16.6 9.2 %collective-permute-start.6 = (bf16[32,4096]{1,0:T(8,128)(2,1)}, bf16[32,4096]{1,0:T(8,128)(2,1)}, u32[]{:S(2)}, u32[]{:S(2)}) collective-permute-start(bf16[32,4096]{1,0:T(8,128)(2,1)} %get-tuple-element.48), channel_id=1, source_target_pairs={{0,16},{8,24},{16,0},{24,8},{1,17},{9,25},{17,1},{25,9},{2,18},{10... | collective-permute-start | bytes 786440 | tf_op jit(solution)/shard_map/ppermute | solution.py:285
  17.2 5.9 %collective-permute-start.8 = (bf16[4,2,16,512]{3,2,1,0:T(8,128)(2,1)}, bf16[4,2,16,512]{3,2,1,0:T(8,128)(2,1)}, u32[]{:S(2)}, u32[]{:S(2)}) collective-permute-start(bf16[4,2,16,512]{3,2,1,0:T(8,128)(2,1)} %pad_maximum_fusion.1), channel_id=1, source_target_pairs={{0,1},{1,0},{2,3},{3,2},{4,5},{5,4},{6,7},{7,6},{8,9},{9,8},{10,11... | collective-permute-start | bytes 393224 | tf_op jit(solution)/shard_map/ppermute | solution.py:285
  18.7 0.8 %copy-start.14 = (s32[1,64]{1,0:T(1,128)S(1)}, s32[1,64]{1,0:T(1,128)}, u32[]{:S(2)}) copy-start(s32[1,64]{1,0:T(1,128)} %positives.1) | copy-start | bytes 772
  18.7 0.8 %copy-start.15 = (s32[1,64]{1,0:T(1,128)S(1)}, s32[1,64]{1,0:T(1,128)}, u32[]{:S(2)}) copy-start(s32[1,64]{1,0:T(1,128)} %hard.1) | copy-start | bytes 772
  19.5 4.6 %copy-start.2 = (bf16[1,1,80,4096]{3,2,1,0:T(8,128)(2,1)S(1)}, bf16[1,1,80,4096]{3,2,1,0:T(8,128)(2,1)}, u32[]{:S(2)}) copy-start(bf16[1,1,80,4096]{3,2,1,0:T(8,128)(2,1)} %param.13) | copy-start | bytes 1966084
  20.6 3.5 %copy-start.3 = (bf16[1,64,4096]{2,1,0:T(8,128)(2,1)S(1)}, bf16[1,64,4096]{2,1,0:T(8,128)(2,1)}, u32[]{:S(2)}) copy-start(bf16[1,64,4096]{2,1,0:T(8,128)(2,1)} %param.12) | copy-start | bytes 1572868
  20.6 5.3 %collective-permute-start.7 = (f32[8,64]{1,0:T(8,128)S(1)}, f32[8,64]{1,0:T(8,128)S(1)}, u32[]{:S(2)}, u32[]{:S(2)}) collective-permute-start(f32[8,64]{1,0:T(8,128)S(1)} %get-tuple-element.28.refs_10_), channel_id=1, source_target_pairs={{0,16},{8,24},{16,0},{24,8},{1,17},{9,25},{17,1},{25,9},{2,18},{10... | collective-permute-start | bytes 6152 | tf_op jit(solution)/shard_map/ppermute | solution.py:285
  24.0 1.8 %copy-start.9 = (bf16[32,4096]{1,0:T(8,128)(2,1)S(1)}, bf16[32,4096]{1,0:T(8,128)(2,1)}, u32[]{:S(2)}) copy-start(bf16[32,4096]{1,0:T(8,128)(2,1)} %copy-done.8) | copy-start | bytes 786436
  27.5 6.1 %copy-start.4 = (bf16[64,4096]{1,0:T(8,128)(2,1)}, bf16[64,4096]{1,0:T(8,128)(2,1)S(1)}, u32[]{:S(2)}) copy-start(bf16[64,4096]{1,0:T(8,128)(2,1)S(1)} %get-tuple-element.32.refs_4_.rest_2_) | copy-start | bytes 1572868
  27.5 6.1 %collective-permute-start.11 = (bf16[64,4096]{1,0:T(8,128)(2,1)S(1)}, bf16[64,4096]{1,0:T(8,128)(2,1)S(1)}, u32[]{:S(2)}, u32[]{:S(2)}) collective-permute-start(bf16[64,4096]{1,0:T(8,128)(2,1)S(1)} %get-tuple-element.32.refs_4_.rest_2_), channel_id=1, source_target_pairs={{0,8},{8,0},{16,24},{24,16},{1,9},{9,1},{17,25},{25,17},{2,10},{10... | collective-permute-start | bytes 1572872 | tf_op jit(solution)/shard_map/ppermute | solution.py:285
  27.5 6.1 %collective-permute-start.15 = (bf16[160,64]{1,0:T(8,128)(2,1)S(1)}, bf16[160,64]{1,0:T(8,128)(2,1)S(1)}, u32[]{:S(2)}, u32[]{:S(2)}) collective-permute-start(bf16[160,64]{1,0:T(8,128)(2,1)S(1)} %get-tuple-element.34.weights.refs_14_), channel_id=1, source_target_pairs={{0,8},{8,0},{16,24},{24,16},{1,9},{9,1},{17,25},{25,17},{2,10},{10... | collective-permute-start | bytes 61448 | tf_op jit(solution)/shard_map/ppermute | solution.py:285
  28.1 1.9 %collective-permute-start.12 = (f32[8,64]{1,0:T(8,128)S(1)}, f32[8,64]{1,0:T(8,128)S(1)}, u32[]{:S(2)}, u32[]{:S(2)}) collective-permute-start(f32[8,64]{1,0:T(8,128)S(1)} %get-tuple-element.28.refs_10_), channel_id=1, source_target_pairs={{0,8},{8,0},{16,24},{24,16},{1,9},{9,1},{17,25},{25,17},{2,10},{10... | collective-permute-start | bytes 6152 | tf_op jit(solution)/shard_map/ppermute | solution.py:285
  28.1 5.5 %collective-permute-start.16 = (f32[16,128]{1,0:T(8,128)S(1)}, f32[16,128]{1,0:T(8,128)S(1)}, u32[]{:S(2)}, u32[]{:S(2)}) collective-permute-start(f32[16,128]{1,0:T(8,128)S(1)} %get-tuple-element.35.refs_16_), channel_id=1, source_target_pairs={{0,16},{8,24},{16,0},{24,8},{1,17},{9,25},{17,1},{25,9},{2,18},{10... | collective-permute-start | bytes 24584 | tf_op jit(solution)/shard_map/ppermute | solution.py:285
  29.6 3.1 %collective-permute-start.14 = (f32[24,64]{1,0:T(8,128)S(1)}, f32[24,64]{1,0:T(8,128)S(1)}, u32[]{:S(2)}, u32[]{:S(2)}) collective-permute-start(f32[24,64]{1,0:T(8,128)S(1)} %get-tuple-element.33), channel_id=1, source_target_pairs={{0,24},{8,16},{16,8},{24,0},{1,25},{9,17},{17,9},{25,1},{2,26},{10... | collective-permute-start | bytes 18440 | tf_op jit(solution)/shard_map/ppermute | solution.py:285
  29.9 3.7 %collective-permute-start.13 = (f32[24,64]{1,0:T(8,128)S(1)}, f32[24,64]{1,0:T(8,128)S(1)}, u32[]{:S(2)}, u32[]{:S(2)}) collective-permute-start(f32[24,64]{1,0:T(8,128)S(1)} %get-tuple-element.33), channel_id=1, source_target_pairs={{0,16},{8,24},{16,0},{24,8},{1,17},{9,25},{17,1},{25,9},{2,18},{10... | collective-permute-start | bytes 18440 | tf_op jit(solution)/shard_map/ppermute | solution.py:285
  33.6 1.5 %copy-start.6 = (bf16[64,4096]{1,0:T(8,128)(2,1)}, bf16[64,4096]{1,0:T(8,128)(2,1)S(1)}, u32[]{:S(2)}) copy-start(bf16[64,4096]{1,0:T(8,128)(2,1)S(1)} %collective-permute-done.11.refs_5_.rest_3_) | copy-start | bytes 1572868
  35.1 4.4 %copy-start.10 = (bf16[160,64]{1,0:T(8,128)(2,1)}, bf16[160,64]{1,0:T(8,128)(2,1)S(1)}, u32[]{:S(2)}) copy-start(bf16[160,64]{1,0:T(8,128)(2,1)S(1)} %get-tuple-element.42.weights) | copy-start | bytes 61444
  35.1 4.4 %copy-start.12 = (bf16[80,256]{1,0:T(8,128)(2,1)}, bf16[80,256]{1,0:T(8,128)(2,1)S(1)}, u32[]{:S(2)}) copy-start(bf16[80,256]{1,0:T(8,128)(2,1)S(1)} %get-tuple-element.43.weights) | copy-start | bytes 122884
  35.2 20.3 %copy-start.5 = (bf16[64,4096]{1,0:T(8,128)(2,1)S(1)}, bf16[64,4096]{1,0:T(8,128)(2,1)}, u32[]{:S(2)}) copy-start(bf16[64,4096]{1,0:T(8,128)(2,1)} %copy-done.4) | copy-start | bytes 1572868
  35.2 4.3 %collective-permute-start.20 = (bf16[4,16,512]{2,1,0:T(8,128)(2,1)S(1)}, bf16[4,16,512]{2,1,0:T(8,128)(2,1)S(1)}, u32[]{:S(2)}, u32[]{:S(2)}) collective-permute-start(bf16[4,16,512]{2,1,0:T(8,128)(2,1)S(1)} %get-tuple-element.45), channel_id=1, source_target_pairs={{0,1},{1,0},{2,3},{3,2},{4,5},{5,4},{6,7},{7,6},{8,9},{9,8},{10,11... | collective-permute-start | bytes 196616 | tf_op jit(solution)/shard_map/ppermute | solution.py:285
  36.8 6.4 %collective-permute-start.17 = (bf16[64,1024]{1,0:T(8,128)(2,1)S(1)}, bf16[64,1024]{1,0:T(8,128)(2,1)S(1)}, u32[]{:S(2)}, u32[]{:S(2)}) collective-permute-start(bf16[64,1024]{1,0:T(8,128)(2,1)S(1)} %get-tuple-element.37), channel_id=1, source_target_pairs={{0,16},{8,24},{16,0},{24,8},{1,17},{9,25},{17,1},{25,9},{2,18},{10... | collective-permute-start | bytes 393224 | tf_op jit(solution)/shard_map/ppermute | solution.py:285
  38.2 13.2 %collective-permute-start.18 = (bf16[64,2048]{1,0:T(8,128)(2,1)S(1)}, bf16[64,2048]{1,0:T(8,128)(2,1)S(1)}, u32[]{:S(2)}, u32[]{:S(2)}) collective-permute-start(bf16[64,2048]{1,0:T(8,128)(2,1)S(1)} %get-tuple-element.38), channel_id=1, source_target_pairs={{0,16},{8,24},{16,0},{24,8},{1,17},{9,25},{17,1},{25,9},{2,18},{10... | collective-permute-start | bytes 786440 | tf_op jit(solution)/shard_map/ppermute | solution.py:285
  43.2 3.8 %collective-permute-start.21 = (bf16[1,16,512]{2,1,0:T(8,128)(2,1)S(1)}, bf16[1,16,512]{2,1,0:T(8,128)(2,1)S(1)}, u32[]{:S(2)}, u32[]{:S(2)}) collective-permute-start(bf16[1,16,512]{2,1,0:T(8,128)(2,1)S(1)} %get-tuple-element.52), channel_id=1, source_target_pairs={{0,2},{1,3},{2,0},{3,1},{4,6},{5,7},{6,4},{7,5},{8,10},{9,11},{10,... | collective-permute-start | bytes 49160 | tf_op jit(solution)/shard_map/ppermute | solution.py:285
  43.3 5.6 %collective-permute-start.23 = (bf16[1,16,512]{2,1,0:T(8,128)(2,1)S(1)}, bf16[1,16,512]{2,1,0:T(8,128)(2,1)S(1)}, u32[]{:S(2)}, u32[]{:S(2)}) collective-permute-start(bf16[1,16,512]{2,1,0:T(8,128)(2,1)S(1)} %get-tuple-element.53), channel_id=1, source_target_pairs={{0,6},{1,7},{2,4},{3,5},{4,2},{5,3},{6,0},{7,1},{8,14},{9,15},{10,... | collective-permute-start | bytes 49160 | tf_op jit(solution)/shard_map/ppermute | solution.py:285
  46.8 4.6 %collective-permute-start.22 = (bf16[1,16,512]{2,1,0:T(8,128)(2,1)S(1)}, bf16[1,16,512]{2,1,0:T(8,128)(2,1)S(1)}, u32[]{:S(2)}, u32[]{:S(2)}) collective-permute-start(bf16[1,16,512]{2,1,0:T(8,128)(2,1)S(1)} %get-tuple-element.54), channel_id=1, source_target_pairs={{0,4},{1,5},{2,6},{3,7},{4,0},{5,1},{6,2},{7,3},{8,12},{9,13},{10,... | collective-permute-start | bytes 49160 | tf_op jit(solution)/shard_map/ppermute | solution.py:285
  51.4 4.1 %copy-start.13 = (bf16[80,256]{1,0:T(8,128)(2,1)S(1)}, bf16[80,256]{1,0:T(8,128)(2,1)}, u32[]{:S(2)}) copy-start(bf16[80,256]{1,0:T(8,128)(2,1)} %copy-done.12) | copy-start | bytes 122884
  51.4 4.0 %collective-permute-start.24 = (f32[16,512]{1,0:T(8,128)S(1)}, f32[16,512]{1,0:T(8,128)S(1)}, u32[]{:S(2)}, u32[]{:S(2)}) collective-permute-start(f32[16,512]{1,0:T(8,128)S(1)} %add_bitcast_fusion), channel_id=1, source_target_pairs={{0,16},{8,24},{16,0},{24,8},{1,17},{9,25},{17,1},{25,9},{2,18},{10... | collective-permute-start | bytes 98312 | tf_op jit(solution)/shard_map/ppermute | solution.py:285
  53.0 5.2 %collective-permute-start.19 = (bf16[64,1024]{1,0:T(8,128)(2,1)}, bf16[64,1024]{1,0:T(8,128)(2,1)S(1)}, u32[]{:S(2)}, u32[]{:S(2)}) collective-permute-start(bf16[64,1024]{1,0:T(8,128)(2,1)} %get-tuple-element.39), channel_id=1, source_target_pairs={{0,16},{8,24},{16,0},{24,8},{1,17},{9,25},{17,1},{25,9},{2,18},{10... | collective-permute-start | bytes 393224 | tf_op jit(solution)/shard_map/ppermute | solution.py:285
  55.4 3.9 %collective-permute-start.25 = (f32[16,512]{1,0:T(8,128)S(1)}, f32[16,512]{1,0:T(8,128)S(1)}, u32[]{:S(2)}, u32[]{:S(2)}) collective-permute-start(f32[16,512]{1,0:T(8,128)S(1)} %add_multiply_fusion), channel_id=1, source_target_pairs={{0,8},{8,0},{16,24},{24,16},{1,9},{9,1},{17,25},{25,17},{2,10},{10... | collective-permute-start | bytes 98312 | tf_op jit(solution)/shard_map/ppermute | solution.py:285
  55.5 1.0 %copy-start.7 = (bf16[64,4096]{1,0:T(8,128)(2,1)S(1)}, bf16[64,4096]{1,0:T(8,128)(2,1)}, u32[]{:S(2)}) copy-start(bf16[64,4096]{1,0:T(8,128)(2,1)} %copy-done.6) | copy-start | bytes 1572868
  56.6 1.6 %copy-start.11 = (bf16[160,64]{1,0:T(8,128)(2,1)S(1)}, bf16[160,64]{1,0:T(8,128)(2,1)}, u32[]{:S(2)}) copy-start(bf16[160,64]{1,0:T(8,128)(2,1)} %copy-done.10) | copy-start | bytes 61444

commit v5 on v2

v5 whole, which is shorter than its diff:
```python
import functools

import jax
import jax.numpy as jnp
from jax import lax
from jax.experimental import pallas as pl
from jax.experimental.pallas import tpu as pltpu
from jax.sharding import PartitionSpec as P

sharpness_factor = 50.0
adapter_scale = 2.0
STEP = 512
MAX, SUM, POSITIVE, HARD, STATS = 0, 1, 2, 3, 8
EXTRA = 16

f32 = jnp.float32
bf16 = jnp.bfloat16


def dot(left, right, left_dim, right_dim):
    return lax.dot_general(
        left, right, (((left_dim,), (right_dim,)), ((), ())), preferred_element_type=f32
    )


def dot_wide(left, right, left_dim, right_dim):
    high = left.astype(bf16)
    low = (left - high.astype(f32)).astype(bf16)
    return dot(high, right, left_dim, right_dim) + dot(low, right, left_dim, right_dim)


def layout(position, block, shape):
    row = lax.broadcasted_iota(jnp.int32, shape, 0)
    own = row < block
    return jnp.where(own, position, position ^ 1), jnp.where(own, row, row - block)


def allowed(owner, slot, hard, rows):
    return (slot < rows) | (hard.astype(jnp.int32) == owner)


def hits(owner, slot, positive, rows):
    return (slot < rows) & (positive.astype(jnp.int32) == owner * rows + slot)


def merge(stats):
    top = functools.reduce(jnp.maximum, [m for m, _ in stats])
    return top + jnp.log(sum(s * jnp.exp(m - top) for m, s in stats))


def terms_of(row):
    rows = []
    for _ in range(3):
        rows.append(row.astype(bf16))
        row = row - rows[-1].astype(f32)
    return rows


def whole(rows):
    rows = rows.astype(f32)
    return rows[0:1] + rows[1:2] + rows[2:3]


def packed(weights, top, share):
    block, rows = weights.shape[0] // 2, weights.shape[1]
    stats = jnp.concatenate(terms_of(top) + terms_of(share) + [jnp.zeros((EXTRA - 6, rows), bf16)], 0)
    return jnp.concatenate(
        [jnp.concatenate([weights[:block], weights[block:]], 1), jnp.concatenate([stats, stats], 1)], 0
    )


def unpacked(packet, turned=False):
    block, rows = packet.shape[0] - EXTRA, packet.shape[1] // 2
    halves = packet[:block, :rows], packet[:block, rows:]
    return jnp.concatenate(halves[::-1] if turned else halves, 0)


def packet_stats(packet):
    at, rows = packet.shape[0] - EXTRA, packet.shape[1] // 2
    return whole(packet[at : at + 3, :rows]), whole(packet[at + 3 : at + 6, :rows])


def columns(ref, at, width):
    return ref[:, pl.ds(pl.multiple_of(at * width, width), width)]


def scores_kernel(place, c_own, c_sib, q_own, q_sib, positives, hard, scores, stats):
    block, rows = c_own.shape[0], q_own.shape[0]
    c = jnp.concatenate([c_own[...], c_sib[...]], 0)
    q = jnp.concatenate([q_own[...], q_sib[...]], 0)
    total = dot(c, q, 1, 1) * sharpness_factor
    scores[...] = total
    mine = total[:, :rows]
    owner, slot = layout(place[0], block, mine.shape)
    mine = jnp.where(allowed(owner, slot, hard[...], rows), mine, -jnp.inf)
    top = jnp.max(mine, axis=0, keepdims=True)
    stats[...] = jnp.zeros_like(stats)
    stats[MAX : MAX + 1] = top
    stats[SUM : SUM + 1] = jnp.sum(jnp.exp(mine - top), axis=0, keepdims=True)
    stats[POSITIVE : POSITIVE + 1] = positives[...].astype(f32)
    stats[HARD : HARD + 1] = hard[...].astype(f32)


def adapter_kernel(place, maps, hq, hq_sib, hc, hc_sib, c_own, c_sib, q_own, q_sib, factors):
    shards, _, width = maps.shape

    def product(parts):
        total = 0.0
        for at in range(shards):
            rows = jnp.concatenate([r[:, at * width : (at + 1) * width] for r in parts], 0)
            total = total + dot(maps[at], rows, 1, 1)
        return total

    core = place[0] & 1

    @pl.when(core == 0)
    def _():
        factors[...] = product([hq, hq_sib, hc, hc_sib]).astype(bf16).astype(f32)

    @pl.when(core == 1)
    def _():
        factors[...] = product([q_own, q_sib, c_own, c_sib])


def partner_kernel(place, c_own, c_sib, q, stats, packet, q_again):
    block, rows = c_own.shape[0], q.shape[0]
    c = jnp.concatenate([c_own[...], c_sib[...]], 0)
    q_again[...] = q[...]
    total = dot(c, q[...], 1, 1)
    owner, slot = layout(place[0], block, total.shape)
    keep = allowed(owner, slot, stats[HARD : HARD + 1], rows)
    total = jnp.where(keep, total * sharpness_factor, -jnp.inf)
    top = jnp.max(total, axis=0, keepdims=True)
    share = jnp.sum(jnp.exp(total - top), axis=0, keepdims=True)
    log_total = merge([(stats[MAX : MAX + 1], stats[SUM : SUM + 1]), (top, share)])
    hit = hits(owner, slot, stats[POSITIVE : POSITIVE + 1], rows)
    packet[...] = packed((jnp.exp(total - log_total) - hit.astype(f32)).astype(bf16), top, share)


def share_kernel(packet, c_own, c_sib, share):
    weights = unpacked(packet[...])
    for i in range(share.shape[1] // STEP):
        at = slice(i * STEP, (i + 1) * STEP)
        c = jnp.concatenate([c_own[:, at], c_sib[:, at]], 0)
        share[:, at] = (dot(weights, c, 0, 0) * sharpness_factor).astype(bf16)


def question_kernel(weights, c_own, c_sib, *rest):
    shares, out = rest[:-1], rest[-1]
    for i in range(out.shape[1] // STEP):
        at = slice(i * STEP, (i + 1) * STEP)
        c = jnp.concatenate([c_own[:, at], c_sib[:, at]], 0)
        total = dot(weights[...], c, 0, 0) * sharpness_factor
        for share in shares:
            total = total + share[:, at].astype(f32)
        out[:, at] = total.astype(bf16)


def candidate_kernel(weights, *rest):
    queries, out = rest[:-1], rest[-1]
    for i in range(out.shape[1] // STEP):
        at = slice(i * STEP, (i + 1) * STEP)
        q = jnp.concatenate([r[:, at] for r in queries], 0)
        out[:, at] = (dot(weights[...], q, 1, 0) * sharpness_factor).astype(bf16)


def taken(refs, *counts):
    out, at = [], 0
    for count in counts:
        out.append(list(refs[at : at + count]))
        at += count
    return out


def sums_kernel(partners, place, *refs):
    n = partners
    (c, q, far_q, far_q_sib, hq, hc, stats, answers, sib_answers, made, made_sib, (factors,), far_factors,
     (scores,), (w_grad, w_own, terms)) = taken(refs, 2, 2, n, n, 2, 2, 2, n, n, n, n, 1, n, 1, 3)
    block, rows = c[0].shape[0], q[0].shape[0]
    shards, rank, width = terms.shape

    def both(at):
        return jnp.concatenate([ref[at : at + 1] for ref in stats], 1)

    def log_total(own, packets):
        return merge([(own[MAX : MAX + 1], own[SUM : SUM + 1])] + [packet_stats(p) for p in packets])

    owner, slot = layout(place[0], block, scores.shape)
    kept = allowed(owner, slot, both(HARD), rows)
    hit = hits(owner, slot, both(POSITIVE), rows)
    log_totals = jnp.concatenate([log_total(stats[0], answers), log_total(stats[1], sib_answers)], 1)
    near = jnp.exp(jnp.where(kept, scores[...] - log_totals, -jnp.inf)) - hit.astype(f32)
    near = near.astype(bf16)
    w_own[...] = near[:, :rows]
    pieces = [near]
    for mine, other in zip(made, made_sib):
        pieces += [unpacked(mine[...]), unpacked(other[...], turned=True)]
    weights = jnp.concatenate(pieces, 1)
    w_grad[...] = weights[:block]
    by_query = jnp.concatenate([r[:, : 2 * rows] for r in [factors] + far_factors], 1)
    by_candidate = factors[:, 2 * rows :]
    queries = list(q)
    for pair in zip(far_q, far_q_sib):
        queries += pair

    def split(terms):
        high = terms.astype(bf16)
        return jnp.concatenate([high, (terms - high.astype(f32)).astype(bf16)], 0)

    core = place[0] & 1

    @pl.when(core == 0)
    def _():
        over_c = split(dot(by_query.astype(bf16), weights, 1, 1) * sharpness_factor)
        over_q = split(dot(by_candidate.astype(bf16), weights, 1, 0) * sharpness_factor)
        for i in range(shards):
            at = slice(i * width, (i + 1) * width)
            from_c = jnp.concatenate([r[:, at] for r in c], 0)
            from_q = jnp.concatenate([r[:, at] for r in queries], 0)
            total = dot(over_c, from_c, 1, 0) + dot(over_q, from_q, 1, 0)
            terms[i] = (total[:rank] + total[rank:]).astype(bf16)

    @pl.when(core == 1)
    def _():
        back_q = dot_wide(by_candidate, near, 1, 0)
        for far, mine, other in zip(far_factors, answers, sib_answers):
            there = jnp.concatenate([unpacked(mine[...]), unpacked(other[...], turned=True)], 1)
            back_q = back_q + dot_wide(far[:, 2 * rows :], there, 1, 0)
        back_q = (back_q * sharpness_factor).astype(bf16)
        back_c = (dot_wide(by_query, weights, 1, 1) * sharpness_factor).astype(bf16)
        for i in range(shards):
            at = slice(i * width, (i + 1) * width)
            from_q = jnp.concatenate([r[:, at] for r in hq], 0)
            from_c = jnp.concatenate([r[:, at] for r in hc], 0)
            terms[i] = (dot(back_q, from_q, 1, 0) + dot(back_c, from_c, 1, 0)).astype(bf16)


def call(kernel, outs):
    smem = pl.BlockSpec(memory_space=pltpu.SMEM)
    vmem = pl.BlockSpec(memory_space=pltpu.VMEM)

    def run(*args):
        return pl.pallas_call(
            kernel,
            out_shape=outs,
            in_specs=[smem if a.dtype == jnp.int32 and a.ndim == 1 else vmem for a in args],
            out_specs=jax.tree.map(lambda _: vmem, outs),
            compiler_params=pltpu.CompilerParams(vmem_limit_bytes=16 * 2**20),
            cost_estimate=pl.CostEstimate(flops=1000, bytes_accessed=1000, transcendentals=0),
        )(*args)

    return run


def cut(width, weights):
    steps, total = width // STEP, sum(weights)
    edges = [steps * sum(weights[:i]) // total * STEP for i in range(len(weights) + 1)]
    return [slice(a, b) for a, b in zip(edges, edges[1:])]


def shaped(shape, dtype=f32):
    return jax.ShapeDtypeStruct(shape, dtype)


def swap(array, axis, apart):
    return lax.ppermute(array, axis, [(i, i ^ apart) for i in range(lax.axis_size(axis))])


def after(array, *others):
    return lax.optimization_barrier((array, *others))[0]


def on_device(
    queries, candidates, positives, hard_blocks, query_hidden, candidate_hidden, adapter_down, adapter_up
):
    q_own, c_own = queries[0], candidates[0, 0]
    hq, hc = query_hidden[0], candidate_hidden[0, 0]
    rows, width = q_own.shape
    block = c_own.shape[0]
    rank, shard_width = adapter_down.shape
    devices, shards = lax.axis_size("dp"), lax.axis_size("fsdp")
    position, shard = lax.axis_index("dp"), lax.axis_index("fsdp")
    place = jnp.stack([position, shard]).astype(jnp.int32)
    partners = list(range(2, devices, 2))
    even = (position & 1) == 0

    far_q = [swap(q_own, "dp", k) for k in partners]
    c_sib, q_sib, hq_sib, hc_sib = (swap(a, "dp", 1) for a in (c_own, q_own, hq, hc))
    scores, stats = call(scores_kernel, (shaped((2 * block, 2 * rows)), shaped((STATS, rows))))(
        place, c_own, c_sib, q_own, q_sib, positives, hard_blocks
    )
    far_stats = [swap(stats, "dp", k) for k in partners]
    sib_stats = swap(stats, "dp", 1)

    mine = jnp.broadcast_to(jnp.where(even, adapter_down, adapter_up), (shards, rank, shard_width))
    maps = lax.all_to_all(after(mine, scores, c_sib), "fsdp", 0, 0)

    factors = call(adapter_kernel, shaped((rank, 2 * rows + 2 * block)))(
        place, maps, hq, hq_sib, hc, hc_sib, c_own, c_sib, q_own, q_sib
    )
    far_factors = [swap(factors, "dp", k) for k in partners]

    far_stats[0:1] = [after(stat, factors, sib_stats) for stat in far_stats[0:1]]

    made, made_sib, answers, sib_answers, far_q_near, far_q_sib, sent, shares = [], [], [], [], [], [], [], []
    for k, q, far in zip(partners, far_q, far_stats):
        packet, q_again = call(
            partner_kernel, (shaped((block + EXTRA, 2 * rows), bf16), shaped((rows, width), bf16))
        )(place, c_own, c_sib, q, far)
        answers.append(swap(packet, "dp", k))
        sib_answers.append(swap(packet, "dp", k ^ 1))
        made.append(packet)
        made_sib.append(swap(packet, "dp", 1))
        far_q_near.append(q_again)
        far_q_sib.append(swap(q_again, "dp", 1))
        sent.append(call(share_kernel, shaped((rows, width), bf16))(after(packet, made_sib[-1], *far_factors), c_own, c_sib))
        shares.append(swap(after(sent[-1], answers[-1], sib_answers[-1]), "dp", k))
    scores = after(scores, *sent)
    w_grad, w_own, terms = call(
        functools.partial(sums_kernel, len(partners)),
        (
            shaped((block, rows * devices), bf16),
            shaped((2 * block, rows), bf16),
            shaped((shards, rank, shard_width), bf16),
        ),
    )(
        place, c_own, c_sib, q_own, q_sib, *far_q_near, *far_q_sib, hq, hq_sib, hc, hc_sib, stats, sib_stats,
        *answers, *sib_answers, *made, *made_sib, factors, *far_factors, scores,
    )
    queries = [q_own, q_sib]
    for pair in zip(far_q_near, far_q_sib):
        queries += pair
    grad = call(candidate_kernel, shaped((block, width), bf16))(w_grad, *queries)
    question = call(question_kernel, shaped((rows, width), bf16))(w_own, c_own, c_sib, *shares)

    terms = jnp.sum(lax.all_to_all(terms, "fsdp", 0, 0).astype(f32), 0)
    terms = after(terms, *shares)
    apart = 2
    while apart < devices:
        terms = terms + swap(terms, "dp", apart)
        apart *= 2
    terms = terms * adapter_scale
    others = swap(terms, "dp", 1)
    return (
        question[None],
        grad[None, None],
        jnp.where(even, others, terms),
        jnp.where(even, terms, others),
    )


def solution(mesh):
    placed = (
        P("fsdp", "dp", None),
        P("fsdp", "dp", None, None),
        P("fsdp", "dp"),
        P("fsdp", "dp"),
        P("fsdp", "dp", None),
        P("fsdp", "dp", None, None),
        P(None, "fsdp"),
        P(None, "fsdp"),
    )
    return jax.shard_map(
        on_device,
        mesh=mesh,
        in_specs=placed,
        out_specs=(
            P("fsdp", "dp", None),
            P("fsdp", "dp", None, None),
            P(None, "fsdp"),
            P(None, "fsdp"),
        ),
        check_vma=False,
    )
```

time: 62.6 us -> 55.4 us (0.88)
  waiting for transfers between devices: 27.1 us -> 11.5 us
  blocking collectives: 0 us -> 9.8 us
  starting transfers between devices: 22.5 us -> 18.2 us
  local copies, waits for them, and re-layouts: 1.69 us -> 4 us
  Pallas kernels: 8.68 us -> 9.88 us
  other arithmetic: 1.56 us -> 0.75 us
    ppermute x22 -> x15, waiting for transfers between devices: 27.1 us -> 5.64 us  [swap(): lax.ppermute(array, axis, [(i, i ^ apart) for i in range(lax.axis_size(ax...]
    ppermute x22 -> x15, starting transfers between devices: 22.5 us -> 11.5 us  [swap(): lax.ppermute(array, axis, [(i, i ^ apart) for i in range(lax.axis_size(ax...]
    all_to_all x0 -> x1, blocking collectives: none -> 9.8 us  [on_device(): terms = jnp.sum(lax.all_to_all(terms, 'fsdp', 0, 0).astype(f32), 0)]
    all_to_all x0 -> x1, starting transfers between devices: none -> 6.66 us  [on_device(): maps = lax.all_to_all(after(mine, scores, c_sib), 'fsdp', 0, 0)]
    all_to_all x0 -> x1, waiting for transfers between devices: none -> 5.88 us  [on_device(): maps = lax.all_to_all(after(mine, scores, c_sib), 'fsdp', 0, 0)]
    unnamed x14 -> x22, local copies, waits for them, and re-layouts: 1.68 us -> 3.34 us
    pallas_call x7, Pallas kernels: 8.68 us -> 9.88 us  [run(): pl.pallas_call(kernel, out_shape=outs, in_specs=[smem if a.dtype == jnp.i...]
    broadcast_in_dim x1 -> x0, other arithmetic: 0.78 us -> none  [on_device(): maps = jnp.where(even, adapter_down, adapter_up)[None]]
  transfers between devices with their start and end apart: 22 -> 16, of which waited for: 9 -> 4; matrix products, arithmetic and copies ran while one was open for 0% -> 1% of each run, Pallas kernels for 10% -> 15%
where the time goes in v5:
time: 55.4 us; the launch traced here: 54.9 us
  starting transfers between devices  18.2 us (33%)
  waiting for transfers between devices  11.5 us (21%)
  Pallas kernels  9.88 us (18%)
  blocking collectives  9.8 us (18%)
  local copies, waits for them, and re-layouts  4 us (7%)
  between operations  0.79 us (1%)
  other arithmetic  0.75 us (1%)
    ppermute x15, starting transfers between devices, swap(): lax.ppermute(array, axis, [(i, i ^ apart) for i in range(lax.axis_size(ax...  11.5 us
    pallas_call x7, Pallas kernels, run(): pl.pallas_call(kernel, out_shape=outs, in_specs=[smem if a.dtype == jnp.i...  9.88 us
    all_to_all x1, blocking collectives, on_device(): terms = jnp.sum(lax.all_to_all(terms, 'fsdp', 0, 0).astype(f32), 0)  9.8 us
    all_to_all x1, starting transfers between devices, on_device(): maps = lax.all_to_all(after(mine, scores, c_sib), 'fsdp', 0, 0)  6.66 us
    all_to_all x1, waiting for transfers between devices, on_device(): maps = lax.all_to_all(after(mine, scores, c_sib), 'fsdp', 0, 0)  5.88 us
    ppermute x15, waiting for transfers between devices, swap(): lax.ppermute(array, axis, [(i, i ^ apart) for i in range(lax.axis_size(ax...  5.64 us
    unnamed x22, local copies, waits for them, and re-layouts  3.34 us
  transfers between devices with their start and end apart: 16, of which 4 were waited for; matrix products, arithmetic and copies ran while one was open for 1% of the time, Pallas kernels for 15%

profile of v5, /device:TPU:0, one launch (start us, length us, event | category | flops | bytes accessed | tf_op | source)
XLA Modules:
  0.0 54.9 jit_solution(17110618076403838267)
XLA Ops:
  0.6 0.0 copy-start.10
  0.6 0.5 collective-permute-start
  1.2 0.1 collective-permute-start.1
  1.2 0.4 collective-permute-start.5
  1.7 2.6 %collective-permute-start.2 = (bf16[64,4096]{1,0:T(8,128)(2,1)}, bf16[64,4096]{1,0:T(8,128)(2,1)}, u32[]{:S(2)}, u32[]{:S(2)}) collective-permute-start(bf16[64,4096]{1,0:T(8,128)(2,1)} %bitcast.16), channel_id=1, source_target_pairs={{0,16},{8,24},{16,0},{24,8},{1,17},{9,25},{17,1},{25,9},{2,18},{10... | collective-permute-start | bytes 1572872 | tf_op jit(solution)/shard_map/ppermute | solution.py:266
  4.2 0.2 collective-permute-start.4
  4.4 0.1 pad_add_fusion.place
  4.5 0.0 copy-done.10
  4.5 0.0 copy-start.8
  4.5 0.0 copy-start.9
  4.5 0.1 collective-permute-done.1.q_sib.refs_3_.rest_1_
  4.6 0.0 collective-permute-done.c_sib.refs_1_
  4.6 0.5 copy-done.8
  5.1 0.0 copy-done.9
  5.2 0.0 copy-start
  5.2 1.1 %copy-done = bf16[1,1,80,4096]{3,2,1,0:T(8,128)(2,1)S(1)} copy-done((bf16[1,1,80,4096]{3,2,1,0:T(8,128)(2,1)S(1)}, bf16[1,1,80,4096]{3,2,1,0:T(8,128)(2,1)}, u32[]{:S(2)}) %copy-start) | copy-done | bytes 655384
  6.2 0.0 copy-start.2
  6.2 1.0 %copy-done.2 = bf16[1,64,4096]{2,1,0:T(8,128)(2,1)S(1)} copy-done((bf16[1,64,4096]{2,1,0:T(8,128)(2,1)S(1)}, bf16[1,64,4096]{2,1,0:T(8,128)(2,1)}, u32[]{:S(2)}) %copy-start.2) | copy-done | bytes 524312
  7.3 0.0 copy-start.1
  7.3 0.0 copy-start.4
  7.3 0.0 copy-start.5
  7.3 1.1 %shard_map.111 = (f32[160,128]{1,0:T(8,128)S(1)}, f32[8,64]{1,0:T(8,128)S(1)}) custom-call(s32[2]{0:T(128)S(1)} %pad_add_fusion.place, bf16[80,4096]{1,0:T(8,128)(2,1)S(1)} %bitcast.9, bf16[80,4096]{1,0:T(8,128)(2,1)S(1)} %collective-permute-done.c_sib.refs_1_, bf16[64,4096]{1,0:T(8,128)(2,1)S(1)} %bitcast.17, ...), custom_call_target="tpu_custom_call" | custom-call | flops 1000 | bytes 1000 | tf_op jit(solution)/shard_map/pallas_call | solution.py:243
  8.4 0.0 copy-start.6
  8.4 0.6 %copy-done.6 = f32[160,128]{1,0:T(8,128)} copy-done((f32[160,128]{1,0:T(8,128)}, f32[160,128]{1,0:T(8,128)S(1)}, u32[]{:S(2)}) %copy-start.6) | copy-done | bytes 81944
  9.0 0.7 %broadcast_in_dim.9 = bf16[8,16,512]{2,1,0:T(8,128)(2,1)} broadcast(bf16[16,512]{1,0:T(8,128)(2,1)S(1)} %broadcast_select_fusion.2), dimensions={1,2} | broadcast | bytes 147456 | tf_op jit(solution)/shard_map/broadcast_in_dim | solution.py:295
  9.7 6.7 %all-to-all-start = ((bf16[8,16,512]{2,1,0:T(8,128)(2,1)}), bf16[8,16,512]{2,1,0:T(8,128)(2,1)}, u32[]{:S(2)}, u32[]{:S(2)}) async-start(bf16[8,16,512]{2,1,0:T(8,128)(2,1)} %broadcast_in_dim.9), calls=%async_computation | async-start | bytes 262144 | tf_op jit(solution)/shard_map/all_to_all | solution.py:296
  16.3 0.0 collective-permute-start.6
  16.4 1.6 %collective-permute-start.3 = (f32[8,64]{1,0:T(8,128)S(1)}, f32[8,64]{1,0:T(8,128)S(1)}, u32[]{:S(2)}, u32[]{:S(2)}) collective-permute-start(f32[8,64]{1,0:T(8,128)S(1)} %get-tuple-element.17.refs_10_), channel_id=1, source_target_pairs={{0,16},{8,24},{16,0},{24,8},{1,17},{9,25},{17,1},{25,9},{2,18},{10... | collective-permute-start | bytes 6152 | tf_op jit(solution)/shard_map/ppermute | solution.py:266
  17.9 0.0 collective-permute-done.4.hq_sib.refs_7_
  17.9 0.0 collective-permute-done.5.hc_sib.refs_9_
  17.9 5.9 %all-to-all-done.maps = bf16[8,16,512]{2,1,0:T(8,128)(2,1)} async-done(((bf16[8,16,512]{2,1,0:T(8,128)(2,1)}), bf16[8,16,512]{2,1,0:T(8,128)(2,1)}, u32[]{:S(2)}, u32[]{:S(2)}) %all-to-all-start) | async-done | bytes 131104 | tf_op jit(solution)/shard_map/all_to_all | solution.py:296
  23.8 0.0 copy-done.1
  23.8 0.0 copy-done.3
  23.8 0.0 copy-done.4
  23.8 0.0 copy-done.5
  23.8 2.0 %shard_map.112.refs_16_ = f32[16,288]{1,0:T(8,128)S(1)} custom-call(s32[2]{0:T(128)S(1)} %pad_add_fusion.place, bf16[8,16,512]{2,1,0:T(8,128)(2,1)} %all-to-all-done.maps, bf16[64,4096]{1,0:T(8,128)(2,1)S(1)} %bitcast.25, bf16[64,4096]{1,0:T(8,128)(2,1)} %collective-permute-done.4.hq_sib.refs_7_, bf16[80,4096]{1,0:T(8,128)(2,1)S(1)} %bitcast.22, ...), custom_call_target="tpu_custom_call" | custom-call | flops 1000 | bytes 1000 | tf_op jit(solution)/shard_map/pallas_call | solution.py:243
  25.8 0.0 collective-permute-done.6.refs_11_
  25.9 0.0 collective-permute-done.3.stats
  25.9 0.0 collective-permute-done.2.q
  25.9 1.7 %shard_map.113 = (bf16[96,128]{1,0:T(8,128)(2,1)S(1)}, bf16[64,4096]{1,0:T(8,128)(2,1)S(1)}) custom-call(s32[2]{0:T(128)S(1)} %pad_add_fusion.place, bf16[80,4096]{1,0:T(8,128)(2,1)S(1)} %bitcast.11, bf16[80,4096]{1,0:T(8,128)(2,1)S(1)} %collective-permute-done.c_sib.refs_1_, bf16[64,4096]{1,0:T(8,128)(2,1)} %collective-permute-done.2.q, ...), custom_call_target="tpu_custom_call" | custom-call | flops 1000 | bytes 1000 | tf_op jit(solution)/shard_map/pallas_call | solution.py:243
  27.6 0.0 collective-permute-start.7
  27.6 0.0 copy-start.7
  27.6 0.5 collective-permute-start.10
  28.1 1.2 %collective-permute-start.9 = (bf16[96,128]{1,0:T(8,128)(2,1)S(1)}, bf16[96,128]{1,0:T(8,128)(2,1)S(1)}, u32[]{:S(2)}, u32[]{:S(2)}) collective-permute-start(bf16[96,128]{1,0:T(8,128)(2,1)S(1)} %get-tuple-element.23.packet.refs_14_), channel_id=1, source_target_pairs={{0,24},{8,16},{16,8},{24,0},{1,25},{9,17},{17,9},{25,1},{2,26},{10... | collective-permute-start | bytes 73736 | tf_op jit(solution)/shard_map/ppermute | solution.py:266
  29.3 0.5 collective-permute-start.8
  29.9 1.5 %collective-permute-start.11 = (f32[16,288]{1,0:T(8,128)S(1)}, f32[16,288]{1,0:T(8,128)S(1)}, u32[]{:S(2)}, u32[]{:S(2)}) collective-permute-start(f32[16,288]{1,0:T(8,128)S(1)} %shard_map.112.refs_16_), channel_id=1, source_target_pairs={{0,16},{8,24},{16,0},{24,8},{1,17},{9,25},{17,1},{25,9},{2,18},{10... | collective-permute-start | bytes 55304 | tf_op jit(solution)/shard_map/ppermute | solution.py:266
  31.3 2.3 %collective-permute-done.11.refs_17_ = f32[16,288]{1,0:T(8,128)S(1)} collective-permute-done((f32[16,288]{1,0:T(8,128)S(1)}, f32[16,288]{1,0:T(8,128)S(1)}, u32[]{:S(2)}, u32[]{:S(2)}) %collective-permute-start.11) | collective-permute-done | bytes 18464 | tf_op jit(solution)/shard_map/ppermute | solution.py:266
  33.7 0.0 collective-permute-done.10.refs_15_
  33.7 0.4 shard_map.114
  34.1 0.0 collective-permute-done.9.refs_13_
  34.1 0.0 collective-permute-done.8.refs_12_
  34.1 1.6 %collective-permute-start.12 = (bf16[64,4096]{1,0:T(8,128)(2,1)S(1)}, bf16[64,4096]{1,0:T(8,128)(2,1)S(1)}, u32[]{:S(2)}, u32[]{:S(2)}) collective-permute-start(bf16[64,4096]{1,0:T(8,128)(2,1)S(1)} %shard_map.114), channel_id=1, source_target_pairs={{0,16},{8,24},{16,0},{24,8},{1,17},{9,25},{17,1},{25,9},{2,18},{10... | collective-permute-start | bytes 1572872 | tf_op jit(solution)/shard_map/ppermute | solution.py:266
  35.7 0.0 collective-permute-done.7.refs_5_.rest_3_
  35.7 0.0 copy-done.7
  35.7 2.2 %shard_map.115 = (bf16[80,256]{1,0:T(8,128)(2,1)S(1)}, bf16[160,64]{1,0:T(8,128)(2,1)S(1)}, bf16[8,16,512]{2,1,0:T(8,128)(2,1)S(1)}) custom-call(s32[2]{0:T(128)S(1)} %pad_add_fusion.place, bf16[80,4096]{1,0:T(8,128)(2,1)S(1)} %bitcast.13, bf16[80,4096]{1,0:T(8,128)(2,1)S(1)} %collective-permute-done.c_sib.refs_1_, bf16[64,4096]{1,0:T(8,128)(2,1)S(1)} %bitcast.19, ...), custom_call_target="tpu_custom_call" | custom-call | flops 1000 | bytes 1000 | tf_op jit(solution)/shard_map/pallas_call | solution.py:243
  37.9 9.8 %all_to_all.10 = bf16[8,16,512]{2,1,0:T(8,128)(2,1)S(1)} all-to-all(bf16[8,16,512]{2,1,0:T(8,128)(2,1)S(1)} %get-tuple-element.28), channel_id=1, replica_groups=mesh['dp'=4,'fsdp'=8] {'fsdp'}, dimensions={0} | all-to-all | bytes 262144 | tf_op jit(solution)/shard_map/all_to_all | solution.py:336
  47.7 0.0 collective-permute-done.12.rest_0_
  47.7 0.8 %collective-permute-start.13 = (f32[16,512]{1,0:T(8,128)S(1)}, f32[16,512]{1,0:T(8,128)S(1)}, u32[]{:S(2)}, u32[]{:S(2)}) collective-permute-start(f32[16,512]{1,0:T(8,128)S(1)} %convert_reduce_fusion), channel_id=1, source_target_pairs={{0,16},{8,24},{16,0},{24,8},{1,17},{9,25},{17,1},{25,9},{2,18},{10... | collective-permute-start | bytes 98312 | tf_op jit(solution)/shard_map/ppermute | solution.py:266
  48.5 3.1 %collective-permute-done.13 = f32[16,512]{1,0:T(8,128)S(1)} collective-permute-done((f32[16,512]{1,0:T(8,128)S(1)}, f32[16,512]{1,0:T(8,128)S(1)}, u32[]{:S(2)}, u32[]{:S(2)}) %collective-permute-start.13) | collective-permute-done | bytes 32800 | tf_op jit(solution)/shard_map/ppermute | solution.py:266
  51.7 0.1 collective-permute-start.14
  51.8 1.3 %shard_map.117 = bf16[80,4096]{1,0:T(8,128)(2,1)} custom-call(bf16[80,256]{1,0:T(8,128)(2,1)S(1)} %get-tuple-element.27.weights, bf16[64,4096]{1,0:T(8,128)(2,1)S(1)} %bitcast.20, bf16[64,4096]{1,0:T(8,128)(2,1)S(1)} %collective-permute-done.1.q_sib.refs_3_.rest_1_, bf16[64,4096]{1,0:T(8,128)(2,1)S(1)} %get-tuple-element.21.refs_4_.rest_2_, ...), custom_call_target="tpu_custom_call" | custom-call | flops 1000 | bytes 1000 | tf_op jit(solution)/shard_map/pallas_call | solution.py:243
  53.1 1.2 %shard_map.116 = bf16[64,4096]{1,0:T(8,128)(2,1)} custom-call(bf16[160,64]{1,0:T(8,128)(2,1)S(1)} %get-tuple-element.25.weights, bf16[80,4096]{1,0:T(8,128)(2,1)S(1)} %bitcast.14, bf16[80,4096]{1,0:T(8,128)(2,1)S(1)} %collective-permute-done.c_sib.refs_1_, bf16[64,4096]{1,0:T(8,128)(2,1)S(1)} %collective-permute-done.12.rest_0_), custom_call_target="tpu_custom_call" | custom-call | flops 1000 | bytes 1000 | tf_op jit(solution)/shard_map/pallas_call | solution.py:243
  54.3 0.0 collective-permute-done.14
  54.3 0.6 %broadcast_select_fusion = (f32[16,512]{1,0:T(8,128)}, f32[16,512]{1,0:T(8,128)}) fusion(f32[16,512]{1,0:T(8,128)S(1)} %add_multiply_fusion, f32[16,512]{1,0:T(8,128)S(1)} %collective-permute-done.14, pred[]{:T(512)S(6)} %eq.3), kind=kLoop, calls=%fused_computation.2 | loop fusion | flops 16384 | bytes 131073 | tf_op jit(solution)/shard_map/jit(_where)/select_n | solution.py:348
  (4 shorter events, 0.0 us)
Async XLA Ops:
  0.6 3.8 %copy-start.10 = (bf16[16,512]{1,0:T(8,128)(2,1)S(1)}, bf16[16,512]{1,0:T(8,128)(2,1)}, u32[]{:S(2)}) copy-start(bf16[16,512]{1,0:T(8,128)(2,1)} %param.14) | copy-start | bytes 49156
  0.6 4.0 %collective-permute-start = (bf16[80,4096]{1,0:T(8,128)(2,1)}, bf16[80,4096]{1,0:T(8,128)(2,1)S(1)}, u32[]{:S(2)}, u32[]{:S(2)}) collective-permute-start(bf16[80,4096]{1,0:T(8,128)(2,1)} %bitcast.8), channel_id=1, source_target_pairs={{0,8},{8,0},{16,24},{24,16},{1,9},{9,1},{17,25},{25,17},{2,10},{10... | collective-permute-start | bytes 1966088 | tf_op jit(solution)/shard_map/ppermute | solution.py:266
  1.2 3.4 %collective-permute-start.1 = (bf16[64,4096]{1,0:T(8,128)(2,1)}, bf16[64,4096]{1,0:T(8,128)(2,1)S(1)}, u32[]{:S(2)}, u32[]{:S(2)}) collective-permute-start(bf16[64,4096]{1,0:T(8,128)(2,1)} %bitcast.15), channel_id=1, source_target_pairs={{0,8},{8,0},{16,24},{24,16},{1,9},{9,1},{17,25},{25,17},{2,10},{10... | collective-permute-start | bytes 1572872 | tf_op jit(solution)/shard_map/ppermute | solution.py:266
  1.2 16.7 %collective-permute-start.5 = (bf16[80,4096]{1,0:T(8,128)(2,1)}, bf16[80,4096]{1,0:T(8,128)(2,1)}, u32[]{:S(2)}, u32[]{:S(2)}) collective-permute-start(bf16[80,4096]{1,0:T(8,128)(2,1)} %bitcast.21), channel_id=1, source_target_pairs={{0,8},{8,0},{16,24},{24,16},{1,9},{9,1},{17,25},{25,17},{2,10},{10... | collective-permute-start | bytes 1966088 | tf_op jit(solution)/shard_map/ppermute | solution.py:266
  1.7 24.2 %collective-permute-start.2 = (bf16[64,4096]{1,0:T(8,128)(2,1)}, bf16[64,4096]{1,0:T(8,128)(2,1)}, u32[]{:S(2)}, u32[]{:S(2)}) collective-permute-start(bf16[64,4096]{1,0:T(8,128)(2,1)} %bitcast.16), channel_id=1, source_target_pairs={{0,16},{8,24},{16,0},{24,8},{1,17},{9,25},{17,1},{25,9},{2,18},{10... | collective-permute-start | bytes 1572872 | tf_op jit(solution)/shard_map/ppermute | solution.py:266
  4.2 13.7 %collective-permute-start.4 = (bf16[64,4096]{1,0:T(8,128)(2,1)}, bf16[64,4096]{1,0:T(8,128)(2,1)}, u32[]{:S(2)}, u32[]{:S(2)}) collective-permute-start(bf16[64,4096]{1,0:T(8,128)(2,1)} %bitcast.24), channel_id=1, source_target_pairs={{0,8},{8,0},{16,24},{24,16},{1,9},{9,1},{17,25},{25,17},{2,10},{10... | collective-permute-start | bytes 1572872 | tf_op jit(solution)/shard_map/ppermute | solution.py:266
  4.5 0.7 %copy-start.8 = (s32[1,64]{1,0:T(1,128)S(1)}, s32[1,64]{1,0:T(1,128)}, u32[]{:S(2)}) copy-start(s32[1,64]{1,0:T(1,128)} %positives.1) | copy-start | bytes 772
  4.5 0.7 %copy-start.9 = (s32[1,64]{1,0:T(1,128)S(1)}, s32[1,64]{1,0:T(1,128)}, u32[]{:S(2)}) copy-start(s32[1,64]{1,0:T(1,128)} %hard.1) | copy-start | bytes 772
  5.2 1.1 %copy-start = (bf16[1,1,80,4096]{3,2,1,0:T(8,128)(2,1)S(1)}, bf16[1,1,80,4096]{3,2,1,0:T(8,128)(2,1)}, u32[]{:S(2)}) copy-start(bf16[1,1,80,4096]{3,2,1,0:T(8,128)(2,1)} %param.9) | copy-start | bytes 1966084
  6.2 1.0 %copy-start.2 = (bf16[1,64,4096]{2,1,0:T(8,128)(2,1)S(1)}, bf16[1,64,4096]{2,1,0:T(8,128)(2,1)}, u32[]{:S(2)}) copy-start(bf16[1,64,4096]{2,1,0:T(8,128)(2,1)} %param.8) | copy-start | bytes 1572868
  7.3 16.5 %copy-start.1 = (bf16[1,1,80,4096]{3,2,1,0:T(8,128)(2,1)S(1)}, bf16[1,1,80,4096]{3,2,1,0:T(8,128)(2,1)}, u32[]{:S(2)}) copy-start(bf16[1,1,80,4096]{3,2,1,0:T(8,128)(2,1)} %param.9) | copy-start | bytes 1966084
  7.3 16.5 %copy-start.3 = (bf16[1,64,4096]{2,1,0:T(8,128)(2,1)S(1)}, bf16[1,64,4096]{2,1,0:T(8,128)(2,1)}, u32[]{:S(2)}) copy-start(bf16[1,64,4096]{2,1,0:T(8,128)(2,1)} %param.8) | copy-start | bytes 1572868
  7.3 16.5 %copy-start.4 = (bf16[1,1,80,4096]{3,2,1,0:T(8,128)(2,1)S(1)}, bf16[1,1,80,4096]{3,2,1,0:T(8,128)(2,1)}, u32[]{:S(2)}) copy-start(bf16[1,1,80,4096]{3,2,1,0:T(8,128)(2,1)} %param.13) | copy-start | bytes 1966084
  7.3 16.5 %copy-start.5 = (bf16[1,64,4096]{2,1,0:T(8,128)(2,1)S(1)}, bf16[1,64,4096]{2,1,0:T(8,128)(2,1)}, u32[]{:S(2)}) copy-start(bf16[1,64,4096]{2,1,0:T(8,128)(2,1)} %param.12) | copy-start | bytes 1572868
  8.4 0.6 %copy-start.6 = (f32[160,128]{1,0:T(8,128)}, f32[160,128]{1,0:T(8,128)S(1)}, u32[]{:S(2)}) copy-start(f32[160,128]{1,0:T(8,128)S(1)} %get-tuple-element.24.refs_18_) | copy-start | bytes 245764
  9.7 14.1 %all-to-all-start = ((bf16[8,16,512]{2,1,0:T(8,128)(2,1)}), bf16[8,16,512]{2,1,0:T(8,128)(2,1)}, u32[]{:S(2)}, u32[]{:S(2)}) async-start(bf16[8,16,512]{2,1,0:T(8,128)(2,1)} %broadcast_in_dim.9), calls=%async_computation | async-start | bytes 262144 | tf_op jit(solution)/shard_map/all_to_all | solution.py:296
  16.3 9.5 %collective-permute-start.6 = (f32[8,64]{1,0:T(8,128)S(1)}, f32[8,64]{1,0:T(8,128)S(1)}, u32[]{:S(2)}, u32[]{:S(2)}) collective-permute-start(f32[8,64]{1,0:T(8,128)S(1)} %get-tuple-element.17.refs_10_), channel_id=1, source_target_pairs={{0,8},{8,0},{16,24},{24,16},{1,9},{9,1},{17,25},{25,17},{2,10},{10... | collective-permute-start | bytes 6152 | tf_op jit(solution)/shard_map/ppermute | solution.py:266
  16.4 9.5 %collective-permute-start.3 = (f32[8,64]{1,0:T(8,128)S(1)}, f32[8,64]{1,0:T(8,128)S(1)}, u32[]{:S(2)}, u32[]{:S(2)}) collective-permute-start(f32[8,64]{1,0:T(8,128)S(1)} %get-tuple-element.17.refs_10_), channel_id=1, source_target_pairs={{0,16},{8,24},{16,0},{24,8},{1,17},{9,25},{17,1},{25,9},{2,18},{10... | collective-permute-start | bytes 6152 | tf_op jit(solution)/shard_map/ppermute | solution.py:266
  27.6 8.1 %collective-permute-start.7 = (bf16[64,4096]{1,0:T(8,128)(2,1)S(1)}, bf16[64,4096]{1,0:T(8,128)(2,1)S(1)}, u32[]{:S(2)}, u32[]{:S(2)}) collective-permute-start(bf16[64,4096]{1,0:T(8,128)(2,1)S(1)} %get-tuple-element.21.refs_4_.rest_2_), channel_id=1, source_target_pairs={{0,8},{8,0},{16,24},{24,16},{1,9},{9,1},{17,25},{25,17},{2,10},{10... | collective-permute-start | bytes 1572872 | tf_op jit(solution)/shard_map/ppermute | solution.py:266
  27.6 8.1 %copy-start.7 = (f32[160,128]{1,0:T(8,128)S(1)}, f32[160,128]{1,0:T(8,128)}, u32[]{:S(2)}) copy-start(f32[160,128]{1,0:T(8,128)} %copy-done.6) | copy-start | bytes 245764
  27.6 6.0 %collective-permute-start.10 = (bf16[96,128]{1,0:T(8,128)(2,1)S(1)}, bf16[96,128]{1,0:T(8,128)(2,1)S(1)}, u32[]{:S(2)}, u32[]{:S(2)}) collective-permute-start(bf16[96,128]{1,0:T(8,128)(2,1)S(1)} %get-tuple-element.23.packet.refs_14_), channel_id=1, source_target_pairs={{0,8},{8,0},{16,24},{24,16},{1,9},{9,1},{17,25},{25,17},{2,10},{10... | collective-permute-start | bytes 73736 | tf_op jit(solution)/shard_map/ppermute | solution.py:266
  28.1 6.0 %collective-permute-start.9 = (bf16[96,128]{1,0:T(8,128)(2,1)S(1)}, bf16[96,128]{1,0:T(8,128)(2,1)S(1)}, u32[]{:S(2)}, u32[]{:S(2)}) collective-permute-start(bf16[96,128]{1,0:T(8,128)(2,1)S(1)} %get-tuple-element.23.packet.refs_14_), channel_id=1, source_target_pairs={{0,24},{8,16},{16,8},{24,0},{1,25},{9,17},{17,9},{25,1},{2,26},{10... | collective-permute-start | bytes 73736 | tf_op jit(solution)/shard_map/ppermute | solution.py:266
  29.3 4.8 %collective-permute-start.8 = (bf16[96,128]{1,0:T(8,128)(2,1)S(1)}, bf16[96,128]{1,0:T(8,128)(2,1)S(1)}, u32[]{:S(2)}, u32[]{:S(2)}) collective-permute-start(bf16[96,128]{1,0:T(8,128)(2,1)S(1)} %get-tuple-element.23.packet.refs_14_), channel_id=1, source_target_pairs={{0,16},{8,24},{16,0},{24,8},{1,17},{9,25},{17,1},{25,9},{2,18},{10... | collective-permute-start | bytes 73736 | tf_op jit(solution)/shard_map/ppermute | solution.py:266
  29.9 3.8 %collective-permute-start.11 = (f32[16,288]{1,0:T(8,128)S(1)}, f32[16,288]{1,0:T(8,128)S(1)}, u32[]{:S(2)}, u32[]{:S(2)}) collective-permute-start(f32[16,288]{1,0:T(8,128)S(1)} %shard_map.112.refs_16_), channel_id=1, source_target_pairs={{0,16},{8,24},{16,0},{24,8},{1,17},{9,25},{17,1},{25,9},{2,18},{10... | collective-permute-start | bytes 55304 | tf_op jit(solution)/shard_map/ppermute | solution.py:266
  34.1 13.5 %collective-permute-start.12 = (bf16[64,4096]{1,0:T(8,128)(2,1)S(1)}, bf16[64,4096]{1,0:T(8,128)(2,1)S(1)}, u32[]{:S(2)}, u32[]{:S(2)}) collective-permute-start(bf16[64,4096]{1,0:T(8,128)(2,1)S(1)} %shard_map.114), channel_id=1, source_target_pairs={{0,16},{8,24},{16,0},{24,8},{1,17},{9,25},{17,1},{25,9},{2,18},{10... | collective-permute-start | bytes 1572872 | tf_op jit(solution)/shard_map/ppermute | solution.py:266
  47.7 4.0 %collective-permute-start.13 = (f32[16,512]{1,0:T(8,128)S(1)}, f32[16,512]{1,0:T(8,128)S(1)}, u32[]{:S(2)}, u32[]{:S(2)}) collective-permute-start(f32[16,512]{1,0:T(8,128)S(1)} %convert_reduce_fusion), channel_id=1, source_target_pairs={{0,16},{8,24},{16,0},{24,8},{1,17},{9,25},{17,1},{25,9},{2,18},{10... | collective-permute-start | bytes 98312 | tf_op jit(solution)/shard_map/ppermute | solution.py:266
  51.7 2.6 %collective-permute-start.14 = (f32[16,512]{1,0:T(8,128)S(1)}, f32[16,512]{1,0:T(8,128)S(1)}, u32[]{:S(2)}, u32[]{:S(2)}) collective-permute-start(f32[16,512]{1,0:T(8,128)S(1)} %add_multiply_fusion), channel_id=1, source_target_pairs={{0,8},{8,0},{16,24},{24,16},{1,9},{9,1},{17,25},{25,17},{2,10},{10... | collective-permute-start | bytes 98312 | tf_op jit(solution)/shard_map/ppermute | solution.py:266

commit v6 on v5

--- a/solution.py
+++ b/solution.py
@@ -80,18 +80,38 @@
     return whole(packet[at : at + 3, :rows]), whole(packet[at + 3 : at + 6, :rows])
 
 
+def wide_rows(array):
+    high = array.astype(bf16)
+    return [high, (array - high.astype(f32)).astype(bf16)]
+
+
+def factor_rows(factors, rows, block):
+    out = wide_rows(factors[:, : 2 * rows])
+    for start in (2 * rows, 2 * rows + block):
+        part = factors[:, start : start + block]
+        out += [jnp.concatenate([p, jnp.zeros((p.shape[0], 2 * rows - block), bf16)], 1) for p in wide_rows(part)]
+    return jnp.concatenate(out, 0)
+
+
+def factors_of(packed_rows, block):
+    rank = packed_rows.shape[0] // 6
+    high, low = [[packed_rows[(2 * i + j) * rank : (2 * i + j + 1) * rank].astype(f32) for i in range(3)] for j in (0, 1)]
+    query, own, sib = [a + b for a, b in zip(high, low)]
+    return query, jnp.concatenate([own[:, :block], sib[:, :block]], 1)
+
+
 def columns(ref, at, width):
     return ref[:, pl.ds(pl.multiple_of(at * width, width), width)]
 
 
-def scores_kernel(place, c_own, c_sib, q_own, q_sib, positives, hard, scores, stats):
+def scores_kernel(c_own, c_sib, q_own, q_sib, positives, hard, scores, stats):
     block, rows = c_own.shape[0], q_own.shape[0]
     c = jnp.concatenate([c_own[...], c_sib[...]], 0)
     q = jnp.concatenate([q_own[...], q_sib[...]], 0)
     total = dot(c, q, 1, 1) * sharpness_factor
     scores[...] = total
     mine = total[:, :rows]
-    owner, slot = layout(place[0], block, mine.shape)
+    owner, slot = layout(lax.axis_index("dp"), block, mine.shape)
     mine = jnp.where(allowed(owner, slot, hard[...], rows), mine, -jnp.inf)
     top = jnp.max(mine, axis=0, keepdims=True)
     stats[...] = jnp.zeros_like(stats)
@@ -101,17 +121,19 @@
     stats[HARD : HARD + 1] = hard[...].astype(f32)
 
 
-def adapter_kernel(place, maps, hq, hq_sib, hc, hc_sib, c_own, c_sib, q_own, q_sib, factors):
+def adapter_kernel(maps, hq, hq_sib, hc, hc_sib, c_own, c_sib, q_own, q_sib, factors):
     shards, _, width = maps.shape
 
     def product(parts):
-        total = 0.0
-        for at in range(shards):
-            rows = jnp.concatenate([r[:, at * width : (at + 1) * width] for r in parts], 0)
-            total = total + dot(maps[at], rows, 1, 1)
-        return total
-
-    core = place[0] & 1
+        out = []
+        for r in parts:
+            total = 0.0
+            for at in range(shards):
+                total = total + dot(r[:, at * width : (at + 1) * width], maps[at], 1, 1)
+            out.append(total)
+        return jnp.concatenate(out, 0).T
+
+    core = lax.axis_index("dp") & 1
 
     @pl.when(core == 0)
     def _():
@@ -122,19 +144,22 @@
         factors[...] = product([q_own, q_sib, c_own, c_sib])
 
 
-def partner_kernel(place, c_own, c_sib, q, stats, packet, q_again):
+def partner_kernel(c_own, c_sib, q, stats, factors, message, packet, q_again):
     block, rows = c_own.shape[0], q.shape[0]
     c = jnp.concatenate([c_own[...], c_sib[...]], 0)
     q_again[...] = q[...]
     total = dot(c, q[...], 1, 1)
-    owner, slot = layout(place[0], block, total.shape)
+    owner, slot = layout(lax.axis_index("dp"), block, total.shape)
     keep = allowed(owner, slot, stats[HARD : HARD + 1], rows)
     total = jnp.where(keep, total * sharpness_factor, -jnp.inf)
     top = jnp.max(total, axis=0, keepdims=True)
     share = jnp.sum(jnp.exp(total - top), axis=0, keepdims=True)
     log_total = merge([(stats[MAX : MAX + 1], stats[SUM : SUM + 1]), (top, share)])
     hit = hits(owner, slot, stats[POSITIVE : POSITIVE + 1], rows)
-    packet[...] = packed((jnp.exp(total - log_total) - hit.astype(f32)).astype(bf16), top, share)
+    here = packed((jnp.exp(total - log_total) - hit.astype(f32)).astype(bf16), top, share)
+    packet[...] = here
+    message[: here.shape[0]] = here
+    message[here.shape[0] :] = factor_rows(factors[...], rows, block)
 
 
 def share_kernel(packet, c_own, c_sib, share):
@@ -172,12 +197,15 @@
     return out
 
 
-def sums_kernel(partners, place, *refs):
+def sums_kernel(partners, *refs):
     n = partners
-    (c, q, far_q, far_q_sib, hq, hc, stats, answers, sib_answers, made, made_sib, (factors,), far_factors,
-     (scores,), (w_grad, w_own, terms)) = taken(refs, 2, 2, n, n, 2, 2, 2, n, n, n, n, 1, n, 1, 3)
+    (c, q, far_q, far_q_sib, hq, hc, stats, answers, sib_answers, made, made_sib, (factors, scores),
+     (w_grad, w_own, terms)) = taken(refs, 2, 2, n, n, 2, 2, 2, n, n, n, n, 2, 3)
     block, rows = c[0].shape[0], q[0].shape[0]
     shards, rank, width = terms.shape
+    end = block + EXTRA
+    far_factors = [factors_of(a[end:], block) for a in answers]
+    answers = [a[:end] for a in answers]
 
     def both(at):
         return jnp.concatenate([ref[at : at + 1] for ref in stats], 1)
@@ -185,7 +213,7 @@
     def log_total(own, packets):
         return merge([(own[MAX : MAX + 1], own[SUM : SUM + 1])] + [packet_stats(p) for p in packets])
 
-    owner, slot = layout(place[0], block, scores.shape)
+    owner, slot = layout(lax.axis_index("dp"), block, scores.shape)
     kept = allowed(owner, slot, both(HARD), rows)
     hit = hits(owner, slot, both(POSITIVE), rows)
     log_totals = jnp.concatenate([log_total(stats[0], answers), log_total(stats[1], sib_answers)], 1)
@@ -197,7 +225,7 @@
         pieces += [unpacked(mine[...]), unpacked(other[...], turned=True)]
     weights = jnp.concatenate(pieces, 1)
     w_grad[...] = weights[:block]
-    by_query = jnp.concatenate([r[:, : 2 * rows] for r in [factors] + far_factors], 1)
+    by_query = jnp.concatenate([r[:, : 2 * rows] for r in [factors] + [f for f, _ in far_factors]], 1)
     by_candidate = factors[:, 2 * rows :]
     queries = list(q)
     for pair in zip(far_q, far_q_sib):
@@ -207,7 +235,7 @@
         high = terms.astype(bf16)
         return jnp.concatenate([high, (terms - high.astype(f32)).astype(bf16)], 0)
 
-    core = place[0] & 1
+    core = lax.axis_index("dp") & 1
 
     @pl.when(core == 0)
     def _():
@@ -224,8 +252,8 @@
     def _():
         back_q = dot_wide(by_candidate, near, 1, 0)
         for far, mine, other in zip(far_factors, answers, sib_answers):
-            there = jnp.concatenate([unpacked(mine[...]), unpacked(other[...], turned=True)], 1)
-            back_q = back_q + dot_wide(far[:, 2 * rows :], there, 1, 0)
+            there = jnp.concatenate([unpacked(mine), unpacked(other[...], turned=True)], 1)
+            back_q = back_q + dot_wide(far[1], there, 1, 0)
         back_q = (back_q * sharpness_factor).astype(bf16)
         back_c = (dot_wide(by_query, weights, 1, 1) * sharpness_factor).astype(bf16)
         for i in range(shards):
@@ -235,27 +263,24 @@
             terms[i] = (dot(back_q, from_q, 1, 0) + dot(back_c, from_c, 1, 0)).astype(bf16)
 
 
-def call(kernel, outs):
-    smem = pl.BlockSpec(memory_space=pltpu.SMEM)
+def call(kernel, outs, needs=()):
     vmem = pl.BlockSpec(memory_space=pltpu.VMEM)
+    anywhere = pl.BlockSpec(memory_space=pl.ANY)
 
     def run(*args):
+        def body(*refs):
+            kernel(*refs[: len(args)], *refs[len(args) + len(needs) :])
+
         return pl.pallas_call(
-            kernel,
+            body,
             out_shape=outs,
-            in_specs=[smem if a.dtype == jnp.int32 and a.ndim == 1 else vmem for a in args],
+            in_specs=[vmem] * len(args) + [anywhere] * len(needs),
             out_specs=jax.tree.map(lambda _: vmem, outs),
             compiler_params=pltpu.CompilerParams(vmem_limit_bytes=16 * 2**20),
             cost_estimate=pl.CostEstimate(flops=1000, bytes_accessed=1000, transcendentals=0),
-        )(*args)
+        )(*args, *needs)
 
     return run
-
-
-def cut(width, weights):
-    steps, total = width // STEP, sum(weights)
-    edges = [steps * sum(weights[:i]) // total * STEP for i in range(len(weights) + 1)]
-    return [slice(a, b) for a, b in zip(edges, edges[1:])]
 
 
 def shaped(shape, dtype=f32):
@@ -279,43 +304,43 @@
     block = c_own.shape[0]
     rank, shard_width = adapter_down.shape
     devices, shards = lax.axis_size("dp"), lax.axis_size("fsdp")
-    position, shard = lax.axis_index("dp"), lax.axis_index("fsdp")
-    place = jnp.stack([position, shard]).astype(jnp.int32)
+    position = lax.axis_index("dp")
     partners = list(range(2, devices, 2))
     even = (position & 1) == 0
 
     far_q = [swap(q_own, "dp", k) for k in partners]
     c_sib, q_sib, hq_sib, hc_sib = (swap(a, "dp", 1) for a in (c_own, q_own, hq, hc))
-    scores, stats = call(scores_kernel, (shaped((2 * block, 2 * rows)), shaped((STATS, rows))))(
-        place, c_own, c_sib, q_own, q_sib, positives, hard_blocks
+    scores, stats = call(scores_kernel, (shaped((2 * block, 2 * rows)), shaped((STATS, rows))), [hq_sib, hc_sib])(
+        c_own, c_sib, q_own, q_sib, positives, hard_blocks
     )
     far_stats = [swap(stats, "dp", k) for k in partners]
     sib_stats = swap(stats, "dp", 1)
 
     mine = jnp.broadcast_to(jnp.where(even, adapter_down, adapter_up), (shards, rank, shard_width))
-    maps = lax.all_to_all(after(mine, scores, c_sib), "fsdp", 0, 0)
-
-    factors = call(adapter_kernel, shaped((rank, 2 * rows + 2 * block)))(
-        place, maps, hq, hq_sib, hc, hc_sib, c_own, c_sib, q_own, q_sib
-    )
-    far_factors = [swap(factors, "dp", k) for k in partners]
-
-    far_stats[0:1] = [after(stat, factors, sib_stats) for stat in far_stats[0:1]]
-
+    maps = lax.all_to_all(mine, "fsdp", 0, 0)
+
+    factors = call(adapter_kernel, shaped((rank, 2 * rows + 2 * block)), [stats])(
+        maps, hq, hq_sib, hc, hc_sib, c_own, c_sib, q_own, q_sib
+    )
     made, made_sib, answers, sib_answers, far_q_near, far_q_sib, sent, shares = [], [], [], [], [], [], [], []
     for k, q, far in zip(partners, far_q, far_stats):
-        packet, q_again = call(
-            partner_kernel, (shaped((block + EXTRA, 2 * rows), bf16), shaped((rows, width), bf16))
-        )(place, c_own, c_sib, q, far)
-        answers.append(swap(packet, "dp", k))
+        message, packet, q_again = call(
+            partner_kernel,
+            (
+                shaped((block + EXTRA + 6 * rank, 2 * rows), bf16),
+                shaped((block + EXTRA, 2 * rows), bf16),
+                shaped((rows, width), bf16),
+            ),
+            [sib_stats],
+        )(c_own, c_sib, q, far, factors)
+        answers.append(swap(message, "dp", k))
         sib_answers.append(swap(packet, "dp", k ^ 1))
         made.append(packet)
         made_sib.append(swap(packet, "dp", 1))
         far_q_near.append(q_again)
         far_q_sib.append(swap(q_again, "dp", 1))
-        sent.append(call(share_kernel, shaped((rows, width), bf16))(after(packet, made_sib[-1], *far_factors), c_own, c_sib))
+        sent.append(call(share_kernel, shaped((rows, width), bf16), [made_sib[-1]])(packet, c_own, c_sib))
         shares.append(swap(after(sent[-1], answers[-1], sib_answers[-1]), "dp", k))
-    scores = after(scores, *sent)
     w_grad, w_own, terms = call(
         functools.partial(sums_kernel, len(partners)),
         (
@@ -323,9 +348,10 @@
             shaped((2 * block, rows), bf16),
             shaped((shards, rank, shard_width), bf16),
         ),
+        sent,
     )(
-        place, c_own, c_sib, q_own, q_sib, *far_q_near, *far_q_sib, hq, hq_sib, hc, hc_sib, stats, sib_stats,
-        *answers, *sib_answers, *made, *made_sib, factors, *far_factors, scores,
+        c_own, c_sib, q_own, q_sib, *far_q_near, *far_q_sib, hq, hq_sib, hc, hc_sib, stats, sib_stats,
+        *answers, *sib_answers, *made, *made_sib, factors, scores,
     )
     queries = [q_own, q_sib]
     for pair in zip(far_q_near, far_q_sib):
@@ -333,11 +359,11 @@
     grad = call(candidate_kernel, shaped((block, width), bf16))(w_grad, *queries)
     question = call(question_kernel, shaped((rows, width), bf16))(w_own, c_own, c_sib, *shares)
 
-    terms = jnp.sum(lax.all_to_all(terms, "fsdp", 0, 0).astype(f32), 0)
-    terms = after(terms, *shares)
+    terms = lax.all_to_all(terms, "fsdp", 0, 0)
+    terms = after(jnp.sum(terms.astype(f32), 0), *shares)
     apart = 2
     while apart < devices:
-        terms = terms + swap(terms, "dp", apart)
+        terms = terms + after(swap(terms, "dp", apart), question, grad)
         apart *= 2
     terms = terms * adapter_scale
     others = swap(terms, "dp", 1)

time: 55.4 us -> 49.4 us (0.89)
  starting transfers between devices: 18.2 us -> 15.3 us
  waiting for transfers between devices: 11.5 us -> 8.67 us
  Pallas kernels: 9.88 us -> 7.78 us
  local copies, waits for them, and re-layouts: 4 us -> 5.58 us
    ppermute x15 -> x14, starting transfers between devices: 11.5 us -> 9.31 us  [swap(): lax.ppermute(array, axis, [(i, i ^ apart) for i in range(lax.axis_size(ax...]
    pallas_call x7, Pallas kernels: 9.88 us -> 7.78 us  [run(): pl.pallas_call(body, out_shape=outs, in_specs=[vmem] * len(args) + [anywh...]
    all_to_all x1, waiting for transfers between devices: 5.88 us -> 3.85 us  [on_device(): maps = lax.all_to_all(mine, 'fsdp', 0, 0)]
    unnamed x22 -> x26, local copies, waits for them, and re-layouts: 3.34 us -> 4.91 us
    ppermute x15 -> x14, waiting for transfers between devices: 5.64 us -> 4.82 us  [swap(): lax.ppermute(array, axis, [(i, i ^ apart) for i in range(lax.axis_size(ax...]
    all_to_all x1, starting transfers between devices: 6.66 us -> 5.97 us  [on_device(): maps = lax.all_to_all(mine, 'fsdp', 0, 0)]
  transfers between devices with their start and end apart: 16 -> 15, of which waited for: 4 -> 6; matrix products, arithmetic and copies ran while one was open for 1% -> 1% of each run, Pallas kernels for 15% -> 12%
where the time goes in v6:
time: 49.4 us; the launch traced here: 48.9 us
  starting transfers between devices  15.3 us (31%)
  blocking collectives  10.1 us (20%)
  waiting for transfers between devices  8.67 us (18%)
  Pallas kernels  7.78 us (16%)
  local copies, waits for them, and re-layouts  5.58 us (11%)
  between operations  0.79 us (2%)
  other arithmetic  0.67 us (1%)
    all_to_all x1, blocking collectives, on_device(): terms = lax.all_to_all(terms, 'fsdp', 0, 0)  10.1 us
    ppermute x14, starting transfers between devices, swap(): lax.ppermute(array, axis, [(i, i ^ apart) for i in range(lax.axis_size(ax...  9.31 us
    pallas_call x7, Pallas kernels, run(): pl.pallas_call(body, out_shape=outs, in_specs=[vmem] * len(args) + [anywh...  7.78 us
    all_to_all x1, starting transfers between devices, on_device(): maps = lax.all_to_all(mine, 'fsdp', 0, 0)  5.97 us
    unnamed x26, local copies, waits for them, and re-layouts  4.91 us
    ppermute x14, waiting for transfers between devices, swap(): lax.ppermute(array, axis, [(i, i ^ apart) for i in range(lax.axis_size(ax...  4.82 us
    all_to_all x1, waiting for transfers between devices, on_device(): maps = lax.all_to_all(mine, 'fsdp', 0, 0)  3.85 us
  transfers between devices with their start and end apart: 15, of which 6 were waited for; matrix products, arithmetic and copies ran while one was open for 1% of the time, Pallas kernels for 12%

profile of v6, /device:TPU:0, one launch (start us, length us, event | category | flops | bytes accessed | tf_op | source)
XLA Modules:
  0.0 48.9 jit_solution(2244125998232847751)
XLA Ops:
  0.6 0.0 copy-start.12
  0.6 0.5 %collective-permute-start = (bf16[80,4096]{1,0:T(8,128)(2,1)}, bf16[80,4096]{1,0:T(8,128)(2,1)S(1)}, u32[]{:S(2)}, u32[]{:S(2)}) collective-permute-start(bf16[80,4096]{1,0:T(8,128)(2,1)} %bitcast.6), channel_id=1, source_target_pairs={{0,8},{8,0},{16,24},{24,16},{1,9},{9,1},{17,25},{25,17},{2,10},{10... | collective-permute-start | bytes 1966088 | tf_op jit(solution)/shard_map/ppermute | solution.py:291
  1.2 0.1 collective-permute-start.4
  1.2 0.4 collective-permute-start.1
  1.7 0.1 collective-permute-start.3
  1.8 2.9 %collective-permute-start.2 = (bf16[64,4096]{1,0:T(8,128)(2,1)}, bf16[64,4096]{1,0:T(8,128)(2,1)}, u32[]{:S(2)}, u32[]{:S(2)}) collective-permute-start(bf16[64,4096]{1,0:T(8,128)(2,1)} %bitcast.14), channel_id=1, source_target_pairs={{0,16},{8,24},{16,0},{24,8},{1,17},{9,25},{17,1},{25,9},{2,18},{10... | collective-permute-start | bytes 1572872 | tf_op jit(solution)/shard_map/ppermute | solution.py:291
  4.7 0.0 copy-done.12
  4.7 0.7 %broadcast_in_dim.9 = bf16[8,16,512]{2,1,0:T(8,128)(2,1)} broadcast(bf16[16,512]{1,0:T(8,128)(2,1)S(1)} %broadcast_select_fusion.2), dimensions={1,2} | broadcast | bytes 147456 | tf_op jit(solution)/shard_map/broadcast_in_dim | solution.py:319
  5.3 0.0 copy-start.10
  5.3 0.0 copy-start.11
  5.4 6.0 %all-to-all-start = ((bf16[8,16,512]{2,1,0:T(8,128)(2,1)}), bf16[8,16,512]{2,1,0:T(8,128)(2,1)}, u32[]{:S(2)}, u32[]{:S(2)}) async-start(bf16[8,16,512]{2,1,0:T(8,128)(2,1)} %broadcast_in_dim.9), calls=%async_computation | async-start | bytes 262144 | tf_op jit(solution)/shard_map/all_to_all | solution.py:320
  11.3 0.0 collective-permute-done.1.refs_3_.refs_8_.refs_2_
  11.3 0.0 collective-permute-done.3.refs_6_.refs_2_.refs_7_
  11.3 0.0 collective-permute-done.refs_1_.refs_6_.refs_2_
  11.3 0.0 collective-permute-done.4.refs_7_.refs_4_.refs_9_
  11.4 0.0 copy-done.10
  11.4 0.0 copy-done.11
  11.4 0.0 copy-start
  11.4 1.1 %copy-done = bf16[1,1,80,4096]{3,2,1,0:T(8,128)(2,1)S(1)} copy-done((bf16[1,1,80,4096]{3,2,1,0:T(8,128)(2,1)S(1)}, bf16[1,1,80,4096]{3,2,1,0:T(8,128)(2,1)}, u32[]{:S(2)}) %copy-start) | copy-done | bytes 655384
  12.5 0.0 copy-start.2
  12.5 1.0 %copy-done.2 = bf16[1,64,4096]{2,1,0:T(8,128)(2,1)S(1)} copy-done((bf16[1,64,4096]{2,1,0:T(8,128)(2,1)S(1)}, bf16[1,64,4096]{2,1,0:T(8,128)(2,1)}, u32[]{:S(2)}) %copy-start.2) | copy-done | bytes 524312
  13.5 0.0 copy-start.1
  13.5 0.0 copy-start.3
  13.5 0.5 %shard_map.111 = (f32[160,128]{1,0:T(8,128)S(1)}, f32[8,64]{1,0:T(8,128)S(1)}) custom-call(bf16[80,4096]{1,0:T(8,128)(2,1)S(1)} %bitcast.7, bf16[80,4096]{1,0:T(8,128)(2,1)S(1)} %collective-permute-done.refs_1_.refs_6_.refs_2_, bf16[64,4096]{1,0:T(8,128)(2,1)S(1)} %bitcast.15, bf16[64,4096]{1,0:T(8,128)(2,1)S(1)} %collective-permute-done.1.refs_3_.refs_8_.refs_2_, ...), custom_call_target="tpu_custom_call" | custom-call | flops 1000 | bytes 1000 | tf_op jit(solution)/shard_map/pallas_call | solution.py:274
  14.1 0.0 copy-start.8
  14.1 0.6 %copy-done.8 = f32[160,128]{1,0:T(8,128)} copy-done((f32[160,128]{1,0:T(8,128)}, f32[160,128]{1,0:T(8,128)S(1)}, u32[]{:S(2)}) %copy-start.8) | copy-done | bytes 81944
  14.7 0.5 %collective-permute-start.5 = (f32[8,64]{1,0:T(8,128)S(1)}, f32[8,64]{1,0:T(8,128)S(1)}, u32[]{:S(2)}, u32[]{:S(2)}) collective-permute-start(f32[8,64]{1,0:T(8,128)S(1)} %get-tuple-element.15.refs_9_.refs_10_), channel_id=1, source_target_pairs={{0,16},{8,24},{16,0},{24,8},{1,17},{9,25},{17,1},{25,9},{2,18},{10... | collective-permute-start | bytes 6152 | tf_op jit(solution)/shard_map/ppermute | solution.py:291
  15.2 0.0 collective-permute-start.6
  15.2 3.8 %all-to-all-done.refs_0_ = bf16[8,16,512]{2,1,0:T(8,128)(2,1)} async-done(((bf16[8,16,512]{2,1,0:T(8,128)(2,1)}), bf16[8,16,512]{2,1,0:T(8,128)(2,1)}, u32[]{:S(2)}, u32[]{:S(2)}) %all-to-all-start) | async-done | bytes 131104 | tf_op jit(solution)/shard_map/all_to_all | solution.py:320
  19.1 0.0 copy-done.1
  19.1 0.0 copy-done.3
  19.1 0.0 copy-start.4
  19.1 1.1 %copy-done.4 = bf16[1,1,80,4096]{3,2,1,0:T(8,128)(2,1)S(1)} copy-done((bf16[1,1,80,4096]{3,2,1,0:T(8,128)(2,1)S(1)}, bf16[1,1,80,4096]{3,2,1,0:T(8,128)(2,1)}, u32[]{:S(2)}) %copy-start.4) | copy-done | bytes 655384
  20.2 0.0 copy-start.6
  20.2 1.0 %copy-done.6 = bf16[1,64,4096]{2,1,0:T(8,128)(2,1)S(1)} copy-done((bf16[1,64,4096]{2,1,0:T(8,128)(2,1)S(1)}, bf16[1,64,4096]{2,1,0:T(8,128)(2,1)}, u32[]{:S(2)}) %copy-start.6) | copy-done | bytes 524312
  21.2 1.7 %shard_map.112.refs_4_.refs_16_ = f32[16,288]{1,0:T(8,128)S(1)} custom-call(bf16[8,16,512]{2,1,0:T(8,128)(2,1)} %all-to-all-done.refs_0_, bf16[64,4096]{1,0:T(8,128)(2,1)S(1)} %bitcast.23, bf16[64,4096]{1,0:T(8,128)(2,1)S(1)} %collective-permute-done.3.refs_6_.refs_2_.refs_7_, bf16[80,4096]{1,0:T(8,128)(2,1)S(1)} %bitcast.20, ...), custom_call_target="tpu_custom_call" | custom-call | flops 1000 | bytes 1000 | tf_op jit(solution)/shard_map/pallas_call | solution.py:274
  22.9 0.0 collective-permute-done.2.refs_2_
  22.9 0.0 collective-permute-done.5.refs_3_
  22.9 0.0 collective-permute-done.6.refs_5_.refs_11_
  22.9 1.7 %shard_map.113 = (bf16[192,128]{1,0:T(8,128)(2,1)S(1)}, bf16[96,128]{1,0:T(8,128)(2,1)S(1)}, bf16[64,4096]{1,0:T(8,128)(2,1)S(1)}) custom-call(bf16[80,4096]{1,0:T(8,128)(2,1)S(1)} %bitcast.9, bf16[80,4096]{1,0:T(8,128)(2,1)S(1)} %collective-permute-done.refs_1_.refs_6_.refs_2_, bf16[64,4096]{1,0:T(8,128)(2,1)} %collective-permute-done.2.refs_2_, ...), custom_call_target="tpu_custom_call" | custom-call | flops 1000 | bytes 1000 | tf_op jit(solution)/shard_map/pallas_call | solution.py:274
  24.6 0.1 collective-permute-start.7
  24.7 0.6 %collective-permute-start.8 = (bf16[192,128]{1,0:T(8,128)(2,1)S(1)}, bf16[192,128]{1,0:T(8,128)(2,1)S(1)}, u32[]{:S(2)}, u32[]{:S(2)}) collective-permute-start(bf16[192,128]{1,0:T(8,128)(2,1)S(1)} %get-tuple-element.17), channel_id=1, source_target_pairs={{0,16},{8,24},{16,0},{24,8},{1,17},{9,25},{17,1},{25,9},{2,18},{10... | collective-permute-start | bytes 147464 | tf_op jit(solution)/shard_map/ppermute | solution.py:291
  25.3 0.0 copy-start.5
  25.3 0.2 collective-permute-start.10
  25.5 1.4 %collective-permute-start.9 = (bf16[96,128]{1,0:T(8,128)(2,1)S(1)}, bf16[96,128]{1,0:T(8,128)(2,1)S(1)}, u32[]{:S(2)}, u32[]{:S(2)}) collective-permute-start(bf16[96,128]{1,0:T(8,128)(2,1)S(1)} %get-tuple-element.18.refs_0_.refs_14_), channel_id=1, source_target_pairs={{0,24},{8,16},{16,8},{24,0},{1,25},{9,17},{17,9},{25,1},{2,26},{10... | collective-permute-start | bytes 73736 | tf_op jit(solution)/shard_map/ppermute | solution.py:291
  26.9 0.0 collective-permute-done.10.refs_3_.refs_15_
  26.9 0.4 shard_map.114.refs_18_
  27.4 1.6 %collective-permute-done.9.refs_13_ = bf16[96,128]{1,0:T(8,128)(2,1)S(1)} collective-permute-done((bf16[96,128]{1,0:T(8,128)(2,1)S(1)}, bf16[96,128]{1,0:T(8,128)(2,1)S(1)}, u32[]{:S(2)}, u32[]{:S(2)}) %collective-permute-start.9) | collective-permute-done | bytes 24608 | tf_op jit(solution)/shard_map/ppermute | solution.py:291
  29.0 0.1 collective-permute-done.8.refs_12_
  29.1 1.1 %collective-permute-start.11 = (bf16[64,4096]{1,0:T(8,128)(2,1)S(1)}, bf16[64,4096]{1,0:T(8,128)(2,1)S(1)}, u32[]{:S(2)}, u32[]{:S(2)}) collective-permute-start(bf16[64,4096]{1,0:T(8,128)(2,1)S(1)} %shard_map.114.refs_18_), channel_id=1, source_target_pairs={{0,16},{8,24},{16,0},{24,8},{1,17},{9,25},{17,1},{25,9},{2,18},{10... | collective-permute-start | bytes 1572872 | tf_op jit(solution)/shard_map/ppermute | solution.py:291
  30.2 0.0 collective-permute-done.7.refs_5_.refs_4_
  30.2 0.0 copy-done.5
  30.2 0.0 copy-done.7
  30.2 0.0 copy-done.9
  30.2 0.9 %shard_map.115 = (bf16[80,256]{1,0:T(8,128)(2,1)S(1)}, bf16[160,64]{1,0:T(8,128)(2,1)S(1)}, bf16[8,16,512]{2,1,0:T(8,128)(2,1)S(1)}) custom-call(bf16[80,4096]{1,0:T(8,128)(2,1)S(1)} %bitcast.11, bf16[80,4096]{1,0:T(8,128)(2,1)S(1)} %collective-permute-done.refs_1_.refs_6_.refs_2_, bf16[64,4096]{1,0:T(8,128)(2,1)S(1)} %bitcast.17, ...), custom_call_target="tpu_custom_call" | custom-call | flops 1000 | bytes 1000 | tf_op jit(solution)/shard_map/pallas_call | solution.py:274
  31.1 10.1 %all_to_all.10 = bf16[8,16,512]{2,1,0:T(8,128)(2,1)S(1)} all-to-all(bf16[8,16,512]{2,1,0:T(8,128)(2,1)S(1)} %get-tuple-element.23), channel_id=1, replica_groups=mesh['dp'=4,'fsdp'=8] {'fsdp'}, dimensions={0} | all-to-all | bytes 262144 | tf_op jit(solution)/shard_map/all_to_all | solution.py:362
  41.3 1.8 %collective-permute-done.11.refs_3_ = bf16[64,4096]{1,0:T(8,128)(2,1)S(1)} collective-permute-done((bf16[64,4096]{1,0:T(8,128)(2,1)S(1)}, bf16[64,4096]{1,0:T(8,128)(2,1)S(1)}, u32[]{:S(2)}, u32[]{:S(2)}) %collective-permute-start.11) | collective-permute-done | bytes 524320 | tf_op jit(solution)/shard_map/ppermute | solution.py:291
  43.1 1.3 %collective-permute-start.12 = (f32[16,512]{1,0:T(8,128)S(1)}, f32[16,512]{1,0:T(8,128)S(1)}, u32[]{:S(2)}, u32[]{:S(2)}) collective-permute-start(f32[16,512]{1,0:T(8,128)S(1)} %convert_reduce_fusion), channel_id=1, source_target_pairs={{0,16},{8,24},{16,0},{24,8},{1,17},{9,25},{17,1},{25,9},{2,18},{10... | collective-permute-start | bytes 98312 | tf_op jit(solution)/shard_map/ppermute | solution.py:291
  44.4 1.3 %shard_map.117 = bf16[80,4096]{1,0:T(8,128)(2,1)} custom-call(bf16[80,256]{1,0:T(8,128)(2,1)S(1)} %get-tuple-element.22.refs_0_, bf16[64,4096]{1,0:T(8,128)(2,1)S(1)} %bitcast.18, bf16[64,4096]{1,0:T(8,128)(2,1)S(1)} %collective-permute-done.1.refs_3_.refs_8_.refs_2_, bf16[64,4096]{1,0:T(8,128)(2,1)S(1)} %get-tuple-element.16.refs_4_.refs_3_, ...), custom_call_target="tpu_custom_call" | custom-call | flops 1000 | bytes 1000 | tf_op jit(solution)/shard_map/pallas_call | solution.py:274
  45.7 1.2 %shard_map.116 = bf16[64,4096]{1,0:T(8,128)(2,1)} custom-call(bf16[160,64]{1,0:T(8,128)(2,1)S(1)} %get-tuple-element.20.refs_0_, bf16[80,4096]{1,0:T(8,128)(2,1)S(1)} %bitcast.12, bf16[80,4096]{1,0:T(8,128)(2,1)S(1)} %collective-permute-done.refs_1_.refs_6_.refs_2_, bf16[64,4096]{1,0:T(8,128)(2,1)S(1)} %collective-permute-done.11.refs_3_), custom_call_target="tpu_custom_call" | custom-call | flops 1000 | bytes 1000 | tf_op jit(solution)/shard_map/pallas_call | solution.py:274
  46.9 0.1 collective-permute-done.12
  47.0 0.1 collective-permute-start.13
  47.1 1.2 %collective-permute-done.13 = f32[16,512]{1,0:T(8,128)S(1)} collective-permute-done((f32[16,512]{1,0:T(8,128)S(1)}, f32[16,512]{1,0:T(8,128)S(1)}, u32[]{:S(2)}, u32[]{:S(2)}) %collective-permute-start.13) | collective-permute-done | bytes 32800 | tf_op jit(solution)/shard_map/ppermute | solution.py:291
  48.3 0.6 %broadcast_select_fusion = (f32[16,512]{1,0:T(8,128)}, f32[16,512]{1,0:T(8,128)}) fusion(f32[16,512]{1,0:T(8,128)S(1)} %add_multiply_fusion, f32[16,512]{1,0:T(8,128)S(1)} %collective-permute-done.13, pred[]{:T(512)S(6)} %eq.3), kind=kLoop, calls=%fused_computation.2 | loop fusion | flops 16384 | bytes 131073 | tf_op jit(solution)/shard_map/jit(_where)/select_n | solution.py:374
  (5 shorter events, 0.0 us)
Async XLA Ops:
  0.6 4.0 %copy-start.12 = (bf16[16,512]{1,0:T(8,128)(2,1)S(1)}, bf16[16,512]{1,0:T(8,128)(2,1)}, u32[]{:S(2)}) copy-start(bf16[16,512]{1,0:T(8,128)(2,1)} %param.14) | copy-start | bytes 49156
  0.6 10.7 %collective-permute-start = (bf16[80,4096]{1,0:T(8,128)(2,1)}, bf16[80,4096]{1,0:T(8,128)(2,1)S(1)}, u32[]{:S(2)}, u32[]{:S(2)}) collective-permute-start(bf16[80,4096]{1,0:T(8,128)(2,1)} %bitcast.6), channel_id=1, source_target_pairs={{0,8},{8,0},{16,24},{24,16},{1,9},{9,1},{17,25},{25,17},{2,10},{10... | collective-permute-start | bytes 1966088 | tf_op jit(solution)/shard_map/ppermute | solution.py:291
  1.2 10.2 %collective-permute-start.4 = (bf16[80,4096]{1,0:T(8,128)(2,1)}, bf16[80,4096]{1,0:T(8,128)(2,1)S(1)}, u32[]{:S(2)}, u32[]{:S(2)}) collective-permute-start(bf16[80,4096]{1,0:T(8,128)(2,1)} %bitcast.19), channel_id=1, source_target_pairs={{0,8},{8,0},{16,24},{24,16},{1,9},{9,1},{17,25},{25,17},{2,10},{10... | collective-permute-start | bytes 1966088 | tf_op jit(solution)/shard_map/ppermute | solution.py:291
  1.2 10.1 %collective-permute-start.1 = (bf16[64,4096]{1,0:T(8,128)(2,1)}, bf16[64,4096]{1,0:T(8,128)(2,1)S(1)}, u32[]{:S(2)}, u32[]{:S(2)}) collective-permute-start(bf16[64,4096]{1,0:T(8,128)(2,1)} %bitcast.13), channel_id=1, source_target_pairs={{0,8},{8,0},{16,24},{24,16},{1,9},{9,1},{17,25},{25,17},{2,10},{10... | collective-permute-start | bytes 1572872 | tf_op jit(solution)/shard_map/ppermute | solution.py:291
  1.7 9.7 %collective-permute-start.3 = (bf16[64,4096]{1,0:T(8,128)(2,1)}, bf16[64,4096]{1,0:T(8,128)(2,1)S(1)}, u32[]{:S(2)}, u32[]{:S(2)}) collective-permute-start(bf16[64,4096]{1,0:T(8,128)(2,1)} %bitcast.22), channel_id=1, source_target_pairs={{0,8},{8,0},{16,24},{24,16},{1,9},{9,1},{17,25},{25,17},{2,10},{10... | collective-permute-start | bytes 1572872 | tf_op jit(solution)/shard_map/ppermute | solution.py:291
  1.8 21.2 %collective-permute-start.2 = (bf16[64,4096]{1,0:T(8,128)(2,1)}, bf16[64,4096]{1,0:T(8,128)(2,1)}, u32[]{:S(2)}, u32[]{:S(2)}) collective-permute-start(bf16[64,4096]{1,0:T(8,128)(2,1)} %bitcast.14), channel_id=1, source_target_pairs={{0,16},{8,24},{16,0},{24,8},{1,17},{9,25},{17,1},{25,9},{2,18},{10... | collective-permute-start | bytes 1572872 | tf_op jit(solution)/shard_map/ppermute | solution.py:291
  5.3 6.0 %copy-start.10 = (s32[1,64]{1,0:T(1,128)S(1)}, s32[1,64]{1,0:T(1,128)}, u32[]{:S(2)}) copy-start(s32[1,64]{1,0:T(1,128)} %refs_4_.1) | copy-start | bytes 772
  5.3 6.0 %copy-start.11 = (s32[1,64]{1,0:T(1,128)S(1)}, s32[1,64]{1,0:T(1,128)}, u32[]{:S(2)}) copy-start(s32[1,64]{1,0:T(1,128)} %refs_5_.1) | copy-start | bytes 772
  5.4 13.7 %all-to-all-start = ((bf16[8,16,512]{2,1,0:T(8,128)(2,1)}), bf16[8,16,512]{2,1,0:T(8,128)(2,1)}, u32[]{:S(2)}, u32[]{:S(2)}) async-start(bf16[8,16,512]{2,1,0:T(8,128)(2,1)} %broadcast_in_dim.9), calls=%async_computation | async-start | bytes 262144 | tf_op jit(solution)/shard_map/all_to_all | solution.py:320
  11.4 1.1 %copy-start = (bf16[1,1,80,4096]{3,2,1,0:T(8,128)(2,1)S(1)}, bf16[1,1,80,4096]{3,2,1,0:T(8,128)(2,1)}, u32[]{:S(2)}) copy-start(bf16[1,1,80,4096]{3,2,1,0:T(8,128)(2,1)} %param.9) | copy-start | bytes 1966084
  12.5 1.0 %copy-start.2 = (bf16[1,64,4096]{2,1,0:T(8,128)(2,1)S(1)}, bf16[1,64,4096]{2,1,0:T(8,128)(2,1)}, u32[]{:S(2)}) copy-start(bf16[1,64,4096]{2,1,0:T(8,128)(2,1)} %param.8) | copy-start | bytes 1572868
  13.5 5.6 %copy-start.1 = (bf16[1,1,80,4096]{3,2,1,0:T(8,128)(2,1)S(1)}, bf16[1,1,80,4096]{3,2,1,0:T(8,128)(2,1)}, u32[]{:S(2)}) copy-start(bf16[1,1,80,4096]{3,2,1,0:T(8,128)(2,1)} %param.9) | copy-start | bytes 1966084
  13.5 5.6 %copy-start.3 = (bf16[1,64,4096]{2,1,0:T(8,128)(2,1)S(1)}, bf16[1,64,4096]{2,1,0:T(8,128)(2,1)}, u32[]{:S(2)}) copy-start(bf16[1,64,4096]{2,1,0:T(8,128)(2,1)} %param.8) | copy-start | bytes 1572868
  14.1 0.6 %copy-start.8 = (f32[160,128]{1,0:T(8,128)}, f32[160,128]{1,0:T(8,128)S(1)}, u32[]{:S(2)}) copy-start(f32[160,128]{1,0:T(8,128)S(1)} %get-tuple-element.19.refs_17_) | copy-start | bytes 245764
  14.7 8.2 %collective-permute-start.5 = (f32[8,64]{1,0:T(8,128)S(1)}, f32[8,64]{1,0:T(8,128)S(1)}, u32[]{:S(2)}, u32[]{:S(2)}) collective-permute-start(f32[8,64]{1,0:T(8,128)S(1)} %get-tuple-element.15.refs_9_.refs_10_), channel_id=1, source_target_pairs={{0,16},{8,24},{16,0},{24,8},{1,17},{9,25},{17,1},{25,9},{2,18},{10... | collective-permute-start | bytes 6152 | tf_op jit(solution)/shard_map/ppermute | solution.py:291
  15.2 7.7 %collective-permute-start.6 = (f32[8,64]{1,0:T(8,128)S(1)}, f32[8,64]{1,0:T(8,128)S(1)}, u32[]{:S(2)}, u32[]{:S(2)}) collective-permute-start(f32[8,64]{1,0:T(8,128)S(1)} %get-tuple-element.15.refs_9_.refs_10_), channel_id=1, source_target_pairs={{0,8},{8,0},{16,24},{24,16},{1,9},{9,1},{17,25},{25,17},{2,10},{10... | collective-permute-start | bytes 6152 | tf_op jit(solution)/shard_map/ppermute | solution.py:291
  19.1 1.1 %copy-start.4 = (bf16[1,1,80,4096]{3,2,1,0:T(8,128)(2,1)S(1)}, bf16[1,1,80,4096]{3,2,1,0:T(8,128)(2,1)}, u32[]{:S(2)}) copy-start(bf16[1,1,80,4096]{3,2,1,0:T(8,128)(2,1)} %param.13) | copy-start | bytes 1966084
  20.2 1.0 %copy-start.6 = (bf16[1,64,4096]{2,1,0:T(8,128)(2,1)S(1)}, bf16[1,64,4096]{2,1,0:T(8,128)(2,1)}, u32[]{:S(2)}) copy-start(bf16[1,64,4096]{2,1,0:T(8,128)(2,1)} %param.12) | copy-start | bytes 1572868
  24.6 5.6 %collective-permute-start.7 = (bf16[64,4096]{1,0:T(8,128)(2,1)S(1)}, bf16[64,4096]{1,0:T(8,128)(2,1)S(1)}, u32[]{:S(2)}, u32[]{:S(2)}) collective-permute-start(bf16[64,4096]{1,0:T(8,128)(2,1)S(1)} %get-tuple-element.16.refs_4_.refs_3_), channel_id=1, source_target_pairs={{0,8},{8,0},{16,24},{24,16},{1,9},{9,1},{17,25},{25,17},{2,10},{10... | collective-permute-start | bytes 1572872 | tf_op jit(solution)/shard_map/ppermute | solution.py:291
  24.7 4.4 %collective-permute-start.8 = (bf16[192,128]{1,0:T(8,128)(2,1)S(1)}, bf16[192,128]{1,0:T(8,128)(2,1)S(1)}, u32[]{:S(2)}, u32[]{:S(2)}) collective-permute-start(bf16[192,128]{1,0:T(8,128)(2,1)S(1)} %get-tuple-element.17), channel_id=1, source_target_pairs={{0,16},{8,24},{16,0},{24,8},{1,17},{9,25},{17,1},{25,9},{2,18},{10... | collective-permute-start | bytes 147464 | tf_op jit(solution)/shard_map/ppermute | solution.py:291
  25.3 4.9 %copy-start.5 = (bf16[1,1,80,4096]{3,2,1,0:T(8,128)(2,1)S(1)}, bf16[1,1,80,4096]{3,2,1,0:T(8,128)(2,1)}, u32[]{:S(2)}) copy-start(bf16[1,1,80,4096]{3,2,1,0:T(8,128)(2,1)} %param.13) | copy-start | bytes 1966084
  25.3 4.9 %copy-start.7 = (bf16[1,64,4096]{2,1,0:T(8,128)(2,1)S(1)}, bf16[1,64,4096]{2,1,0:T(8,128)(2,1)}, u32[]{:S(2)}) copy-start(bf16[1,64,4096]{2,1,0:T(8,128)(2,1)} %param.12) | copy-start | bytes 1572868
  25.3 4.9 %copy-start.9 = (f32[160,128]{1,0:T(8,128)S(1)}, f32[160,128]{1,0:T(8,128)}, u32[]{:S(2)}) copy-start(f32[160,128]{1,0:T(8,128)} %copy-done.8) | copy-start | bytes 245764
  25.3 1.6 %collective-permute-start.10 = (bf16[96,128]{1,0:T(8,128)(2,1)S(1)}, bf16[96,128]{1,0:T(8,128)(2,1)S(1)}, u32[]{:S(2)}, u32[]{:S(2)}) collective-permute-start(bf16[96,128]{1,0:T(8,128)(2,1)S(1)} %get-tuple-element.18.refs_0_.refs_14_), channel_id=1, source_target_pairs={{0,8},{8,0},{16,24},{24,16},{1,9},{9,1},{17,25},{25,17},{2,10},{10... | collective-permute-start | bytes 73736 | tf_op jit(solution)/shard_map/ppermute | solution.py:291
  25.5 3.5 %collective-permute-start.9 = (bf16[96,128]{1,0:T(8,128)(2,1)S(1)}, bf16[96,128]{1,0:T(8,128)(2,1)S(1)}, u32[]{:S(2)}, u32[]{:S(2)}) collective-permute-start(bf16[96,128]{1,0:T(8,128)(2,1)S(1)} %get-tuple-element.18.refs_0_.refs_14_), channel_id=1, source_target_pairs={{0,24},{8,16},{16,8},{24,0},{1,25},{9,17},{17,9},{25,1},{2,26},{10... | collective-permute-start | bytes 73736 | tf_op jit(solution)/shard_map/ppermute | solution.py:291
  29.1 13.9 %collective-permute-start.11 = (bf16[64,4096]{1,0:T(8,128)(2,1)S(1)}, bf16[64,4096]{1,0:T(8,128)(2,1)S(1)}, u32[]{:S(2)}, u32[]{:S(2)}) collective-permute-start(bf16[64,4096]{1,0:T(8,128)(2,1)S(1)} %shard_map.114.refs_18_), channel_id=1, source_target_pairs={{0,16},{8,24},{16,0},{24,8},{1,17},{9,25},{17,1},{25,9},{2,18},{10... | collective-permute-start | bytes 1572872 | tf_op jit(solution)/shard_map/ppermute | solution.py:291
  43.1 3.9 %collective-permute-start.12 = (f32[16,512]{1,0:T(8,128)S(1)}, f32[16,512]{1,0:T(8,128)S(1)}, u32[]{:S(2)}, u32[]{:S(2)}) collective-permute-start(f32[16,512]{1,0:T(8,128)S(1)} %convert_reduce_fusion), channel_id=1, source_target_pairs={{0,16},{8,24},{16,0},{24,8},{1,17},{9,25},{17,1},{25,9},{2,18},{10... | collective-permute-start | bytes 98312 | tf_op jit(solution)/shard_map/ppermute | solution.py:291
  47.0 1.3 %collective-permute-start.13 = (f32[16,512]{1,0:T(8,128)S(1)}, f32[16,512]{1,0:T(8,128)S(1)}, u32[]{:S(2)}, u32[]{:S(2)}) collective-permute-start(f32[16,512]{1,0:T(8,128)S(1)} %add_multiply_fusion), channel_id=1, source_target_pairs={{0,8},{8,0},{16,24},{24,16},{1,9},{9,1},{17,25},{25,17},{2,10},{10... | collective-permute-start | bytes 98312 | tf_op jit(solution)/shard_map/ppermute | solution.py:291

commit v7 on v6

--- a/solution.py
+++ b/solution.py
@@ -61,11 +61,15 @@
     return rows[0:1] + rows[1:2] + rows[2:3]
 
 
-def packed(weights, top, share):
+def packed(weights, top, share, stats):
     block, rows = weights.shape[0] // 2, weights.shape[1]
-    stats = jnp.concatenate(terms_of(top) + terms_of(share) + [jnp.zeros((EXTRA - 6, rows), bf16)], 0)
+    lines = terms_of(top) + terms_of(share)
+    for at in (MAX, SUM, POSITIVE):
+        lines += terms_of(stats[at : at + 1])
+    lines.append(stats[HARD : HARD + 1].astype(bf16))
+    lines = jnp.concatenate(lines, 0)
     return jnp.concatenate(
-        [jnp.concatenate([weights[:block], weights[block:]], 1), jnp.concatenate([stats, stats], 1)], 0
+        [jnp.concatenate([weights[:block], weights[block:]], 1), jnp.concatenate([lines, lines], 1)], 0
     )
 
 
@@ -78,6 +82,12 @@
 def packet_stats(packet):
     at, rows = packet.shape[0] - EXTRA, packet.shape[1] // 2
     return whole(packet[at : at + 3, :rows]), whole(packet[at + 3 : at + 6, :rows])
+
+
+def sender_stats(packet):
+    at, rows = packet.shape[0] - EXTRA, packet.shape[1] // 2
+    three = [whole(packet[at + i : at + i + 3, :rows]) for i in (6, 9, 12)]
+    return three + [packet[at + 15 : at + 16, :rows].astype(f32)]
 
 
 def wide_rows(array):
@@ -121,6 +131,11 @@
     stats[HARD : HARD + 1] = hard[...].astype(f32)
 
 
+def copies_kernel(own, out):
+    for i in range(out.shape[0]):
+        out[i] = own[...]
+
+
 def adapter_kernel(maps, hq, hq_sib, hc, hc_sib, c_own, c_sib, q_own, q_sib, factors):
     shards, _, width = maps.shape
 
@@ -144,7 +159,7 @@
         factors[...] = product([q_own, q_sib, c_own, c_sib])
 
 
-def partner_kernel(c_own, c_sib, q, stats, factors, message, packet, q_again):
+def partner_kernel(c_own, c_sib, q, stats, own_stats, factors, message, packet, q_again):
     block, rows = c_own.shape[0], q.shape[0]
     c = jnp.concatenate([c_own[...], c_sib[...]], 0)
     q_again[...] = q[...]
@@ -156,7 +171,7 @@
     share = jnp.sum(jnp.exp(total - top), axis=0, keepdims=True)
     log_total = merge([(stats[MAX : MAX + 1], stats[SUM : SUM + 1]), (top, share)])
     hit = hits(owner, slot, stats[POSITIVE : POSITIVE + 1], rows)
-    here = packed((jnp.exp(total - log_total) - hit.astype(f32)).astype(bf16), top, share)
+    here = packed((jnp.exp(total - log_total) - hit.astype(f32)).astype(bf16), top, share, own_stats)
     packet[...] = here
     message[: here.shape[0]] = here
     message[here.shape[0] :] = factor_rows(factors[...], rows, block)
@@ -170,23 +185,31 @@
         share[:, at] = (dot(weights, c, 0, 0) * sharpness_factor).astype(bf16)
 
 
-def question_kernel(weights, c_own, c_sib, *rest):
-    shares, out = rest[:-1], rest[-1]
-    for i in range(out.shape[1] // STEP):
-        at = slice(i * STEP, (i + 1) * STEP)
-        c = jnp.concatenate([c_own[:, at], c_sib[:, at]], 0)
-        total = dot(weights[...], c, 0, 0) * sharpness_factor
-        for share in shares:
-            total = total + share[:, at].astype(f32)
-        out[:, at] = total.astype(bf16)
-
-
-def candidate_kernel(weights, *rest):
-    queries, out = rest[:-1], rest[-1]
-    for i in range(out.shape[1] // STEP):
-        at = slice(i * STEP, (i + 1) * STEP)
-        q = jnp.concatenate([r[:, at] for r in queries], 0)
-        out[:, at] = (dot(weights[...], q, 1, 0) * sharpness_factor).astype(bf16)
+def rows_kernel(partners, w_own, w_grad, c_own, c_sib, *refs):
+    queries, shares, (question, grad), here, (sems,) = taken(refs, 2 * partners + 2, partners, 2, 2, 1)
+    half = question.shape[1] // 2
+    out = []
+    for i, (target, rows) in enumerate(zip((question, grad), here)):
+        for j in range(2):
+            part = pl.ds(j * half, half)
+            out.append(pltpu.make_async_copy(rows.at[:, part], target.at[:, part], sems.at[2 * i + j]))
+    for j in range(2):
+        for start in range(j * half, (j + 1) * half, STEP):
+            at = slice(start, start + STEP)
+            c = jnp.concatenate([c_own[:, at], c_sib[:, at]], 0)
+            total = dot(w_own[...], c, 0, 0) * sharpness_factor
+            for share in shares:
+                total = total + share[:, at].astype(f32)
+            here[0][:, at] = total.astype(bf16)
+        out[j].start()
+    for j in range(2):
+        for start in range(j * half, (j + 1) * half, STEP):
+            at = slice(start, start + STEP)
+            q = jnp.concatenate([r[:, at] for r in queries], 0)
+            here[1][:, at] = (dot(w_grad[...], q, 1, 0) * sharpness_factor).astype(bf16)
+        out[2 + j].start()
+    for copy in out:
+        copy.wait()
 
 
 def taken(refs, *counts):
@@ -199,24 +222,24 @@
 
 def sums_kernel(partners, *refs):
     n = partners
-    (c, q, far_q, far_q_sib, hq, hc, stats, answers, sib_answers, made, made_sib, (factors, scores),
-     (w_grad, w_own, terms)) = taken(refs, 2, 2, n, n, 2, 2, 2, n, n, n, n, 2, 3)
+    (c, q, far_q, far_q_sib, hq, hc, (stats,), answers, sib_answers, made, made_sib, (factors, scores),
+     (w_grad, w_own, terms)) = taken(refs, 2, 2, n, n, 2, 2, 1, n, n, n, n, 2, 3)
     block, rows = c[0].shape[0], q[0].shape[0]
     shards, rank, width = terms.shape
     end = block + EXTRA
     far_factors = [factors_of(a[end:], block) for a in answers]
-    answers = [a[:end] for a in answers]
-
-    def both(at):
-        return jnp.concatenate([ref[at : at + 1] for ref in stats], 1)
-
-    def log_total(own, packets):
-        return merge([(own[MAX : MAX + 1], own[SUM : SUM + 1])] + [packet_stats(p) for p in packets])
+    answers, sib_answers = [[a[:end] for a in group] for group in (answers, sib_answers)]
+
+    own = [stats[at : at + 1] for at in (MAX, SUM, POSITIVE, HARD)]
+    sib = sender_stats(made_sib[0])
+
+    def log_total(chip, packets):
+        return merge([(chip[0], chip[1])] + [packet_stats(p) for p in packets])
 
     owner, slot = layout(lax.axis_index("dp"), block, scores.shape)
-    kept = allowed(owner, slot, both(HARD), rows)
-    hit = hits(owner, slot, both(POSITIVE), rows)
-    log_totals = jnp.concatenate([log_total(stats[0], answers), log_total(stats[1], sib_answers)], 1)
+    kept = allowed(owner, slot, jnp.concatenate([own[3], sib[3]], 1), rows)
+    hit = hits(owner, slot, jnp.concatenate([own[2], sib[2]], 1), rows)
+    log_totals = jnp.concatenate([log_total(own, answers), log_total(sib, sib_answers)], 1)
     near = jnp.exp(jnp.where(kept, scores[...] - log_totals, -jnp.inf)) - hit.astype(f32)
     near = near.astype(bf16)
     w_own[...] = near[:, :rows]
@@ -252,7 +275,7 @@
     def _():
         back_q = dot_wide(by_candidate, near, 1, 0)
         for far, mine, other in zip(far_factors, answers, sib_answers):
-            there = jnp.concatenate([unpacked(mine), unpacked(other[...], turned=True)], 1)
+            there = jnp.concatenate([unpacked(mine), unpacked(other, turned=True)], 1)
             back_q = back_q + dot_wide(far[1], there, 1, 0)
         back_q = (back_q * sharpness_factor).astype(bf16)
         back_c = (dot_wide(by_query, weights, 1, 1) * sharpness_factor).astype(bf16)
@@ -263,7 +286,7 @@
             terms[i] = (dot(back_q, from_q, 1, 0) + dot(back_c, from_c, 1, 0)).astype(bf16)
 
 
-def call(kernel, outs, needs=()):
+def call(kernel, outs, needs=(), cost=0, scratch=(), away=False):
     vmem = pl.BlockSpec(memory_space=pltpu.VMEM)
     anywhere = pl.BlockSpec(memory_space=pl.ANY)
 
@@ -275,9 +298,10 @@
             body,
             out_shape=outs,
             in_specs=[vmem] * len(args) + [anywhere] * len(needs),
-            out_specs=jax.tree.map(lambda _: vmem, outs),
+            out_specs=jax.tree.map(lambda _: anywhere if away else vmem, outs),
+            scratch_shapes=list(scratch),
             compiler_params=pltpu.CompilerParams(vmem_limit_bytes=16 * 2**20),
-            cost_estimate=pl.CostEstimate(flops=1000, bytes_accessed=1000, transcendentals=0),
+            cost_estimate=pl.CostEstimate(flops=1000 + cost, bytes_accessed=1000 + cost // 300, transcendentals=0),
         )(*args, *needs)
 
     return run
@@ -310,14 +334,15 @@
 
     far_q = [swap(q_own, "dp", k) for k in partners]
     c_sib, q_sib, hq_sib, hc_sib = (swap(a, "dp", 1) for a in (c_own, q_own, hq, hc))
-    scores, stats = call(scores_kernel, (shaped((2 * block, 2 * rows)), shaped((STATS, rows))), [hq_sib, hc_sib])(
+    mine = call(copies_kernel, shaped((shards, rank, shard_width), bf16), cost=5_000_000_000)(
+        jnp.where(even, adapter_down, adapter_up)
+    )
+    maps = lax.all_to_all(mine, "fsdp", 0, 0)
+
+    scores, stats = call(scores_kernel, (shaped((2 * block, 2 * rows)), shaped((STATS, rows))), [maps])(
         c_own, c_sib, q_own, q_sib, positives, hard_blocks
     )
     far_stats = [swap(stats, "dp", k) for k in partners]
-    sib_stats = swap(stats, "dp", 1)
-
-    mine = jnp.broadcast_to(jnp.where(even, adapter_down, adapter_up), (shards, rank, shard_width))
-    maps = lax.all_to_all(mine, "fsdp", 0, 0)
 
     factors = call(adapter_kernel, shaped((rank, 2 * rows + 2 * block)), [stats])(
         maps, hq, hq_sib, hc, hc_sib, c_own, c_sib, q_own, q_sib
@@ -331,16 +356,15 @@
                 shaped((block + EXTRA, 2 * rows), bf16),
                 shaped((rows, width), bf16),
             ),
-            [sib_stats],
-        )(c_own, c_sib, q, far, factors)
+        )(c_own, c_sib, q, far, stats, factors)
         answers.append(swap(message, "dp", k))
-        sib_answers.append(swap(packet, "dp", k ^ 1))
+        sib_answers.append(swap(answers[-1], "dp", 1))
         made.append(packet)
         made_sib.append(swap(packet, "dp", 1))
         far_q_near.append(q_again)
         far_q_sib.append(swap(q_again, "dp", 1))
         sent.append(call(share_kernel, shaped((rows, width), bf16), [made_sib[-1]])(packet, c_own, c_sib))
-        shares.append(swap(after(sent[-1], answers[-1], sib_answers[-1]), "dp", k))
+        shares.append(swap(after(sent[-1], answers[-1]), "dp", k))
     w_grad, w_own, terms = call(
         functools.partial(sums_kernel, len(partners)),
         (
@@ -350,23 +374,30 @@
         ),
         sent,
     )(
-        c_own, c_sib, q_own, q_sib, *far_q_near, *far_q_sib, hq, hq_sib, hc, hc_sib, stats, sib_stats,
+        c_own, c_sib, q_own, q_sib, *far_q_near, *far_q_sib, hq, hq_sib, hc, hc_sib, stats,
         *answers, *sib_answers, *made, *made_sib, factors, scores,
     )
     queries = [q_own, q_sib]
     for pair in zip(far_q_near, far_q_sib):
         queries += pair
-    grad = call(candidate_kernel, shaped((block, width), bf16))(w_grad, *queries)
-    question = call(question_kernel, shaped((rows, width), bf16))(w_own, c_own, c_sib, *shares)
+    kinds = [shaped((rows, width), bf16), shaped((block, width), bf16)]
+    question, grad = call(
+        functools.partial(rows_kernel, len(partners)),
+        kinds,
+        scratch=[pltpu.VMEM(kind.shape, bf16) for kind in kinds] + [pltpu.SemaphoreType.DMA((4,))],
+        away=True,
+    )(w_own, w_grad, c_own, c_sib, *queries, *shares)
 
     terms = lax.all_to_all(terms, "fsdp", 0, 0)
     terms = after(jnp.sum(terms.astype(f32), 0), *shares)
     apart = 2
-    while apart < devices:
-        terms = terms + after(swap(terms, "dp", apart), question, grad)
+    while 2 * apart < devices:
+        terms = terms + swap(terms, "dp", apart)
         apart *= 2
-    terms = terms * adapter_scale
-    others = swap(terms, "dp", 1)
+    got = [swap(terms, "dp", k) for k in (apart, apart ^ 1, 1)]
+    got[0] = after(got[0], question, grad)
+    others = (got[1] + got[2]) * adapter_scale
+    terms = (terms + got[0]) * adapter_scale
     return (
         question[None],
         grad[None, None],

time: 49.4 us -> 46.2 us (0.935)
  blocking collectives: 10.1 us -> 23.8 us
  starting transfers between devices: 15.3 us -> 7.85 us
  local copies, waits for them, and re-layouts: 5.58 us -> 0.05 us
  Pallas kernels: 7.78 us -> 4.86 us
  waiting for transfers between devices: 8.67 us -> 7.92 us
    all_to_all x0 -> x1, blocking collectives: none -> 13.9 us  [on_device(): maps = lax.all_to_all(mine, 'fsdp', 0, 0)]
    all_to_all x1 -> x0, starting transfers between devices: 5.97 us -> none  [on_device(): maps = lax.all_to_all(mine, 'fsdp', 0, 0)]
    unnamed x26 -> x14, local copies, waits for them, and re-layouts: 4.91 us -> 0.05 us
    all_to_all x1 -> x0, waiting for transfers between devices: 3.85 us -> none  [on_device(): maps = lax.all_to_all(mine, 'fsdp', 0, 0)]
    ppermute x14, waiting for transfers between devices: 4.82 us -> 7.92 us  [swap(): lax.ppermute(array, axis, [(i, i ^ apart) for i in range(lax.axis_size(ax...]
    pallas_call x7, Pallas kernels: 7.78 us -> 4.86 us  [run(): pl.pallas_call(body, out_shape=outs, in_specs=[vmem] * len(args) + [anywh...]
    ppermute x14, starting transfers between devices: 9.31 us -> 7.85 us  [swap(): lax.ppermute(array, axis, [(i, i ^ apart) for i in range(lax.axis_size(ax...]
    broadcast_in_dim x1 -> x0, local copies, waits for them, and re-layouts: 0.66 us -> none  [on_device(): jnp.broadcast_to(jnp.where(even, adapter_down, adapter_up), (shards, rank...]
  transfers between devices with their start and end apart: 15 -> 14, of which waited for: 6 -> 7; matrix products, arithmetic and copies ran while one was open for 1% -> 0% of each run, Pallas kernels for 12% -> 9%
where the time goes in v7:
time: 46.2 us; the launch traced here: 46 us
  blocking collectives  23.8 us (52%)
  waiting for transfers between devices  7.92 us (17%)
  starting transfers between devices  7.85 us (17%)
  Pallas kernels  4.86 us (11%)
  between operations  0.77 us (2%)
  other arithmetic  0.67 us (1%)
    all_to_all x1, blocking collectives, on_device(): maps = lax.all_to_all(mine, 'fsdp', 0, 0)  13.9 us
    all_to_all x1, blocking collectives, on_device(): terms = lax.all_to_all(terms, 'fsdp', 0, 0)  9.88 us
    ppermute x14, waiting for transfers between devices, swap(): lax.ppermute(array, axis, [(i, i ^ apart) for i in range(lax.axis_size(ax...  7.92 us
    ppermute x14, starting transfers between devices, swap(): lax.ppermute(array, axis, [(i, i ^ apart) for i in range(lax.axis_size(ax...  7.85 us
    pallas_call x7, Pallas kernels, run(): pl.pallas_call(body, out_shape=outs, in_specs=[vmem] * len(args) + [anywh...  4.86 us
  transfers between devices with their start and end apart: 14, of which 7 were waited for; matrix products, arithmetic and copies ran while one was open for 0% of the time, Pallas kernels for 9%

profile of v7, /device:TPU:0, one launch (start us, length us, event | category | flops | bytes accessed | tf_op | source)
XLA Modules:
  0.0 46.0 jit_solution(10685301654793204906)
XLA Ops:
  0.6 0.0 copy-start.6
  0.6 0.5 %collective-permute-start.1 = (bf16[64,4096]{1,0:T(8,128)(2,1)}, bf16[64,4096]{1,0:T(8,128)(2,1)S(1)}, u32[]{:S(2)}, u32[]{:S(2)}) collective-permute-start(bf16[64,4096]{1,0:T(8,128)(2,1)} %bitcast.13), channel_id=1, source_target_pairs={{0,8},{8,0},{16,24},{24,16},{1,9},{9,1},{17,25},{25,17},{2,10},{10... | collective-permute-start | bytes 1572872 | tf_op jit(solution)/shard_map/ppermute | solution.py:315
  1.2 2.6 %collective-permute-start.2 = (bf16[64,4096]{1,0:T(8,128)(2,1)}, bf16[64,4096]{1,0:T(8,128)(2,1)S(1)}, u32[]{:S(2)}, u32[]{:S(2)}) collective-permute-start(bf16[64,4096]{1,0:T(8,128)(2,1)} %bitcast.14), channel_id=1, source_target_pairs={{0,16},{8,24},{16,0},{24,8},{1,17},{9,25},{17,1},{25,9},{2,18},{10... | collective-permute-start | bytes 1572872 | tf_op jit(solution)/shard_map/ppermute | solution.py:315
  3.7 0.2 collective-permute-start
  3.9 0.3 collective-permute-start.4
  4.2 0.2 collective-permute-start.5
  4.4 0.0 copy-done.6
  4.4 0.0 copy-start
  4.4 0.0 copy-start.1
  4.5 0.0 copy-start.4
  4.5 0.0 copy-start.5
  4.5 13.9 %all_to_all.10.refs_6_.refs_0_ = bf16[8,16,512]{2,1,0:T(8,128)(2,1)S(1)} all-to-all(bf16[8,16,512]{2,1,0:T(8,128)(2,1)S(1)} %shard_map.111), channel_id=1, replica_groups=mesh['dp'=4,'fsdp'=8] {'fsdp'}, dimensions={0} | all-to-all | bytes 262144 | tf_op jit(solution)/shard_map/all_to_all | solution.py:340
  18.4 0.0 copy-start.2
  18.4 0.0 copy-start.3
  18.4 0.0 collective-permute-done.1.refs_3_.refs_8_.refs_5_
  18.4 0.0 collective-permute-done.refs_1_.refs_6_.refs_2_.refs_3_
  18.4 0.0 copy-done
  18.4 0.0 copy-done.1
  18.5 0.0 copy-done.4
  18.5 0.0 copy-done.5
  18.5 0.6 %shard_map.112 = (f32[160,128]{1,0:T(8,128)S(1)}, f32[8,64]{1,0:T(8,128)S(1)}) custom-call(bf16[80,4096]{1,0:T(8,128)(2,1)S(1)} %bitcast.7, bf16[80,4096]{1,0:T(8,128)(2,1)S(1)} %collective-permute-done.refs_1_.refs_6_.refs_2_.refs_3_, bf16[64,4096]{1,0:T(8,128)(2,1)S(1)} %bitcast.15, bf16[64,4096]{1,0:T(8,128)(2,1)S(1)} %collective-permute-done.1.refs_3_.refs_8_.refs_5_, ...), custom_call_target="tpu_custom_call" | custom-call | flops 1000 | bytes 1000 | tf_op jit(solution)/shard_map/pallas_call | solution.py:297
  19.0 0.6 %collective-permute-start.3 = (f32[8,64]{1,0:T(8,128)S(1)}, f32[8,64]{1,0:T(8,128)S(1)}, u32[]{:S(2)}, u32[]{:S(2)}) collective-permute-start(f32[8,64]{1,0:T(8,128)S(1)} %get-tuple-element.17.refs_9_.refs_4_.refs_10_), channel_id=1, source_target_pairs={{0,16},{8,24},{16,0},{24,8},{1,17},{9,25},{17,1},{25,9},{2,18},{10... | collective-permute-start | bytes 6152 | tf_op jit(solution)/shard_map/ppermute | solution.py:315
  19.6 0.0 collective-permute-done.4.refs_2_.refs_7_
  19.6 0.0 collective-permute-done.5.refs_4_.refs_9_
  19.6 0.0 copy-done.2
  19.6 0.0 copy-done.3
  19.7 0.8 %shard_map.113.refs_5_.refs_15_ = f32[16,288]{1,0:T(8,128)S(1)} custom-call(bf16[8,16,512]{2,1,0:T(8,128)(2,1)S(1)} %all_to_all.10.refs_6_.refs_0_, bf16[64,4096]{1,0:T(8,128)(2,1)S(1)} %bitcast.23, bf16[64,4096]{1,0:T(8,128)(2,1)S(1)} %collective-permute-done.4.refs_2_.refs_7_, bf16[80,4096]{1,0:T(8,128)(2,1)S(1)} %bitcast.20, ...), custom_call_target="tpu_custom_call" | custom-call | flops 1000 | bytes 1000 | tf_op jit(solution)/shard_map/pallas_call | solution.py:297
  20.5 0.0 collective-permute-done.2.refs_2_
  20.5 2.2 %collective-permute-done.3.refs_3_ = f32[8,64]{1,0:T(8,128)S(1)} collective-permute-done((f32[8,64]{1,0:T(8,128)S(1)}, f32[8,64]{1,0:T(8,128)S(1)}, u32[]{:S(2)}, u32[]{:S(2)}) %collective-permute-start.3) | collective-permute-done | bytes 2080 | tf_op jit(solution)/shard_map/ppermute | solution.py:315
  22.7 0.6 %shard_map.114 = (bf16[192,128]{1,0:T(8,128)(2,1)S(1)}, bf16[96,128]{1,0:T(8,128)(2,1)S(1)}, bf16[64,4096]{1,0:T(8,128)(2,1)S(1)}) custom-call(bf16[80,4096]{1,0:T(8,128)(2,1)S(1)} %bitcast.9, bf16[80,4096]{1,0:T(8,128)(2,1)S(1)} %collective-permute-done.refs_1_.refs_6_.refs_2_.refs_3_, bf16[64,4096]{1,0:T(8,128)(2,1)S(1)} %collective-permute-done.2.refs_2_, ...), custom_call_target="tpu_custom_call" | custom-call | flops 1000 | bytes 1000 | tf_op jit(solution)/shard_map/pallas_call | solution.py:297
  23.4 0.0 collective-permute-start.6
  23.4 0.6 %collective-permute-start.7 = (bf16[192,128]{1,0:T(8,128)(2,1)S(1)}, bf16[192,128]{1,0:T(8,128)(2,1)S(1)}, u32[]{:S(2)}, u32[]{:S(2)}) collective-permute-start(bf16[192,128]{1,0:T(8,128)(2,1)S(1)} %get-tuple-element.19), channel_id=1, source_target_pairs={{0,16},{8,24},{16,0},{24,8},{1,17},{9,25},{17,1},{25,9},{2,18},{10... | collective-permute-start | bytes 147464 | tf_op jit(solution)/shard_map/ppermute | solution.py:315
  24.0 0.2 collective-permute-start.9
  24.2 1.2 %collective-permute-done.9.refs_3_.refs_14_ = bf16[96,128]{1,0:T(8,128)(2,1)S(1)} collective-permute-done((bf16[96,128]{1,0:T(8,128)(2,1)S(1)}, bf16[96,128]{1,0:T(8,128)(2,1)S(1)}, u32[]{:S(2)}, u32[]{:S(2)}) %collective-permute-start.9) | collective-permute-done | bytes 24608 | tf_op jit(solution)/shard_map/ppermute | solution.py:315
  25.3 0.4 shard_map.115.refs_17_
  25.8 1.8 %collective-permute-done.7.refs_11_ = bf16[192,128]{1,0:T(8,128)(2,1)S(1)} collective-permute-done((bf16[192,128]{1,0:T(8,128)(2,1)S(1)}, bf16[192,128]{1,0:T(8,128)(2,1)S(1)}, u32[]{:S(2)}, u32[]{:S(2)}) %collective-permute-start.7) | collective-permute-done | bytes 49184 | tf_op jit(solution)/shard_map/ppermute | solution.py:315
  27.6 0.5 %collective-permute-start.10 = (bf16[64,4096]{1,0:T(8,128)(2,1)S(1)}, bf16[64,4096]{1,0:T(8,128)(2,1)S(1)}, u32[]{:S(2)}, u32[]{:S(2)}) collective-permute-start(bf16[64,4096]{1,0:T(8,128)(2,1)S(1)} %shard_map.115.refs_17_), channel_id=1, source_target_pairs={{0,16},{8,24},{16,0},{24,8},{1,17},{9,25},{17,1},{25,9},{2,18},{10... | collective-permute-start | bytes 1572872 | tf_op jit(solution)/shard_map/ppermute | solution.py:315
  28.1 0.0 collective-permute-start.8
  28.1 1.2 %collective-permute-done.8.refs_12_ = bf16[192,128]{1,0:T(8,128)(2,1)S(1)} collective-permute-done((bf16[192,128]{1,0:T(8,128)(2,1)S(1)}, bf16[192,128]{1,0:T(8,128)(2,1)S(1)}, u32[]{:S(2)}, u32[]{:S(2)}) %collective-permute-start.8) | collective-permute-done | bytes 49184 | tf_op jit(solution)/shard_map/ppermute | solution.py:315
  29.3 0.0 collective-permute-done.6.refs_5_.refs_7_
  29.3 0.9 %shard_map.116 = (bf16[80,256]{1,0:T(8,128)(2,1)S(1)}, bf16[160,64]{1,0:T(8,128)(2,1)S(1)}, bf16[8,16,512]{2,1,0:T(8,128)(2,1)S(1)}) custom-call(bf16[80,4096]{1,0:T(8,128)(2,1)S(1)} %bitcast.11, bf16[80,4096]{1,0:T(8,128)(2,1)S(1)} %collective-permute-done.refs_1_.refs_6_.refs_2_.refs_3_, bf16[64,4096]{1,0:T(8,128)(2,1)S(1)} %bitcast.17, ...), custom_call_target="tpu_custom_call" | custom-call | flops 1000 | bytes 1000 | tf_op jit(solution)/shard_map/pallas_call | solution.py:297
  30.2 9.9 %all_to_all.11 = bf16[8,16,512]{2,1,0:T(8,128)(2,1)S(1)} all-to-all(bf16[8,16,512]{2,1,0:T(8,128)(2,1)S(1)} %get-tuple-element.27), channel_id=1, replica_groups=mesh['dp'=4,'fsdp'=8] {'fsdp'}, dimensions={0} | all-to-all | bytes 262144 | tf_op jit(solution)/shard_map/all_to_all | solution.py:391
  40.1 0.6 %collective-permute-done.10.refs_8_ = bf16[64,4096]{1,0:T(8,128)(2,1)S(1)} collective-permute-done((bf16[64,4096]{1,0:T(8,128)(2,1)S(1)}, bf16[64,4096]{1,0:T(8,128)(2,1)S(1)}, u32[]{:S(2)}, u32[]{:S(2)}) %collective-permute-start.10) | collective-permute-done | bytes 524320 | tf_op jit(solution)/shard_map/ppermute | solution.py:315
  40.7 1.0 %collective-permute-start.13 = (f32[16,512]{1,0:T(8,128)S(1)}, f32[16,512]{1,0:T(8,128)S(1)}, u32[]{:S(2)}, u32[]{:S(2)}) collective-permute-start(f32[16,512]{1,0:T(8,128)S(1)} %convert_reduce_fusion), channel_id=1, source_target_pairs={{0,16},{8,24},{16,0},{24,8},{1,17},{9,25},{17,1},{25,9},{2,18},{10... | collective-permute-start | bytes 98312 | tf_op jit(solution)/shard_map/ppermute | solution.py:315
  41.7 0.0 collective-permute-start.11
  41.7 1.1 %collective-permute-start.12 = (f32[16,512]{1,0:T(8,128)S(1)}, f32[16,512]{1,0:T(8,128)S(1)}, u32[]{:S(2)}, u32[]{:S(2)}) collective-permute-start(f32[16,512]{1,0:T(8,128)S(1)} %convert_reduce_fusion), channel_id=1, source_target_pairs={{0,8},{8,0},{16,24},{24,16},{1,9},{9,1},{17,25},{25,17},{2,10},{10... | collective-permute-start | bytes 98312 | tf_op jit(solution)/shard_map/ppermute | solution.py:315
  42.8 1.5 %shard_map.117 = (bf16[64,4096]{1,0:T(8,128)(2,1)}, bf16[80,4096]{1,0:T(8,128)(2,1)}) custom-call(bf16[160,64]{1,0:T(8,128)(2,1)S(1)} %get-tuple-element.22.refs_0_, bf16[80,256]{1,0:T(8,128)(2,1)S(1)} %get-tuple-element.23.refs_1_, bf16[80,4096]{1,0:T(8,128)(2,1)S(1)} %bitcast.12, bf16[80,4096]{1,0:T(8,128)(2,1)S(1)} %collective-permute-done.refs_1_.refs_6_.refs_2_.refs_3_, ...), custom_call_target="tpu_custom_call" | custom-call | flops 1000 | bytes 1000 | tf_op jit(solution)/shard_map/pallas_call | solution.py:297
  44.4 0.2 collective-permute-done.13
  44.6 0.7 %collective-permute-done.11 = f32[16,512]{1,0:T(8,128)S(1)} collective-permute-done((f32[16,512]{1,0:T(8,128)S(1)}, f32[16,512]{1,0:T(8,128)S(1)}, u32[]{:S(2)}, u32[]{:S(2)}) %collective-permute-start.11) | collective-permute-done | bytes 32800 | tf_op jit(solution)/shard_map/ppermute | solution.py:315
  45.3 0.0 collective-permute-done.12
  45.3 0.6 %broadcast_select_fusion = (f32[16,512]{1,0:T(8,128)}, f32[16,512]{1,0:T(8,128)}) fusion(pred[]{:T(512)S(6)} %eq.3, f32[16,512]{1,0:T(8,128)S(1)} %collective-permute-done.11, f32[16,512]{1,0:T(8,128)S(1)} %collective-permute-done.12, f32[16,512]{1,0:T(8,128)S(1)} %convert_reduce_fusion, f32[16,512]{1,0:T(8,128)S(1)} %collective-permute-done.13), kind=kLoop, calls=%fused_computation.3 | loop fusion | flops 49152 | bytes 196609 | tf_op jit(solution)/shard_map/jit(_where)/select_n | solution.py:405
  (3 shorter events, 0.0 us)
Async XLA Ops:
  0.6 3.8 %copy-start.6 = (bf16[16,512]{1,0:T(8,128)(2,1)S(1)}, bf16[16,512]{1,0:T(8,128)(2,1)}, u32[]{:S(2)}) copy-start(bf16[16,512]{1,0:T(8,128)(2,1)} %param.14) | copy-start | bytes 49156
  0.6 17.8 %collective-permute-start.1 = (bf16[64,4096]{1,0:T(8,128)(2,1)}, bf16[64,4096]{1,0:T(8,128)(2,1)S(1)}, u32[]{:S(2)}, u32[]{:S(2)}) collective-permute-start(bf16[64,4096]{1,0:T(8,128)(2,1)} %bitcast.13), channel_id=1, source_target_pairs={{0,8},{8,0},{16,24},{24,16},{1,9},{9,1},{17,25},{25,17},{2,10},{10... | collective-permute-start | bytes 1572872 | tf_op jit(solution)/shard_map/ppermute | solution.py:315
  1.2 19.3 %collective-permute-start.2 = (bf16[64,4096]{1,0:T(8,128)(2,1)}, bf16[64,4096]{1,0:T(8,128)(2,1)S(1)}, u32[]{:S(2)}, u32[]{:S(2)}) collective-permute-start(bf16[64,4096]{1,0:T(8,128)(2,1)} %bitcast.14), channel_id=1, source_target_pairs={{0,16},{8,24},{16,0},{24,8},{1,17},{9,25},{17,1},{25,9},{2,18},{10... | collective-permute-start | bytes 1572872 | tf_op jit(solution)/shard_map/ppermute | solution.py:315
  3.7 14.7 %collective-permute-start = (bf16[80,4096]{1,0:T(8,128)(2,1)}, bf16[80,4096]{1,0:T(8,128)(2,1)S(1)}, u32[]{:S(2)}, u32[]{:S(2)}) collective-permute-start(bf16[80,4096]{1,0:T(8,128)(2,1)} %bitcast.6), channel_id=1, source_target_pairs={{0,8},{8,0},{16,24},{24,16},{1,9},{9,1},{17,25},{25,17},{2,10},{10... | collective-permute-start | bytes 1966088 | tf_op jit(solution)/shard_map/ppermute | solution.py:315
  3.9 15.7 %collective-permute-start.4 = (bf16[64,4096]{1,0:T(8,128)(2,1)}, bf16[64,4096]{1,0:T(8,128)(2,1)S(1)}, u32[]{:S(2)}, u32[]{:S(2)}) collective-permute-start(bf16[64,4096]{1,0:T(8,128)(2,1)} %bitcast.22), channel_id=1, source_target_pairs={{0,8},{8,0},{16,24},{24,16},{1,9},{9,1},{17,25},{25,17},{2,10},{10... | collective-permute-start | bytes 1572872 | tf_op jit(solution)/shard_map/ppermute | solution.py:315
  4.2 15.4 %collective-permute-start.5 = (bf16[80,4096]{1,0:T(8,128)(2,1)}, bf16[80,4096]{1,0:T(8,128)(2,1)S(1)}, u32[]{:S(2)}, u32[]{:S(2)}) collective-permute-start(bf16[80,4096]{1,0:T(8,128)(2,1)} %bitcast.19), channel_id=1, source_target_pairs={{0,8},{8,0},{16,24},{24,16},{1,9},{9,1},{17,25},{25,17},{2,10},{10... | collective-permute-start | bytes 1966088 | tf_op jit(solution)/shard_map/ppermute | solution.py:315
  4.4 14.0 %copy-start = (bf16[1,1,80,4096]{3,2,1,0:T(8,128)(2,1)S(1)}, bf16[1,1,80,4096]{3,2,1,0:T(8,128)(2,1)}, u32[]{:S(2)}) copy-start(bf16[1,1,80,4096]{3,2,1,0:T(8,128)(2,1)} %param.9) | copy-start | bytes 1966084
  4.4 14.0 %copy-start.1 = (bf16[1,64,4096]{2,1,0:T(8,128)(2,1)S(1)}, bf16[1,64,4096]{2,1,0:T(8,128)(2,1)}, u32[]{:S(2)}) copy-start(bf16[1,64,4096]{2,1,0:T(8,128)(2,1)} %param.8) | copy-start | bytes 1572868
  4.5 14.0 %copy-start.4 = (s32[1,64]{1,0:T(1,128)S(1)}, s32[1,64]{1,0:T(1,128)}, u32[]{:S(2)}) copy-start(s32[1,64]{1,0:T(1,128)} %refs_4_.1) | copy-start | bytes 772
  4.5 14.0 %copy-start.5 = (s32[1,64]{1,0:T(1,128)S(1)}, s32[1,64]{1,0:T(1,128)}, u32[]{:S(2)}) copy-start(s32[1,64]{1,0:T(1,128)} %refs_5_.1) | copy-start | bytes 772
  18.4 1.2 %copy-start.2 = (bf16[1,1,80,4096]{3,2,1,0:T(8,128)(2,1)S(1)}, bf16[1,1,80,4096]{3,2,1,0:T(8,128)(2,1)}, u32[]{:S(2)}) copy-start(bf16[1,1,80,4096]{3,2,1,0:T(8,128)(2,1)} %param.13) | copy-start | bytes 1966084
  18.4 1.2 %copy-start.3 = (bf16[1,64,4096]{2,1,0:T(8,128)(2,1)S(1)}, bf16[1,64,4096]{2,1,0:T(8,128)(2,1)}, u32[]{:S(2)}) copy-start(bf16[1,64,4096]{2,1,0:T(8,128)(2,1)} %param.12) | copy-start | bytes 1572868
  19.0 3.7 %collective-permute-start.3 = (f32[8,64]{1,0:T(8,128)S(1)}, f32[8,64]{1,0:T(8,128)S(1)}, u32[]{:S(2)}, u32[]{:S(2)}) collective-permute-start(f32[8,64]{1,0:T(8,128)S(1)} %get-tuple-element.17.refs_9_.refs_4_.refs_10_), channel_id=1, source_target_pairs={{0,16},{8,24},{16,0},{24,8},{1,17},{9,25},{17,1},{25,9},{2,18},{10... | collective-permute-start | bytes 6152 | tf_op jit(solution)/shard_map/ppermute | solution.py:315
  23.4 6.0 %collective-permute-start.6 = (bf16[64,4096]{1,0:T(8,128)(2,1)S(1)}, bf16[64,4096]{1,0:T(8,128)(2,1)S(1)}, u32[]{:S(2)}, u32[]{:S(2)}) collective-permute-start(bf16[64,4096]{1,0:T(8,128)(2,1)S(1)} %get-tuple-element.18.refs_4_.refs_6_), channel_id=1, source_target_pairs={{0,8},{8,0},{16,24},{24,16},{1,9},{9,1},{17,25},{25,17},{2,10},{10... | collective-permute-start | bytes 1572872 | tf_op jit(solution)/shard_map/ppermute | solution.py:315
  23.4 4.2 %collective-permute-start.7 = (bf16[192,128]{1,0:T(8,128)(2,1)S(1)}, bf16[192,128]{1,0:T(8,128)(2,1)S(1)}, u32[]{:S(2)}, u32[]{:S(2)}) collective-permute-start(bf16[192,128]{1,0:T(8,128)(2,1)S(1)} %get-tuple-element.19), channel_id=1, source_target_pairs={{0,16},{8,24},{16,0},{24,8},{1,17},{9,25},{17,1},{25,9},{2,18},{10... | collective-permute-start | bytes 147464 | tf_op jit(solution)/shard_map/ppermute | solution.py:315
  24.0 1.3 %collective-permute-start.9 = (bf16[96,128]{1,0:T(8,128)(2,1)S(1)}, bf16[96,128]{1,0:T(8,128)(2,1)S(1)}, u32[]{:S(2)}, u32[]{:S(2)}) collective-permute-start(bf16[96,128]{1,0:T(8,128)(2,1)S(1)} %get-tuple-element.20.refs_0_.refs_13_), channel_id=1, source_target_pairs={{0,8},{8,0},{16,24},{24,16},{1,9},{9,1},{17,25},{25,17},{2,10},{10... | collective-permute-start | bytes 73736 | tf_op jit(solution)/shard_map/ppermute | solution.py:315
  27.6 13.1 %collective-permute-start.10 = (bf16[64,4096]{1,0:T(8,128)(2,1)S(1)}, bf16[64,4096]{1,0:T(8,128)(2,1)S(1)}, u32[]{:S(2)}, u32[]{:S(2)}) collective-permute-start(bf16[64,4096]{1,0:T(8,128)(2,1)S(1)} %shard_map.115.refs_17_), channel_id=1, source_target_pairs={{0,16},{8,24},{16,0},{24,8},{1,17},{9,25},{17,1},{25,9},{2,18},{10... | collective-permute-start | bytes 1572872 | tf_op jit(solution)/shard_map/ppermute | solution.py:315
  28.1 1.2 %collective-permute-start.8 = (bf16[192,128]{1,0:T(8,128)(2,1)S(1)}, bf16[192,128]{1,0:T(8,128)(2,1)S(1)}, u32[]{:S(2)}, u32[]{:S(2)}) collective-permute-start(bf16[192,128]{1,0:T(8,128)(2,1)S(1)} %collective-permute-done.7.refs_11_), channel_id=1, source_target_pairs={{0,8},{8,0},{16,24},{24,16},{1,9},{9,1},{17,25},{25,17},{2,10},{10... | collective-permute-start | bytes 147464 | tf_op jit(solution)/shard_map/ppermute | solution.py:315
  40.7 3.9 %collective-permute-start.13 = (f32[16,512]{1,0:T(8,128)S(1)}, f32[16,512]{1,0:T(8,128)S(1)}, u32[]{:S(2)}, u32[]{:S(2)}) collective-permute-start(f32[16,512]{1,0:T(8,128)S(1)} %convert_reduce_fusion), channel_id=1, source_target_pairs={{0,16},{8,24},{16,0},{24,8},{1,17},{9,25},{17,1},{25,9},{2,18},{10... | collective-permute-start | bytes 98312 | tf_op jit(solution)/shard_map/ppermute | solution.py:315
  41.7 3.6 %collective-permute-start.11 = (f32[16,512]{1,0:T(8,128)S(1)}, f32[16,512]{1,0:T(8,128)S(1)}, u32[]{:S(2)}, u32[]{:S(2)}) collective-permute-start(f32[16,512]{1,0:T(8,128)S(1)} %convert_reduce_fusion), channel_id=1, source_target_pairs={{0,24},{8,16},{16,8},{24,0},{1,25},{9,17},{17,9},{25,1},{2,26},{10... | collective-permute-start | bytes 98312 | tf_op jit(solution)/shard_map/ppermute | solution.py:315
  41.7 3.6 %collective-permute-start.12 = (f32[16,512]{1,0:T(8,128)S(1)}, f32[16,512]{1,0:T(8,128)S(1)}, u32[]{:S(2)}, u32[]{:S(2)}) collective-permute-start(f32[16,512]{1,0:T(8,128)S(1)} %convert_reduce_fusion), channel_id=1, source_target_pairs={{0,8},{8,0},{16,24},{24,16},{1,9},{9,1},{17,25},{25,17},{2,10},{10... | collective-permute-start | bytes 98312 | tf_op jit(solution)/shard_map/ppermute | solution.py:315

commit v8 on v7

--- a/solution.py
+++ b/solution.py
@@ -12,6 +12,7 @@
 STEP = 512
 MAX, SUM, POSITIVE, HARD, STATS = 0, 1, 2, 3, 8
 EXTRA = 16
+SEGMENTS = 32
 
 f32 = jnp.float32
 bf16 = jnp.bfloat16
@@ -61,33 +62,51 @@
     return rows[0:1] + rows[1:2] + rows[2:3]
 
 
-def packed(weights, top, share, stats):
-    block, rows = weights.shape[0] // 2, weights.shape[1]
-    lines = terms_of(top) + terms_of(share)
+def packed(weights, stats):
+    lines = []
     for at in (MAX, SUM, POSITIVE):
         lines += terms_of(stats[at : at + 1])
     lines.append(stats[HARD : HARD + 1].astype(bf16))
+    lines.append(jnp.zeros((EXTRA - len(lines), weights.shape[1]), bf16))
     lines = jnp.concatenate(lines, 0)
-    return jnp.concatenate(
-        [jnp.concatenate([weights[:block], weights[block:]], 1), jnp.concatenate([lines, lines], 1)], 0
-    )
+    return jnp.concatenate([side_by_side(weights), jnp.concatenate([lines, lines], 1)], 0)
+
+
+def side_by_side(rows):
+    block = rows.shape[0] // 2
+    return jnp.concatenate([rows[:block], rows[block:]], 1)
+
+
+def stacked(rows, turned=False):
+    half = rows.shape[1] // 2
+    halves = rows[:, :half], rows[:, half:]
+    return jnp.concatenate(halves[::-1] if turned else halves, 0)
 
 
 def unpacked(packet, turned=False):
-    block, rows = packet.shape[0] - EXTRA, packet.shape[1] // 2
-    halves = packet[:block, :rows], packet[:block, rows:]
-    return jnp.concatenate(halves[::-1] if turned else halves, 0)
-
-
-def packet_stats(packet):
-    at, rows = packet.shape[0] - EXTRA, packet.shape[1] // 2
-    return whole(packet[at : at + 3, :rows]), whole(packet[at + 3 : at + 6, :rows])
+    return stacked(packet[: packet.shape[0] - EXTRA], turned)
+
+
+def message_of(shares, pairs, factors, rows, block):
+    high, low = wide_rows(shares)
+    lines = [term for pair in pairs for value in pair for term in terms_of(value)]
+    lines = jnp.concatenate(lines + [jnp.zeros((SEGMENTS - len(lines), rows), bf16)], 0)
+    parts = [side_by_side(high), side_by_side(low), jnp.concatenate([lines, lines], 1)]
+    return jnp.concatenate(parts + [factor_rows(factors, rows, block)], 0)
+
+
+def message_parts(message, block, turned=False):
+    high, low = (stacked(message[i * block : (i + 1) * block], turned).astype(f32) for i in (0, 1))
+    at, rows = 2 * block, message.shape[1] // 2
+    values = [whole(message[at + 3 * i : at + 3 * i + 3, :rows]) for i in range(6)]
+    pairs = list(zip(values[::2], values[1::2]))
+    return high + low, pairs[:1] + (pairs[:0:-1] if turned else pairs[1:]), message[at + SEGMENTS :]
 
 
 def sender_stats(packet):
     at, rows = packet.shape[0] - EXTRA, packet.shape[1] // 2
-    three = [whole(packet[at + i : at + i + 3, :rows]) for i in (6, 9, 12)]
-    return three + [packet[at + 15 : at + 16, :rows].astype(f32)]
+    three = [whole(packet[at + i : at + i + 3, :rows]) for i in (0, 3, 6)]
+    return three + [packet[at + 9 : at + 10, :rows].astype(f32)]
 
 
 def wide_rows(array):
@@ -159,26 +178,30 @@
         factors[...] = product([q_own, q_sib, c_own, c_sib])
 
 
-def partner_kernel(c_own, c_sib, q, stats, own_stats, factors, message, packet, q_again):
+def partner_kernel(c_own, c_sib, q, factors, message, scores, q_again):
     block, rows = c_own.shape[0], q.shape[0]
     c = jnp.concatenate([c_own[...], c_sib[...]], 0)
     q_again[...] = q[...]
-    total = dot(c, q[...], 1, 1)
-    owner, slot = layout(lax.axis_index("dp"), block, total.shape)
-    keep = allowed(owner, slot, stats[HARD : HARD + 1], rows)
-    total = jnp.where(keep, total * sharpness_factor, -jnp.inf)
+    total = dot(c, q[...], 1, 1) * sharpness_factor
+    scores[...] = total
+    owner, slot = layout(0, block, total.shape)
+    parts = [slot < rows, (slot >= rows) & (owner == 0), (slot >= rows) & (owner == 1)]
+    tops = [jnp.max(jnp.where(part, total, -jnp.inf), axis=0, keepdims=True) for part in parts]
+    shares = jnp.exp(total - jnp.where(parts[0], tops[0], jnp.where(parts[1], tops[1], tops[2])))
+    sums = [jnp.sum(jnp.where(part, shares, 0.0), axis=0, keepdims=True) for part in parts]
+    message[...] = message_of(shares, list(zip(tops, sums)), factors[...], rows, block)
+
+
+def share_kernel(scores, stats, own_stats, c_own, c_sib, packet, share):
+    block, rows = c_own.shape[0], scores.shape[1]
+    owner, slot = layout(lax.axis_index("dp"), block, scores.shape)
+    total = jnp.where(allowed(owner, slot, stats[HARD : HARD + 1], rows), scores[...], -jnp.inf)
     top = jnp.max(total, axis=0, keepdims=True)
-    share = jnp.sum(jnp.exp(total - top), axis=0, keepdims=True)
-    log_total = merge([(stats[MAX : MAX + 1], stats[SUM : SUM + 1]), (top, share)])
+    here = jnp.sum(jnp.exp(total - top), axis=0, keepdims=True)
+    log_total = merge([(stats[MAX : MAX + 1], stats[SUM : SUM + 1]), (top, here)])
     hit = hits(owner, slot, stats[POSITIVE : POSITIVE + 1], rows)
-    here = packed((jnp.exp(total - log_total) - hit.astype(f32)).astype(bf16), top, share, own_stats)
-    packet[...] = here
-    message[: here.shape[0]] = here
-    message[here.shape[0] :] = factor_rows(factors[...], rows, block)
-
-
-def share_kernel(packet, c_own, c_sib, share):
-    weights = unpacked(packet[...])
+    weights = (jnp.exp(total - log_total) - hit.astype(f32)).astype(bf16)
+    packet[...] = packed(weights, own_stats)
     for i in range(share.shape[1] // STEP):
         at = slice(i * STEP, (i + 1) * STEP)
         c = jnp.concatenate([c_own[:, at], c_sib[:, at]], 0)
@@ -226,19 +249,30 @@
      (w_grad, w_own, terms)) = taken(refs, 2, 2, n, n, 2, 2, 1, n, n, n, n, 2, 3)
     block, rows = c[0].shape[0], q[0].shape[0]
     shards, rank, width = terms.shape
-    end = block + EXTRA
-    far_factors = [factors_of(a[end:], block) for a in answers]
-    answers, sib_answers = [[a[:end] for a in group] for group in (answers, sib_answers)]
+    position = lax.axis_index("dp")
+    answers = [message_parts(a, block) for a in answers]
+    sib_answers = [message_parts(a, block, turned=True) for a in sib_answers]
+    far_factors = [factors_of(rest, block) for _, _, rest in answers]
 
     own = [stats[at : at + 1] for at in (MAX, SUM, POSITIVE, HARD)]
     sib = sender_stats(made_sib[0])
 
-    def log_total(chip, packets):
-        return merge([(chip[0], chip[1])] + [packet_stats(p) for p in packets])
-
-    owner, slot = layout(lax.axis_index("dp"), block, scores.shape)
-    kept = allowed(owner, slot, jnp.concatenate([own[3], sib[3]], 1), rows)
-    hit = hits(owner, slot, jnp.concatenate([own[2], sib[2]], 1), rows)
+    def kept_pairs(i, pairs, hard):
+        first = position ^ (2 * i + 2)
+        out = [pairs[0]]
+        for (top, total), at in zip(pairs[1:], (first, first ^ 1)):
+            counts = hard.astype(jnp.int32) == at
+            out.append((jnp.where(counts, top, pairs[0][0]), jnp.where(counts, total, 0.0)))
+        return out
+
+    def log_total(chip, parts):
+        return merge([(chip[0], chip[1])] + [p for i, part in enumerate(parts) for p in kept_pairs(i, part[1], chip[3])])
+
+    owner, slot = layout(position, block, scores.shape)
+    hard = jnp.concatenate([own[3], sib[3]], 1)
+    kept = allowed(owner, slot, hard, rows)
+    positive = jnp.concatenate([own[2], sib[2]], 1)
+    hit = hits(owner, slot, positive, rows)
     log_totals = jnp.concatenate([log_total(own, answers), log_total(sib, sib_answers)], 1)
     near = jnp.exp(jnp.where(kept, scores[...] - log_totals, -jnp.inf)) - hit.astype(f32)
     near = near.astype(bf16)
@@ -274,9 +308,16 @@
     @pl.when(core == 1)
     def _():
         back_q = dot_wide(by_candidate, near, 1, 0)
-        for far, mine, other in zip(far_factors, answers, sib_answers):
-            there = jnp.concatenate([unpacked(mine), unpacked(other, turned=True)], 1)
-            back_q = back_q + dot_wide(far[1], there, 1, 0)
+        for i in range(n):
+            first = position ^ (2 * i + 2)
+            owner, slot = layout(first, block, scores.shape)
+            kept = allowed(owner, slot, hard, rows)
+            shares = jnp.concatenate([answers[i][0], sib_answers[i][0]], 1)
+            tops = [jnp.concatenate([a[0], b[0]], 1) for a, b in zip(answers[i][1], sib_answers[i][1])]
+            top = jnp.where(slot < rows, tops[0], jnp.where(owner == first, tops[1], tops[2]))
+            there = shares * jnp.exp(jnp.where(kept, top - log_totals, -jnp.inf))
+            there = there - hits(owner, slot, positive, rows).astype(f32)
+            back_q = back_q + dot_wide(far_factors[i][1], there.astype(bf16), 1, 0)
         back_q = (back_q * sharpness_factor).astype(bf16)
         back_c = (dot_wide(by_query, weights, 1, 1) * sharpness_factor).astype(bf16)
         for i in range(shards):
@@ -286,23 +327,23 @@
             terms[i] = (dot(back_q, from_q, 1, 0) + dot(back_c, from_c, 1, 0)).astype(bf16)
 
 
-def call(kernel, outs, needs=(), cost=0, scratch=(), away=False):
+def call(kernel, outs, needs=(), cost=0, scratch=(), away=False, keeps=()):
     vmem = pl.BlockSpec(memory_space=pltpu.VMEM)
     anywhere = pl.BlockSpec(memory_space=pl.ANY)
 
     def run(*args):
         def body(*refs):
-            kernel(*refs[: len(args)], *refs[len(args) + len(needs) :])
+            kernel(*refs[: len(args)], *refs[len(args) + len(keeps) + len(needs) :])
 
         return pl.pallas_call(
             body,
             out_shape=outs,
-            in_specs=[vmem] * len(args) + [anywhere] * len(needs),
+            in_specs=[vmem] * (len(args) + len(keeps)) + [anywhere] * len(needs),
             out_specs=jax.tree.map(lambda _: anywhere if away else vmem, outs),
             scratch_shapes=list(scratch),
             compiler_params=pltpu.CompilerParams(vmem_limit_bytes=16 * 2**20),
             cost_estimate=pl.CostEstimate(flops=1000 + cost, bytes_accessed=1000 + cost // 300, transcendentals=0),
-        )(*args, *needs)
+        )(*args, *keeps, *needs)
 
     return run
 
@@ -344,27 +385,31 @@
     )
     far_stats = [swap(stats, "dp", k) for k in partners]
 
-    factors = call(adapter_kernel, shaped((rank, 2 * rows + 2 * block)), [stats])(
+    factors = call(adapter_kernel, shaped((rank, 2 * rows + 2 * block)))(
         maps, hq, hq_sib, hc, hc_sib, c_own, c_sib, q_own, q_sib
     )
     made, made_sib, answers, sib_answers, far_q_near, far_q_sib, sent, shares = [], [], [], [], [], [], [], []
     for k, q, far in zip(partners, far_q, far_stats):
-        message, packet, q_again = call(
+        message, far_scores, q_again = call(
             partner_kernel,
             (
-                shaped((block + EXTRA + 6 * rank, 2 * rows), bf16),
-                shaped((block + EXTRA, 2 * rows), bf16),
+                shaped((2 * block + SEGMENTS + 6 * rank, 2 * rows), bf16),
+                shaped((2 * block, rows)),
                 shaped((rows, width), bf16),
             ),
-        )(c_own, c_sib, q, far, stats, factors)
+        )(c_own, c_sib, q, factors)
         answers.append(swap(message, "dp", k))
         sib_answers.append(swap(answers[-1], "dp", 1))
+        packet, share = call(share_kernel, (shaped((block + EXTRA, 2 * rows), bf16), shaped((rows, width), bf16)))(
+            far_scores, far, stats, c_own, c_sib
+        )
         made.append(packet)
         made_sib.append(swap(packet, "dp", 1))
         far_q_near.append(q_again)
         far_q_sib.append(swap(q_again, "dp", 1))
-        sent.append(call(share_kernel, shaped((rows, width), bf16), [made_sib[-1]])(packet, c_own, c_sib))
-        shares.append(swap(after(sent[-1], answers[-1]), "dp", k))
+        sent.append(share)
+        shares.append(swap(after(share, answers[-1]), "dp", k))
+
     w_grad, w_own, terms = call(
         functools.partial(sums_kernel, len(partners)),
         (
@@ -389,7 +434,7 @@
     )(w_own, w_grad, c_own, c_sib, *queries, *shares)
 
     terms = lax.all_to_all(terms, "fsdp", 0, 0)
-    terms = after(jnp.sum(terms.astype(f32), 0), *shares)
+    terms = jnp.sum(terms.astype(f32), 0)
     apart = 2
     while 2 * apart < devices:
         terms = terms + swap(terms, "dp", apart)

time: 46.2 us -> 44.8 us (0.970)
  waiting for transfers between devices: 7.92 us -> 3.85 us
  starting transfers between devices: 7.85 us -> 10.6 us
    ppermute x14, waiting for transfers between devices: 7.92 us -> 3.85 us  [swap(): lax.ppermute(array, axis, [(i, i ^ apart) for i in range(lax.axis_size(ax...]
    ppermute x14, starting transfers between devices: 7.85 us -> 10.6 us  [swap(): lax.ppermute(array, axis, [(i, i ^ apart) for i in range(lax.axis_size(ax...]
  transfers between devices with their start and end apart: 14 -> 14, of which waited for: 7 -> 4; matrix products, arithmetic and copies ran while one was open for 0% -> 0% of each run, Pallas kernels for 9% -> 10%
where the time goes in v8:
time: 44.8 us; the launch traced here: 44.5 us
  blocking collectives  23.6 us (53%)
  starting transfers between devices  10.6 us (24%)
  Pallas kernels  4.94 us (11%)
  waiting for transfers between devices  3.85 us (9%)
  between operations  0.78 us (2%)
  other arithmetic  0.67 us (1%)
    all_to_all x1, blocking collectives, on_device(): maps = lax.all_to_all(mine, 'fsdp', 0, 0)  13.6 us
    ppermute x14, starting transfers between devices, swap(): lax.ppermute(array, axis, [(i, i ^ apart) for i in range(lax.axis_size(ax...  10.6 us
    all_to_all x1, blocking collectives, on_device(): terms = lax.all_to_all(terms, 'fsdp', 0, 0)  10 us
    pallas_call x7, Pallas kernels, run(): pl.pallas_call(body, out_shape=outs, in_specs=[vmem] * (len(args) + len(k...  4.94 us
    ppermute x14, waiting for transfers between devices, swap(): lax.ppermute(array, axis, [(i, i ^ apart) for i in range(lax.axis_size(ax...  3.85 us
  transfers between devices with their start and end apart: 14, of which 4 were waited for; matrix products, arithmetic and copies ran while one was open for 0% of the time, Pallas kernels for 10%

profile of v8, /device:TPU:0, one launch (start us, length us, event | category | flops | bytes accessed | tf_op | source)
XLA Modules:
  0.0 44.5 jit_solution(7512034411718290728)
XLA Ops:
  0.6 0.0 copy-start.6
  0.6 3.0 %collective-permute-start.2 = (bf16[64,4096]{1,0:T(8,128)(2,1)}, bf16[64,4096]{1,0:T(8,128)(2,1)S(1)}, u32[]{:S(2)}, u32[]{:S(2)}) collective-permute-start(bf16[64,4096]{1,0:T(8,128)(2,1)} %bitcast.13), channel_id=1, source_target_pairs={{0,16},{8,24},{16,0},{24,8},{1,17},{9,25},{17,1},{25,9},{2,18},{10... | collective-permute-start | bytes 1572872 | tf_op jit(solution)/shard_map/ppermute | solution.py:356
  3.6 0.0 collective-permute-start.1
  3.6 0.5 %collective-permute-start.3 = (bf16[64,4096]{1,0:T(8,128)(2,1)}, bf16[64,4096]{1,0:T(8,128)(2,1)S(1)}, u32[]{:S(2)}, u32[]{:S(2)}) collective-permute-start(bf16[64,4096]{1,0:T(8,128)(2,1)} %bitcast.22), channel_id=1, source_target_pairs={{0,8},{8,0},{16,24},{24,16},{1,9},{9,1},{17,25},{25,17},{2,10},{10... | collective-permute-start | bytes 1572872 | tf_op jit(solution)/shard_map/ppermute | solution.py:356
  4.2 0.0 collective-permute-start
  4.2 0.5 %collective-permute-start.4 = (bf16[80,4096]{1,0:T(8,128)(2,1)}, bf16[80,4096]{1,0:T(8,128)(2,1)S(1)}, u32[]{:S(2)}, u32[]{:S(2)}) collective-permute-start(bf16[80,4096]{1,0:T(8,128)(2,1)} %bitcast.19), channel_id=1, source_target_pairs={{0,8},{8,0},{16,24},{24,16},{1,9},{9,1},{17,25},{25,17},{2,10},{10... | collective-permute-start | bytes 1966088 | tf_op jit(solution)/shard_map/ppermute | solution.py:356
  4.7 0.0 copy-done.6
  4.7 0.0 copy-start
  4.7 0.0 copy-start.1
  4.7 0.0 copy-start.2
  4.7 0.0 copy-start.3
  4.7 13.6 %all_to_all.10.refs_0_.refs_6_ = bf16[8,16,512]{2,1,0:T(8,128)(2,1)S(1)} all-to-all(bf16[8,16,512]{2,1,0:T(8,128)(2,1)S(1)} %shard_map.111), channel_id=1, replica_groups=mesh['dp'=4,'fsdp'=8] {'fsdp'}, dimensions={0} | all-to-all | bytes 262144 | tf_op jit(solution)/shard_map/all_to_all | solution.py:381
  18.4 0.0 collective-permute-done.1.refs_8_.refs_3_.refs_5_
  18.4 0.0 collective-permute-done.3.refs_2_.refs_7_
  18.4 0.0 collective-permute-done.refs_6_.refs_1_.refs_4_.refs_3_
  18.4 0.0 collective-permute-done.4.refs_4_.refs_9_
  18.4 0.0 copy-done
  18.4 0.0 copy-done.1
  18.4 0.0 copy-done.2
  18.4 0.0 copy-done.3
  18.4 0.8 %shard_map.112.refs_3_.refs_15_ = f32[16,288]{1,0:T(8,128)S(1)} custom-call(bf16[8,16,512]{2,1,0:T(8,128)(2,1)S(1)} %all_to_all.10.refs_0_.refs_6_, bf16[64,4096]{1,0:T(8,128)(2,1)S(1)} %bitcast.23, bf16[64,4096]{1,0:T(8,128)(2,1)S(1)} %collective-permute-done.3.refs_2_.refs_7_, bf16[80,4096]{1,0:T(8,128)(2,1)S(1)} %bitcast.20, ...), custom_call_target="tpu_custom_call" | custom-call | flops 1000 | bytes 1000 | tf_op jit(solution)/shard_map/pallas_call | solution.py:338
  19.2 0.0 collective-permute-done.2.refs_2_
  19.3 0.6 %shard_map.113 = (bf16[288,128]{1,0:T(8,128)(2,1)S(1)}, f32[160,64]{1,0:T(8,128)S(1)}, bf16[64,4096]{1,0:T(8,128)(2,1)S(1)}) custom-call(bf16[80,4096]{1,0:T(8,128)(2,1)S(1)} %bitcast.8, bf16[80,4096]{1,0:T(8,128)(2,1)S(1)} %collective-permute-done.refs_6_.refs_1_.refs_4_.refs_3_, bf16[64,4096]{1,0:T(8,128)(2,1)S(1)} %collective-permute-done.2.refs_2_, ...), custom_call_target="tpu_custom_call" | custom-call | flops 1000 | bytes 1000 | tf_op jit(solution)/shard_map/pallas_call | solution.py:338
  19.9 0.0 copy-start.4
  19.9 0.0 copy-start.5
  19.9 0.1 collective-permute-start.5
  20.0 0.6 %collective-permute-start.6 = (bf16[288,128]{1,0:T(8,128)(2,1)S(1)}, bf16[288,128]{1,0:T(8,128)(2,1)S(1)}, u32[]{:S(2)}, u32[]{:S(2)}) collective-permute-start(bf16[288,128]{1,0:T(8,128)(2,1)S(1)} %get-tuple-element.20), channel_id=1, source_target_pairs={{0,16},{8,24},{16,0},{24,8},{1,17},{9,25},{17,1},{25,9},{2,18},{10... | collective-permute-start | bytes 221192 | tf_op jit(solution)/shard_map/ppermute | solution.py:356
  20.6 0.0 copy-done.4
  20.6 0.0 copy-done.5
  20.6 0.6 %shard_map.114 = (f32[160,128]{1,0:T(8,128)S(1)}, f32[8,64]{1,0:T(8,128)S(1)}) custom-call(bf16[80,4096]{1,0:T(8,128)(2,1)S(1)} %bitcast.9, bf16[80,4096]{1,0:T(8,128)(2,1)S(1)} %collective-permute-done.refs_6_.refs_1_.refs_4_.refs_3_, bf16[64,4096]{1,0:T(8,128)(2,1)S(1)} %bitcast.16, bf16[64,4096]{1,0:T(8,128)(2,1)S(1)} %collective-permute-done.1.refs_8_.refs_3_.refs_5_, ...), custom_call_target="tpu_custom_call" | custom-call | flops 1000 | bytes 1000 | tf_op jit(solution)/shard_map/pallas_call | solution.py:338
  21.1 1.6 %collective-permute-start.8 = (f32[8,64]{1,0:T(8,128)S(1)}, f32[8,64]{1,0:T(8,128)S(1)}, u32[]{:S(2)}, u32[]{:S(2)}) collective-permute-start(f32[8,64]{1,0:T(8,128)S(1)} %get-tuple-element.19.refs_2_.refs_10_), channel_id=1, source_target_pairs={{0,16},{8,24},{16,0},{24,8},{1,17},{9,25},{17,1},{25,9},{2,18},{10... | collective-permute-start | bytes 6152 | tf_op jit(solution)/shard_map/ppermute | solution.py:356
  22.7 2.1 %collective-permute-done.8.refs_1_ = f32[8,64]{1,0:T(8,128)S(1)} collective-permute-done((f32[8,64]{1,0:T(8,128)S(1)}, f32[8,64]{1,0:T(8,128)S(1)}, u32[]{:S(2)}, u32[]{:S(2)}) %collective-permute-start.8) | collective-permute-done | bytes 2080 | tf_op jit(solution)/shard_map/ppermute | solution.py:356
  24.8 0.5 %shard_map.115 = (bf16[96,128]{1,0:T(8,128)(2,1)S(1)}, bf16[64,4096]{1,0:T(8,128)(2,1)S(1)}) custom-call(f32[160,64]{1,0:T(8,128)S(1)} %get-tuple-element.21.refs_0_, f32[8,64]{1,0:T(8,128)S(1)} %collective-permute-done.8.refs_1_, f32[8,64]{1,0:T(8,128)S(1)} %get-tuple-element.19.refs_2_.refs_10_, bf16[80,4096]{1,0:T(8,128)(2,1)S(1)} %bitcast.10, ...), custom_call_target="tpu_custom_call" | custom-call | flops 1000 | bytes 1000 | tf_op jit(solution)/shard_map/pallas_call | solution.py:338
  25.3 0.0 collective-permute-done.6.refs_11_
  25.3 1.6 %collective-permute-start.10 = (bf16[64,4096]{1,0:T(8,128)(2,1)S(1)}, bf16[64,4096]{1,0:T(8,128)(2,1)S(1)}, u32[]{:S(2)}, u32[]{:S(2)}) collective-permute-start(bf16[64,4096]{1,0:T(8,128)(2,1)S(1)} %get-tuple-element.27.refs_17_), channel_id=1, source_target_pairs={{0,16},{8,24},{16,0},{24,8},{1,17},{9,25},{17,1},{25,9},{2,18},{10... | collective-permute-start | bytes 1572872 | tf_op jit(solution)/shard_map/ppermute | solution.py:356
  26.9 0.0 collective-permute-start.7
  26.9 0.5 %collective-permute-start.9 = (bf16[96,128]{1,0:T(8,128)(2,1)S(1)}, bf16[96,128]{1,0:T(8,128)(2,1)S(1)}, u32[]{:S(2)}, u32[]{:S(2)}) collective-permute-start(bf16[96,128]{1,0:T(8,128)(2,1)S(1)} %get-tuple-element.22.refs_13_), channel_id=1, source_target_pairs={{0,8},{8,0},{16,24},{24,16},{1,9},{9,1},{17,25},{25,17},{2,10},{10... | collective-permute-start | bytes 73736 | tf_op jit(solution)/shard_map/ppermute | solution.py:356
  27.4 0.8 %collective-permute-done.9.refs_14_ = bf16[96,128]{1,0:T(8,128)(2,1)S(1)} collective-permute-done((bf16[96,128]{1,0:T(8,128)(2,1)S(1)}, bf16[96,128]{1,0:T(8,128)(2,1)S(1)}, u32[]{:S(2)}, u32[]{:S(2)}) %collective-permute-start.9) | collective-permute-done | bytes 24608 | tf_op jit(solution)/shard_map/ppermute | solution.py:356
  28.3 0.0 collective-permute-done.7.refs_12_
  28.3 0.0 collective-permute-done.5.refs_5_.refs_7_
  28.3 0.9 %shard_map.116 = (bf16[80,256]{1,0:T(8,128)(2,1)S(1)}, bf16[160,64]{1,0:T(8,128)(2,1)S(1)}, bf16[8,16,512]{2,1,0:T(8,128)(2,1)S(1)}) custom-call(bf16[80,4096]{1,0:T(8,128)(2,1)S(1)} %bitcast.11, bf16[80,4096]{1,0:T(8,128)(2,1)S(1)} %collective-permute-done.refs_6_.refs_1_.refs_4_.refs_3_, bf16[64,4096]{1,0:T(8,128)(2,1)S(1)} %bitcast.17, ...), custom_call_target="tpu_custom_call" | custom-call | flops 1000 | bytes 1000 | tf_op jit(solution)/shard_map/pallas_call | solution.py:338
  29.2 10.0 %all_to_all.11 = bf16[8,16,512]{2,1,0:T(8,128)(2,1)S(1)} all-to-all(bf16[8,16,512]{2,1,0:T(8,128)(2,1)S(1)} %get-tuple-element.30), channel_id=1, replica_groups=mesh['dp'=4,'fsdp'=8] {'fsdp'}, dimensions={0} | all-to-all | bytes 262144 | tf_op jit(solution)/shard_map/all_to_all | solution.py:436
  39.2 1.3 %collective-permute-start.13 = (f32[16,512]{1,0:T(8,128)S(1)}, f32[16,512]{1,0:T(8,128)S(1)}, u32[]{:S(2)}, u32[]{:S(2)}) collective-permute-start(f32[16,512]{1,0:T(8,128)S(1)} %convert_reduce_fusion), channel_id=1, source_target_pairs={{0,16},{8,24},{16,0},{24,8},{1,17},{9,25},{17,1},{25,9},{2,18},{10... | collective-permute-start | bytes 98312 | tf_op jit(solution)/shard_map/ppermute | solution.py:356
  40.5 0.0 collective-permute-start.12
  40.5 0.9 %collective-permute-start.11 = (f32[16,512]{1,0:T(8,128)S(1)}, f32[16,512]{1,0:T(8,128)S(1)}, u32[]{:S(2)}, u32[]{:S(2)}) collective-permute-start(f32[16,512]{1,0:T(8,128)S(1)} %convert_reduce_fusion), channel_id=1, source_target_pairs={{0,24},{8,16},{16,8},{24,0},{1,25},{9,17},{17,9},{25,1},{2,26},{10... | collective-permute-start | bytes 98312 | tf_op jit(solution)/shard_map/ppermute | solution.py:356
  41.4 0.0 collective-permute-done.10.refs_8_
  41.4 1.5 %shard_map.117 = (bf16[64,4096]{1,0:T(8,128)(2,1)}, bf16[80,4096]{1,0:T(8,128)(2,1)}) custom-call(bf16[160,64]{1,0:T(8,128)(2,1)S(1)} %get-tuple-element.25.refs_0_, bf16[80,256]{1,0:T(8,128)(2,1)S(1)} %get-tuple-element.26.refs_1_, bf16[80,4096]{1,0:T(8,128)(2,1)S(1)} %bitcast.12, bf16[80,4096]{1,0:T(8,128)(2,1)S(1)} %collective-permute-done.refs_6_.refs_1_.refs_4_.refs_3_, ...), custom_call_target="tpu_custom_call" | custom-call | flops 1000 | bytes 1000 | tf_op jit(solution)/shard_map/pallas_call | solution.py:338
  43.0 0.2 collective-permute-done.13
  43.2 0.0 collective-permute-done.12
  43.2 0.7 %collective-permute-done.11 = f32[16,512]{1,0:T(8,128)S(1)} collective-permute-done((f32[16,512]{1,0:T(8,128)S(1)}, f32[16,512]{1,0:T(8,128)S(1)}, u32[]{:S(2)}, u32[]{:S(2)}) %collective-permute-start.11) | collective-permute-done | bytes 32800 | tf_op jit(solution)/shard_map/ppermute | solution.py:356
  43.9 0.6 %broadcast_select_fusion = (f32[16,512]{1,0:T(8,128)}, f32[16,512]{1,0:T(8,128)}) fusion(pred[]{:T(512)S(6)} %eq.3, f32[16,512]{1,0:T(8,128)S(1)} %collective-permute-done.11, f32[16,512]{1,0:T(8,128)S(1)} %collective-permute-done.12, f32[16,512]{1,0:T(8,128)S(1)} %convert_reduce_fusion, f32[16,512]{1,0:T(8,128)S(1)} %collective-permute-done.13), kind=kLoop, calls=%fused_computation.3 | loop fusion | flops 49152 | bytes 196609 | tf_op jit(solution)/shard_map/jit(_where)/select_n | solution.py:450
  (3 shorter events, 0.0 us)
Async XLA Ops:
  0.6 4.0 %copy-start.6 = (bf16[16,512]{1,0:T(8,128)(2,1)S(1)}, bf16[16,512]{1,0:T(8,128)(2,1)}, u32[]{:S(2)}) copy-start(bf16[16,512]{1,0:T(8,128)(2,1)} %param.14) | copy-start | bytes 49156
  0.6 18.6 %collective-permute-start.2 = (bf16[64,4096]{1,0:T(8,128)(2,1)}, bf16[64,4096]{1,0:T(8,128)(2,1)S(1)}, u32[]{:S(2)}, u32[]{:S(2)}) collective-permute-start(bf16[64,4096]{1,0:T(8,128)(2,1)} %bitcast.13), channel_id=1, source_target_pairs={{0,16},{8,24},{16,0},{24,8},{1,17},{9,25},{17,1},{25,9},{2,18},{10... | collective-permute-start | bytes 1572872 | tf_op jit(solution)/shard_map/ppermute | solution.py:356
  3.6 14.7 %collective-permute-start.1 = (bf16[64,4096]{1,0:T(8,128)(2,1)}, bf16[64,4096]{1,0:T(8,128)(2,1)S(1)}, u32[]{:S(2)}, u32[]{:S(2)}) collective-permute-start(bf16[64,4096]{1,0:T(8,128)(2,1)} %bitcast.14), channel_id=1, source_target_pairs={{0,8},{8,0},{16,24},{24,16},{1,9},{9,1},{17,25},{25,17},{2,10},{10... | collective-permute-start | bytes 1572872 | tf_op jit(solution)/shard_map/ppermute | solution.py:356
  3.6 14.7 %collective-permute-start.3 = (bf16[64,4096]{1,0:T(8,128)(2,1)}, bf16[64,4096]{1,0:T(8,128)(2,1)S(1)}, u32[]{:S(2)}, u32[]{:S(2)}) collective-permute-start(bf16[64,4096]{1,0:T(8,128)(2,1)} %bitcast.22), channel_id=1, source_target_pairs={{0,8},{8,0},{16,24},{24,16},{1,9},{9,1},{17,25},{25,17},{2,10},{10... | collective-permute-start | bytes 1572872 | tf_op jit(solution)/shard_map/ppermute | solution.py:356
  4.2 14.2 %collective-permute-start = (bf16[80,4096]{1,0:T(8,128)(2,1)}, bf16[80,4096]{1,0:T(8,128)(2,1)S(1)}, u32[]{:S(2)}, u32[]{:S(2)}) collective-permute-start(bf16[80,4096]{1,0:T(8,128)(2,1)} %bitcast.6), channel_id=1, source_target_pairs={{0,8},{8,0},{16,24},{24,16},{1,9},{9,1},{17,25},{25,17},{2,10},{10... | collective-permute-start | bytes 1966088 | tf_op jit(solution)/shard_map/ppermute | solution.py:356
  4.2 14.2 %collective-permute-start.4 = (bf16[80,4096]{1,0:T(8,128)(2,1)}, bf16[80,4096]{1,0:T(8,128)(2,1)S(1)}, u32[]{:S(2)}, u32[]{:S(2)}) collective-permute-start(bf16[80,4096]{1,0:T(8,128)(2,1)} %bitcast.19), channel_id=1, source_target_pairs={{0,8},{8,0},{16,24},{24,16},{1,9},{9,1},{17,25},{25,17},{2,10},{10... | collective-permute-start | bytes 1966088 | tf_op jit(solution)/shard_map/ppermute | solution.py:356
  4.7 13.7 %copy-start = (bf16[1,1,80,4096]{3,2,1,0:T(8,128)(2,1)S(1)}, bf16[1,1,80,4096]{3,2,1,0:T(8,128)(2,1)}, u32[]{:S(2)}) copy-start(bf16[1,1,80,4096]{3,2,1,0:T(8,128)(2,1)} %param.9) | copy-start | bytes 1966084
  4.7 13.7 %copy-start.1 = (bf16[1,64,4096]{2,1,0:T(8,128)(2,1)S(1)}, bf16[1,64,4096]{2,1,0:T(8,128)(2,1)}, u32[]{:S(2)}) copy-start(bf16[1,64,4096]{2,1,0:T(8,128)(2,1)} %param.8) | copy-start | bytes 1572868
  4.7 13.7 %copy-start.2 = (bf16[1,1,80,4096]{3,2,1,0:T(8,128)(2,1)S(1)}, bf16[1,1,80,4096]{3,2,1,0:T(8,128)(2,1)}, u32[]{:S(2)}) copy-start(bf16[1,1,80,4096]{3,2,1,0:T(8,128)(2,1)} %param.13) | copy-start | bytes 1966084
  4.7 13.7 %copy-start.3 = (bf16[1,64,4096]{2,1,0:T(8,128)(2,1)S(1)}, bf16[1,64,4096]{2,1,0:T(8,128)(2,1)}, u32[]{:S(2)}) copy-start(bf16[1,64,4096]{2,1,0:T(8,128)(2,1)} %param.12) | copy-start | bytes 1572868
  19.9 0.7 %copy-start.4 = (s32[1,64]{1,0:T(1,128)S(1)}, s32[1,64]{1,0:T(1,128)}, u32[]{:S(2)}) copy-start(s32[1,64]{1,0:T(1,128)} %refs_4_.1) | copy-start | bytes 772
  19.9 0.7 %copy-start.5 = (s32[1,64]{1,0:T(1,128)S(1)}, s32[1,64]{1,0:T(1,128)}, u32[]{:S(2)}) copy-start(s32[1,64]{1,0:T(1,128)} %refs_5_.1) | copy-start | bytes 772
  19.9 8.4 %collective-permute-start.5 = (bf16[64,4096]{1,0:T(8,128)(2,1)S(1)}, bf16[64,4096]{1,0:T(8,128)(2,1)S(1)}, u32[]{:S(2)}, u32[]{:S(2)}) collective-permute-start(bf16[64,4096]{1,0:T(8,128)(2,1)S(1)} %get-tuple-element.18.refs_4_.refs_6_), channel_id=1, source_target_pairs={{0,8},{8,0},{16,24},{24,16},{1,9},{9,1},{17,25},{25,17},{2,10},{10... | collective-permute-start | bytes 1572872 | tf_op jit(solution)/shard_map/ppermute | solution.py:356
  20.0 5.3 %collective-permute-start.6 = (bf16[288,128]{1,0:T(8,128)(2,1)S(1)}, bf16[288,128]{1,0:T(8,128)(2,1)S(1)}, u32[]{:S(2)}, u32[]{:S(2)}) collective-permute-start(bf16[288,128]{1,0:T(8,128)(2,1)S(1)} %get-tuple-element.20), channel_id=1, source_target_pairs={{0,16},{8,24},{16,0},{24,8},{1,17},{9,25},{17,1},{25,9},{2,18},{10... | collective-permute-start | bytes 221192 | tf_op jit(solution)/shard_map/ppermute | solution.py:356
  21.1 3.7 %collective-permute-start.8 = (f32[8,64]{1,0:T(8,128)S(1)}, f32[8,64]{1,0:T(8,128)S(1)}, u32[]{:S(2)}, u32[]{:S(2)}) collective-permute-start(f32[8,64]{1,0:T(8,128)S(1)} %get-tuple-element.19.refs_2_.refs_10_), channel_id=1, source_target_pairs={{0,16},{8,24},{16,0},{24,8},{1,17},{9,25},{17,1},{25,9},{2,18},{10... | collective-permute-start | bytes 6152 | tf_op jit(solution)/shard_map/ppermute | solution.py:356
  25.3 16.1 %collective-permute-start.10 = (bf16[64,4096]{1,0:T(8,128)(2,1)S(1)}, bf16[64,4096]{1,0:T(8,128)(2,1)S(1)}, u32[]{:S(2)}, u32[]{:S(2)}) collective-permute-start(bf16[64,4096]{1,0:T(8,128)(2,1)S(1)} %get-tuple-element.27.refs_17_), channel_id=1, source_target_pairs={{0,16},{8,24},{16,0},{24,8},{1,17},{9,25},{17,1},{25,9},{2,18},{10... | collective-permute-start | bytes 1572872 | tf_op jit(solution)/shard_map/ppermute | solution.py:356
  26.9 1.4 %collective-permute-start.7 = (bf16[288,128]{1,0:T(8,128)(2,1)S(1)}, bf16[288,128]{1,0:T(8,128)(2,1)S(1)}, u32[]{:S(2)}, u32[]{:S(2)}) collective-permute-start(bf16[288,128]{1,0:T(8,128)(2,1)S(1)} %collective-permute-done.6.refs_11_), channel_id=1, source_target_pairs={{0,8},{8,0},{16,24},{24,16},{1,9},{9,1},{17,25},{25,17},{2,10},{10... | collective-permute-start | bytes 221192 | tf_op jit(solution)/shard_map/ppermute | solution.py:356
  26.9 1.4 %collective-permute-start.9 = (bf16[96,128]{1,0:T(8,128)(2,1)S(1)}, bf16[96,128]{1,0:T(8,128)(2,1)S(1)}, u32[]{:S(2)}, u32[]{:S(2)}) collective-permute-start(bf16[96,128]{1,0:T(8,128)(2,1)S(1)} %get-tuple-element.22.refs_13_), channel_id=1, source_target_pairs={{0,8},{8,0},{16,24},{24,16},{1,9},{9,1},{17,25},{25,17},{2,10},{10... | collective-permute-start | bytes 73736 | tf_op jit(solution)/shard_map/ppermute | solution.py:356
  39.2 4.0 %collective-permute-start.13 = (f32[16,512]{1,0:T(8,128)S(1)}, f32[16,512]{1,0:T(8,128)S(1)}, u32[]{:S(2)}, u32[]{:S(2)}) collective-permute-start(f32[16,512]{1,0:T(8,128)S(1)} %convert_reduce_fusion), channel_id=1, source_target_pairs={{0,16},{8,24},{16,0},{24,8},{1,17},{9,25},{17,1},{25,9},{2,18},{10... | collective-permute-start | bytes 98312 | tf_op jit(solution)/shard_map/ppermute | solution.py:356
  40.5 2.7 %collective-permute-start.12 = (f32[16,512]{1,0:T(8,128)S(1)}, f32[16,512]{1,0:T(8,128)S(1)}, u32[]{:S(2)}, u32[]{:S(2)}) collective-permute-start(f32[16,512]{1,0:T(8,128)S(1)} %convert_reduce_fusion), channel_id=1, source_target_pairs={{0,8},{8,0},{16,24},{24,16},{1,9},{9,1},{17,25},{25,17},{2,10},{10... | collective-permute-start | bytes 98312 | tf_op jit(solution)/shard_map/ppermute | solution.py:356
  40.5 3.3 %collective-permute-start.11 = (f32[16,512]{1,0:T(8,128)S(1)}, f32[16,512]{1,0:T(8,128)S(1)}, u32[]{:S(2)}, u32[]{:S(2)}) collective-permute-start(f32[16,512]{1,0:T(8,128)S(1)} %convert_reduce_fusion), channel_id=1, source_target_pairs={{0,24},{8,16},{16,8},{24,0},{1,25},{9,17},{17,9},{25,1},{2,26},{10... | collective-permute-start | bytes 98312 | tf_op jit(solution)/shard_map/ppermute | solution.py:356

commit v9 on v8

--- a/solution.py
+++ b/solution.py
@@ -11,8 +11,7 @@
 adapter_scale = 2.0
 STEP = 512
 MAX, SUM, POSITIVE, HARD, STATS = 0, 1, 2, 3, 8
-EXTRA = 16
-SEGMENTS = 32
+EXTRA = 32
 
 f32 = jnp.float32
 bf16 = jnp.bfloat16
@@ -58,18 +57,7 @@
 
 
 def whole(rows):
-    rows = rows.astype(f32)
     return rows[0:1] + rows[1:2] + rows[2:3]
-
-
-def packed(weights, stats):
-    lines = []
-    for at in (MAX, SUM, POSITIVE):
-        lines += terms_of(stats[at : at + 1])
-    lines.append(stats[HARD : HARD + 1].astype(bf16))
-    lines.append(jnp.zeros((EXTRA - len(lines), weights.shape[1]), bf16))
-    lines = jnp.concatenate(lines, 0)
-    return jnp.concatenate([side_by_side(weights), jnp.concatenate([lines, lines], 1)], 0)
 
 
 def side_by_side(rows):
@@ -83,30 +71,30 @@
     return jnp.concatenate(halves[::-1] if turned else halves, 0)
 
 
-def unpacked(packet, turned=False):
-    return stacked(packet[: packet.shape[0] - EXTRA], turned)
-
-
-def message_of(shares, pairs, factors, rows, block):
+def message_of(shares, pairs, stats, factors, rows, block):
     high, low = wide_rows(shares)
-    lines = [term for pair in pairs for value in pair for term in terms_of(value)]
-    lines = jnp.concatenate(lines + [jnp.zeros((SEGMENTS - len(lines), rows), bf16)], 0)
+    values = [value for pair in pairs for value in pair] + [stats[at : at + 1] for at in (MAX, SUM, POSITIVE)]
+    lines = [term for value in values for term in terms_of(value)] + [stats[HARD : HARD + 1].astype(bf16)]
+    lines = jnp.concatenate(lines + [jnp.zeros((EXTRA - len(lines), rows), bf16)], 0)
     parts = [side_by_side(high), side_by_side(low), jnp.concatenate([lines, lines], 1)]
     return jnp.concatenate(parts + [factor_rows(factors, rows, block)], 0)
 
 
+def message_lines(message, block):
+    at, rows = 2 * block, message.shape[1] // 2
+    lines = message[at : at + EXTRA].astype(f32)[:, :rows]
+    return [whole(lines[3 * i : 3 * i + 3]) for i in range(9)] + [lines[27:28]]
+
+
+def sender_stats(message, block):
+    return message_lines(message, block)[6:]
+
+
 def message_parts(message, block, turned=False):
     high, low = (stacked(message[i * block : (i + 1) * block], turned).astype(f32) for i in (0, 1))
-    at, rows = 2 * block, message.shape[1] // 2
-    values = [whole(message[at + 3 * i : at + 3 * i + 3, :rows]) for i in range(6)]
-    pairs = list(zip(values[::2], values[1::2]))
-    return high + low, pairs[:1] + (pairs[:0:-1] if turned else pairs[1:]), message[at + SEGMENTS :]
-
-
-def sender_stats(packet):
-    at, rows = packet.shape[0] - EXTRA, packet.shape[1] // 2
-    three = [whole(packet[at + i : at + i + 3, :rows]) for i in (0, 3, 6)]
-    return three + [packet[at + 9 : at + 10, :rows].astype(f32)]
+    values = message_lines(message, block)
+    pairs = list(zip(values[0:6:2], values[1:6:2]))
+    return high + low, pairs[:1] + (pairs[:0:-1] if turned else pairs[1:])
 
 
 def wide_rows(array):
@@ -178,7 +166,7 @@
         factors[...] = product([q_own, q_sib, c_own, c_sib])
 
 
-def partner_kernel(c_own, c_sib, q, factors, message, scores, q_again):
+def partner_kernel(c_own, c_sib, q, stats, factors, message, scores, q_again):
     block, rows = c_own.shape[0], q.shape[0]
     c = jnp.concatenate([c_own[...], c_sib[...]], 0)
     q_again[...] = q[...]
@@ -189,23 +177,23 @@
     tops = [jnp.max(jnp.where(part, total, -jnp.inf), axis=0, keepdims=True) for part in parts]
     shares = jnp.exp(total - jnp.where(parts[0], tops[0], jnp.where(parts[1], tops[1], tops[2])))
     sums = [jnp.sum(jnp.where(part, shares, 0.0), axis=0, keepdims=True) for part in parts]
-    message[...] = message_of(shares, list(zip(tops, sums)), factors[...], rows, block)
-
-
-def share_kernel(scores, stats, own_stats, c_own, c_sib, packet, share):
+    message[...] = message_of(shares, list(zip(tops, sums)), stats, factors[...], rows, block)
+
+
+def share_kernel(scores, answer, c_own, c_sib, weights, share):
     block, rows = c_own.shape[0], scores.shape[1]
+    far_top, far_total, positive, hard = sender_stats(answer, block)
     owner, slot = layout(lax.axis_index("dp"), block, scores.shape)
-    total = jnp.where(allowed(owner, slot, stats[HARD : HARD + 1], rows), scores[...], -jnp.inf)
+    total = jnp.where(allowed(owner, slot, hard, rows), scores[...], -jnp.inf)
     top = jnp.max(total, axis=0, keepdims=True)
     here = jnp.sum(jnp.exp(total - top), axis=0, keepdims=True)
-    log_total = merge([(stats[MAX : MAX + 1], stats[SUM : SUM + 1]), (top, here)])
-    hit = hits(owner, slot, stats[POSITIVE : POSITIVE + 1], rows)
-    weights = (jnp.exp(total - log_total) - hit.astype(f32)).astype(bf16)
-    packet[...] = packed(weights, own_stats)
+    log_total = merge([(far_top, far_total), (top, here)])
+    hit = hits(owner, slot, positive, rows)
+    weights[...] = (jnp.exp(total - log_total) - hit.astype(f32)).astype(bf16)
     for i in range(share.shape[1] // STEP):
         at = slice(i * STEP, (i + 1) * STEP)
         c = jnp.concatenate([c_own[:, at], c_sib[:, at]], 0)
-        share[:, at] = (dot(weights, c, 0, 0) * sharpness_factor).astype(bf16)
+        share[:, at] = (dot(weights[...], c, 0, 0) * sharpness_factor).astype(bf16)
 
 
 def rows_kernel(partners, w_own, w_grad, c_own, c_sib, *refs):
@@ -250,36 +238,46 @@
     block, rows = c[0].shape[0], q[0].shape[0]
     shards, rank, width = terms.shape
     position = lax.axis_index("dp")
+    own = [stats[at : at + 1] for at in (MAX, SUM, POSITIVE, HARD)]
+    sib = sender_stats(made_sib[0], block)
+    far_factors = [factors_of(a[2 * block + EXTRA :], block) for a in answers]
+    far_stats = [sender_stats(a, block) for a in sib_answers]
     answers = [message_parts(a, block) for a in answers]
     sib_answers = [message_parts(a, block, turned=True) for a in sib_answers]
-    far_factors = [factors_of(rest, block) for _, _, rest in answers]
-
-    own = [stats[at : at + 1] for at in (MAX, SUM, POSITIVE, HARD)]
-    sib = sender_stats(made_sib[0])
-
-    def kept_pairs(i, pairs, hard):
-        first = position ^ (2 * i + 2)
-        out = [pairs[0]]
-        for (top, total), at in zip(pairs[1:], (first, first ^ 1)):
-            counts = hard.astype(jnp.int32) == at
-            out.append((jnp.where(counts, top, pairs[0][0]), jnp.where(counts, total, 0.0)))
-        return out
 
     def log_total(chip, parts):
-        return merge([(chip[0], chip[1])] + [p for i, part in enumerate(parts) for p in kept_pairs(i, part[1], chip[3])])
-
+        terms = [(chip[0], chip[1])]
+        for first, pairs in parts:
+            terms.append(pairs[0])
+            for (top, total), at in zip(pairs[1:], (first, first ^ 1)):
+                counts = chip[3].astype(jnp.int32) == at
+                terms.append((jnp.where(counts, top, pairs[0][0]), jnp.where(counts, total, 0.0)))
+        return merge(terms)
+
+    def scaled(first, shares, tops, log_totals, positive, hard):
+        owner, slot = layout(first, block, shares.shape)
+        top = jnp.where(slot < rows, tops[0], jnp.where(owner == first, tops[1], tops[2]))
+        kept = allowed(owner, slot, hard, rows)
+        weights = shares * jnp.exp(jnp.where(kept, top - log_totals, -jnp.inf))
+        return (weights - hits(owner, slot, positive, rows).astype(f32)).astype(bf16)
+
+    firsts = [position ^ (2 * i + 2) for i in range(n)]
+    hard, positive = (jnp.concatenate([own[i], sib[i]], 1) for i in (3, 2))
     owner, slot = layout(position, block, scores.shape)
-    hard = jnp.concatenate([own[3], sib[3]], 1)
     kept = allowed(owner, slot, hard, rows)
-    positive = jnp.concatenate([own[2], sib[2]], 1)
     hit = hits(owner, slot, positive, rows)
-    log_totals = jnp.concatenate([log_total(own, answers), log_total(sib, sib_answers)], 1)
+    log_totals = jnp.concatenate(
+        [log_total(c, [(f, p[1]) for f, p in zip(firsts, parts)]) for c, parts in ((own, answers), (sib, sib_answers))],
+        1,
+    )
     near = jnp.exp(jnp.where(kept, scores[...] - log_totals, -jnp.inf)) - hit.astype(f32)
     near = near.astype(bf16)
     w_own[...] = near[:, :rows]
     pieces = [near]
-    for mine, other in zip(made, made_sib):
-        pieces += [unpacked(mine[...]), unpacked(other[...], turned=True)]
+    for mine, other, chip in zip(made, made_sib, far_stats):
+        shares, pairs = message_parts(other, block, turned=True)
+        far_total = log_total(chip, [(position, pairs)])
+        pieces += [mine[...], scaled(position, shares, [top for top, _ in pairs], far_total, chip[2], chip[3])]
     weights = jnp.concatenate(pieces, 1)
     w_grad[...] = weights[:block]
     by_query = jnp.concatenate([r[:, : 2 * rows] for r in [factors] + [f for f, _ in far_factors]], 1)
@@ -309,15 +307,10 @@
     def _():
         back_q = dot_wide(by_candidate, near, 1, 0)
         for i in range(n):
-            first = position ^ (2 * i + 2)
-            owner, slot = layout(first, block, scores.shape)
-            kept = allowed(owner, slot, hard, rows)
             shares = jnp.concatenate([answers[i][0], sib_answers[i][0]], 1)
             tops = [jnp.concatenate([a[0], b[0]], 1) for a, b in zip(answers[i][1], sib_answers[i][1])]
-            top = jnp.where(slot < rows, tops[0], jnp.where(owner == first, tops[1], tops[2]))
-            there = shares * jnp.exp(jnp.where(kept, top - log_totals, -jnp.inf))
-            there = there - hits(owner, slot, positive, rows).astype(f32)
-            back_q = back_q + dot_wide(far_factors[i][1], there.astype(bf16), 1, 0)
+            there = scaled(firsts[i], shares, tops, log_totals, positive, hard)
+            back_q = back_q + dot_wide(far_factors[i][1], there, 1, 0)
         back_q = (back_q * sharpness_factor).astype(bf16)
         back_c = (dot_wide(by_query, weights, 1, 1) * sharpness_factor).astype(bf16)
         for i in range(shards):
@@ -380,35 +373,34 @@
     )
     maps = lax.all_to_all(mine, "fsdp", 0, 0)
 
-    scores, stats = call(scores_kernel, (shaped((2 * block, 2 * rows)), shaped((STATS, rows))), [maps])(
-        c_own, c_sib, q_own, q_sib, positives, hard_blocks
-    )
-    far_stats = [swap(stats, "dp", k) for k in partners]
-
     factors = call(adapter_kernel, shaped((rank, 2 * rows + 2 * block)))(
         maps, hq, hq_sib, hc, hc_sib, c_own, c_sib, q_own, q_sib
     )
+    scores, stats = call(scores_kernel, (shaped((2 * block, 2 * rows)), shaped((STATS, rows))), [factors])(
+        c_own, c_sib, q_own, q_sib, positives, hard_blocks
+    )
+
     made, made_sib, answers, sib_answers, far_q_near, far_q_sib, sent, shares = [], [], [], [], [], [], [], []
-    for k, q, far in zip(partners, far_q, far_stats):
+    for k, q in zip(partners, far_q):
         message, far_scores, q_again = call(
             partner_kernel,
             (
-                shaped((2 * block + SEGMENTS + 6 * rank, 2 * rows), bf16),
+                shaped((2 * block + EXTRA + 6 * rank, 2 * rows), bf16),
                 shaped((2 * block, rows)),
                 shaped((rows, width), bf16),
             ),
-        )(c_own, c_sib, q, factors)
+        )(c_own, c_sib, q, stats, factors)
         answers.append(swap(message, "dp", k))
+        made_sib.append(swap(message, "dp", 1))
         sib_answers.append(swap(answers[-1], "dp", 1))
-        packet, share = call(share_kernel, (shaped((block + EXTRA, 2 * rows), bf16), shaped((rows, width), bf16)))(
-            far_scores, far, stats, c_own, c_sib
+        weights, share = call(share_kernel, (shaped((2 * block, rows), bf16), shaped((rows, width), bf16)), [made_sib[-1]])(
+            far_scores, answers[-1], c_own, c_sib
         )
-        made.append(packet)
-        made_sib.append(swap(packet, "dp", 1))
+        made.append(weights)
         far_q_near.append(q_again)
         far_q_sib.append(swap(q_again, "dp", 1))
         sent.append(share)
-        shares.append(swap(after(share, answers[-1]), "dp", k))
+        shares.append(swap(after(share, sib_answers[-1]), "dp", k))
 
     w_grad, w_own, terms = call(
         functools.partial(sums_kernel, len(partners)),

time: 44.8 us -> 44.1 us (0.984)
  starting transfers between devices: 10.6 us -> 7.3 us
  waiting for transfers between devices: 3.85 us -> 5.32 us
  blocking collectives: 23.6 us -> 24.7 us
    ppermute x14 -> x13, starting transfers between devices: 10.6 us -> 7.3 us  [swap(): lax.ppermute(array, axis, [(i, i ^ apart) for i in range(lax.axis_size(ax...]
    ppermute x14 -> x13, waiting for transfers between devices: 3.85 us -> 5.32 us  [swap(): lax.ppermute(array, axis, [(i, i ^ apart) for i in range(lax.axis_size(ax...]
    all_to_all x1, blocking collectives: 10 us -> 10.8 us  [on_device(): terms = lax.all_to_all(terms, 'fsdp', 0, 0)]
  transfers between devices with their start and end apart: 14 -> 13, of which waited for: 4 -> 4; matrix products, arithmetic and copies ran while one was open for 0% -> 0% of each run, Pallas kernels for 10% -> 10%
where the time goes in v9:
time: 44.1 us; the launch traced here: 43.8 us
  blocking collectives  24.7 us (56%)
  starting transfers between devices  7.3 us (17%)
  waiting for transfers between devices  5.32 us (12%)
  Pallas kernels  4.99 us (11%)
  between operations  0.79 us (2%)
  other arithmetic  0.67 us (2%)
    all_to_all x1, blocking collectives, on_device(): maps = lax.all_to_all(mine, 'fsdp', 0, 0)  13.9 us
    all_to_all x1, blocking collectives, on_device(): terms = lax.all_to_all(terms, 'fsdp', 0, 0)  10.8 us
    ppermute x13, starting transfers between devices, swap(): lax.ppermute(array, axis, [(i, i ^ apart) for i in range(lax.axis_size(ax...  7.3 us
    ppermute x13, waiting for transfers between devices, swap(): lax.ppermute(array, axis, [(i, i ^ apart) for i in range(lax.axis_size(ax...  5.32 us
    pallas_call x7, Pallas kernels, run(): pl.pallas_call(body, out_shape=outs, in_specs=[vmem] * (len(args) + len(k...  4.99 us
  transfers between devices with their start and end apart: 13, of which 4 were waited for; matrix products, arithmetic and copies ran while one was open for 0% of the time, Pallas kernels for 10%

profile of v9, /device:TPU:0, one launch (start us, length us, event | category | flops | bytes accessed | tf_op | source)
XLA Modules:
  0.0 43.8 jit_solution(11468020464560106180)
XLA Ops:
  0.6 0.0 copy-start.6
  0.6 0.5 %collective-permute-start.1 = (bf16[64,4096]{1,0:T(8,128)(2,1)}, bf16[64,4096]{1,0:T(8,128)(2,1)S(1)}, u32[]{:S(2)}, u32[]{:S(2)}) collective-permute-start(bf16[64,4096]{1,0:T(8,128)(2,1)} %bitcast.13), channel_id=1, source_target_pairs={{0,8},{8,0},{16,24},{24,16},{1,9},{9,1},{17,25},{25,17},{2,10},{10... | collective-permute-start | bytes 1572872 | tf_op jit(solution)/shard_map/ppermute | solution.py:349
  1.2 2.6 %collective-permute-start.2 = (bf16[64,4096]{1,0:T(8,128)(2,1)}, bf16[64,4096]{1,0:T(8,128)(2,1)S(1)}, u32[]{:S(2)}, u32[]{:S(2)}) collective-permute-start(bf16[64,4096]{1,0:T(8,128)(2,1)} %bitcast.14), channel_id=1, source_target_pairs={{0,16},{8,24},{16,0},{24,8},{1,17},{9,25},{17,1},{25,9},{2,18},{10... | collective-permute-start | bytes 1572872 | tf_op jit(solution)/shard_map/ppermute | solution.py:349
  3.7 0.2 collective-permute-start
  3.9 0.3 collective-permute-start.3
  4.2 0.2 collective-permute-start.4
  4.4 0.0 copy-done.6
  4.4 0.0 copy-start
  4.4 0.0 copy-start.1
  4.4 0.0 copy-start.2
  4.5 0.0 copy-start.3
  4.5 13.9 %all_to_all.10.refs_0_ = bf16[8,16,512]{2,1,0:T(8,128)(2,1)S(1)} all-to-all(bf16[8,16,512]{2,1,0:T(8,128)(2,1)S(1)} %shard_map.111), channel_id=1, replica_groups=mesh['dp'=4,'fsdp'=8] {'fsdp'}, dimensions={0} | all-to-all | bytes 262144 | tf_op jit(solution)/shard_map/all_to_all | solution.py:374
  18.4 0.0 copy-start.4
  18.4 0.0 copy-start.5
  18.4 0.0 collective-permute-done.1.refs_8_.refs_3_.refs_5_
  18.4 0.0 collective-permute-done.3.refs_2_.refs_7_
  18.4 0.0 collective-permute-done.refs_6_.refs_1_.refs_3_
  18.5 0.0 collective-permute-done.4.refs_4_.refs_9_
  18.5 0.0 copy-done
  18.5 0.0 copy-done.1
  18.5 0.0 copy-done.2
  18.5 0.0 copy-done.3
  18.5 0.8 %shard_map.112.refs_6_.refs_4_.refs_15_ = f32[16,288]{1,0:T(8,128)S(1)} custom-call(bf16[8,16,512]{2,1,0:T(8,128)(2,1)S(1)} %all_to_all.10.refs_0_, bf16[64,4096]{1,0:T(8,128)(2,1)S(1)} %bitcast.23, bf16[64,4096]{1,0:T(8,128)(2,1)S(1)} %collective-permute-done.3.refs_2_.refs_7_, bf16[80,4096]{1,0:T(8,128)(2,1)S(1)} %bitcast.20, ...), custom_call_target="tpu_custom_call" | custom-call | flops 1000 | bytes 1000 | tf_op jit(solution)/shard_map/pallas_call | solution.py:331
  19.3 0.0 copy-done.4
  19.3 0.0 copy-done.5
  19.3 0.6 %shard_map.113 = (f32[160,128]{1,0:T(8,128)S(1)}, f32[8,64]{1,0:T(8,128)S(1)}) custom-call(bf16[80,4096]{1,0:T(8,128)(2,1)S(1)} %bitcast.8, bf16[80,4096]{1,0:T(8,128)(2,1)S(1)} %collective-permute-done.refs_6_.refs_1_.refs_3_, bf16[64,4096]{1,0:T(8,128)(2,1)S(1)} %bitcast.16, bf16[64,4096]{1,0:T(8,128)(2,1)S(1)} %collective-permute-done.1.refs_8_.refs_3_.refs_5_, ...), custom_call_target="tpu_custom_call" | custom-call | flops 1000 | bytes 1000 | tf_op jit(solution)/shard_map/pallas_call | solution.py:331
  19.9 0.0 collective-permute-done.2.refs_2_
  19.9 0.6 %shard_map.114 = (bf16[288,128]{1,0:T(8,128)(2,1)S(1)}, f32[160,64]{1,0:T(8,128)S(1)}, bf16[64,4096]{1,0:T(8,128)(2,1)S(1)}) custom-call(bf16[80,4096]{1,0:T(8,128)(2,1)S(1)} %bitcast.9, bf16[80,4096]{1,0:T(8,128)(2,1)S(1)} %collective-permute-done.refs_6_.refs_1_.refs_3_, bf16[64,4096]{1,0:T(8,128)(2,1)S(1)} %collective-permute-done.2.refs_2_, ...), custom_call_target="tpu_custom_call" | custom-call | flops 1000 | bytes 1000 | tf_op jit(solution)/shard_map/pallas_call | solution.py:331
  20.5 0.1 collective-permute-start.5
  20.6 0.6 %collective-permute-start.6 = (bf16[288,128]{1,0:T(8,128)(2,1)S(1)}, bf16[288,128]{1,0:T(8,128)(2,1)S(1)}, u32[]{:S(2)}, u32[]{:S(2)}) collective-permute-start(bf16[288,128]{1,0:T(8,128)(2,1)S(1)} %get-tuple-element.20), channel_id=1, source_target_pairs={{0,16},{8,24},{16,0},{24,8},{1,17},{9,25},{17,1},{25,9},{2,18},{10... | collective-permute-start | bytes 221192 | tf_op jit(solution)/shard_map/ppermute | solution.py:349
  21.2 0.2 collective-permute-start.8
  21.4 3.9 %collective-permute-done.6.refs_1_.refs_11_ = bf16[288,128]{1,0:T(8,128)(2,1)S(1)} collective-permute-done((bf16[288,128]{1,0:T(8,128)(2,1)S(1)}, bf16[288,128]{1,0:T(8,128)(2,1)S(1)}, u32[]{:S(2)}, u32[]{:S(2)}) %collective-permute-start.6) | collective-permute-done | bytes 73760 | tf_op jit(solution)/shard_map/ppermute | solution.py:349
  25.3 0.0 collective-permute-start.7
  25.3 0.0 collective-permute-done.8.refs_4_.refs_14_
  25.3 0.5 %shard_map.115 = (bf16[160,64]{1,0:T(8,128)(2,1)S(1)}, bf16[64,4096]{1,0:T(8,128)(2,1)S(1)}) custom-call(f32[160,64]{1,0:T(8,128)S(1)} %get-tuple-element.21.refs_0_, bf16[288,128]{1,0:T(8,128)(2,1)S(1)} %collective-permute-done.6.refs_1_.refs_11_, bf16[80,4096]{1,0:T(8,128)(2,1)S(1)} %bitcast.10, ...), custom_call_target="tpu_custom_call" | custom-call | flops 1000 | bytes 1000 | tf_op jit(solution)/shard_map/pallas_call | solution.py:331
  25.8 0.8 %collective-permute-done.7.refs_12_ = bf16[288,128]{1,0:T(8,128)(2,1)S(1)} collective-permute-done((bf16[288,128]{1,0:T(8,128)(2,1)S(1)}, bf16[288,128]{1,0:T(8,128)(2,1)S(1)}, u32[]{:S(2)}, u32[]{:S(2)}) %collective-permute-start.7) | collective-permute-done | bytes 73760 | tf_op jit(solution)/shard_map/ppermute | solution.py:349
  26.6 0.5 %collective-permute-start.9 = (bf16[64,4096]{1,0:T(8,128)(2,1)S(1)}, bf16[64,4096]{1,0:T(8,128)(2,1)S(1)}, u32[]{:S(2)}, u32[]{:S(2)}) collective-permute-start(bf16[64,4096]{1,0:T(8,128)(2,1)S(1)} %get-tuple-element.27.refs_17_), channel_id=1, source_target_pairs={{0,16},{8,24},{16,0},{24,8},{1,17},{9,25},{17,1},{25,9},{2,18},{10... | collective-permute-start | bytes 1572872 | tf_op jit(solution)/shard_map/ppermute | solution.py:349
  27.1 0.0 collective-permute-done.5.refs_5_.refs_7_
  27.1 0.9 %shard_map.116 = (bf16[80,256]{1,0:T(8,128)(2,1)S(1)}, bf16[160,64]{1,0:T(8,128)(2,1)S(1)}, bf16[8,16,512]{2,1,0:T(8,128)(2,1)S(1)}) custom-call(bf16[80,4096]{1,0:T(8,128)(2,1)S(1)} %bitcast.11, bf16[80,4096]{1,0:T(8,128)(2,1)S(1)} %collective-permute-done.refs_6_.refs_1_.refs_3_, bf16[64,4096]{1,0:T(8,128)(2,1)S(1)} %bitcast.17, ...), custom_call_target="tpu_custom_call" | custom-call | flops 1000 | bytes 1000 | tf_op jit(solution)/shard_map/pallas_call | solution.py:331
  28.0 10.8 %all_to_all.11 = bf16[8,16,512]{2,1,0:T(8,128)(2,1)S(1)} all-to-all(bf16[8,16,512]{2,1,0:T(8,128)(2,1)S(1)} %get-tuple-element.30), channel_id=1, replica_groups=mesh['dp'=4,'fsdp'=8] {'fsdp'}, dimensions={0} | all-to-all | bytes 262144 | tf_op jit(solution)/shard_map/all_to_all | solution.py:428
  38.8 0.7 %collective-permute-start.12 = (f32[16,512]{1,0:T(8,128)S(1)}, f32[16,512]{1,0:T(8,128)S(1)}, u32[]{:S(2)}, u32[]{:S(2)}) collective-permute-start(f32[16,512]{1,0:T(8,128)S(1)} %convert_reduce_fusion), channel_id=1, source_target_pairs={{0,16},{8,24},{16,0},{24,8},{1,17},{9,25},{17,1},{25,9},{2,18},{10... | collective-permute-start | bytes 98312 | tf_op jit(solution)/shard_map/ppermute | solution.py:349
  39.5 0.0 collective-permute-start.10
  39.5 1.5 %collective-permute-start.11 = (f32[16,512]{1,0:T(8,128)S(1)}, f32[16,512]{1,0:T(8,128)S(1)}, u32[]{:S(2)}, u32[]{:S(2)}) collective-permute-start(f32[16,512]{1,0:T(8,128)S(1)} %convert_reduce_fusion), channel_id=1, source_target_pairs={{0,8},{8,0},{16,24},{24,16},{1,9},{9,1},{17,25},{25,17},{2,10},{10... | collective-permute-start | bytes 98312 | tf_op jit(solution)/shard_map/ppermute | solution.py:349
  41.0 0.0 collective-permute-done.9.refs_8_
  41.0 1.5 %shard_map.117 = (bf16[64,4096]{1,0:T(8,128)(2,1)}, bf16[80,4096]{1,0:T(8,128)(2,1)}) custom-call(bf16[160,64]{1,0:T(8,128)(2,1)S(1)} %get-tuple-element.25.refs_0_, bf16[80,256]{1,0:T(8,128)(2,1)S(1)} %get-tuple-element.26.refs_1_, bf16[80,4096]{1,0:T(8,128)(2,1)S(1)} %bitcast.12, bf16[80,4096]{1,0:T(8,128)(2,1)S(1)} %collective-permute-done.refs_6_.refs_1_.refs_3_, ...), custom_call_target="tpu_custom_call" | custom-call | flops 1000 | bytes 1000 | tf_op jit(solution)/shard_map/pallas_call | solution.py:331
  42.6 0.5 %collective-permute-done.12 = f32[16,512]{1,0:T(8,128)S(1)} collective-permute-done((f32[16,512]{1,0:T(8,128)S(1)}, f32[16,512]{1,0:T(8,128)S(1)}, u32[]{:S(2)}, u32[]{:S(2)}) %collective-permute-start.12) | collective-permute-done | bytes 32800 | tf_op jit(solution)/shard_map/ppermute | solution.py:349
  43.1 0.1 collective-permute-done.10
  43.2 0.0 collective-permute-done.11
  43.2 0.6 %broadcast_select_fusion = (f32[16,512]{1,0:T(8,128)}, f32[16,512]{1,0:T(8,128)}) fusion(pred[]{:T(512)S(6)} %eq.3, f32[16,512]{1,0:T(8,128)S(1)} %collective-permute-done.10, f32[16,512]{1,0:T(8,128)S(1)} %collective-permute-done.11, f32[16,512]{1,0:T(8,128)S(1)} %convert_reduce_fusion, f32[16,512]{1,0:T(8,128)S(1)} %collective-permute-done.12), kind=kLoop, calls=%fused_computation.3 | loop fusion | flops 49152 | bytes 196609 | tf_op jit(solution)/shard_map/jit(_where)/select_n | solution.py:442
  (3 shorter events, 0.0 us)
Async XLA Ops:
  0.6 3.8 %copy-start.6 = (bf16[16,512]{1,0:T(8,128)(2,1)S(1)}, bf16[16,512]{1,0:T(8,128)(2,1)}, u32[]{:S(2)}) copy-start(bf16[16,512]{1,0:T(8,128)(2,1)} %param.14) | copy-start | bytes 49156
  0.6 17.8 %collective-permute-start.1 = (bf16[64,4096]{1,0:T(8,128)(2,1)}, bf16[64,4096]{1,0:T(8,128)(2,1)S(1)}, u32[]{:S(2)}, u32[]{:S(2)}) collective-permute-start(bf16[64,4096]{1,0:T(8,128)(2,1)} %bitcast.13), channel_id=1, source_target_pairs={{0,8},{8,0},{16,24},{24,16},{1,9},{9,1},{17,25},{25,17},{2,10},{10... | collective-permute-start | bytes 1572872 | tf_op jit(solution)/shard_map/ppermute | solution.py:349
  1.2 18.7 %collective-permute-start.2 = (bf16[64,4096]{1,0:T(8,128)(2,1)}, bf16[64,4096]{1,0:T(8,128)(2,1)S(1)}, u32[]{:S(2)}, u32[]{:S(2)}) collective-permute-start(bf16[64,4096]{1,0:T(8,128)(2,1)} %bitcast.14), channel_id=1, source_target_pairs={{0,16},{8,24},{16,0},{24,8},{1,17},{9,25},{17,1},{25,9},{2,18},{10... | collective-permute-start | bytes 1572872 | tf_op jit(solution)/shard_map/ppermute | solution.py:349
  3.7 14.7 %collective-permute-start = (bf16[80,4096]{1,0:T(8,128)(2,1)}, bf16[80,4096]{1,0:T(8,128)(2,1)S(1)}, u32[]{:S(2)}, u32[]{:S(2)}) collective-permute-start(bf16[80,4096]{1,0:T(8,128)(2,1)} %bitcast.6), channel_id=1, source_target_pairs={{0,8},{8,0},{16,24},{24,16},{1,9},{9,1},{17,25},{25,17},{2,10},{10... | collective-permute-start | bytes 1966088 | tf_op jit(solution)/shard_map/ppermute | solution.py:349
  3.9 14.5 %collective-permute-start.3 = (bf16[64,4096]{1,0:T(8,128)(2,1)}, bf16[64,4096]{1,0:T(8,128)(2,1)S(1)}, u32[]{:S(2)}, u32[]{:S(2)}) collective-permute-start(bf16[64,4096]{1,0:T(8,128)(2,1)} %bitcast.22), channel_id=1, source_target_pairs={{0,8},{8,0},{16,24},{24,16},{1,9},{9,1},{17,25},{25,17},{2,10},{10... | collective-permute-start | bytes 1572872 | tf_op jit(solution)/shard_map/ppermute | solution.py:349
  4.2 14.2 %collective-permute-start.4 = (bf16[80,4096]{1,0:T(8,128)(2,1)}, bf16[80,4096]{1,0:T(8,128)(2,1)S(1)}, u32[]{:S(2)}, u32[]{:S(2)}) collective-permute-start(bf16[80,4096]{1,0:T(8,128)(2,1)} %bitcast.19), channel_id=1, source_target_pairs={{0,8},{8,0},{16,24},{24,16},{1,9},{9,1},{17,25},{25,17},{2,10},{10... | collective-permute-start | bytes 1966088 | tf_op jit(solution)/shard_map/ppermute | solution.py:349
  4.4 14.0 %copy-start = (bf16[1,1,80,4096]{3,2,1,0:T(8,128)(2,1)S(1)}, bf16[1,1,80,4096]{3,2,1,0:T(8,128)(2,1)}, u32[]{:S(2)}) copy-start(bf16[1,1,80,4096]{3,2,1,0:T(8,128)(2,1)} %param.9) | copy-start | bytes 1966084
  4.4 14.0 %copy-start.1 = (bf16[1,64,4096]{2,1,0:T(8,128)(2,1)S(1)}, bf16[1,64,4096]{2,1,0:T(8,128)(2,1)}, u32[]{:S(2)}) copy-start(bf16[1,64,4096]{2,1,0:T(8,128)(2,1)} %param.8) | copy-start | bytes 1572868
  4.4 14.0 %copy-start.2 = (bf16[1,1,80,4096]{3,2,1,0:T(8,128)(2,1)S(1)}, bf16[1,1,80,4096]{3,2,1,0:T(8,128)(2,1)}, u32[]{:S(2)}) copy-start(bf16[1,1,80,4096]{3,2,1,0:T(8,128)(2,1)} %param.13) | copy-start | bytes 1966084
  4.5 14.0 %copy-start.3 = (bf16[1,64,4096]{2,1,0:T(8,128)(2,1)S(1)}, bf16[1,64,4096]{2,1,0:T(8,128)(2,1)}, u32[]{:S(2)}) copy-start(bf16[1,64,4096]{2,1,0:T(8,128)(2,1)} %param.12) | copy-start | bytes 1572868
  18.4 0.9 %copy-start.4 = (s32[1,64]{1,0:T(1,128)S(1)}, s32[1,64]{1,0:T(1,128)}, u32[]{:S(2)}) copy-start(s32[1,64]{1,0:T(1,128)} %refs_4_.1) | copy-start | bytes 772
  18.4 0.9 %copy-start.5 = (s32[1,64]{1,0:T(1,128)S(1)}, s32[1,64]{1,0:T(1,128)}, u32[]{:S(2)}) copy-start(s32[1,64]{1,0:T(1,128)} %refs_5_.1) | copy-start | bytes 772
  20.5 6.5 %collective-permute-start.5 = (bf16[64,4096]{1,0:T(8,128)(2,1)S(1)}, bf16[64,4096]{1,0:T(8,128)(2,1)S(1)}, u32[]{:S(2)}, u32[]{:S(2)}) collective-permute-start(bf16[64,4096]{1,0:T(8,128)(2,1)S(1)} %get-tuple-element.19.refs_4_.refs_6_), channel_id=1, source_target_pairs={{0,8},{8,0},{16,24},{24,16},{1,9},{9,1},{17,25},{25,17},{2,10},{10... | collective-permute-start | bytes 1572872 | tf_op jit(solution)/shard_map/ppermute | solution.py:349
  20.6 4.7 %collective-permute-start.6 = (bf16[288,128]{1,0:T(8,128)(2,1)S(1)}, bf16[288,128]{1,0:T(8,128)(2,1)S(1)}, u32[]{:S(2)}, u32[]{:S(2)}) collective-permute-start(bf16[288,128]{1,0:T(8,128)(2,1)S(1)} %get-tuple-element.20), channel_id=1, source_target_pairs={{0,16},{8,24},{16,0},{24,8},{1,17},{9,25},{17,1},{25,9},{2,18},{10... | collective-permute-start | bytes 221192 | tf_op jit(solution)/shard_map/ppermute | solution.py:349
  21.2 4.1 %collective-permute-start.8 = (bf16[288,128]{1,0:T(8,128)(2,1)S(1)}, bf16[288,128]{1,0:T(8,128)(2,1)S(1)}, u32[]{:S(2)}, u32[]{:S(2)}) collective-permute-start(bf16[288,128]{1,0:T(8,128)(2,1)S(1)} %get-tuple-element.20), channel_id=1, source_target_pairs={{0,8},{8,0},{16,24},{24,16},{1,9},{9,1},{17,25},{25,17},{2,10},{10... | collective-permute-start | bytes 221192 | tf_op jit(solution)/shard_map/ppermute | solution.py:349
  25.3 1.3 %collective-permute-start.7 = (bf16[288,128]{1,0:T(8,128)(2,1)S(1)}, bf16[288,128]{1,0:T(8,128)(2,1)S(1)}, u32[]{:S(2)}, u32[]{:S(2)}) collective-permute-start(bf16[288,128]{1,0:T(8,128)(2,1)S(1)} %collective-permute-done.6.refs_1_.refs_11_), channel_id=1, source_target_pairs={{0,8},{8,0},{16,24},{24,16},{1,9},{9,1},{17,25},{25,17},{2,10},{10... | collective-permute-start | bytes 221192 | tf_op jit(solution)/shard_map/ppermute | solution.py:349
  26.6 14.5 %collective-permute-start.9 = (bf16[64,4096]{1,0:T(8,128)(2,1)S(1)}, bf16[64,4096]{1,0:T(8,128)(2,1)S(1)}, u32[]{:S(2)}, u32[]{:S(2)}) collective-permute-start(bf16[64,4096]{1,0:T(8,128)(2,1)S(1)} %get-tuple-element.27.refs_17_), channel_id=1, source_target_pairs={{0,16},{8,24},{16,0},{24,8},{1,17},{9,25},{17,1},{25,9},{2,18},{10... | collective-permute-start | bytes 1572872 | tf_op jit(solution)/shard_map/ppermute | solution.py:349
  38.8 4.3 %collective-permute-start.12 = (f32[16,512]{1,0:T(8,128)S(1)}, f32[16,512]{1,0:T(8,128)S(1)}, u32[]{:S(2)}, u32[]{:S(2)}) collective-permute-start(f32[16,512]{1,0:T(8,128)S(1)} %convert_reduce_fusion), channel_id=1, source_target_pairs={{0,16},{8,24},{16,0},{24,8},{1,17},{9,25},{17,1},{25,9},{2,18},{10... | collective-permute-start | bytes 98312 | tf_op jit(solution)/shard_map/ppermute | solution.py:349
  39.5 3.7 %collective-permute-start.10 = (f32[16,512]{1,0:T(8,128)S(1)}, f32[16,512]{1,0:T(8,128)S(1)}, u32[]{:S(2)}, u32[]{:S(2)}) collective-permute-start(f32[16,512]{1,0:T(8,128)S(1)} %convert_reduce_fusion), channel_id=1, source_target_pairs={{0,24},{8,16},{16,8},{24,0},{1,25},{9,17},{17,9},{25,1},{2,26},{10... | collective-permute-start | bytes 98312 | tf_op jit(solution)/shard_map/ppermute | solution.py:349
  39.5 3.7 %collective-permute-start.11 = (f32[16,512]{1,0:T(8,128)S(1)}, f32[16,512]{1,0:T(8,128)S(1)}, u32[]{:S(2)}, u32[]{:S(2)}) collective-permute-start(f32[16,512]{1,0:T(8,128)S(1)} %convert_reduce_fusion), channel_id=1, source_target_pairs={{0,8},{8,0},{16,24},{24,16},{1,9},{9,1},{17,25},{25,17},{2,10},{10... | collective-permute-start | bytes 98312 | tf_op jit(solution)/shard_map/ppermute | solution.py:349

commit v10 on v9

--- a/solution.py
+++ b/solution.py
@@ -115,10 +115,6 @@
     high, low = [[packed_rows[(2 * i + j) * rank : (2 * i + j + 1) * rank].astype(f32) for i in range(3)] for j in (0, 1)]
     query, own, sib = [a + b for a, b in zip(high, low)]
     return query, jnp.concatenate([own[:, :block], sib[:, :block]], 1)
-
-
-def columns(ref, at, width):
-    return ref[:, pl.ds(pl.multiple_of(at * width, width), width)]
 
 
 def scores_kernel(c_own, c_sib, q_own, q_sib, positives, hard, scores, stats):
@@ -180,16 +176,39 @@
     message[...] = message_of(shares, list(zip(tops, sums)), stats, factors[...], rows, block)
 
 
-def share_kernel(scores, answer, c_own, c_sib, weights, share):
+def log_total(chip, parts):
+    terms = [(chip[0], chip[1])]
+    for first, pairs in parts:
+        terms.append(pairs[0])
+        for (top, total), at in zip(pairs[1:], (first, first ^ 1)):
+            counts = chip[3].astype(jnp.int32) == at
+            terms.append((jnp.where(counts, top, pairs[0][0]), jnp.where(counts, total, 0.0)))
+    return merge(terms)
+
+
+def totals_kernel(block, stats, *refs):
+    answers, out = refs[:-1], refs[-1]
+    position = lax.axis_index("dp")
+    own = [stats[at : at + 1] for at in (MAX, SUM, POSITIVE, HARD)]
+    pairs = [message_parts(a, block)[1] for a in answers]
+    out[...] = stats[...]
+    out[MAX : MAX + 1] = log_total(own, [(position ^ (2 * i + 2), p) for i, p in enumerate(pairs)])
+
+
+def share_kernel(scores, answer, c_own, c_sib, *refs):
+    *totals, weights, share = refs
     block, rows = c_own.shape[0], scores.shape[1]
     far_top, far_total, positive, hard = sender_stats(answer, block)
     owner, slot = layout(lax.axis_index("dp"), block, scores.shape)
     total = jnp.where(allowed(owner, slot, hard, rows), scores[...], -jnp.inf)
     top = jnp.max(total, axis=0, keepdims=True)
     here = jnp.sum(jnp.exp(total - top), axis=0, keepdims=True)
-    log_total = merge([(far_top, far_total), (top, here)])
+    if totals:
+        log_sum = totals[0][MAX : MAX + 1]
+    else:
+        log_sum = merge([(far_top, far_total), (top, here)])
     hit = hits(owner, slot, positive, rows)
-    weights[...] = (jnp.exp(total - log_total) - hit.astype(f32)).astype(bf16)
+    weights[...] = (jnp.exp(total - log_sum) - hit.astype(f32)).astype(bf16)
     for i in range(share.shape[1] // STEP):
         at = slice(i * STEP, (i + 1) * STEP)
         c = jnp.concatenate([c_own[:, at], c_sib[:, at]], 0)
@@ -233,8 +252,8 @@
 
 def sums_kernel(partners, *refs):
     n = partners
-    (c, q, far_q, far_q_sib, hq, hc, (stats,), answers, sib_answers, made, made_sib, (factors, scores),
-     (w_grad, w_own, terms)) = taken(refs, 2, 2, n, n, 2, 2, 1, n, n, n, n, 2, 3)
+    (c, q, far_q, far_q_sib, hq, hc, (stats,), answers, sib_answers, made, made_sib, (factors, scores), totals,
+     (w_grad, w_own, terms)) = taken(refs, 2, 2, n, n, 2, 2, 1, n, n, n, n, 2, n if n > 1 else 0, 3)
     block, rows = c[0].shape[0], q[0].shape[0]
     shards, rank, width = terms.shape
     position = lax.axis_index("dp")
@@ -245,15 +264,6 @@
     answers = [message_parts(a, block) for a in answers]
     sib_answers = [message_parts(a, block, turned=True) for a in sib_answers]
 
-    def log_total(chip, parts):
-        terms = [(chip[0], chip[1])]
-        for first, pairs in parts:
-            terms.append(pairs[0])
-            for (top, total), at in zip(pairs[1:], (first, first ^ 1)):
-                counts = chip[3].astype(jnp.int32) == at
-                terms.append((jnp.where(counts, top, pairs[0][0]), jnp.where(counts, total, 0.0)))
-        return merge(terms)
-
     def scaled(first, shares, tops, log_totals, positive, hard):
         owner, slot = layout(first, block, shares.shape)
         top = jnp.where(slot < rows, tops[0], jnp.where(owner == first, tops[1], tops[2]))
@@ -274,9 +284,9 @@
     near = near.astype(bf16)
     w_own[...] = near[:, :rows]
     pieces = [near]
-    for mine, other, chip in zip(made, made_sib, far_stats):
+    for i, (mine, other, chip) in enumerate(zip(made, made_sib, far_stats)):
         shares, pairs = message_parts(other, block, turned=True)
-        far_total = log_total(chip, [(position, pairs)])
+        far_total = totals[i][MAX : MAX + 1] if totals else log_total(chip, [(position, pairs)])
         pieces += [mine[...], scaled(position, shares, [top for top, _ in pairs], far_total, chip[2], chip[3])]
     weights = jnp.concatenate(pieces, 1)
     w_grad[...] = weights[:block]
@@ -320,23 +330,23 @@
             terms[i] = (dot(back_q, from_q, 1, 0) + dot(back_c, from_c, 1, 0)).astype(bf16)
 
 
-def call(kernel, outs, needs=(), cost=0, scratch=(), away=False, keeps=()):
+def call(kernel, outs, needs=(), cost=0, scratch=(), away=False):
     vmem = pl.BlockSpec(memory_space=pltpu.VMEM)
     anywhere = pl.BlockSpec(memory_space=pl.ANY)
 
     def run(*args):
         def body(*refs):
-            kernel(*refs[: len(args)], *refs[len(args) + len(keeps) + len(needs) :])
+            kernel(*refs[: len(args)], *refs[len(args) + len(needs) :])
 
         return pl.pallas_call(
             body,
             out_shape=outs,
-            in_specs=[vmem] * (len(args) + len(keeps)) + [anywhere] * len(needs),
+            in_specs=[vmem] * len(args) + [anywhere] * len(needs),
             out_specs=jax.tree.map(lambda _: anywhere if away else vmem, outs),
             scratch_shapes=list(scratch),
             compiler_params=pltpu.CompilerParams(vmem_limit_bytes=16 * 2**20),
             cost_estimate=pl.CostEstimate(flops=1000 + cost, bytes_accessed=1000 + cost // 300, transcendentals=0),
-        )(*args, *keeps, *needs)
+        )(*args, *needs)
 
     return run
 
@@ -381,8 +391,9 @@
     )
 
     made, made_sib, answers, sib_answers, far_q_near, far_q_sib, sent, shares = [], [], [], [], [], [], [], []
+    far_scores = []
     for k, q in zip(partners, far_q):
-        message, far_scores, q_again = call(
+        message, far, q_again = call(
             partner_kernel,
             (
                 shaped((2 * block + EXTRA + 6 * rank, 2 * rows), bf16),
@@ -393,14 +404,21 @@
         answers.append(swap(message, "dp", k))
         made_sib.append(swap(message, "dp", 1))
         sib_answers.append(swap(answers[-1], "dp", 1))
-        weights, share = call(share_kernel, (shaped((2 * block, rows), bf16), shaped((rows, width), bf16)), [made_sib[-1]])(
-            far_scores, answers[-1], c_own, c_sib
-        )
-        made.append(weights)
+        far_scores.append(far)
         far_q_near.append(q_again)
         far_q_sib.append(swap(q_again, "dp", 1))
+    far_totals, sib_totals = [], []
+    if len(partners) > 1:
+        totals = call(functools.partial(totals_kernel, block), shaped((STATS, rows)))(stats, *answers)
+        far_totals = [swap(totals, "dp", k) for k in partners]
+        sib_totals = [swap(total, "dp", 1) for total in far_totals]
+    for i, k in enumerate(partners):
+        weights, share = call(
+            share_kernel, (shaped((2 * block, rows), bf16), shaped((rows, width), bf16)), [made_sib[i]]
+        )(far_scores[i], answers[i], c_own, c_sib, *far_totals[i : i + 1])
+        made.append(weights)
         sent.append(share)
-        shares.append(swap(after(share, sib_answers[-1]), "dp", k))
+        shares.append(swap(after(share, sib_answers[i]), "dp", k))
 
     w_grad, w_own, terms = call(
         functools.partial(sums_kernel, len(partners)),
@@ -412,7 +430,7 @@
         sent,
     )(
         c_own, c_sib, q_own, q_sib, *far_q_near, *far_q_sib, hq, hq_sib, hc, hc_sib, stats,
-        *answers, *sib_answers, *made, *made_sib, factors, scores,
+        *answers, *sib_answers, *made, *made_sib, factors, scores, *sib_totals,
     )
     queries = [q_own, q_sib]
     for pair in zip(far_q_near, far_q_sib):

time: 44.1 us -> 44.1 us (level)
  no operation moved by 1% of the time
where the time goes in v10:
time: 44.1 us; the launch traced here: 43.8 us
  blocking collectives  24.7 us (56%)
  starting transfers between devices  7.3 us (17%)
  waiting for transfers between devices  5.32 us (12%)
  Pallas kernels  4.99 us (11%)
  between operations  0.79 us (2%)
  other arithmetic  0.67 us (2%)
    all_to_all x1, blocking collectives, on_device(): maps = lax.all_to_all(mine, 'fsdp', 0, 0)  13.9 us
    all_to_all x1, blocking collectives, on_device(): terms = lax.all_to_all(terms, 'fsdp', 0, 0)  10.8 us
    ppermute x13, starting transfers between devices, swap(): lax.ppermute(array, axis, [(i, i ^ apart) for i in range(lax.axis_size(ax...  7.3 us
    ppermute x13, waiting for transfers between devices, swap(): lax.ppermute(array, axis, [(i, i ^ apart) for i in range(lax.axis_size(ax...  5.32 us
    pallas_call x7, Pallas kernels, run(): pl.pallas_call(body, out_shape=outs, in_specs=[vmem] * len(args) + [anywh...  4.99 us
  transfers between devices with their start and end apart: 13, of which 4 were waited for; matrix products, arithmetic and copies ran while one was open for 0% of the time, Pallas kernels for 10%

profile of v10, /device:TPU:0, one launch (start us, length us, event | category | flops | bytes accessed | tf_op | source)
XLA Modules:
  0.0 43.8 jit_solution(11468020464560106180)
XLA Ops:
  0.6 0.0 copy-start.6
  0.6 0.5 %collective-permute-start.1 = (bf16[64,4096]{1,0:T(8,128)(2,1)}, bf16[64,4096]{1,0:T(8,128)(2,1)S(1)}, u32[]{:S(2)}, u32[]{:S(2)}) collective-permute-start(bf16[64,4096]{1,0:T(8,128)(2,1)} %bitcast.13), channel_id=1, source_target_pairs={{0,8},{8,0},{16,24},{24,16},{1,9},{9,1},{17,25},{25,17},{2,10},{10... | collective-permute-start | bytes 1572872 | tf_op jit(solution)/shard_map/ppermute | solution.py:359
  1.2 2.6 %collective-permute-start.2 = (bf16[64,4096]{1,0:T(8,128)(2,1)}, bf16[64,4096]{1,0:T(8,128)(2,1)S(1)}, u32[]{:S(2)}, u32[]{:S(2)}) collective-permute-start(bf16[64,4096]{1,0:T(8,128)(2,1)} %bitcast.14), channel_id=1, source_target_pairs={{0,16},{8,24},{16,0},{24,8},{1,17},{9,25},{17,1},{25,9},{2,18},{10... | collective-permute-start | bytes 1572872 | tf_op jit(solution)/shard_map/ppermute | solution.py:359
  3.7 0.2 collective-permute-start
  3.9 0.3 collective-permute-start.3
  4.2 0.2 collective-permute-start.4
  4.4 0.0 copy-done.6
  4.4 0.0 copy-start
  4.4 0.0 copy-start.1
  4.4 0.0 copy-start.2
  4.5 0.0 copy-start.3
  4.5 13.9 %all_to_all.10.refs_0_ = bf16[8,16,512]{2,1,0:T(8,128)(2,1)S(1)} all-to-all(bf16[8,16,512]{2,1,0:T(8,128)(2,1)S(1)} %shard_map.111), channel_id=1, replica_groups=mesh['dp'=4,'fsdp'=8] {'fsdp'}, dimensions={0} | all-to-all | bytes 262144 | tf_op jit(solution)/shard_map/all_to_all | solution.py:384
  18.4 0.0 copy-start.4
  18.4 0.0 copy-start.5
  18.4 0.0 collective-permute-done.1.refs_8_.refs_3_.refs_5_
  18.4 0.0 collective-permute-done.3.refs_2_.refs_7_
  18.4 0.0 collective-permute-done.refs_6_.refs_1_.refs_3_
  18.5 0.0 collective-permute-done.4.refs_4_.refs_9_
  18.5 0.0 copy-done
  18.5 0.0 copy-done.1
  18.5 0.0 copy-done.2
  18.5 0.0 copy-done.3
  18.5 0.8 %shard_map.112.refs_6_.refs_4_.refs_15_ = f32[16,288]{1,0:T(8,128)S(1)} custom-call(bf16[8,16,512]{2,1,0:T(8,128)(2,1)S(1)} %all_to_all.10.refs_0_, bf16[64,4096]{1,0:T(8,128)(2,1)S(1)} %bitcast.23, bf16[64,4096]{1,0:T(8,128)(2,1)S(1)} %collective-permute-done.3.refs_2_.refs_7_, bf16[80,4096]{1,0:T(8,128)(2,1)S(1)} %bitcast.20, ...), custom_call_target="tpu_custom_call" | custom-call | flops 1000 | bytes 1000 | tf_op jit(solution)/shard_map/pallas_call | solution.py:341
  19.3 0.0 copy-done.4
  19.3 0.0 copy-done.5
  19.3 0.6 %shard_map.113 = (f32[160,128]{1,0:T(8,128)S(1)}, f32[8,64]{1,0:T(8,128)S(1)}) custom-call(bf16[80,4096]{1,0:T(8,128)(2,1)S(1)} %bitcast.8, bf16[80,4096]{1,0:T(8,128)(2,1)S(1)} %collective-permute-done.refs_6_.refs_1_.refs_3_, bf16[64,4096]{1,0:T(8,128)(2,1)S(1)} %bitcast.16, bf16[64,4096]{1,0:T(8,128)(2,1)S(1)} %collective-permute-done.1.refs_8_.refs_3_.refs_5_, ...), custom_call_target="tpu_custom_call" | custom-call | flops 1000 | bytes 1000 | tf_op jit(solution)/shard_map/pallas_call | solution.py:341
  19.9 0.0 collective-permute-done.2.refs_2_
  19.9 0.6 %shard_map.114 = (bf16[288,128]{1,0:T(8,128)(2,1)S(1)}, f32[160,64]{1,0:T(8,128)S(1)}, bf16[64,4096]{1,0:T(8,128)(2,1)S(1)}) custom-call(bf16[80,4096]{1,0:T(8,128)(2,1)S(1)} %bitcast.9, bf16[80,4096]{1,0:T(8,128)(2,1)S(1)} %collective-permute-done.refs_6_.refs_1_.refs_3_, bf16[64,4096]{1,0:T(8,128)(2,1)S(1)} %collective-permute-done.2.refs_2_, ...), custom_call_target="tpu_custom_call" | custom-call | flops 1000 | bytes 1000 | tf_op jit(solution)/shard_map/pallas_call | solution.py:341
  20.5 0.1 collective-permute-start.5
  20.6 0.6 %collective-permute-start.6 = (bf16[288,128]{1,0:T(8,128)(2,1)S(1)}, bf16[288,128]{1,0:T(8,128)(2,1)S(1)}, u32[]{:S(2)}, u32[]{:S(2)}) collective-permute-start(bf16[288,128]{1,0:T(8,128)(2,1)S(1)} %get-tuple-element.20), channel_id=1, source_target_pairs={{0,16},{8,24},{16,0},{24,8},{1,17},{9,25},{17,1},{25,9},{2,18},{10... | collective-permute-start | bytes 221192 | tf_op jit(solution)/shard_map/ppermute | solution.py:359
  21.2 0.2 collective-permute-start.8
  21.4 3.9 %collective-permute-done.6.refs_1_.refs_11_ = bf16[288,128]{1,0:T(8,128)(2,1)S(1)} collective-permute-done((bf16[288,128]{1,0:T(8,128)(2,1)S(1)}, bf16[288,128]{1,0:T(8,128)(2,1)S(1)}, u32[]{:S(2)}, u32[]{:S(2)}) %collective-permute-start.6) | collective-permute-done | bytes 73760 | tf_op jit(solution)/shard_map/ppermute | solution.py:359
  25.3 0.0 collective-permute-start.7
  25.3 0.0 collective-permute-done.8.refs_4_.refs_14_
  25.3 0.5 %shard_map.115 = (bf16[160,64]{1,0:T(8,128)(2,1)S(1)}, bf16[64,4096]{1,0:T(8,128)(2,1)S(1)}) custom-call(f32[160,64]{1,0:T(8,128)S(1)} %get-tuple-element.21.refs_0_, bf16[288,128]{1,0:T(8,128)(2,1)S(1)} %collective-permute-done.6.refs_1_.refs_11_, bf16[80,4096]{1,0:T(8,128)(2,1)S(1)} %bitcast.10, ...), custom_call_target="tpu_custom_call" | custom-call | flops 1000 | bytes 1000 | tf_op jit(solution)/shard_map/pallas_call | solution.py:341
  25.8 0.8 %collective-permute-done.7.refs_12_ = bf16[288,128]{1,0:T(8,128)(2,1)S(1)} collective-permute-done((bf16[288,128]{1,0:T(8,128)(2,1)S(1)}, bf16[288,128]{1,0:T(8,128)(2,1)S(1)}, u32[]{:S(2)}, u32[]{:S(2)}) %collective-permute-start.7) | collective-permute-done | bytes 73760 | tf_op jit(solution)/shard_map/ppermute | solution.py:359
  26.6 0.5 %collective-permute-start.9 = (bf16[64,4096]{1,0:T(8,128)(2,1)S(1)}, bf16[64,4096]{1,0:T(8,128)(2,1)S(1)}, u32[]{:S(2)}, u32[]{:S(2)}) collective-permute-start(bf16[64,4096]{1,0:T(8,128)(2,1)S(1)} %get-tuple-element.27.refs_17_), channel_id=1, source_target_pairs={{0,16},{8,24},{16,0},{24,8},{1,17},{9,25},{17,1},{25,9},{2,18},{10... | collective-permute-start | bytes 1572872 | tf_op jit(solution)/shard_map/ppermute | solution.py:359
  27.1 0.0 collective-permute-done.5.refs_5_.refs_7_
  27.1 0.9 %shard_map.116 = (bf16[80,256]{1,0:T(8,128)(2,1)S(1)}, bf16[160,64]{1,0:T(8,128)(2,1)S(1)}, bf16[8,16,512]{2,1,0:T(8,128)(2,1)S(1)}) custom-call(bf16[80,4096]{1,0:T(8,128)(2,1)S(1)} %bitcast.11, bf16[80,4096]{1,0:T(8,128)(2,1)S(1)} %collective-permute-done.refs_6_.refs_1_.refs_3_, bf16[64,4096]{1,0:T(8,128)(2,1)S(1)} %bitcast.17, ...), custom_call_target="tpu_custom_call" | custom-call | flops 1000 | bytes 1000 | tf_op jit(solution)/shard_map/pallas_call | solution.py:341
  28.0 10.8 %all_to_all.11 = bf16[8,16,512]{2,1,0:T(8,128)(2,1)S(1)} all-to-all(bf16[8,16,512]{2,1,0:T(8,128)(2,1)S(1)} %get-tuple-element.30), channel_id=1, replica_groups=mesh['dp'=4,'fsdp'=8] {'fsdp'}, dimensions={0} | all-to-all | bytes 262144 | tf_op jit(solution)/shard_map/all_to_all | solution.py:446
  38.8 0.7 %collective-permute-start.12 = (f32[16,512]{1,0:T(8,128)S(1)}, f32[16,512]{1,0:T(8,128)S(1)}, u32[]{:S(2)}, u32[]{:S(2)}) collective-permute-start(f32[16,512]{1,0:T(8,128)S(1)} %convert_reduce_fusion), channel_id=1, source_target_pairs={{0,16},{8,24},{16,0},{24,8},{1,17},{9,25},{17,1},{25,9},{2,18},{10... | collective-permute-start | bytes 98312 | tf_op jit(solution)/shard_map/ppermute | solution.py:359
  39.5 0.0 collective-permute-start.10
  39.5 1.5 %collective-permute-start.11 = (f32[16,512]{1,0:T(8,128)S(1)}, f32[16,512]{1,0:T(8,128)S(1)}, u32[]{:S(2)}, u32[]{:S(2)}) collective-permute-start(f32[16,512]{1,0:T(8,128)S(1)} %convert_reduce_fusion), channel_id=1, source_target_pairs={{0,8},{8,0},{16,24},{24,16},{1,9},{9,1},{17,25},{25,17},{2,10},{10... | collective-permute-start | bytes 98312 | tf_op jit(solution)/shard_map/ppermute | solution.py:359
  41.0 0.0 collective-permute-done.9.refs_8_
  41.0 1.5 %shard_map.117 = (bf16[64,4096]{1,0:T(8,128)(2,1)}, bf16[80,4096]{1,0:T(8,128)(2,1)}) custom-call(bf16[160,64]{1,0:T(8,128)(2,1)S(1)} %get-tuple-element.25.refs_0_, bf16[80,256]{1,0:T(8,128)(2,1)S(1)} %get-tuple-element.26.refs_1_, bf16[80,4096]{1,0:T(8,128)(2,1)S(1)} %bitcast.12, bf16[80,4096]{1,0:T(8,128)(2,1)S(1)} %collective-permute-done.refs_6_.refs_1_.refs_3_, ...), custom_call_target="tpu_custom_call" | custom-call | flops 1000 | bytes 1000 | tf_op jit(solution)/shard_map/pallas_call | solution.py:341
  42.6 0.5 %collective-permute-done.12 = f32[16,512]{1,0:T(8,128)S(1)} collective-permute-done((f32[16,512]{1,0:T(8,128)S(1)}, f32[16,512]{1,0:T(8,128)S(1)}, u32[]{:S(2)}, u32[]{:S(2)}) %collective-permute-start.12) | collective-permute-done | bytes 32800 | tf_op jit(solution)/shard_map/ppermute | solution.py:359
  43.1 0.1 collective-permute-done.10
  43.2 0.0 collective-permute-done.11
  43.2 0.6 %broadcast_select_fusion = (f32[16,512]{1,0:T(8,128)}, f32[16,512]{1,0:T(8,128)}) fusion(pred[]{:T(512)S(6)} %eq.3, f32[16,512]{1,0:T(8,128)S(1)} %collective-permute-done.10, f32[16,512]{1,0:T(8,128)S(1)} %collective-permute-done.11, f32[16,512]{1,0:T(8,128)S(1)} %convert_reduce_fusion, f32[16,512]{1,0:T(8,128)S(1)} %collective-permute-done.12), kind=kLoop, calls=%fused_computation.3 | loop fusion | flops 49152 | bytes 196609 | tf_op jit(solution)/shard_map/jit(_where)/select_n | solution.py:460
  (3 shorter events, 0.0 us)
Async XLA Ops:
  0.6 3.8 %copy-start.6 = (bf16[16,512]{1,0:T(8,128)(2,1)S(1)}, bf16[16,512]{1,0:T(8,128)(2,1)}, u32[]{:S(2)}) copy-start(bf16[16,512]{1,0:T(8,128)(2,1)} %param.14) | copy-start | bytes 49156
  0.6 17.8 %collective-permute-start.1 = (bf16[64,4096]{1,0:T(8,128)(2,1)}, bf16[64,4096]{1,0:T(8,128)(2,1)S(1)}, u32[]{:S(2)}, u32[]{:S(2)}) collective-permute-start(bf16[64,4096]{1,0:T(8,128)(2,1)} %bitcast.13), channel_id=1, source_target_pairs={{0,8},{8,0},{16,24},{24,16},{1,9},{9,1},{17,25},{25,17},{2,10},{10... | collective-permute-start | bytes 1572872 | tf_op jit(solution)/shard_map/ppermute | solution.py:359
  1.2 18.7 %collective-permute-start.2 = (bf16[64,4096]{1,0:T(8,128)(2,1)}, bf16[64,4096]{1,0:T(8,128)(2,1)S(1)}, u32[]{:S(2)}, u32[]{:S(2)}) collective-permute-start(bf16[64,4096]{1,0:T(8,128)(2,1)} %bitcast.14), channel_id=1, source_target_pairs={{0,16},{8,24},{16,0},{24,8},{1,17},{9,25},{17,1},{25,9},{2,18},{10... | collective-permute-start | bytes 1572872 | tf_op jit(solution)/shard_map/ppermute | solution.py:359
  3.7 14.7 %collective-permute-start = (bf16[80,4096]{1,0:T(8,128)(2,1)}, bf16[80,4096]{1,0:T(8,128)(2,1)S(1)}, u32[]{:S(2)}, u32[]{:S(2)}) collective-permute-start(bf16[80,4096]{1,0:T(8,128)(2,1)} %bitcast.6), channel_id=1, source_target_pairs={{0,8},{8,0},{16,24},{24,16},{1,9},{9,1},{17,25},{25,17},{2,10},{10... | collective-permute-start | bytes 1966088 | tf_op jit(solution)/shard_map/ppermute | solution.py:359
  3.9 14.5 %collective-permute-start.3 = (bf16[64,4096]{1,0:T(8,128)(2,1)}, bf16[64,4096]{1,0:T(8,128)(2,1)S(1)}, u32[]{:S(2)}, u32[]{:S(2)}) collective-permute-start(bf16[64,4096]{1,0:T(8,128)(2,1)} %bitcast.22), channel_id=1, source_target_pairs={{0,8},{8,0},{16,24},{24,16},{1,9},{9,1},{17,25},{25,17},{2,10},{10... | collective-permute-start | bytes 1572872 | tf_op jit(solution)/shard_map/ppermute | solution.py:359
  4.2 14.2 %collective-permute-start.4 = (bf16[80,4096]{1,0:T(8,128)(2,1)}, bf16[80,4096]{1,0:T(8,128)(2,1)S(1)}, u32[]{:S(2)}, u32[]{:S(2)}) collective-permute-start(bf16[80,4096]{1,0:T(8,128)(2,1)} %bitcast.19), channel_id=1, source_target_pairs={{0,8},{8,0},{16,24},{24,16},{1,9},{9,1},{17,25},{25,17},{2,10},{10... | collective-permute-start | bytes 1966088 | tf_op jit(solution)/shard_map/ppermute | solution.py:359
  4.4 14.0 %copy-start = (bf16[1,1,80,4096]{3,2,1,0:T(8,128)(2,1)S(1)}, bf16[1,1,80,4096]{3,2,1,0:T(8,128)(2,1)}, u32[]{:S(2)}) copy-start(bf16[1,1,80,4096]{3,2,1,0:T(8,128)(2,1)} %param.9) | copy-start | bytes 1966084
  4.4 14.0 %copy-start.1 = (bf16[1,64,4096]{2,1,0:T(8,128)(2,1)S(1)}, bf16[1,64,4096]{2,1,0:T(8,128)(2,1)}, u32[]{:S(2)}) copy-start(bf16[1,64,4096]{2,1,0:T(8,128)(2,1)} %param.8) | copy-start | bytes 1572868
  4.4 14.0 %copy-start.2 = (bf16[1,1,80,4096]{3,2,1,0:T(8,128)(2,1)S(1)}, bf16[1,1,80,4096]{3,2,1,0:T(8,128)(2,1)}, u32[]{:S(2)}) copy-start(bf16[1,1,80,4096]{3,2,1,0:T(8,128)(2,1)} %param.13) | copy-start | bytes 1966084
  4.5 14.0 %copy-start.3 = (bf16[1,64,4096]{2,1,0:T(8,128)(2,1)S(1)}, bf16[1,64,4096]{2,1,0:T(8,128)(2,1)}, u32[]{:S(2)}) copy-start(bf16[1,64,4096]{2,1,0:T(8,128)(2,1)} %param.12) | copy-start | bytes 1572868
  18.4 0.9 %copy-start.4 = (s32[1,64]{1,0:T(1,128)S(1)}, s32[1,64]{1,0:T(1,128)}, u32[]{:S(2)}) copy-start(s32[1,64]{1,0:T(1,128)} %refs_4_.1) | copy-start | bytes 772
  18.4 0.9 %copy-start.5 = (s32[1,64]{1,0:T(1,128)S(1)}, s32[1,64]{1,0:T(1,128)}, u32[]{:S(2)}) copy-start(s32[1,64]{1,0:T(1,128)} %refs_5_.1) | copy-start | bytes 772
  20.5 6.5 %collective-permute-start.5 = (bf16[64,4096]{1,0:T(8,128)(2,1)S(1)}, bf16[64,4096]{1,0:T(8,128)(2,1)S(1)}, u32[]{:S(2)}, u32[]{:S(2)}) collective-permute-start(bf16[64,4096]{1,0:T(8,128)(2,1)S(1)} %get-tuple-element.19.refs_4_.refs_6_), channel_id=1, source_target_pairs={{0,8},{8,0},{16,24},{24,16},{1,9},{9,1},{17,25},{25,17},{2,10},{10... | collective-permute-start | bytes 1572872 | tf_op jit(solution)/shard_map/ppermute | solution.py:359
  20.6 4.7 %collective-permute-start.6 = (bf16[288,128]{1,0:T(8,128)(2,1)S(1)}, bf16[288,128]{1,0:T(8,128)(2,1)S(1)}, u32[]{:S(2)}, u32[]{:S(2)}) collective-permute-start(bf16[288,128]{1,0:T(8,128)(2,1)S(1)} %get-tuple-element.20), channel_id=1, source_target_pairs={{0,16},{8,24},{16,0},{24,8},{1,17},{9,25},{17,1},{25,9},{2,18},{10... | collective-permute-start | bytes 221192 | tf_op jit(solution)/shard_map/ppermute | solution.py:359
  21.2 4.1 %collective-permute-start.8 = (bf16[288,128]{1,0:T(8,128)(2,1)S(1)}, bf16[288,128]{1,0:T(8,128)(2,1)S(1)}, u32[]{:S(2)}, u32[]{:S(2)}) collective-permute-start(bf16[288,128]{1,0:T(8,128)(2,1)S(1)} %get-tuple-element.20), channel_id=1, source_target_pairs={{0,8},{8,0},{16,24},{24,16},{1,9},{9,1},{17,25},{25,17},{2,10},{10... | collective-permute-start | bytes 221192 | tf_op jit(solution)/shard_map/ppermute | solution.py:359
  25.3 1.3 %collective-permute-start.7 = (bf16[288,128]{1,0:T(8,128)(2,1)S(1)}, bf16[288,128]{1,0:T(8,128)(2,1)S(1)}, u32[]{:S(2)}, u32[]{:S(2)}) collective-permute-start(bf16[288,128]{1,0:T(8,128)(2,1)S(1)} %collective-permute-done.6.refs_1_.refs_11_), channel_id=1, source_target_pairs={{0,8},{8,0},{16,24},{24,16},{1,9},{9,1},{17,25},{25,17},{2,10},{10... | collective-permute-start | bytes 221192 | tf_op jit(solution)/shard_map/ppermute | solution.py:359
  26.6 14.5 %collective-permute-start.9 = (bf16[64,4096]{1,0:T(8,128)(2,1)S(1)}, bf16[64,4096]{1,0:T(8,128)(2,1)S(1)}, u32[]{:S(2)}, u32[]{:S(2)}) collective-permute-start(bf16[64,4096]{1,0:T(8,128)(2,1)S(1)} %get-tuple-element.27.refs_17_), channel_id=1, source_target_pairs={{0,16},{8,24},{16,0},{24,8},{1,17},{9,25},{17,1},{25,9},{2,18},{10... | collective-permute-start | bytes 1572872 | tf_op jit(solution)/shard_map/ppermute | solution.py:359
  38.8 4.3 %collective-permute-start.12 = (f32[16,512]{1,0:T(8,128)S(1)}, f32[16,512]{1,0:T(8,128)S(1)}, u32[]{:S(2)}, u32[]{:S(2)}) collective-permute-start(f32[16,512]{1,0:T(8,128)S(1)} %convert_reduce_fusion), channel_id=1, source_target_pairs={{0,16},{8,24},{16,0},{24,8},{1,17},{9,25},{17,1},{25,9},{2,18},{10... | collective-permute-start | bytes 98312 | tf_op jit(solution)/shard_map/ppermute | solution.py:359
  39.5 3.7 %collective-permute-start.10 = (f32[16,512]{1,0:T(8,128)S(1)}, f32[16,512]{1,0:T(8,128)S(1)}, u32[]{:S(2)}, u32[]{:S(2)}) collective-permute-start(f32[16,512]{1,0:T(8,128)S(1)} %convert_reduce_fusion), channel_id=1, source_target_pairs={{0,24},{8,16},{16,8},{24,0},{1,25},{9,17},{17,9},{25,1},{2,26},{10... | collective-permute-start | bytes 98312 | tf_op jit(solution)/shard_map/ppermute | solution.py:359
  39.5 3.7 %collective-permute-start.11 = (f32[16,512]{1,0:T(8,128)S(1)}, f32[16,512]{1,0:T(8,128)S(1)}, u32[]{:S(2)}, u32[]{:S(2)}) collective-permute-start(f32[16,512]{1,0:T(8,128)S(1)} %convert_reduce_fusion), channel_id=1, source_target_pairs={{0,8},{8,0},{16,24},{24,16},{1,9},{9,1},{17,25},{25,17},{2,10},{10... | collective-permute-start | bytes 98312 | tf_op jit(solution)/shard_map/ppermute | solution.py:359

commit v11 on v10

--- a/solution.py
+++ b/solution.py
@@ -139,7 +139,8 @@
         out[i] = own[...]
 
 
-def adapter_kernel(maps, hq, hq_sib, hc, hc_sib, c_own, c_sib, q_own, q_sib, factors):
+def chip_kernel(maps, hq, hq_sib, hc, hc_sib, c_own, c_sib, q_own, q_sib, positives, hard, factors, scores, stats):
+    scores_kernel(c_own, c_sib, q_own, q_sib, positives, hard, scores, stats)
     shards, _, width = maps.shape
 
     def product(parts):
@@ -383,12 +384,10 @@
     )
     maps = lax.all_to_all(mine, "fsdp", 0, 0)
 
-    factors = call(adapter_kernel, shaped((rank, 2 * rows + 2 * block)))(
-        maps, hq, hq_sib, hc, hc_sib, c_own, c_sib, q_own, q_sib
-    )
-    scores, stats = call(scores_kernel, (shaped((2 * block, 2 * rows)), shaped((STATS, rows))), [factors])(
-        c_own, c_sib, q_own, q_sib, positives, hard_blocks
-    )
+    factors, scores, stats = call(
+        chip_kernel,
+        (shaped((rank, 2 * rows + 2 * block)), shaped((2 * block, 2 * rows)), shaped((STATS, rows))),
+    )(maps, hq, hq_sib, hc, hc_sib, c_own, c_sib, q_own, q_sib, positives, hard_blocks)
 
     made, made_sib, answers, sib_answers, far_q_near, far_q_sib, sent, shares = [], [], [], [], [], [], [], []
     far_scores = []

time: 44.1 us -> 44 us (level)
    pallas_call x7 -> x6, Pallas kernels: 4.99 us -> 4.93 us  [run(): pl.pallas_call(body, out_shape=outs, in_specs=[vmem] * len(args) + [anywh...]
  transfers between devices with their start and end apart: 13 -> 13, of which waited for: 4 -> 3; matrix products, arithmetic and copies ran while one was open for 0% -> 0% of each run, Pallas kernels for 10% -> 10%
where the time goes in v11:
time: 44 us; the launch traced here: 43.8 us
  blocking collectives  24.7 us (56%)
  starting transfers between devices  7.31 us (17%)
  waiting for transfers between devices  5.29 us (12%)
  Pallas kernels  4.93 us (11%)
  between operations  0.81 us (2%)
  other arithmetic  0.67 us (2%)
    all_to_all x1, blocking collectives, on_device(): maps = lax.all_to_all(mine, 'fsdp', 0, 0)  13.9 us
    all_to_all x1, blocking collectives, on_device(): terms = lax.all_to_all(terms, 'fsdp', 0, 0)  10.8 us
    ppermute x13, starting transfers between devices, swap(): lax.ppermute(array, axis, [(i, i ^ apart) for i in range(lax.axis_size(ax...  7.31 us
    ppermute x13, waiting for transfers between devices, swap(): lax.ppermute(array, axis, [(i, i ^ apart) for i in range(lax.axis_size(ax...  5.29 us
    pallas_call x6, Pallas kernels, run(): pl.pallas_call(body, out_shape=outs, in_specs=[vmem] * len(args) + [anywh...  4.93 us
  transfers between devices with their start and end apart: 13, of which 3 were waited for; matrix products, arithmetic and copies ran while one was open for 0% of the time, Pallas kernels for 10%

profile of v11, /device:TPU:0, one launch (start us, length us, event | category | flops | bytes accessed | tf_op | source)
XLA Modules:
  0.0 43.8 jit_solution(4220240390828202159)
XLA Ops:
  0.6 0.0 copy-start.6
  0.6 0.5 %collective-permute-start.1 = (bf16[64,4096]{1,0:T(8,128)(2,1)}, bf16[64,4096]{1,0:T(8,128)(2,1)S(1)}, u32[]{:S(2)}, u32[]{:S(2)}) collective-permute-start(bf16[64,4096]{1,0:T(8,128)(2,1)} %bitcast.12), channel_id=1, source_target_pairs={{0,8},{8,0},{16,24},{24,16},{1,9},{9,1},{17,25},{25,17},{2,10},{10... | collective-permute-start | bytes 1572872 | tf_op jit(solution)/shard_map/ppermute | solution.py:360
  1.2 2.6 %collective-permute-start.2 = (bf16[64,4096]{1,0:T(8,128)(2,1)}, bf16[64,4096]{1,0:T(8,128)(2,1)S(1)}, u32[]{:S(2)}, u32[]{:S(2)}) collective-permute-start(bf16[64,4096]{1,0:T(8,128)(2,1)} %bitcast.13), channel_id=1, source_target_pairs={{0,16},{8,24},{16,0},{24,8},{1,17},{9,25},{17,1},{25,9},{2,18},{10... | collective-permute-start | bytes 1572872 | tf_op jit(solution)/shard_map/ppermute | solution.py:360
  3.7 0.2 collective-permute-start
  3.9 0.3 collective-permute-start.3
  4.2 0.2 collective-permute-start.4
  4.4 0.0 copy-done.6
  4.4 0.0 copy-start
  4.4 0.0 copy-start.1
  4.4 0.0 copy-start.2
  4.5 0.0 copy-start.3
  4.5 0.0 copy-start.4
  4.5 0.0 copy-start.5
  4.5 13.9 %all_to_all.10.refs_0_ = bf16[8,16,512]{2,1,0:T(8,128)(2,1)S(1)} all-to-all(bf16[8,16,512]{2,1,0:T(8,128)(2,1)S(1)} %shard_map.111), channel_id=1, replica_groups=mesh['dp'=4,'fsdp'=8] {'fsdp'}, dimensions={0} | all-to-all | bytes 262144 | tf_op jit(solution)/shard_map/all_to_all | solution.py:385
  18.5 0.0 collective-permute-done.1.refs_8_.refs_3_.refs_5_
  18.5 0.0 collective-permute-done.3.refs_2_.refs_7_
  18.5 0.0 collective-permute-done.refs_6_.refs_1_.refs_3_
  18.5 0.0 collective-permute-done.4.refs_4_.refs_9_
  18.5 0.0 copy-done
  18.5 0.0 copy-done.1
  18.5 0.0 copy-done.2
  18.5 0.0 copy-done.3
  18.5 0.0 copy-done.4
  18.5 0.0 copy-done.5
  18.5 1.3 %shard_map.112 = (f32[16,288]{1,0:T(8,128)S(1)}, f32[160,128]{1,0:T(8,128)S(1)}, f32[8,64]{1,0:T(8,128)S(1)}) custom-call(bf16[8,16,512]{2,1,0:T(8,128)(2,1)S(1)} %all_to_all.10.refs_0_, bf16[64,4096]{1,0:T(8,128)(2,1)S(1)} %bitcast.21, bf16[64,4096]{1,0:T(8,128)(2,1)S(1)} %collective-permute-done.3.refs_2_.refs_7_, bf16[80,4096]{1,0:T(8,128)(2,1)S(1)} %bitcast.18, ...), custom_call_target="tpu_custom_call" | custom-call | flops 1000 | bytes 1000 | tf_op jit(solution)/shard_map/pallas_call | solution.py:342
  19.9 0.0 collective-permute-done.2.refs_2_
  19.9 0.6 %shard_map.113 = (bf16[288,128]{1,0:T(8,128)(2,1)S(1)}, f32[160,64]{1,0:T(8,128)S(1)}, bf16[64,4096]{1,0:T(8,128)(2,1)S(1)}) custom-call(bf16[80,4096]{1,0:T(8,128)(2,1)S(1)} %bitcast.8, bf16[80,4096]{1,0:T(8,128)(2,1)S(1)} %collective-permute-done.refs_6_.refs_1_.refs_3_, bf16[64,4096]{1,0:T(8,128)(2,1)S(1)} %collective-permute-done.2.refs_2_, ...), custom_call_target="tpu_custom_call" | custom-call | flops 1000 | bytes 1000 | tf_op jit(solution)/shard_map/pallas_call | solution.py:342
  20.5 0.1 collective-permute-start.5
  20.6 0.6 %collective-permute-start.6 = (bf16[288,128]{1,0:T(8,128)(2,1)S(1)}, bf16[288,128]{1,0:T(8,128)(2,1)S(1)}, u32[]{:S(2)}, u32[]{:S(2)}) collective-permute-start(bf16[288,128]{1,0:T(8,128)(2,1)S(1)} %get-tuple-element.22), channel_id=1, source_target_pairs={{0,16},{8,24},{16,0},{24,8},{1,17},{9,25},{17,1},{25,9},{2,18},{10... | collective-permute-start | bytes 221192 | tf_op jit(solution)/shard_map/ppermute | solution.py:360
  21.2 0.2 collective-permute-start.8
  21.3 3.9 %collective-permute-done.6.refs_1_.refs_11_ = bf16[288,128]{1,0:T(8,128)(2,1)S(1)} collective-permute-done((bf16[288,128]{1,0:T(8,128)(2,1)S(1)}, bf16[288,128]{1,0:T(8,128)(2,1)S(1)}, u32[]{:S(2)}, u32[]{:S(2)}) %collective-permute-start.6) | collective-permute-done | bytes 73760 | tf_op jit(solution)/shard_map/ppermute | solution.py:360
  25.3 0.0 collective-permute-start.7
  25.3 0.0 collective-permute-done.8.refs_4_.refs_14_
  25.3 0.5 %shard_map.114 = (bf16[160,64]{1,0:T(8,128)(2,1)S(1)}, bf16[64,4096]{1,0:T(8,128)(2,1)S(1)}) custom-call(f32[160,64]{1,0:T(8,128)S(1)} %get-tuple-element.23.refs_0_, bf16[288,128]{1,0:T(8,128)(2,1)S(1)} %collective-permute-done.6.refs_1_.refs_11_, bf16[80,4096]{1,0:T(8,128)(2,1)S(1)} %bitcast.9, ...), custom_call_target="tpu_custom_call" | custom-call | flops 1000 | bytes 1000 | tf_op jit(solution)/shard_map/pallas_call | solution.py:342
  25.8 0.8 %collective-permute-done.7.refs_12_ = bf16[288,128]{1,0:T(8,128)(2,1)S(1)} collective-permute-done((bf16[288,128]{1,0:T(8,128)(2,1)S(1)}, bf16[288,128]{1,0:T(8,128)(2,1)S(1)}, u32[]{:S(2)}, u32[]{:S(2)}) %collective-permute-start.7) | collective-permute-done | bytes 73760 | tf_op jit(solution)/shard_map/ppermute | solution.py:360
  26.5 0.5 %collective-permute-start.9 = (bf16[64,4096]{1,0:T(8,128)(2,1)S(1)}, bf16[64,4096]{1,0:T(8,128)(2,1)S(1)}, u32[]{:S(2)}, u32[]{:S(2)}) collective-permute-start(bf16[64,4096]{1,0:T(8,128)(2,1)S(1)} %get-tuple-element.29.refs_17_), channel_id=1, source_target_pairs={{0,16},{8,24},{16,0},{24,8},{1,17},{9,25},{17,1},{25,9},{2,18},{10... | collective-permute-start | bytes 1572872 | tf_op jit(solution)/shard_map/ppermute | solution.py:360
  27.1 0.0 collective-permute-done.5.refs_5_.refs_7_
  27.1 0.9 %shard_map.115 = (bf16[80,256]{1,0:T(8,128)(2,1)S(1)}, bf16[160,64]{1,0:T(8,128)(2,1)S(1)}, bf16[8,16,512]{2,1,0:T(8,128)(2,1)S(1)}) custom-call(bf16[80,4096]{1,0:T(8,128)(2,1)S(1)} %bitcast.10, bf16[80,4096]{1,0:T(8,128)(2,1)S(1)} %collective-permute-done.refs_6_.refs_1_.refs_3_, bf16[64,4096]{1,0:T(8,128)(2,1)S(1)} %bitcast.15, ...), custom_call_target="tpu_custom_call" | custom-call | flops 1000 | bytes 1000 | tf_op jit(solution)/shard_map/pallas_call | solution.py:342
  28.0 10.8 %all_to_all.11 = bf16[8,16,512]{2,1,0:T(8,128)(2,1)S(1)} all-to-all(bf16[8,16,512]{2,1,0:T(8,128)(2,1)S(1)} %get-tuple-element.32), channel_id=1, replica_groups=mesh['dp'=4,'fsdp'=8] {'fsdp'}, dimensions={0} | all-to-all | bytes 262144 | tf_op jit(solution)/shard_map/all_to_all | solution.py:445
  38.8 0.6 %collective-permute-start.12 = (f32[16,512]{1,0:T(8,128)S(1)}, f32[16,512]{1,0:T(8,128)S(1)}, u32[]{:S(2)}, u32[]{:S(2)}) collective-permute-start(f32[16,512]{1,0:T(8,128)S(1)} %convert_reduce_fusion), channel_id=1, source_target_pairs={{0,16},{8,24},{16,0},{24,8},{1,17},{9,25},{17,1},{25,9},{2,18},{10... | collective-permute-start | bytes 98312 | tf_op jit(solution)/shard_map/ppermute | solution.py:360
  39.4 0.0 collective-permute-start.10
  39.4 1.6 %collective-permute-start.11 = (f32[16,512]{1,0:T(8,128)S(1)}, f32[16,512]{1,0:T(8,128)S(1)}, u32[]{:S(2)}, u32[]{:S(2)}) collective-permute-start(f32[16,512]{1,0:T(8,128)S(1)} %convert_reduce_fusion), channel_id=1, source_target_pairs={{0,8},{8,0},{16,24},{24,16},{1,9},{9,1},{17,25},{25,17},{2,10},{10... | collective-permute-start | bytes 98312 | tf_op jit(solution)/shard_map/ppermute | solution.py:360
  41.0 0.0 collective-permute-done.9.refs_8_
  41.0 1.6 %shard_map.116 = (bf16[64,4096]{1,0:T(8,128)(2,1)}, bf16[80,4096]{1,0:T(8,128)(2,1)}) custom-call(bf16[160,64]{1,0:T(8,128)(2,1)S(1)} %get-tuple-element.27.refs_0_, bf16[80,256]{1,0:T(8,128)(2,1)S(1)} %get-tuple-element.28.refs_1_, bf16[80,4096]{1,0:T(8,128)(2,1)S(1)} %bitcast.11, bf16[80,4096]{1,0:T(8,128)(2,1)S(1)} %collective-permute-done.refs_6_.refs_1_.refs_3_, ...), custom_call_target="tpu_custom_call" | custom-call | flops 1000 | bytes 1000 | tf_op jit(solution)/shard_map/pallas_call | solution.py:342
  42.6 0.6 %collective-permute-done.12 = f32[16,512]{1,0:T(8,128)S(1)} collective-permute-done((f32[16,512]{1,0:T(8,128)S(1)}, f32[16,512]{1,0:T(8,128)S(1)}, u32[]{:S(2)}, u32[]{:S(2)}) %collective-permute-start.12) | collective-permute-done | bytes 32800 | tf_op jit(solution)/shard_map/ppermute | solution.py:360
  43.1 0.0 collective-permute-done.10
  43.1 0.0 collective-permute-done.11
  43.1 0.6 %broadcast_select_fusion = (f32[16,512]{1,0:T(8,128)}, f32[16,512]{1,0:T(8,128)}) fusion(pred[]{:T(512)S(6)} %eq.3, f32[16,512]{1,0:T(8,128)S(1)} %collective-permute-done.10, f32[16,512]{1,0:T(8,128)S(1)} %collective-permute-done.11, f32[16,512]{1,0:T(8,128)S(1)} %convert_reduce_fusion, f32[16,512]{1,0:T(8,128)S(1)} %collective-permute-done.12), kind=kLoop, calls=%fused_computation.3 | loop fusion | flops 49152 | bytes 196609 | tf_op jit(solution)/shard_map/jit(_where)/select_n | solution.py:459
  (3 shorter events, 0.0 us)
Async XLA Ops:
  0.6 3.8 %copy-start.6 = (bf16[16,512]{1,0:T(8,128)(2,1)S(1)}, bf16[16,512]{1,0:T(8,128)(2,1)}, u32[]{:S(2)}) copy-start(bf16[16,512]{1,0:T(8,128)(2,1)} %param.14) | copy-start | bytes 49156
  0.6 17.8 %collective-permute-start.1 = (bf16[64,4096]{1,0:T(8,128)(2,1)}, bf16[64,4096]{1,0:T(8,128)(2,1)S(1)}, u32[]{:S(2)}, u32[]{:S(2)}) collective-permute-start(bf16[64,4096]{1,0:T(8,128)(2,1)} %bitcast.12), channel_id=1, source_target_pairs={{0,8},{8,0},{16,24},{24,16},{1,9},{9,1},{17,25},{25,17},{2,10},{10... | collective-permute-start | bytes 1572872 | tf_op jit(solution)/shard_map/ppermute | solution.py:360
  1.2 18.7 %collective-permute-start.2 = (bf16[64,4096]{1,0:T(8,128)(2,1)}, bf16[64,4096]{1,0:T(8,128)(2,1)S(1)}, u32[]{:S(2)}, u32[]{:S(2)}) collective-permute-start(bf16[64,4096]{1,0:T(8,128)(2,1)} %bitcast.13), channel_id=1, source_target_pairs={{0,16},{8,24},{16,0},{24,8},{1,17},{9,25},{17,1},{25,9},{2,18},{10... | collective-permute-start | bytes 1572872 | tf_op jit(solution)/shard_map/ppermute | solution.py:360
  3.7 14.7 %collective-permute-start = (bf16[80,4096]{1,0:T(8,128)(2,1)}, bf16[80,4096]{1,0:T(8,128)(2,1)S(1)}, u32[]{:S(2)}, u32[]{:S(2)}) collective-permute-start(bf16[80,4096]{1,0:T(8,128)(2,1)} %bitcast.6), channel_id=1, source_target_pairs={{0,8},{8,0},{16,24},{24,16},{1,9},{9,1},{17,25},{25,17},{2,10},{10... | collective-permute-start | bytes 1966088 | tf_op jit(solution)/shard_map/ppermute | solution.py:360
  3.9 14.6 %collective-permute-start.3 = (bf16[64,4096]{1,0:T(8,128)(2,1)}, bf16[64,4096]{1,0:T(8,128)(2,1)S(1)}, u32[]{:S(2)}, u32[]{:S(2)}) collective-permute-start(bf16[64,4096]{1,0:T(8,128)(2,1)} %bitcast.20), channel_id=1, source_target_pairs={{0,8},{8,0},{16,24},{24,16},{1,9},{9,1},{17,25},{25,17},{2,10},{10... | collective-permute-start | bytes 1572872 | tf_op jit(solution)/shard_map/ppermute | solution.py:360
  4.2 14.2 %collective-permute-start.4 = (bf16[80,4096]{1,0:T(8,128)(2,1)}, bf16[80,4096]{1,0:T(8,128)(2,1)S(1)}, u32[]{:S(2)}, u32[]{:S(2)}) collective-permute-start(bf16[80,4096]{1,0:T(8,128)(2,1)} %bitcast.17), channel_id=1, source_target_pairs={{0,8},{8,0},{16,24},{24,16},{1,9},{9,1},{17,25},{25,17},{2,10},{10... | collective-permute-start | bytes 1966088 | tf_op jit(solution)/shard_map/ppermute | solution.py:360
  4.4 14.1 %copy-start = (bf16[1,1,80,4096]{3,2,1,0:T(8,128)(2,1)S(1)}, bf16[1,1,80,4096]{3,2,1,0:T(8,128)(2,1)}, u32[]{:S(2)}) copy-start(bf16[1,1,80,4096]{3,2,1,0:T(8,128)(2,1)} %param.9) | copy-start | bytes 1966084
  4.4 14.1 %copy-start.1 = (bf16[1,64,4096]{2,1,0:T(8,128)(2,1)S(1)}, bf16[1,64,4096]{2,1,0:T(8,128)(2,1)}, u32[]{:S(2)}) copy-start(bf16[1,64,4096]{2,1,0:T(8,128)(2,1)} %param.8) | copy-start | bytes 1572868
  4.4 14.1 %copy-start.2 = (bf16[1,1,80,4096]{3,2,1,0:T(8,128)(2,1)S(1)}, bf16[1,1,80,4096]{3,2,1,0:T(8,128)(2,1)}, u32[]{:S(2)}) copy-start(bf16[1,1,80,4096]{3,2,1,0:T(8,128)(2,1)} %param.13) | copy-start | bytes 1966084
  4.5 14.1 %copy-start.3 = (bf16[1,64,4096]{2,1,0:T(8,128)(2,1)S(1)}, bf16[1,64,4096]{2,1,0:T(8,128)(2,1)}, u32[]{:S(2)}) copy-start(bf16[1,64,4096]{2,1,0:T(8,128)(2,1)} %param.12) | copy-start | bytes 1572868
  4.5 14.0 %copy-start.4 = (s32[1,64]{1,0:T(1,128)S(1)}, s32[1,64]{1,0:T(1,128)}, u32[]{:S(2)}) copy-start(s32[1,64]{1,0:T(1,128)} %refs_9_.1) | copy-start | bytes 772
  4.5 14.0 %copy-start.5 = (s32[1,64]{1,0:T(1,128)S(1)}, s32[1,64]{1,0:T(1,128)}, u32[]{:S(2)}) copy-start(s32[1,64]{1,0:T(1,128)} %refs_10_.1) | copy-start | bytes 772
  20.5 6.5 %collective-permute-start.5 = (bf16[64,4096]{1,0:T(8,128)(2,1)S(1)}, bf16[64,4096]{1,0:T(8,128)(2,1)S(1)}, u32[]{:S(2)}, u32[]{:S(2)}) collective-permute-start(bf16[64,4096]{1,0:T(8,128)(2,1)S(1)} %get-tuple-element.21.refs_4_.refs_6_), channel_id=1, source_target_pairs={{0,8},{8,0},{16,24},{24,16},{1,9},{9,1},{17,25},{25,17},{2,10},{10... | collective-permute-start | bytes 1572872 | tf_op jit(solution)/shard_map/ppermute | solution.py:360
  20.6 4.7 %collective-permute-start.6 = (bf16[288,128]{1,0:T(8,128)(2,1)S(1)}, bf16[288,128]{1,0:T(8,128)(2,1)S(1)}, u32[]{:S(2)}, u32[]{:S(2)}) collective-permute-start(bf16[288,128]{1,0:T(8,128)(2,1)S(1)} %get-tuple-element.22), channel_id=1, source_target_pairs={{0,16},{8,24},{16,0},{24,8},{1,17},{9,25},{17,1},{25,9},{2,18},{10... | collective-permute-start | bytes 221192 | tf_op jit(solution)/shard_map/ppermute | solution.py:360
  21.2 4.1 %collective-permute-start.8 = (bf16[288,128]{1,0:T(8,128)(2,1)S(1)}, bf16[288,128]{1,0:T(8,128)(2,1)S(1)}, u32[]{:S(2)}, u32[]{:S(2)}) collective-permute-start(bf16[288,128]{1,0:T(8,128)(2,1)S(1)} %get-tuple-element.22), channel_id=1, source_target_pairs={{0,8},{8,0},{16,24},{24,16},{1,9},{9,1},{17,25},{25,17},{2,10},{10... | collective-permute-start | bytes 221192 | tf_op jit(solution)/shard_map/ppermute | solution.py:360
  25.3 1.3 %collective-permute-start.7 = (bf16[288,128]{1,0:T(8,128)(2,1)S(1)}, bf16[288,128]{1,0:T(8,128)(2,1)S(1)}, u32[]{:S(2)}, u32[]{:S(2)}) collective-permute-start(bf16[288,128]{1,0:T(8,128)(2,1)S(1)} %collective-permute-done.6.refs_1_.refs_11_), channel_id=1, source_target_pairs={{0,8},{8,0},{16,24},{24,16},{1,9},{9,1},{17,25},{25,17},{2,10},{10... | collective-permute-start | bytes 221192 | tf_op jit(solution)/shard_map/ppermute | solution.py:360
  26.5 14.5 %collective-permute-start.9 = (bf16[64,4096]{1,0:T(8,128)(2,1)S(1)}, bf16[64,4096]{1,0:T(8,128)(2,1)S(1)}, u32[]{:S(2)}, u32[]{:S(2)}) collective-permute-start(bf16[64,4096]{1,0:T(8,128)(2,1)S(1)} %get-tuple-element.29.refs_17_), channel_id=1, source_target_pairs={{0,16},{8,24},{16,0},{24,8},{1,17},{9,25},{17,1},{25,9},{2,18},{10... | collective-permute-start | bytes 1572872 | tf_op jit(solution)/shard_map/ppermute | solution.py:360
  38.8 4.3 %collective-permute-start.12 = (f32[16,512]{1,0:T(8,128)S(1)}, f32[16,512]{1,0:T(8,128)S(1)}, u32[]{:S(2)}, u32[]{:S(2)}) collective-permute-start(f32[16,512]{1,0:T(8,128)S(1)} %convert_reduce_fusion), channel_id=1, source_target_pairs={{0,16},{8,24},{16,0},{24,8},{1,17},{9,25},{17,1},{25,9},{2,18},{10... | collective-permute-start | bytes 98312 | tf_op jit(solution)/shard_map/ppermute | solution.py:360
  39.4 3.7 %collective-permute-start.10 = (f32[16,512]{1,0:T(8,128)S(1)}, f32[16,512]{1,0:T(8,128)S(1)}, u32[]{:S(2)}, u32[]{:S(2)}) collective-permute-start(f32[16,512]{1,0:T(8,128)S(1)} %convert_reduce_fusion), channel_id=1, source_target_pairs={{0,24},{8,16},{16,8},{24,0},{1,25},{9,17},{17,9},{25,1},{2,26},{10... | collective-permute-start | bytes 98312 | tf_op jit(solution)/shard_map/ppermute | solution.py:360
  39.4 3.7 %collective-permute-start.11 = (f32[16,512]{1,0:T(8,128)S(1)}, f32[16,512]{1,0:T(8,128)S(1)}, u32[]{:S(2)}, u32[]{:S(2)}) collective-permute-start(f32[16,512]{1,0:T(8,128)S(1)} %convert_reduce_fusion), channel_id=1, source_target_pairs={{0,8},{8,0},{16,24},{24,16},{1,9},{9,1},{17,25},{25,17},{2,10},{10... | collective-permute-start | bytes 98312 | tf_op jit(solution)/shard_map/ppermute | solution.py:360

commit v12 on v10

--- a/solution.py
+++ b/solution.py
@@ -449,7 +449,9 @@
     while 2 * apart < devices:
         terms = terms + swap(terms, "dp", apart)
         apart *= 2
-    got = [swap(terms, "dp", k) for k in (apart, apart ^ 1, 1)]
+    terms = terms.astype(bf16)
+    got = [swap(terms, "dp", k).astype(f32) for k in (apart, apart ^ 1, 1)]
+    terms = terms.astype(f32)
     got[0] = after(got[0], question, grad)
     others = (got[1] + got[2]) * adapter_scale
     terms = (terms + got[0]) * adapter_scale

time: 44.1 us -> 49.2 us (1.12)
  local copies, waits for them, and re-layouts: 0.04 us -> 3.37 us
  Pallas kernels: 4.99 us -> 7.82 us
  waiting for transfers between devices: 5.32 us -> 3.95 us
    unnamed x14 -> x30, local copies, waits for them, and re-layouts: 0.04 us -> 3.37 us
    pallas_call x7, Pallas kernels: 4.99 us -> 7.82 us  [run(): pl.pallas_call(body, out_shape=outs, in_specs=[vmem] * len(args) + [anywh...]
    ppermute x13, waiting for transfers between devices: 5.32 us -> 3.95 us  [swap(): lax.ppermute(array, axis, [(i, i ^ apart) for i in range(lax.axis_size(ax...]
  transfers between devices with their start and end apart: 13 -> 13, of which waited for: 4 -> 1; matrix products, arithmetic and copies ran while one was open for 0% -> 0% of each run, Pallas kernels for 10% -> 13%
where the time goes in v12:
time: 49.2 us; the launch traced here: 48.8 us
  blocking collectives  24.8 us (50%)
  Pallas kernels  7.82 us (16%)
  starting transfers between devices  7.33 us (15%)
  waiting for transfers between devices  3.95 us (8%)
  local copies, waits for them, and re-layouts  3.37 us (7%)
  between operations  0.85 us (2%)
  other arithmetic  0.68 us (1%)
    all_to_all x1, blocking collectives, on_device(): maps = lax.all_to_all(mine, 'fsdp', 0, 0)  13.9 us
    all_to_all x1, blocking collectives, on_device(): terms = lax.all_to_all(terms, 'fsdp', 0, 0)  10.8 us
    pallas_call x7, Pallas kernels, run(): pl.pallas_call(body, out_shape=outs, in_specs=[vmem] * len(args) + [anywh...  7.82 us
    ppermute x13, starting transfers between devices, swap(): lax.ppermute(array, axis, [(i, i ^ apart) for i in range(lax.axis_size(ax...  7.33 us
    ppermute x13, waiting for transfers between devices, swap(): lax.ppermute(array, axis, [(i, i ^ apart) for i in range(lax.axis_size(ax...  3.95 us
    unnamed x30, local copies, waits for them, and re-layouts  3.37 us
  transfers between devices with their start and end apart: 13, of which 1 were waited for; matrix products, arithmetic and copies ran while one was open for 0% of the time, Pallas kernels for 13%

profile of v12, /device:TPU:0, one launch (start us, length us, event | category | flops | bytes accessed | tf_op | source)
XLA Modules:
  0.0 48.8 jit_solution(16818920110418086962)
XLA Ops:
  0.6 0.0 copy-start.14
  0.6 0.5 %collective-permute-start.1 = (bf16[64,4096]{1,0:T(8,128)(2,1)}, bf16[64,4096]{1,0:T(8,128)(2,1)S(1)}, u32[]{:S(2)}, u32[]{:S(2)}) collective-permute-start(bf16[64,4096]{1,0:T(8,128)(2,1)} %bitcast.13), channel_id=1, source_target_pairs={{0,8},{8,0},{16,24},{24,16},{1,9},{9,1},{17,25},{25,17},{2,10},{10... | collective-permute-start | bytes 1572872 | tf_op jit(solution)/shard_map/ppermute | solution.py:359
  1.2 2.6 %collective-permute-start.2 = (bf16[64,4096]{1,0:T(8,128)(2,1)}, bf16[64,4096]{1,0:T(8,128)(2,1)}, u32[]{:S(2)}, u32[]{:S(2)}) collective-permute-start(bf16[64,4096]{1,0:T(8,128)(2,1)} %bitcast.14), channel_id=1, source_target_pairs={{0,16},{8,24},{16,0},{24,8},{1,17},{9,25},{17,1},{25,9},{2,18},{10... | collective-permute-start | bytes 1572872 | tf_op jit(solution)/shard_map/ppermute | solution.py:359
  3.7 0.2 collective-permute-start
  3.9 0.3 collective-permute-start.3
  4.2 0.2 collective-permute-start.4
  4.4 0.0 copy-done.14
  4.4 0.0 copy-start
  4.4 0.0 copy-start.1
  4.4 0.0 copy-start.2
  4.5 0.0 copy-start.3
  4.5 13.9 %all_to_all.10.refs_0_ = bf16[8,16,512]{2,1,0:T(8,128)(2,1)S(1)} all-to-all(bf16[8,16,512]{2,1,0:T(8,128)(2,1)S(1)} %shard_map.111), channel_id=1, replica_groups=mesh['dp'=4,'fsdp'=8] {'fsdp'}, dimensions={0} | all-to-all | bytes 262144 | tf_op jit(solution)/shard_map/all_to_all | solution.py:384
  18.4 0.0 copy-start.12
  18.4 0.0 copy-start.13
  18.4 0.0 collective-permute-done.1.refs_8_.refs_3_.refs_5_
  18.4 0.0 collective-permute-done.3.refs_2_.refs_7_
  18.4 0.0 collective-permute-done.refs_6_.refs_1_.refs_3_
  18.5 0.0 collective-permute-done.4.refs_4_.refs_9_
  18.5 0.0 copy-done
  18.5 0.0 copy-done.1
  18.5 0.0 copy-done.2
  18.5 0.0 copy-done.3
  18.5 0.8 %shard_map.112.refs_6_.refs_4_.refs_15_ = f32[16,288]{1,0:T(8,128)S(1)} custom-call(bf16[8,16,512]{2,1,0:T(8,128)(2,1)S(1)} %all_to_all.10.refs_0_, bf16[64,4096]{1,0:T(8,128)(2,1)S(1)} %bitcast.23, bf16[64,4096]{1,0:T(8,128)(2,1)S(1)} %collective-permute-done.3.refs_2_.refs_7_, bf16[80,4096]{1,0:T(8,128)(2,1)S(1)} %bitcast.20, ...), custom_call_target="tpu_custom_call" | custom-call | flops 1000 | bytes 1000 | tf_op jit(solution)/shard_map/pallas_call | solution.py:341
  19.3 0.0 copy-done.12
  19.3 0.0 copy-done.13
  19.3 0.6 %shard_map.113 = (f32[160,128]{1,0:T(8,128)S(1)}, f32[8,64]{1,0:T(8,128)S(1)}) custom-call(bf16[80,4096]{1,0:T(8,128)(2,1)S(1)} %bitcast.8, bf16[80,4096]{1,0:T(8,128)(2,1)S(1)} %collective-permute-done.refs_6_.refs_1_.refs_3_, bf16[64,4096]{1,0:T(8,128)(2,1)S(1)} %bitcast.16, bf16[64,4096]{1,0:T(8,128)(2,1)S(1)} %collective-permute-done.1.refs_8_.refs_3_.refs_5_, ...), custom_call_target="tpu_custom_call" | custom-call | flops 1000 | bytes 1000 | tf_op jit(solution)/shard_map/pallas_call | solution.py:341
  19.9 0.0 collective-permute-done.2.refs_2_
  19.9 1.7 %shard_map.114 = (bf16[288,128]{1,0:T(8,128)(2,1)S(1)}, f32[160,64]{1,0:T(8,128)S(1)}, bf16[64,4096]{1,0:T(8,128)(2,1)S(1)}) custom-call(bf16[80,4096]{1,0:T(8,128)(2,1)S(1)} %bitcast.9, bf16[80,4096]{1,0:T(8,128)(2,1)S(1)} %collective-permute-done.refs_6_.refs_1_.refs_3_, bf16[64,4096]{1,0:T(8,128)(2,1)} %collective-permute-done.2.refs_2_, ...), custom_call_target="tpu_custom_call" | custom-call | flops 1000 | bytes 1000 | tf_op jit(solution)/shard_map/pallas_call | solution.py:341
  21.6 0.0 copy-start.4
  21.6 0.1 collective-permute-start.5
  21.6 0.6 %collective-permute-start.6 = (bf16[288,128]{1,0:T(8,128)(2,1)S(1)}, bf16[288,128]{1,0:T(8,128)(2,1)S(1)}, u32[]{:S(2)}, u32[]{:S(2)}) collective-permute-start(bf16[288,128]{1,0:T(8,128)(2,1)S(1)} %get-tuple-element.20), channel_id=1, source_target_pairs={{0,16},{8,24},{16,0},{24,8},{1,17},{9,25},{17,1},{25,9},{2,18},{10... | collective-permute-start | bytes 221192 | tf_op jit(solution)/shard_map/ppermute | solution.py:359
  22.2 0.2 collective-permute-start.8
  22.4 3.9 %collective-permute-done.6.refs_1_.refs_11_ = bf16[288,128]{1,0:T(8,128)(2,1)S(1)} collective-permute-done((bf16[288,128]{1,0:T(8,128)(2,1)S(1)}, bf16[288,128]{1,0:T(8,128)(2,1)S(1)}, u32[]{:S(2)}, u32[]{:S(2)}) %collective-permute-start.6) | collective-permute-done | bytes 73760 | tf_op jit(solution)/shard_map/ppermute | solution.py:359
  26.3 0.0 collective-permute-start.7
  26.3 0.0 collective-permute-done.8.refs_4_.refs_14_
  26.3 1.3 %shard_map.115 = (bf16[160,64]{1,0:T(8,128)(2,1)S(1)}, bf16[64,4096]{1,0:T(8,128)(2,1)}) custom-call(f32[160,64]{1,0:T(8,128)S(1)} %get-tuple-element.21.refs_0_, bf16[288,128]{1,0:T(8,128)(2,1)S(1)} %collective-permute-done.6.refs_1_.refs_11_, bf16[80,4096]{1,0:T(8,128)(2,1)S(1)} %bitcast.10, ...), custom_call_target="tpu_custom_call" | custom-call | flops 1000 | bytes 1000 | tf_op jit(solution)/shard_map/pallas_call | solution.py:341
  27.6 0.0 collective-permute-done.7.refs_12_
  27.6 0.5 %collective-permute-start.9 = (bf16[64,4096]{1,0:T(8,128)(2,1)}, bf16[64,4096]{1,0:T(8,128)(2,1)}, u32[]{:S(2)}, u32[]{:S(2)}) collective-permute-start(bf16[64,4096]{1,0:T(8,128)(2,1)} %get-tuple-element.27.refs_17_), channel_id=1, source_target_pairs={{0,16},{8,24},{16,0},{24,8},{1,17},{9,25},{17,1},{25,9},{2,18},{10... | collective-permute-start | bytes 1572872 | tf_op jit(solution)/shard_map/ppermute | solution.py:359
  28.1 0.0 collective-permute-done.5.refs_5_.refs_7_
  28.2 0.0 copy-done.4
  28.2 0.9 %shard_map.116 = (bf16[80,256]{1,0:T(8,128)(2,1)S(1)}, bf16[160,64]{1,0:T(8,128)(2,1)S(1)}, bf16[8,16,512]{2,1,0:T(8,128)(2,1)S(1)}) custom-call(bf16[80,4096]{1,0:T(8,128)(2,1)S(1)} %bitcast.11, bf16[80,4096]{1,0:T(8,128)(2,1)S(1)} %collective-permute-done.refs_6_.refs_1_.refs_3_, bf16[64,4096]{1,0:T(8,128)(2,1)S(1)} %bitcast.17, ...), custom_call_target="tpu_custom_call" | custom-call | flops 1000 | bytes 1000 | tf_op jit(solution)/shard_map/pallas_call | solution.py:341
  29.1 0.0 copy-done.6
  29.1 0.0 copy-start.8
  29.1 0.6 %copy-done.8 = bf16[80,256]{1,0:T(8,128)(2,1)} copy-done((bf16[80,256]{1,0:T(8,128)(2,1)}, bf16[80,256]{1,0:T(8,128)(2,1)S(1)}, u32[]{:S(2)}) %copy-start.8) | copy-done | bytes 40984
  29.7 0.0 copy-start.10
  29.7 0.6 %copy-done.10 = bf16[160,64]{1,0:T(8,128)(2,1)} copy-done((bf16[160,64]{1,0:T(8,128)(2,1)}, bf16[160,64]{1,0:T(8,128)(2,1)S(1)}, u32[]{:S(2)}) %copy-start.10) | copy-done | bytes 20504
  30.3 10.8 %all_to_all.11 = bf16[8,16,512]{2,1,0:T(8,128)(2,1)S(1)} all-to-all(bf16[8,16,512]{2,1,0:T(8,128)(2,1)S(1)} %get-tuple-element.30), channel_id=1, replica_groups=mesh['dp'=4,'fsdp'=8] {'fsdp'}, dimensions={0} | all-to-all | bytes 262144 | tf_op jit(solution)/shard_map/all_to_all | solution.py:446
  41.2 0.0 copy-start.9
  41.2 0.0 copy-start.11
  41.2 0.6 %collective-permute-start.12 = (bf16[16,512]{1,0:T(8,128)(2,1)S(1)}, bf16[16,512]{1,0:T(8,128)(2,1)S(1)}, u32[]{:S(2)}, u32[]{:S(2)}) collective-permute-start(bf16[16,512]{1,0:T(8,128)(2,1)S(1)} %reduce_sum.12), channel_id=1, source_target_pairs={{0,16},{8,24},{16,0},{24,8},{1,17},{9,25},{17,1},{25,9},{2,18},{10... | collective-permute-start | bytes 49160 | tf_op jit(solution)/shard_map/ppermute | solution.py:359
  41.8 0.0 collective-permute-start.11
  41.8 1.6 %collective-permute-start.10 = (bf16[16,512]{1,0:T(8,128)(2,1)S(1)}, bf16[16,512]{1,0:T(8,128)(2,1)S(1)}, u32[]{:S(2)}, u32[]{:S(2)}) collective-permute-start(bf16[16,512]{1,0:T(8,128)(2,1)S(1)} %reduce_sum.12), channel_id=1, source_target_pairs={{0,24},{8,16},{16,8},{24,0},{1,25},{9,17},{17,9},{25,1},{2,26},{10... | collective-permute-start | bytes 49160 | tf_op jit(solution)/shard_map/ppermute | solution.py:359
  43.4 0.0 collective-permute-done.9.refs_8_
  43.4 0.0 copy-done.9
  43.4 0.0 copy-done.11
  43.4 0.0 copy-start.5
  43.5 1.0 %copy-done.5 = bf16[64,4096]{1,0:T(8,128)(2,1)S(1)} copy-done((bf16[64,4096]{1,0:T(8,128)(2,1)S(1)}, bf16[64,4096]{1,0:T(8,128)(2,1)}, u32[]{:S(2)}) %copy-start.5) | copy-done | bytes 524312
  44.5 0.0 copy-start.7
  44.5 1.0 %copy-done.7 = bf16[64,4096]{1,0:T(8,128)(2,1)S(1)} copy-done((bf16[64,4096]{1,0:T(8,128)(2,1)S(1)}, bf16[64,4096]{1,0:T(8,128)(2,1)}, u32[]{:S(2)}) %copy-start.7) | copy-done | bytes 524312
  45.5 2.6 %shard_map.117 = (bf16[64,4096]{1,0:T(8,128)(2,1)}, bf16[80,4096]{1,0:T(8,128)(2,1)}) custom-call(bf16[160,64]{1,0:T(8,128)(2,1)S(1)} %copy-done.11, bf16[80,256]{1,0:T(8,128)(2,1)S(1)} %copy-done.9, bf16[80,4096]{1,0:T(8,128)(2,1)S(1)} %bitcast.12, bf16[80,4096]{1,0:T(8,128)(2,1)S(1)} %collective-permute-done.refs_6_.refs_1_.refs_3_, ...), custom_call_target="tpu_custom_call" | custom-call | flops 1000 | bytes 1000 | tf_op jit(solution)/shard_map/pallas_call | solution.py:341
  48.1 0.0 collective-permute-done.12
  48.1 0.0 collective-permute-done.11
  48.1 0.0 collective-permute-done.10
  48.1 0.6 %fusion = (f32[16,512]{1,0:T(8,128)}, f32[16,512]{1,0:T(8,128)}) fusion(bf16[16,512]{1,0:T(8,128)(2,1)S(1)} %collective-permute-done.11, bf16[16,512]{1,0:T(8,128)(2,1)S(1)} %collective-permute-done.10, f32[16,512]{1,0:T(8,128)S(1)} %convert_element_type.17, bf16[16,512]{1,0:T(8,128)(2,1)S(1)} %reduce_sum.12, pred[]{:T(512)S(6)} %eq.3), kind=kLoop, calls=%fused_computation.2 | loop fusion | flops 73728 | bytes 147457 | tf_op jit(solution)/shard_map/jit(_where)/select_n | solution.py:462
  (5 shorter events, 0.0 us)
Async XLA Ops:
  0.6 3.8 %copy-start.14 = (bf16[16,512]{1,0:T(8,128)(2,1)S(1)}, bf16[16,512]{1,0:T(8,128)(2,1)}, u32[]{:S(2)}) copy-start(bf16[16,512]{1,0:T(8,128)(2,1)} %param.14) | copy-start | bytes 49156
  0.6 17.8 %collective-permute-start.1 = (bf16[64,4096]{1,0:T(8,128)(2,1)}, bf16[64,4096]{1,0:T(8,128)(2,1)S(1)}, u32[]{:S(2)}, u32[]{:S(2)}) collective-permute-start(bf16[64,4096]{1,0:T(8,128)(2,1)} %bitcast.13), channel_id=1, source_target_pairs={{0,8},{8,0},{16,24},{24,16},{1,9},{9,1},{17,25},{25,17},{2,10},{10... | collective-permute-start | bytes 1572872 | tf_op jit(solution)/shard_map/ppermute | solution.py:359
  1.2 18.7 %collective-permute-start.2 = (bf16[64,4096]{1,0:T(8,128)(2,1)}, bf16[64,4096]{1,0:T(8,128)(2,1)}, u32[]{:S(2)}, u32[]{:S(2)}) collective-permute-start(bf16[64,4096]{1,0:T(8,128)(2,1)} %bitcast.14), channel_id=1, source_target_pairs={{0,16},{8,24},{16,0},{24,8},{1,17},{9,25},{17,1},{25,9},{2,18},{10... | collective-permute-start | bytes 1572872 | tf_op jit(solution)/shard_map/ppermute | solution.py:359
  3.7 14.7 %collective-permute-start = (bf16[80,4096]{1,0:T(8,128)(2,1)}, bf16[80,4096]{1,0:T(8,128)(2,1)S(1)}, u32[]{:S(2)}, u32[]{:S(2)}) collective-permute-start(bf16[80,4096]{1,0:T(8,128)(2,1)} %bitcast.6), channel_id=1, source_target_pairs={{0,8},{8,0},{16,24},{24,16},{1,9},{9,1},{17,25},{25,17},{2,10},{10... | collective-permute-start | bytes 1966088 | tf_op jit(solution)/shard_map/ppermute | solution.py:359
  3.9 14.5 %collective-permute-start.3 = (bf16[64,4096]{1,0:T(8,128)(2,1)}, bf16[64,4096]{1,0:T(8,128)(2,1)S(1)}, u32[]{:S(2)}, u32[]{:S(2)}) collective-permute-start(bf16[64,4096]{1,0:T(8,128)(2,1)} %bitcast.22), channel_id=1, source_target_pairs={{0,8},{8,0},{16,24},{24,16},{1,9},{9,1},{17,25},{25,17},{2,10},{10... | collective-permute-start | bytes 1572872 | tf_op jit(solution)/shard_map/ppermute | solution.py:359
  4.2 14.2 %collective-permute-start.4 = (bf16[80,4096]{1,0:T(8,128)(2,1)}, bf16[80,4096]{1,0:T(8,128)(2,1)S(1)}, u32[]{:S(2)}, u32[]{:S(2)}) collective-permute-start(bf16[80,4096]{1,0:T(8,128)(2,1)} %bitcast.19), channel_id=1, source_target_pairs={{0,8},{8,0},{16,24},{24,16},{1,9},{9,1},{17,25},{25,17},{2,10},{10... | collective-permute-start | bytes 1966088 | tf_op jit(solution)/shard_map/ppermute | solution.py:359
  4.4 14.0 %copy-start = (bf16[1,1,80,4096]{3,2,1,0:T(8,128)(2,1)S(1)}, bf16[1,1,80,4096]{3,2,1,0:T(8,128)(2,1)}, u32[]{:S(2)}) copy-start(bf16[1,1,80,4096]{3,2,1,0:T(8,128)(2,1)} %param.9) | copy-start | bytes 1966084
  4.4 14.0 %copy-start.1 = (bf16[1,64,4096]{2,1,0:T(8,128)(2,1)S(1)}, bf16[1,64,4096]{2,1,0:T(8,128)(2,1)}, u32[]{:S(2)}) copy-start(bf16[1,64,4096]{2,1,0:T(8,128)(2,1)} %param.8) | copy-start | bytes 1572868
  4.4 14.0 %copy-start.2 = (bf16[1,1,80,4096]{3,2,1,0:T(8,128)(2,1)S(1)}, bf16[1,1,80,4096]{3,2,1,0:T(8,128)(2,1)}, u32[]{:S(2)}) copy-start(bf16[1,1,80,4096]{3,2,1,0:T(8,128)(2,1)} %param.13) | copy-start | bytes 1966084
  4.5 14.0 %copy-start.3 = (bf16[1,64,4096]{2,1,0:T(8,128)(2,1)S(1)}, bf16[1,64,4096]{2,1,0:T(8,128)(2,1)}, u32[]{:S(2)}) copy-start(bf16[1,64,4096]{2,1,0:T(8,128)(2,1)} %param.12) | copy-start | bytes 1572868
  18.4 0.9 %copy-start.12 = (s32[1,64]{1,0:T(1,128)S(1)}, s32[1,64]{1,0:T(1,128)}, u32[]{:S(2)}) copy-start(s32[1,64]{1,0:T(1,128)} %refs_4_.1) | copy-start | bytes 772
  18.4 0.9 %copy-start.13 = (s32[1,64]{1,0:T(1,128)S(1)}, s32[1,64]{1,0:T(1,128)}, u32[]{:S(2)}) copy-start(s32[1,64]{1,0:T(1,128)} %refs_5_.1) | copy-start | bytes 772
  21.6 6.6 %copy-start.4 = (bf16[64,4096]{1,0:T(8,128)(2,1)}, bf16[64,4096]{1,0:T(8,128)(2,1)S(1)}, u32[]{:S(2)}) copy-start(bf16[64,4096]{1,0:T(8,128)(2,1)S(1)} %get-tuple-element.19.refs_4_.refs_6_) | copy-start | bytes 1572868
  21.6 6.6 %collective-permute-start.5 = (bf16[64,4096]{1,0:T(8,128)(2,1)S(1)}, bf16[64,4096]{1,0:T(8,128)(2,1)S(1)}, u32[]{:S(2)}, u32[]{:S(2)}) collective-permute-start(bf16[64,4096]{1,0:T(8,128)(2,1)S(1)} %get-tuple-element.19.refs_4_.refs_6_), channel_id=1, source_target_pairs={{0,8},{8,0},{16,24},{24,16},{1,9},{9,1},{17,25},{25,17},{2,10},{10... | collective-permute-start | bytes 1572872 | tf_op jit(solution)/shard_map/ppermute | solution.py:359
  21.6 4.7 %collective-permute-start.6 = (bf16[288,128]{1,0:T(8,128)(2,1)S(1)}, bf16[288,128]{1,0:T(8,128)(2,1)S(1)}, u32[]{:S(2)}, u32[]{:S(2)}) collective-permute-start(bf16[288,128]{1,0:T(8,128)(2,1)S(1)} %get-tuple-element.20), channel_id=1, source_target_pairs={{0,16},{8,24},{16,0},{24,8},{1,17},{9,25},{17,1},{25,9},{2,18},{10... | collective-permute-start | bytes 221192 | tf_op jit(solution)/shard_map/ppermute | solution.py:359
  22.2 4.1 %collective-permute-start.8 = (bf16[288,128]{1,0:T(8,128)(2,1)S(1)}, bf16[288,128]{1,0:T(8,128)(2,1)S(1)}, u32[]{:S(2)}, u32[]{:S(2)}) collective-permute-start(bf16[288,128]{1,0:T(8,128)(2,1)S(1)} %get-tuple-element.20), channel_id=1, source_target_pairs={{0,8},{8,0},{16,24},{24,16},{1,9},{9,1},{17,25},{25,17},{2,10},{10... | collective-permute-start | bytes 221192 | tf_op jit(solution)/shard_map/ppermute | solution.py:359
  26.3 1.3 %collective-permute-start.7 = (bf16[288,128]{1,0:T(8,128)(2,1)S(1)}, bf16[288,128]{1,0:T(8,128)(2,1)S(1)}, u32[]{:S(2)}, u32[]{:S(2)}) collective-permute-start(bf16[288,128]{1,0:T(8,128)(2,1)S(1)} %collective-permute-done.6.refs_1_.refs_11_), channel_id=1, source_target_pairs={{0,8},{8,0},{16,24},{24,16},{1,9},{9,1},{17,25},{25,17},{2,10},{10... | collective-permute-start | bytes 221192 | tf_op jit(solution)/shard_map/ppermute | solution.py:359
  27.6 15.8 %collective-permute-start.9 = (bf16[64,4096]{1,0:T(8,128)(2,1)}, bf16[64,4096]{1,0:T(8,128)(2,1)}, u32[]{:S(2)}, u32[]{:S(2)}) collective-permute-start(bf16[64,4096]{1,0:T(8,128)(2,1)} %get-tuple-element.27.refs_17_), channel_id=1, source_target_pairs={{0,16},{8,24},{16,0},{24,8},{1,17},{9,25},{17,1},{25,9},{2,18},{10... | collective-permute-start | bytes 1572872 | tf_op jit(solution)/shard_map/ppermute | solution.py:359
  28.2 1.0 %copy-start.6 = (bf16[64,4096]{1,0:T(8,128)(2,1)}, bf16[64,4096]{1,0:T(8,128)(2,1)S(1)}, u32[]{:S(2)}) copy-start(bf16[64,4096]{1,0:T(8,128)(2,1)S(1)} %collective-permute-done.5.refs_5_.refs_7_) | copy-start | bytes 1572868
  29.1 0.6 %copy-start.8 = (bf16[80,256]{1,0:T(8,128)(2,1)}, bf16[80,256]{1,0:T(8,128)(2,1)S(1)}, u32[]{:S(2)}) copy-start(bf16[80,256]{1,0:T(8,128)(2,1)S(1)} %get-tuple-element.26.refs_1_) | copy-start | bytes 122884
  29.7 0.6 %copy-start.10 = (bf16[160,64]{1,0:T(8,128)(2,1)}, bf16[160,64]{1,0:T(8,128)(2,1)S(1)}, u32[]{:S(2)}) copy-start(bf16[160,64]{1,0:T(8,128)(2,1)S(1)} %get-tuple-element.25.refs_0_) | copy-start | bytes 61444
  41.2 2.2 %copy-start.9 = (bf16[80,256]{1,0:T(8,128)(2,1)S(1)}, bf16[80,256]{1,0:T(8,128)(2,1)}, u32[]{:S(2)}) copy-start(bf16[80,256]{1,0:T(8,128)(2,1)} %copy-done.8) | copy-start | bytes 122884
  41.2 2.2 %copy-start.11 = (bf16[160,64]{1,0:T(8,128)(2,1)S(1)}, bf16[160,64]{1,0:T(8,128)(2,1)}, u32[]{:S(2)}) copy-start(bf16[160,64]{1,0:T(8,128)(2,1)} %copy-done.10) | copy-start | bytes 61444
  41.2 6.9 %collective-permute-start.12 = (bf16[16,512]{1,0:T(8,128)(2,1)S(1)}, bf16[16,512]{1,0:T(8,128)(2,1)S(1)}, u32[]{:S(2)}, u32[]{:S(2)}) collective-permute-start(bf16[16,512]{1,0:T(8,128)(2,1)S(1)} %reduce_sum.12), channel_id=1, source_target_pairs={{0,16},{8,24},{16,0},{24,8},{1,17},{9,25},{17,1},{25,9},{2,18},{10... | collective-permute-start | bytes 49160 | tf_op jit(solution)/shard_map/ppermute | solution.py:359
  41.8 6.3 %collective-permute-start.11 = (bf16[16,512]{1,0:T(8,128)(2,1)S(1)}, bf16[16,512]{1,0:T(8,128)(2,1)S(1)}, u32[]{:S(2)}, u32[]{:S(2)}) collective-permute-start(bf16[16,512]{1,0:T(8,128)(2,1)S(1)} %reduce_sum.12), channel_id=1, source_target_pairs={{0,8},{8,0},{16,24},{24,16},{1,9},{9,1},{17,25},{25,17},{2,10},{10... | collective-permute-start | bytes 49160 | tf_op jit(solution)/shard_map/ppermute | solution.py:359
  41.8 6.3 %collective-permute-start.10 = (bf16[16,512]{1,0:T(8,128)(2,1)S(1)}, bf16[16,512]{1,0:T(8,128)(2,1)S(1)}, u32[]{:S(2)}, u32[]{:S(2)}) collective-permute-start(bf16[16,512]{1,0:T(8,128)(2,1)S(1)} %reduce_sum.12), channel_id=1, source_target_pairs={{0,24},{8,16},{16,8},{24,0},{1,25},{9,17},{17,9},{25,1},{2,26},{10... | collective-permute-start | bytes 49160 | tf_op jit(solution)/shard_map/ppermute | solution.py:359
  43.4 1.0 %copy-start.5 = (bf16[64,4096]{1,0:T(8,128)(2,1)S(1)}, bf16[64,4096]{1,0:T(8,128)(2,1)}, u32[]{:S(2)}) copy-start(bf16[64,4096]{1,0:T(8,128)(2,1)} %copy-done.4) | copy-start | bytes 1572868
  44.5 1.0 %copy-start.7 = (bf16[64,4096]{1,0:T(8,128)(2,1)S(1)}, bf16[64,4096]{1,0:T(8,128)(2,1)}, u32[]{:S(2)}) copy-start(bf16[64,4096]{1,0:T(8,128)(2,1)} %copy-done.6) | copy-start | bytes 1572868
